TPU v7x, 32 devices: a whole 2x2x4 slice. The times are simulated.
32 devices in a mesh: groups: 2 (over y), vox: 4 (over z), spot: 2 (over x), rep: 2 (over core).
Axes of the slice: x: 2, y: 2, z: 4, core: 2. Of those that a mesh axis runs over, the one named last changes fastest.
Arguments:
- dose_blocks: bfloat16 [128, 2, 48, 128, 128], P(('groups', 'vox'), 'spot', 'rep'), parts along dimension 0, may hold values from -0.078125 to 0.078125
- block_cols: int32 [128, 2, 48], P(('groups', 'vox'), 'spot', 'rep'), parts along dimension 0, may hold values from 0 to 63, as said below
- block_exps: int32 [128, 2, 48], P(('groups', 'vox'), 'spot', 'rep'), parts along dimension 0, may hold values from -1 to 1
- live_counts: int32 [128, 2], P(('groups', 'vox'), 'spot'), parts along dimension 0, may hold values from 1 to 48
- labels: int32 [16384], P(('groups', 'vox', 'spot', 'rep')), parts along dimension 0, may hold values from 0 to 7
- upper_dose: float32 [16], P('groups'), parts along dimension 0, may hold values from -0.5 to 1
- upper_weight: float32 [16], P('groups'), parts along dimension 0, may hold values from 0.5 to 2
- lower_dose: float32 [16], P('groups'), parts along dimension 0, may hold values from -1.5 to 0
- lower_weight: float32 [16], P('groups'), parts along dimension 0, may hold values from 0.5 to 2
- initial_spot_weights: float32 [32, 2, 8192], P('groups', 'spot', 'vox'), parts along dimension 0, may hold values from 0.5 to 2
Outputs:
- final_weights: float32 [32, 2, 8192], P('groups', 'spot', 'vox'), parts along dimension 0
- last_gradient: float32 [32, 2, 8192], P('groups', 'spot', 'vox'), parts along dimension 0
There are 2 independent parts, one for each index of `groups`. A program takes and returns all parts, laid end to end along the dimension named above; each array names one. Nothing has to cross between parts.
Inputs may be any that keep to these rules, and one draw needn't show every extreme that they name: `block_cols`: within one block-row and spot range all 48 entries differ.
All inputs are finite; a program needn't handle non-finite values.
Results may differ from a plain program's by a relative error of at most 0.0075.
The roundings to bfloat16 on the way count: a program that leaves them out, or rounds other values in their place, can miss the bound.
Values may be sent and summed in bfloat16 or wider, within the bound.
No kernel may reach another device: no remote copies, remote signals or barrier semaphores. Data moves between devices by JAX's collectives and lax.ppermute only.
A program may use at most 64 MiB of HBM per device.

v0:
```python
import jax
import jax.numpy as jnp
from jax import lax
from jax.sharding import PartitionSpec as P

ITERS = 4


def risk_slope(dose, labels, upper_dose, upper_weight, lower_dose, lower_weight):
    onehot = (labels[:, None] == jnp.arange(upper_dose.shape[0], dtype=jnp.int32)[None, :]).astype(
        jnp.float32
    )
    table = jnp.stack([upper_dose, upper_weight, lower_dose, lower_weight], axis=1)
    params = jnp.dot(onehot, table, precision=lax.Precision.HIGHEST)
    slope = params[:, 1] * jax.nn.sigmoid(4.0 * (dose - params[:, 0])) - params[
        :, 3
    ] * jax.nn.sigmoid(4.0 * (params[:, 2] - dose))
    return slope.astype(jnp.bfloat16)


def per_device(
    dose_blocks,
    block_cols,
    block_exps,
    live_counts,
    labels,
    upper_dose,
    upper_weight,
    lower_dose,
    lower_weight,
    initial_spot_weights,
):
    matrix_tiles = dose_blocks[:, 0]
    cols = block_cols[:, 0]
    rows_here, slots_here, width = (
        matrix_tiles.shape[0],
        matrix_tiles.shape[1],
        matrix_tiles.shape[-1],
    )
    weight_rows = initial_spot_weights.shape[0]
    position = lax.axis_index("rep") * slots_here + jnp.arange(slots_here, dtype=jnp.int32)
    factor = jnp.where(
        position[None, :] < live_counts,
        jnp.exp2(block_exps[:, 0].astype(jnp.float32)),
        jnp.float32(0.0),
    )
    weights = initial_spot_weights[:, 0, :]
    objective_gradient = jnp.zeros_like(weights)
    for step in range(ITERS):
        whole = lax.all_gather(weights.astype(jnp.bfloat16), "vox", axis=1, tiled=True)
        columns = whole.shape[1] // width
        selected_spots = jnp.take(whole.reshape(weight_rows, columns, width), cols, axis=1)
        dose_product = jnp.einsum(
            "jbks,bkvs->bkjv", selected_spots, matrix_tiles, preferred_element_type=jnp.float32
        )
        partial_value = jnp.einsum(
            "bkjv,bk->jbv", dose_product, factor, precision=lax.Precision.HIGHEST
        ).reshape(weight_rows, rows_here * width)
        dose = lax.psum_scatter(partial_value, ("spot", "rep"), scatter_dimension=1, tiled=True)
        slope = risk_slope(dose, labels, upper_dose, upper_weight, lower_dose, lower_weight)
        slope_all = lax.all_gather(slope, ("spot", "rep"), axis=1, tiled=True)
        slope_rows = slope_all.reshape(weight_rows, rows_here, width)
        back = (
            jnp.einsum(
                "jbv,bkvs->bkjs", slope_rows, matrix_tiles, preferred_element_type=jnp.float32
            )
            * factor[:, :, None, None]
        )
        summed = jax.ops.segment_sum(
            back.reshape(rows_here * slots_here, weight_rows, width),
            cols.reshape(-1),
            num_segments=columns,
        )
        local_grad = jnp.transpose(summed, (1, 0, 2)).reshape(weight_rows, columns * width)
        objective_gradient = lax.psum_scatter(local_grad, "vox", scatter_dimension=1, tiled=True)
        objective_gradient = lax.psum(objective_gradient, "rep")
        weights = jnp.maximum(weights - 0.5 * objective_gradient, 0.0)
    return (weights[:, None, :], objective_gradient[:, None, :])


def solution(mesh):
    placed = (
        P(("groups", "vox"), "spot", "rep", None, None),
        P(("groups", "vox"), "spot", "rep"),
        P(("groups", "vox"), "spot", "rep"),
        P(("groups", "vox"), "spot"),
        P(("groups", "vox", "spot", "rep")),
        P("groups"),
        P("groups"),
        P("groups"),
        P("groups"),
        P("groups", "spot", "vox"),
    )
    return jax.shard_map(
        per_device,
        mesh=mesh,
        in_specs=placed,
        out_specs=(P("groups", "spot", "vox"), P("groups", "spot", "vox")),
        check_vma=False,
    )
```

profile of v0, /device:TPU:0, one launch (start us, length us, event | category | flops | bytes accessed | tf_op | source)
XLA Modules:
  0.0 568.9 jit_solution(18397215666638990981)
XLA Ops:
  9.7 15.6 %all_gather.24 = bf16[16,8192]{1,0:T(8,128)(2,1)S(1)} all-gather(bf16[16,2048]{1,0:T(8,128)(2,1)S(1)} %bitcast.194), channel_id=1, replica_groups=mesh['groups'=2,'vox'=4,'spot'=2,'rep'=2] {'vox'}, dimensions={1}, use_global_device_ids=true | all-gather | bytes 327680 | tf_op jit(solution)/shard_map/all_gather | solution.py:50
  28.0 9.2 %fusion.14 = f32[16,24,16,128]{3,2,1,0:T(8,128)S(1)} fusion(bf16[16,1,24,128,128]{4,3,2,1,0:T(8,128)(2,1)} %param.12, bf16[16,24,16,128]{3,2,1,0:T(8,128)(2,1)S(1)} %bitcast.174, pred[16,24]{1,0:T(8,128)(4,1)S(1)} %compare_and_fusion), kind=kOutput, calls=%fused_computation.22 | convolution fusion | flops 202113024 | bytes 17301888 | tf_op jit(solution)/shard_map/jbks,bkvs->bkjv/dot_general | solution.py:53
  42.4 19.5 %reduce-scatter.9.cloned.1.call-done = f32[16,512]{1,0:T(8,128)} async-done(((f32[16,2048]{1,0:T(8,128)}), f32[16,512]{1,0:T(8,128)}) %reduce-scatter.9.cloned.1.call-update) | async-done | bytes 32784 | tf_op jit(solution)/shard_map/reduce_scatter | solution.py:59
  62.8 5.2 all_gather.25
  68.0 8.0 %fusion.24 = f32[16,16,24,128]{3,1,2,0:T(8,128)} fusion(bf16[16,1,24,128,128]{4,3,2,1,0:T(8,128)(2,1)} %param.12, f32[16,24]{1,0:T(8,128)S(1)} %compare_select_fusion.1, bf16[16,16,128,1]{2,1,0,3:T(8,128)(2,1)S(1)} %bitcast.191), kind=kOutput, calls=%fused_computation.32 | convolution fusion | flops 202113024 | bytes 15795712 | tf_op jit(solution)/shard_map/jbv,bkvs->bkjs/dot_general | solution.py:64
  76.1 30.5 %scatter_fusion = f32[64,16,128]{2,1,0:T(8,128)S(1)} fusion(f32[64,16,128]{2,1,0:T(8,128)S(1)} %broadcast.56.clone.1, s32[384]{0:T(512)S(1)} %reshape.173, f32[384,16,128]{2,1,0:T(8,128)} %bitcast.170), kind=kCustom, calls=%fused_computation.4 | custom fusion | flops 786432 | bytes 9438720 | tf_op jit(solution)/shard_map/scatter-add | solution.py:69
  107.5 21.8 %reduce-scatter.11.cloned.1.call-done = f32[16,2048]{1,0:T(8,128)} async-done(((f32[16,8192]{1,0:T(8,128)}), f32[16,2048]{1,0:T(8,128)}) %reduce-scatter.11.cloned.1.call-update) | async-done | bytes 131088 | tf_op jit(solution)/shard_map/reduce_scatter | solution.py:75
  129.3 18.6 %all-reduce.5.cloned.1.call-done = f32[16,2048]{1,0:T(8,128)} async-done(((f32[16,2048]{1,0:T(8,128)}), f32[16,2048]{1,0:T(8,128)}) %all-reduce.5.cloned.1.call-update) | async-done | bytes 131088 | tf_op jit(solution)/shard_map/psum | solution.py:76
  148.9 14.4 %all_gather.26 = bf16[16,8192]{1,0:T(8,128)(2,1)S(1)} all-gather(bf16[16,2048]{1,0:T(8,128)(2,1)S(1)} %get-tuple-element.5), channel_id=1, replica_groups=mesh['groups'=2,'vox'=4,'spot'=2,'rep'=2] {'vox'}, dimensions={1}, use_global_device_ids=true | all-gather | bytes 327680 | tf_op jit(solution)/shard_map/all_gather | solution.py:50
  165.3 9.2 %fusion.10 = f32[16,24,16,128]{3,2,1,0:T(8,128)S(1)} fusion(bf16[16,1,24,128,128]{4,3,2,1,0:T(8,128)(2,1)} %param.12, bf16[16,24,16,128]{3,2,1,0:T(8,128)(2,1)S(1)} %bitcast.175, pred[16,24]{1,0:T(8,128)(4,1)S(1)} %compare_and_fusion), kind=kOutput, calls=%fused_computation.18 | convolution fusion | flops 202113024 | bytes 17301888 | tf_op jit(solution)/shard_map/jbks,bkvs->bkjv/dot_general | solution.py:53
  177.9 21.1 %reduce-scatter.13.cloned.1.call-done = f32[16,512]{1,0:T(8,128)} async-done(((f32[16,2048]{1,0:T(8,128)}), f32[16,512]{1,0:T(8,128)}) %reduce-scatter.13.cloned.1.call-update) | async-done | bytes 32784 | tf_op jit(solution)/shard_map/reduce_scatter | solution.py:59
  199.8 5.2 all_gather.27
  205.0 8.0 %fusion.27 = f32[16,16,24,128]{3,1,2,0:T(8,128)} fusion(bf16[16,1,24,128,128]{4,3,2,1,0:T(8,128)(2,1)} %param.12, f32[16,24]{1,0:T(8,128)S(1)} %compare_select_fusion.1, bf16[16,16,128,1]{2,1,0,3:T(8,128)(2,1)S(1)} %bitcast.192), kind=kOutput, calls=%fused_computation.33 | convolution fusion | flops 202113024 | bytes 15795712 | tf_op jit(solution)/shard_map/jbv,bkvs->bkjs/dot_general | solution.py:64
  213.1 30.5 %scatter_fusion.1 = f32[64,16,128]{2,1,0:T(8,128)S(1)} fusion(f32[64,16,128]{2,1,0:T(8,128)S(1)} %broadcast.56.clone.2, s32[384]{0:T(512)S(1)} %reshape.173, f32[384,16,128]{2,1,0:T(8,128)} %bitcast.171), kind=kCustom, calls=%fused_computation.5 | custom fusion | flops 786432 | bytes 9438720 | tf_op jit(solution)/shard_map/scatter-add | solution.py:69
  244.5 21.8 %reduce-scatter.15.cloned.1.call-done = f32[16,2048]{1,0:T(8,128)} async-done(((f32[16,8192]{1,0:T(8,128)}), f32[16,2048]{1,0:T(8,128)}) %reduce-scatter.15.cloned.1.call-update) | async-done | bytes 131088 | tf_op jit(solution)/shard_map/reduce_scatter | solution.py:75
  266.4 18.3 %all-reduce.7.cloned.1.call-done = f32[16,2048]{1,0:T(8,128)} async-done(((f32[16,2048]{1,0:T(8,128)}), f32[16,2048]{1,0:T(8,128)}) %all-reduce.7.cloned.1.call-update) | async-done | bytes 131088 | tf_op jit(solution)/shard_map/psum | solution.py:76
  285.6 14.5 %all_gather.28 = bf16[16,8192]{1,0:T(8,128)(2,1)S(1)} all-gather(bf16[16,2048]{1,0:T(8,128)(2,1)S(1)} %fusion.59), channel_id=1, replica_groups=mesh['groups'=2,'vox'=4,'spot'=2,'rep'=2] {'vox'}, dimensions={1}, use_global_device_ids=true | all-gather | bytes 327680 | tf_op jit(solution)/shard_map/all_gather | solution.py:50
  302.0 9.2 %fusion.6 = f32[16,24,16,128]{3,2,1,0:T(8,128)S(1)} fusion(bf16[16,1,24,128,128]{4,3,2,1,0:T(8,128)(2,1)} %param.12, bf16[16,24,16,128]{3,2,1,0:T(8,128)(2,1)S(1)} %bitcast.176, pred[16,24]{1,0:T(8,128)(4,1)S(1)} %compare_and_fusion), kind=kOutput, calls=%fused_computation.14 | convolution fusion | flops 202113024 | bytes 17301888 | tf_op jit(solution)/shard_map/jbks,bkvs->bkjv/dot_general | solution.py:53
  314.7 21.1 %reduce-scatter.17.cloned.1.call-done = f32[16,512]{1,0:T(8,128)} async-done(((f32[16,2048]{1,0:T(8,128)}), f32[16,512]{1,0:T(8,128)}) %reduce-scatter.17.cloned.1.call-update) | async-done | bytes 32784 | tf_op jit(solution)/shard_map/reduce_scatter | solution.py:59
  336.6 5.2 all_gather.29
  341.8 8.0 %fusion.30 = f32[16,16,24,128]{3,1,2,0:T(8,128)} fusion(bf16[16,1,24,128,128]{4,3,2,1,0:T(8,128)(2,1)} %param.12, f32[16,24]{1,0:T(8,128)S(1)} %compare_select_fusion.1, bf16[16,16,128,1]{2,1,0,3:T(8,128)(2,1)S(1)} %bitcast.193), kind=kOutput, calls=%fused_computation.34 | convolution fusion | flops 202113024 | bytes 15795712 | tf_op jit(solution)/shard_map/jbv,bkvs->bkjs/dot_general | solution.py:64
  349.9 30.5 %scatter_fusion.2 = f32[64,16,128]{2,1,0:T(8,128)S(1)} fusion(f32[64,16,128]{2,1,0:T(8,128)S(1)} %broadcast.56.clone, s32[384]{0:T(512)S(1)} %reshape.173, f32[384,16,128]{2,1,0:T(8,128)} %bitcast.172), kind=kCustom, calls=%fused_computation.6 | custom fusion | flops 786432 | bytes 9438720 | tf_op jit(solution)/shard_map/scatter-add | solution.py:69
  381.3 21.8 %reduce-scatter.19.cloned.1.call-done = f32[16,2048]{1,0:T(8,128)} async-done(((f32[16,8192]{1,0:T(8,128)}), f32[16,2048]{1,0:T(8,128)}) %reduce-scatter.19.cloned.1.call-update) | async-done | bytes 131088 | tf_op jit(solution)/shard_map/reduce_scatter | solution.py:75
  403.2 18.5 %all-reduce.9.cloned.1.call-done = f32[16,2048]{1,0:T(8,128)} async-done(((f32[16,2048]{1,0:T(8,128)}), f32[16,2048]{1,0:T(8,128)}) %all-reduce.9.cloned.1.call-update) | async-done | bytes 131088 | tf_op jit(solution)/shard_map/psum | solution.py:76
  422.7 14.5 %all_gather.30 = bf16[16,8192]{1,0:T(8,128)(2,1)S(1)} all-gather(bf16[16,2048]{1,0:T(8,128)(2,1)S(1)} %fusion.72), channel_id=1, replica_groups=mesh['groups'=2,'vox'=4,'spot'=2,'rep'=2] {'vox'}, dimensions={1}, use_global_device_ids=true | all-gather | bytes 327680 | tf_op jit(solution)/shard_map/all_gather | solution.py:50
  439.1 9.2 %fusion.2 = f32[16,24,16,128]{3,2,1,0:T(8,128)S(1)} fusion(bf16[16,1,24,128,128]{4,3,2,1,0:T(8,128)(2,1)} %param.12, bf16[16,24,16,128]{3,2,1,0:T(8,128)(2,1)S(1)} %bitcast.173, pred[16,24]{1,0:T(8,128)(4,1)S(1)} %compare_and_fusion), kind=kOutput, calls=%fused_computation.10 | convolution fusion | flops 202113024 | bytes 17301888 | tf_op jit(solution)/shard_map/jbks,bkvs->bkjv/dot_general | solution.py:53
  451.7 21.1 %reduce-scatter.21.cloned.1.call-done = f32[16,512]{1,0:T(8,128)} async-done(((f32[16,2048]{1,0:T(8,128)}), f32[16,512]{1,0:T(8,128)}) %reduce-scatter.21.cloned.1.call-update) | async-done | bytes 32784 | tf_op jit(solution)/shard_map/reduce_scatter | solution.py:59
  473.7 5.2 all_gather.31
  478.9 8.0 %fusion.33 = f32[16,16,24,128]{3,1,2,0:T(8,128)} fusion(bf16[16,1,24,128,128]{4,3,2,1,0:T(8,128)(2,1)} %param.12, f32[16,24]{1,0:T(8,128)S(1)} %compare_select_fusion.1, bf16[16,16,128,1]{2,1,0,3:T(8,128)(2,1)S(1)} %bitcast.190), kind=kOutput, calls=%fused_computation.35 | convolution fusion | flops 202113024 | bytes 15795712 | tf_op jit(solution)/shard_map/jbv,bkvs->bkjs/dot_general | solution.py:64
  487.0 30.5 %scatter_fusion.3 = f32[64,16,128]{2,1,0:T(8,128)S(1)} fusion(f32[64,16,128]{2,1,0:T(8,128)S(1)} %broadcast.56, s32[384]{0:T(512)S(1)} %reshape.173, f32[384,16,128]{2,1,0:T(8,128)} %bitcast.169), kind=kCustom, calls=%fused_computation.7 | custom fusion | flops 786432 | bytes 9438720 | tf_op jit(solution)/shard_map/scatter-add | solution.py:69
  518.4 21.8 %reduce-scatter.23.cloned.1.call-done = f32[16,2048]{1,0:T(8,128)} async-done(((f32[16,8192]{1,0:T(8,128)}), f32[16,2048]{1,0:T(8,128)}) %reduce-scatter.23.cloned.1.call-update) | async-done | bytes 131088 | tf_op jit(solution)/shard_map/reduce_scatter | solution.py:75
  540.2 18.3 %all-reduce.11.cloned.1.call-done = f32[16,2048]{1,0:T(8,128)} async-done(((f32[16,2048]{1,0:T(8,128)}), f32[16,2048]{1,0:T(8,128)}) %all-reduce.11.cloned.1.call-update) | async-done | bytes 131088 | tf_op jit(solution)/shard_map/psum | solution.py:76
  (99 shorter events, 39.6 us)
Async XLA Ops:
  7.2 54.8 %reduce-scatter.9.cloned.1.call-start = ((), (), s32[]{:S(2)}) async-start(), calls=%async_computation.8 | async-start | bytes 163840 | tf_op jit(solution)/shard_map/reduce_scatter | solution.py:59
  28.0 9.3 %copy-start.4 = (s32[16,1]{0,1:T(1,128)S(1)}, s32[16,1]{0,1:T(1,128)}, u32[]{:S(2)}) copy-start(s32[16,1]{0,1:T(1,128)} %param.15) | copy-start | bytes 196
  37.2 3.5 copy-start.5
  37.2 3.5 copy-start.6
  37.2 3.5 copy-start.7
  37.3 3.5 copy-start.8
  37.3 3.5 copy-start.9
  37.3 4.4 copy-start.3
  40.7 88.6 %reduce-scatter.11.cloned.1.call-start = ((), (), s32[]{:S(2)}) async-start(), calls=%async_computation.9 | async-start | bytes 655360 | tf_op jit(solution)/shard_map/reduce_scatter | solution.py:75
  76.1 71.8 %copy-start.2 = (f32[16,1,2048]{2,1,0:T(1,128)S(1)}, f32[16,1,2048]{2,1,0:T(1,128)}, u32[]{:S(2)}) copy-start(f32[16,1,2048]{2,1,0:T(1,128)} %param.21) | copy-start | bytes 393220
  107.4 40.5 %all-reduce.5.cloned.1.call-start = ((), (), s32[]{:S(2)}) async-start(), calls=%async_computation.10 | async-start | bytes 262144 | tf_op jit(solution)/shard_map/psum | solution.py:76
  129.3 69.7 %reduce-scatter.13.cloned.1.call-start = ((), (), s32[]{:S(2)}) async-start(), calls=%async_computation.11 | async-start | bytes 163840 | tf_op jit(solution)/shard_map/reduce_scatter | solution.py:59
  177.8 88.5 %reduce-scatter.15.cloned.1.call-start = ((), (), s32[]{:S(2)}) async-start(), calls=%async_computation.12 | async-start | bytes 655360 | tf_op jit(solution)/shard_map/reduce_scatter | solution.py:75
  244.4 40.2 %all-reduce.7.cloned.1.call-start = ((), (), s32[]{:S(2)}) async-start(), calls=%async_computation.13 | async-start | bytes 262144 | tf_op jit(solution)/shard_map/psum | solution.py:76
  266.3 69.4 %reduce-scatter.17.cloned.1.call-start = ((), (), s32[]{:S(2)}) async-start(), calls=%async_computation.14 | async-start | bytes 163840 | tf_op jit(solution)/shard_map/reduce_scatter | solution.py:59
  314.6 88.5 %reduce-scatter.19.cloned.1.call-start = ((), (), s32[]{:S(2)}) async-start(), calls=%async_computation.15 | async-start | bytes 655360 | tf_op jit(solution)/shard_map/reduce_scatter | solution.py:75
  349.9 71.9 %copy-start = (f32[16,2048]{1,0:T(8,128)S(1)}, f32[16,2048]{1,0:T(8,128)}, u32[]{:S(2)}) copy-start(f32[16,2048]{1,0:T(8,128)} %all-reduce.7.cloned.1.call-done) | copy-start | bytes 393220
  381.2 40.5 %all-reduce.9.cloned.1.call-start = ((), (), s32[]{:S(2)}) async-start(), calls=%async_computation.16 | async-start | bytes 262144 | tf_op jit(solution)/shard_map/psum | solution.py:76
  403.1 69.7 %reduce-scatter.21.cloned.1.call-start = ((), (), s32[]{:S(2)}) async-start(), calls=%async_computation.17 | async-start | bytes 163840 | tf_op jit(solution)/shard_map/reduce_scatter | solution.py:59
  451.7 88.5 %reduce-scatter.23.cloned.1.call-start = ((), (), s32[]{:S(2)}) async-start(), calls=%async_computation.18 | async-start | bytes 655360 | tf_op jit(solution)/shard_map/reduce_scatter | solution.py:75
  487.0 71.6 %copy-start.1 = (f32[16,2048]{1,0:T(8,128)S(1)}, f32[16,2048]{1,0:T(8,128)}, u32[]{:S(2)}) copy-start(f32[16,2048]{1,0:T(8,128)} %all-reduce.9.cloned.1.call-done) | copy-start | bytes 393220
  518.3 40.2 %all-reduce.11.cloned.1.call-start = ((), (), s32[]{:S(2)}) async-start(), calls=%async_computation.19 | async-start | bytes 262144 | tf_op jit(solution)/shard_map/psum | solution.py:76
Sparse Core Ops, SparseCore 0:
  40.8 21.0 reduce-scatter.8
  107.5 21.6 reduce-scatter.10
  131.7 16.1 all-reduce.4
  177.9 21.0 reduce-scatter.12
  244.6 21.7 reduce-scatter.14
  268.5 16.1 all-reduce.6
  314.7 21.0 reduce-scatter.16
  381.3 21.7 reduce-scatter.18
  405.5 16.1 all-reduce.8
  451.8 21.0 reduce-scatter.20
  518.4 21.7 reduce-scatter.22
  542.4 16.1 all-reduce.10
where the time goes:
time: 571 us; the launch traced here: 569 us
  waiting for transfers between devices  244 us (43%)
  other arithmetic  132 us (23%)
  blocking collectives  80 us (14%)
  matrix products  79.4 us (14%)
  local copies, waits for them, and re-layouts  18.5 us (3%)
  between operations  14.6 us (3%)
    scatter-add x4, other arithmetic, per_device(): jax.ops.segment_sum(back.reshape(rows_here * slots_here, weight_rows, wid...  122 us
    reduce_scatter x4, waiting for transfers between devices, per_device(): lax.psum_scatter(local_grad, 'vox', scatter_dimension=1, tiled=True)  87.3 us
    reduce_scatter x4, waiting for transfers between devices, per_device(): lax.psum_scatter(partial_value, ('spot', 'rep'), scatter_dimension=1, til...  82.9 us
    psum x4, waiting for transfers between devices, per_device(): objective_gradient = lax.psum(objective_gradient, 'rep')  73.7 us
    all_gather x4, blocking collectives, per_device(): lax.all_gather(weights.astype(jnp.bfloat16), 'vox', axis=1, tiled=True)  59 us
    dot_general x4, matrix products, per_device(): jnp.einsum('jbks,bkvs->bkjv', selected_spots, matrix_tiles, preferred_ele...  36.9 us
    dot_general x4, matrix products, per_device(): jnp.einsum('jbv,bkvs->bkjs', slope_rows, matrix_tiles, preferred_element_...  32 us
    all_gather x4, blocking collectives, per_device(): slope_all = lax.all_gather(slope, ('spot', 'rep'), axis=1, tiled=True)  21 us
  transfers between devices with their start and end apart: 12, of which 12 were waited for; matrix products, arithmetic and copies ran while one was open for 0% of the time, Pallas kernels for 0%

commit v1 on v0

v1 whole, which is shorter than its diff:
```python
import functools

import jax
import jax.numpy as jnp
from jax import lax
from jax.experimental import pallas as pl
from jax.experimental.pallas import tpu as pltpu
from jax.sharding import PartitionSpec as P

ITERS = 4
F32 = jnp.float32
BF16 = jnp.bfloat16
PARAMS = pltpu.CompilerParams(vmem_limit_bytes=20 * 2**20)


def in_vmem():
    return pl.BlockSpec(memory_space=pltpu.VMEM)


def in_smem():
    return pl.BlockSpec(memory_space=pltpu.SMEM)


def held(array):
    return pltpu.with_memory_space_constraint(array, pltpu.VMEM)


def load_kernel(pieces, stored, kept, turned, sems):
    size = stored.shape[0] // pieces
    copies = [
        pltpu.make_async_copy(
            stored.at[pl.ds(i * size, size)], kept.at[pl.ds(i * size, size)], sems.at[i]
        )
        for i in range(pieces)
    ]
    for copy in copies:
        copy.start()
    step = 8 if size % 8 == 0 else 1
    for i, copy in enumerate(copies):
        copy.wait()

        def turn(t, carry, i=i):
            for u in range(step):
                n = i * size + t * step + u
                turned[n] = kept[n].T
            return carry

        lax.fori_loop(0, size // step, turn, 0)


def load_matrix(tiles):
    pieces = 16 if tiles.shape[0] % 16 == 0 else 1
    return pl.pallas_call(
        functools.partial(load_kernel, pieces),
        in_specs=[pl.BlockSpec(memory_space=pltpu.HBM)],
        out_specs=[in_vmem(), in_vmem()],
        out_shape=[pltpu.VMEM(tiles.shape, tiles.dtype)] * 2,
        scratch_shapes=[pltpu.SemaphoreType.DMA((pieces,))],
        compiler_params=PARAMS,
        cost_estimate=pl.CostEstimate(
            flops=0, bytes_accessed=2 * tiles.size * 2, transcendentals=0
        ),
        name="load_matrix",
    )(tiles)


def forward_kernel(slots, index, *refs):
    pieces, turned, dose, scaled = refs[:-3], refs[-3], refs[-2], refs[-1]
    columns = (scaled.shape[0] - 1) // 3
    at = 0
    for piece in pieces:
        n = piece.shape[0]
        values = piece[...]
        scaled[at : at + n] = values * BF16(0.5)
        scaled[columns + at : columns + at + n] = values
        scaled[2 * columns + at : 2 * columns + at + n] = values * BF16(2.0)
        at += n
    scaled[3 * columns] = jnp.zeros(scaled.shape[1:], BF16)
    rows = dose.shape[0]
    unroll = 4 if rows % 4 == 0 else 1

    def some_rows(t, carry):
        for u in range(unroll):
            b = t * unroll + u
            left = jnp.concatenate([scaled[index[b * slots + k]] for k in range(slots)], axis=1)
            right = turned[pl.ds(b * slots, slots)]
            right = right.reshape(slots * right.shape[1], right.shape[2])
            dose[b] = jnp.dot(left, right, preferred_element_type=F32)
        return carry

    lax.fori_loop(0, rows // unroll, some_rows, 0)


def forward(index, pieces, turned, rows, slots):
    columns = sum(p.shape[0] for p in pieces)
    weightings, width = pieces[0].shape[1:]
    return pl.pallas_call(
        functools.partial(forward_kernel, slots),
        in_specs=[in_smem()] + [in_vmem()] * (len(pieces) + 1),
        out_specs=in_vmem(),
        out_shape=jax.ShapeDtypeStruct((rows, weightings, width), F32),
        scratch_shapes=[pltpu.VMEM((3 * columns + 1, weightings, width), BF16)],
        compiler_params=PARAMS,
        name="forward",
    )(index, *pieces, held(turned))


def backward_kernel(slots, index, factor, own, other, levels, kept, far, near, slope, total):
    dose = own[...] + other[...]
    upper_dose, upper_weight, lower_dose, lower_weight = (levels[i] for i in range(4))
    slope[...] = (
        upper_weight * jax.nn.sigmoid(4.0 * (dose - upper_dose))
        - lower_weight * jax.nn.sigmoid(4.0 * (lower_dose - dose))
    ).astype(BF16)
    total[...] = jnp.zeros_like(total)
    rows = own.shape[0]
    width = kept.shape[-1]
    unroll = 4 if rows % 4 == 0 else 1
    group = 12 if slots % 12 == 0 else 1

    def some_rows(t, carry):
        for u in range(unroll):
            b = t * unroll + u
            left = slope[b]
            for k0 in range(0, slots, group):
                places = [b * slots + k0 + k for k in range(group)]
                right = jnp.concatenate([kept[p] for p in places], axis=1)
                product = jnp.dot(left, right, preferred_element_type=F32)
                columns = [index[p] for p in places]
                old = [total[c] for c in columns]
                for k, p in enumerate(places):
                    part = product[:, k * width : (k + 1) * width]
                    total[columns[k]] = old[k] + part * factor[p]
        return carry

    lax.fori_loop(0, rows // unroll, some_rows, 0)
    half = near.shape[0]
    near[...] = total[:half]
    far[...] = total[half:]


def backward(index, factor, own, other, levels, kept, columns, slots):
    rows, weightings, width = own.shape
    half = (columns // 2, weightings, width)
    return pl.pallas_call(
        functools.partial(backward_kernel, slots),
        in_specs=[in_smem()] * 2 + [in_vmem()] * 4,
        out_specs=[in_vmem()] * 2,
        out_shape=[jax.ShapeDtypeStruct(half, F32)] * 2,
        scratch_shapes=[
            pltpu.VMEM((rows, weightings, width), BF16),
            pltpu.VMEM((columns, weightings, width), F32),
        ],
        compiler_params=PARAMS,
        name="slope_backward",
    )(index, factor, own, other, levels, held(kept))


def swap(array, axis, size, bit):
    return lax.ppermute(array, axis, [(i, i ^ bit) for i in range(size)])


def per_device(
    sizes,
    dose_blocks,
    block_cols,
    block_exps,
    live_counts,
    labels,
    upper_dose,
    upper_weight,
    lower_dose,
    lower_weight,
    initial_spot_weights,
):
    n_vox, n_spot, n_rep = sizes
    z, x, core = (lax.axis_index(a) for a in ("vox", "spot", "rep"))
    rows, _, slots, width, _ = dose_blocks.shape
    weightings, _, chunk_spots = initial_spot_weights.shape
    chunk = chunk_spots // width
    columns = chunk * n_vox
    vox_bits = n_vox.bit_length() - 1
    top = 1 << (vox_bits - 1)

    mine = core * top + z % top
    places = block_cols[:, 0] ^ (mine * chunk)
    position = core * slots + jnp.arange(slots, dtype=jnp.int32)
    live = position[None, :] < live_counts
    exps = block_exps[:, 0]
    factor = jnp.where(live, jnp.where(exps < 0, 0.5, jnp.where(exps > 0, 2.0, 1.0)), 0.0)
    factor = factor.astype(F32).reshape(-1)
    forward_index = jnp.where(live, (exps + 1) * columns + places, 3 * columns).reshape(-1)
    places = places.reshape(-1)

    weights = initial_spot_weights[:, 0].reshape(weightings, chunk, width).transpose(1, 0, 2)
    moves = []
    for to_z in range(n_vox):
        for to_core in range(2):
            from_z, from_core = to_core * top + to_z % top, to_z // top
            moves.append((from_z * 2 + from_core, to_z * 2 + to_core))
    weights = lax.ppermute(weights, ("vox", "rep"), moves)

    kept, turned = load_matrix(dose_blocks.reshape(rows * slots, width, width))

    all_labels = labels
    for axis, size, place in (("rep", n_rep, core), ("spot", n_spot, x)):
        bit = 1
        while bit < size:
            got = swap(all_labels, axis, size, bit)
            first = (place // bit) % 2 == 0
            all_labels = jnp.concatenate(
                [jnp.where(first, all_labels, got), jnp.where(first, got, all_labels)]
            )
            bit *= 2
    all_labels = all_labels.reshape(rows, 1, width)
    table = jnp.stack([upper_dose, upper_weight, lower_dose, lower_weight], axis=0)
    levels = jnp.zeros((4, rows, 1, width), F32)
    for c in range(table.shape[1]):
        levels = jnp.where(all_labels[None] == c, table[:, c][:, None, None, None], levels)

    for step in range(ITERS):
        piece = weights.astype(BF16)
        pieces = [piece]
        for bit in range(vox_bits - 1):
            whole = jnp.concatenate(pieces, axis=0) if len(pieces) > 1 else piece
            pieces = pieces + [swap(whole, "vox", n_vox, 1 << bit)]
        whole = jnp.concatenate(pieces, axis=0) if len(pieces) > 1 else piece
        pieces = [whole, swap(whole, "rep", n_rep, 1)]

        dose = forward(forward_index, pieces, turned, rows, slots)
        dose = dose + swap(dose, "rep", n_rep, 1)
        bit = 1
        while bit < n_spot // 2:
            dose = dose + swap(dose, "spot", n_spot, bit)
            bit *= 2
        other = swap(dose, "spot", n_spot, bit)

        far, near = backward(places, factor, dose, other, levels, kept, columns, slots)
        part = near + swap(far, "rep", n_rep, 1)
        for bit in reversed(range(vox_bits - 1)):
            half = part.shape[0] // 2
            part = part[:half] + swap(part[half:], "vox", n_vox, 1 << bit)
        gradient = part + swap(part, "vox", n_vox, top)
        weights = jnp.maximum(weights - 0.5 * gradient, 0.0)

    both = jnp.stack([weights, gradient])
    both = jnp.where(z // top == core, both, swap(both, "rep", n_rep, 1))
    both = both.transpose(0, 2, 1, 3).reshape(2, weightings, 1, chunk_spots)
    return both[0], both[1]


def solution(mesh):
    placed = (
        P(("groups", "vox"), "spot", "rep", None, None),
        P(("groups", "vox"), "spot", "rep"),
        P(("groups", "vox"), "spot", "rep"),
        P(("groups", "vox"), "spot"),
        P(("groups", "vox", "spot", "rep")),
        P("groups"),
        P("groups"),
        P("groups"),
        P("groups"),
        P("groups", "spot", "vox"),
    )
    sizes = tuple(mesh.shape[a] for a in ("vox", "spot", "rep"))
    return jax.shard_map(
        functools.partial(per_device, sizes),
        mesh=mesh,
        in_specs=placed,
        out_specs=(P("groups", "spot", "vox"), P("groups", "spot", "vox")),
        check_vma=False,
    )
```

time: 571 us -> 160 us (0.28)
  waiting for transfers between devices: 244 us -> 92.5 us
  other arithmetic: 132 us -> 5.2 us
  blocking collectives: 80 us -> 0 us
  matrix products: 79.4 us -> 0 us
  Pallas kernels: 0 us -> 30.2 us
  starting transfers between devices: 0.49 us -> 28.2 us
  local copies, waits for them, and re-layouts: 18.5 us -> 3.05 us
  between operations: 14.6 us -> 1.06 us
    reduce_scatter x8 -> x0, waiting for transfers between devices: 170 us -> none  [the longest x4 87.3 us: per_device(): lax.psum_scatter(local_grad, 'vox', scatter_dimension=1, tiled=True)]
    scatter-add x4 -> x0, other arithmetic: 122 us -> none  [per_device(): jax.ops.segment_sum(back.reshape(rows_here * slots_here, weight_rows, wid...]
    ppermute x0 -> x32, waiting for transfers between devices: none -> 92.5 us  [the longest x31 92.5 us: swap(): return lax.ppermute(array, axis, [(i, i ^ bit) for i in range(size)])]
    all_gather x8 -> x0, blocking collectives: 80 us -> none  [the longest x4 59 us: per_device(): lax.all_gather(weights.astype(jnp.bfloat16), 'vox', axis=1, tiled=True)]
    dot_general x13 -> x0, matrix products: 79.4 us -> none  [the longest x4 36.9 us: per_device(): jnp.einsum('jbks,bkvs->bkjv', selected_spots, matrix_tiles, preferred_ele...]
    psum x4 -> x0, waiting for transfers between devices: 73.7 us -> none  [per_device(): objective_gradient = lax.psum(objective_gradient, 'rep')]
    pallas_call x0 -> x9, Pallas kernels: none -> 30.2 us  [the longest x4 11.5 us: backward(): pl.pallas_call(functools.partial(backward_kernel, slots), in_specs=[in_sm...]
    ppermute x0 -> x32, starting transfers between devices: none -> 28.2 us  [the longest x31 27.5 us: swap(): return lax.ppermute(array, axis, [(i, i ^ bit) for i in range(size)])]
  transfers between devices with their start and end apart: 12 -> 32, of which waited for: 12 -> 28; matrix products, arithmetic and copies ran while one was open for 0% -> 4% of each run, Pallas kernels for 0% -> 6%
where the time goes in v1:
time: 160 us
  waiting for transfers between devices  92.5 us (58%)
  Pallas kernels  30.2 us (19%)
  starting transfers between devices  28.2 us (18%)
  other arithmetic  5.2 us (3%)
  local copies, waits for them, and re-layouts  3.05 us (2%)
    ppermute x31, waiting for transfers between devices, swap(): return lax.ppermute(array, axis, [(i, i ^ bit) for i in range(size)])  92.5 us
    ppermute x31, starting transfers between devices, swap(): return lax.ppermute(array, axis, [(i, i ^ bit) for i in range(size)])  27.5 us
    pallas_call x4, Pallas kernels, backward(): pl.pallas_call(functools.partial(backward_kernel, slots), in_specs=[in_sm...  11.5 us
    pallas_call x4, Pallas kernels, forward(): pl.pallas_call(functools.partial(forward_kernel, slots), in_specs=[in_sme...  11.4 us
    pallas_call x1, Pallas kernels, load_matrix(): pl.pallas_call(functools.partial(load_kernel, pieces), in_specs=[pl.Block...  7.16 us
  transfers between devices with their start and end apart: 32, of which 28 were waited for; matrix products, arithmetic and copies ran while one was open for 4% of the time, Pallas kernels for 6%

profile of v1, /device:TPU:0, one launch (start us, length us, event | category | flops | bytes accessed | tf_op | source)
XLA Modules:
  0.0 160.1 jit_solution(13914825631984976776)
XLA Ops:
  6.9 2.7 %collective-permute-start.1 = (bf16[16,16,128]{2,1,0:T(8,128)(2,1)S(1)}, bf16[16,16,128]{2,1,0:T(8,128)(2,1)S(1)}, u32[]{:S(2)}, u32[]{:S(2)}) collective-permute-start(bf16[16,16,128]{2,1,0:T(8,128)(2,1)S(1)} %convert_element_type.12), channel_id=1, source_target_pairs={{0,4},{4,0},{8,12},{12,8},{1,5},{5,1},{9,13},{13,9},{2,6},{6,2},{1... | collective-permute-start | bytes 196616 | tf_op jit(solution)/shard_map/ppermute | solution.py:160
  10.2 1.6 collective-permute-done.1
  11.8 3.3 %collective-permute-start.2 = (bf16[32,16,128]{2,1,0:T(8,128)(2,1)S(1)}, bf16[32,16,128]{2,1,0:T(8,128)(2,1)S(1)}, u32[]{:S(2)}, u32[]{:S(2)}) collective-permute-start(bf16[32,16,128]{2,1,0:T(8,128)(2,1)S(1)} %pad_maximum_fusion.1.refs_0_), channel_id=1, source_target_pairs={{0,1},{1,0},{2,3},{3,2},{4,5},{5,4},{6,7},{7,6},{8,9},{9,8},{10,11... | collective-permute-start | bytes 393224 | tf_op jit(solution)/shard_map/ppermute | solution.py:160
  15.1 2.0 %collective-permute-start.6 = (s32[1024]{0:T(1024)S(1)}, s32[1024]{0:T(1024)S(1)}, u32[]{:S(2)}, u32[]{:S(2)}) collective-permute-start(s32[1024]{0:T(1024)S(1)} %pad_add_fusion.1), channel_id=1, source_target_pairs={{0,2},{2,0},{1,3},{3,1},{4,6},{6,4},{5,7},{7,5},{8,10},{10,8},{9,1... | collective-permute-start | bytes 12296 | tf_op jit(solution)/shard_map/ppermute | solution.py:160
  17.4 7.2 %load_matrix.1 = (bf16[384,128,128]{2,1,0:T(8,128)(2,1)S(1)}, bf16[384,128,128]{2,1,0:T(8,128)(2,1)S(1)}) custom-call(bf16[384,128,128]{2,1,0:T(8,128)(2,1)} %bitcast.22), custom_call_target="tpu_custom_call" | custom-call | bytes 25165824 | tf_op jit(solution)/shard_map/load_matrix/pallas_call | solution.py:53
  24.6 2.9 %forward.4 = f32[16,16,128]{2,1,0:T(8,128)S(1)} custom-call(s32[384]{0:T(512)S(1)} %add_select_fusion.index, bf16[32,16,128]{2,1,0:T(8,128)(2,1)S(1)} %pad_maximum_fusion.1.refs_0_, bf16[32,16,128]{2,1,0:T(8,128)(2,1)S(1)} %collective-permute-done.2.refs_1_, bf16[384,128,128]{2,1,0:T(8,128)(2,1)S(1)} %get-tuple-element.12.refs_2_), custom_call_target="tpu_custom_call" | custom-call | tf_op jit(solution)/shard_map/forward/pallas_call | solution.py:97
  29.3 5.2 %collective-permute-done.4.other = f32[16,16,128]{2,1,0:T(8,128)S(1)} collective-permute-done((f32[16,16,128]{2,1,0:T(8,128)S(1)}, f32[16,16,128]{2,1,0:T(8,128)S(1)}, u32[]{:S(2)}, u32[]{:S(2)}) %collective-permute-start.4) | collective-permute-done | bytes 131104 | tf_op jit(solution)/shard_map/ppermute | solution.py:160
  34.5 2.9 %slope_backward.4 = (f32[32,16,128]{2,1,0:T(8,128)S(1)}, f32[32,16,128]{2,1,0:T(8,128)S(1)}) custom-call(s32[384]{0:T(512)S(1)} %xor.13.index, f32[384]{0:T(512)S(1)} %broadcast_select_fusion.8.factor, f32[16,16,128]{2,1,0:T(8,128)S(1)} %add.93.own, f32[16,16,128]{2,1,0:T(8,128)S(1)} %collective-permute-done.4.other, ...), custom_call_target="tpu_custom_call" | custom-call | tf_op jit(solution)/shard_map/slope_backward/pallas_call | solution.py:145
  40.2 4.4 %collective-permute-done.8 = f32[16,16,128]{2,1,0:T(8,128)S(1)} collective-permute-done((f32[16,16,128]{2,1,0:T(8,128)S(1)}, f32[16,16,128]{2,1,0:T(8,128)S(1)}, u32[]{:S(2)}, u32[]{:S(2)}) %collective-permute-start.8) | collective-permute-done | bytes 131104 | tf_op jit(solution)/shard_map/ppermute | solution.py:160
  44.7 3.1 %collective-permute-start.9 = (f32[16,16,128]{2,1,0:T(8,128)S(1)}, f32[16,16,128]{2,1,0:T(8,128)S(1)}, u32[]{:S(2)}, u32[]{:S(2)}) collective-permute-start(f32[16,16,128]{2,1,0:T(8,128)S(1)} %slice_add_fusion.3), channel_id=1, source_target_pairs={{0,8},{4,12},{8,0},{12,4},{1,9},{5,13},{9,1},{13,5},{2,10},{6,14},... | collective-permute-start | bytes 393224 | tf_op jit(solution)/shard_map/ppermute | solution.py:160
  47.7 6.1 %collective-permute-done.9 = f32[16,16,128]{2,1,0:T(8,128)S(1)} collective-permute-done((f32[16,16,128]{2,1,0:T(8,128)S(1)}, f32[16,16,128]{2,1,0:T(8,128)S(1)}, u32[]{:S(2)}, u32[]{:S(2)}) %collective-permute-start.9) | collective-permute-done | bytes 131104 | tf_op jit(solution)/shard_map/ppermute | solution.py:160
  54.6 3.6 %collective-permute-done.10 = bf16[16,16,128]{2,1,0:T(8,128)(2,1)S(1)} collective-permute-done((bf16[16,16,128]{2,1,0:T(8,128)(2,1)S(1)}, bf16[16,16,128]{2,1,0:T(8,128)(2,1)S(1)}, u32[]{:S(2)}, u32[]{:S(2)}) %collective-permute-start.10) | collective-permute-done | bytes 65568 | tf_op jit(solution)/shard_map/ppermute | solution.py:160
  59.6 2.9 %forward.5 = f32[16,16,128]{2,1,0:T(8,128)S(1)} custom-call(s32[384]{0:T(512)S(1)} %add_select_fusion.index, bf16[32,16,128]{2,1,0:T(8,128)(2,1)S(1)} %pad_maximum_fusion.2.refs_0_, bf16[32,16,128]{2,1,0:T(8,128)(2,1)S(1)} %collective-permute-done.11.refs_1_, bf16[384,128,128]{2,1,0:T(8,128)(2,1)S(1)} %get-tuple-element.12.refs_2_), custom_call_target="tpu_custom_call" | custom-call | tf_op jit(solution)/shard_map/forward/pallas_call | solution.py:97
  64.5 5.0 %collective-permute-done.13.other = f32[16,16,128]{2,1,0:T(8,128)S(1)} collective-permute-done((f32[16,16,128]{2,1,0:T(8,128)S(1)}, f32[16,16,128]{2,1,0:T(8,128)S(1)}, u32[]{:S(2)}, u32[]{:S(2)}) %collective-permute-start.13) | collective-permute-done | bytes 131104 | tf_op jit(solution)/shard_map/ppermute | solution.py:160
  69.5 2.9 %slope_backward.5 = (f32[32,16,128]{2,1,0:T(8,128)S(1)}, f32[32,16,128]{2,1,0:T(8,128)S(1)}) custom-call(s32[384]{0:T(512)S(1)} %xor.13.index, f32[384]{0:T(512)S(1)} %broadcast_select_fusion.8.factor, f32[16,16,128]{2,1,0:T(8,128)S(1)} %add.99.own, f32[16,16,128]{2,1,0:T(8,128)S(1)} %collective-permute-done.13.other, ...), custom_call_target="tpu_custom_call" | custom-call | tf_op jit(solution)/shard_map/slope_backward/pallas_call | solution.py:145
  74.8 4.9 %collective-permute-done.15 = f32[16,16,128]{2,1,0:T(8,128)S(1)} collective-permute-done((f32[16,16,128]{2,1,0:T(8,128)S(1)}, f32[16,16,128]{2,1,0:T(8,128)S(1)}, u32[]{:S(2)}, u32[]{:S(2)}) %collective-permute-start.15) | collective-permute-done | bytes 131104 | tf_op jit(solution)/shard_map/ppermute | solution.py:160
  79.7 2.4 %collective-permute-start.16 = (f32[16,16,128]{2,1,0:T(8,128)S(1)}, f32[16,16,128]{2,1,0:T(8,128)S(1)}, u32[]{:S(2)}, u32[]{:S(2)}) collective-permute-start(f32[16,16,128]{2,1,0:T(8,128)S(1)} %slice_add_fusion.2), channel_id=1, source_target_pairs={{0,8},{4,12},{8,0},{12,4},{1,9},{5,13},{9,1},{13,5},{2,10},{6,14},... | collective-permute-start | bytes 393224 | tf_op jit(solution)/shard_map/ppermute | solution.py:160
  82.1 6.1 %collective-permute-done.16 = f32[16,16,128]{2,1,0:T(8,128)S(1)} collective-permute-done((f32[16,16,128]{2,1,0:T(8,128)S(1)}, f32[16,16,128]{2,1,0:T(8,128)S(1)}, u32[]{:S(2)}, u32[]{:S(2)}) %collective-permute-start.16) | collective-permute-done | bytes 131104 | tf_op jit(solution)/shard_map/ppermute | solution.py:160
  89.0 3.6 %collective-permute-done.17 = bf16[16,16,128]{2,1,0:T(8,128)(2,1)S(1)} collective-permute-done((bf16[16,16,128]{2,1,0:T(8,128)(2,1)S(1)}, bf16[16,16,128]{2,1,0:T(8,128)(2,1)S(1)}, u32[]{:S(2)}, u32[]{:S(2)}) %collective-permute-start.17) | collective-permute-done | bytes 65568 | tf_op jit(solution)/shard_map/ppermute | solution.py:160
  94.0 2.9 %forward.6 = f32[16,16,128]{2,1,0:T(8,128)S(1)} custom-call(s32[384]{0:T(512)S(1)} %add_select_fusion.index, bf16[32,16,128]{2,1,0:T(8,128)(2,1)S(1)} %pad_maximum_fusion.3.refs_0_, bf16[32,16,128]{2,1,0:T(8,128)(2,1)S(1)} %collective-permute-done.18.refs_1_, bf16[384,128,128]{2,1,0:T(8,128)(2,1)S(1)} %get-tuple-element.12.refs_2_), custom_call_target="tpu_custom_call" | custom-call | tf_op jit(solution)/shard_map/forward/pallas_call | solution.py:97
  98.9 5.0 %collective-permute-done.20.other = f32[16,16,128]{2,1,0:T(8,128)S(1)} collective-permute-done((f32[16,16,128]{2,1,0:T(8,128)S(1)}, f32[16,16,128]{2,1,0:T(8,128)S(1)}, u32[]{:S(2)}, u32[]{:S(2)}) %collective-permute-start.20) | collective-permute-done | bytes 131104 | tf_op jit(solution)/shard_map/ppermute | solution.py:160
  103.9 2.9 %slope_backward.6 = (f32[32,16,128]{2,1,0:T(8,128)S(1)}, f32[32,16,128]{2,1,0:T(8,128)S(1)}) custom-call(s32[384]{0:T(512)S(1)} %xor.13.index, f32[384]{0:T(512)S(1)} %broadcast_select_fusion.8.factor, f32[16,16,128]{2,1,0:T(8,128)S(1)} %add.103.own, f32[16,16,128]{2,1,0:T(8,128)S(1)} %collective-permute-done.20.other, ...), custom_call_target="tpu_custom_call" | custom-call | tf_op jit(solution)/shard_map/slope_backward/pallas_call | solution.py:145
  109.2 4.9 %collective-permute-done.22 = f32[16,16,128]{2,1,0:T(8,128)S(1)} collective-permute-done((f32[16,16,128]{2,1,0:T(8,128)S(1)}, f32[16,16,128]{2,1,0:T(8,128)S(1)}, u32[]{:S(2)}, u32[]{:S(2)}) %collective-permute-start.22) | collective-permute-done | bytes 131104 | tf_op jit(solution)/shard_map/ppermute | solution.py:160
  114.1 2.4 %collective-permute-start.23 = (f32[16,16,128]{2,1,0:T(8,128)S(1)}, f32[16,16,128]{2,1,0:T(8,128)S(1)}, u32[]{:S(2)}, u32[]{:S(2)}) collective-permute-start(f32[16,16,128]{2,1,0:T(8,128)S(1)} %slice_add_fusion.1), channel_id=1, source_target_pairs={{0,8},{4,12},{8,0},{12,4},{1,9},{5,13},{9,1},{13,5},{2,10},{6,14},... | collective-permute-start | bytes 393224 | tf_op jit(solution)/shard_map/ppermute | solution.py:160
  116.5 6.1 %collective-permute-done.23 = f32[16,16,128]{2,1,0:T(8,128)S(1)} collective-permute-done((f32[16,16,128]{2,1,0:T(8,128)S(1)}, f32[16,16,128]{2,1,0:T(8,128)S(1)}, u32[]{:S(2)}, u32[]{:S(2)}) %collective-permute-start.23) | collective-permute-done | bytes 131104 | tf_op jit(solution)/shard_map/ppermute | solution.py:160
  123.4 3.6 %collective-permute-done.24 = bf16[16,16,128]{2,1,0:T(8,128)(2,1)S(1)} collective-permute-done((bf16[16,16,128]{2,1,0:T(8,128)(2,1)S(1)}, bf16[16,16,128]{2,1,0:T(8,128)(2,1)S(1)}, u32[]{:S(2)}, u32[]{:S(2)}) %collective-permute-start.24) | collective-permute-done | bytes 65568 | tf_op jit(solution)/shard_map/ppermute | solution.py:160
  128.4 2.9 %forward.7 = f32[16,16,128]{2,1,0:T(8,128)S(1)} custom-call(s32[384]{0:T(512)S(1)} %add_select_fusion.index, bf16[32,16,128]{2,1,0:T(8,128)(2,1)S(1)} %pad_maximum_fusion.4.refs_0_, bf16[32,16,128]{2,1,0:T(8,128)(2,1)S(1)} %collective-permute-done.25.refs_1_, bf16[384,128,128]{2,1,0:T(8,128)(2,1)S(1)} %get-tuple-element.12.refs_2_), custom_call_target="tpu_custom_call" | custom-call | tf_op jit(solution)/shard_map/forward/pallas_call | solution.py:97
  133.3 5.0 %collective-permute-done.27.other = f32[16,16,128]{2,1,0:T(8,128)S(1)} collective-permute-done((f32[16,16,128]{2,1,0:T(8,128)S(1)}, f32[16,16,128]{2,1,0:T(8,128)S(1)}, u32[]{:S(2)}, u32[]{:S(2)}) %collective-permute-start.27) | collective-permute-done | bytes 131104 | tf_op jit(solution)/shard_map/ppermute | solution.py:160
  138.3 2.9 %slope_backward.7 = (f32[32,16,128]{2,1,0:T(8,128)S(1)}, f32[32,16,128]{2,1,0:T(8,128)S(1)}) custom-call(s32[384]{0:T(512)S(1)} %xor.13.index, f32[384]{0:T(512)S(1)} %broadcast_select_fusion.8.factor, f32[16,16,128]{2,1,0:T(8,128)S(1)} %add.107.own, f32[16,16,128]{2,1,0:T(8,128)S(1)} %collective-permute-done.27.other, ...), custom_call_target="tpu_custom_call" | custom-call | tf_op jit(solution)/shard_map/slope_backward/pallas_call | solution.py:145
  143.6 4.9 %collective-permute-done.29 = f32[16,16,128]{2,1,0:T(8,128)S(1)} collective-permute-done((f32[16,16,128]{2,1,0:T(8,128)S(1)}, f32[16,16,128]{2,1,0:T(8,128)S(1)}, u32[]{:S(2)}, u32[]{:S(2)}) %collective-permute-start.29) | collective-permute-done | bytes 131104 | tf_op jit(solution)/shard_map/ppermute | solution.py:160
  148.5 2.4 %collective-permute-start.30 = (f32[16,16,128]{2,1,0:T(8,128)S(1)}, f32[16,16,128]{2,1,0:T(8,128)S(1)}, u32[]{:S(2)}, u32[]{:S(2)}) collective-permute-start(f32[16,16,128]{2,1,0:T(8,128)S(1)} %slice_add_fusion), channel_id=1, source_target_pairs={{0,8},{4,12},{8,0},{12,4},{1,9},{5,13},{9,1},{13,5},{2,10},{6,14},... | collective-permute-start | bytes 393224 | tf_op jit(solution)/shard_map/ppermute | solution.py:160
  150.8 6.1 %collective-permute-done.30 = f32[16,16,128]{2,1,0:T(8,128)S(1)} collective-permute-done((f32[16,16,128]{2,1,0:T(8,128)S(1)}, f32[16,16,128]{2,1,0:T(8,128)S(1)}, u32[]{:S(2)}, u32[]{:S(2)}) %collective-permute-start.30) | collective-permute-done | bytes 131104 | tf_op jit(solution)/shard_map/ppermute | solution.py:160
  (90 shorter events, 34.8 us)
Async XLA Ops:
  0.6 8.9 %collective-permute-start.5 = (s32[512]{0:T(512)}, s32[512]{0:T(512)S(1)}, u32[]{:S(2)}, u32[]{:S(2)}) collective-permute-start(s32[512]{0:T(512)} %param.14), channel_id=1, source_target_pairs={{0,1},{1,0},{2,3},{3,2},{4,5},{5,4},{6,7},{7,6},{8,9},{9,8},{10,11... | collective-permute-start | bytes 6152 | tf_op jit(solution)/shard_map/ppermute | solution.py:160
  2.1 4.8 %collective-permute-start = (f32[16,16,128]{2,1,0:T(8,128)S(1)}, f32[16,16,128]{2,1,0:T(8,128)S(1)}, u32[]{:S(2)}, u32[]{:S(2)}) collective-permute-start(f32[16,16,128]{2,1,0:T(8,128)S(1)} %bitcast.24), channel_id=1, source_target_pairs={{0,0},{8,1},{4,4},{12,5},{1,8},{9,9},{5,12},{13,13},{2,2},{10,3},{... | collective-permute-start | bytes 393224 | tf_op jit(solution)/shard_map/ppermute | solution.py:201
  6.9 4.9 %collective-permute-start.1 = (bf16[16,16,128]{2,1,0:T(8,128)(2,1)S(1)}, bf16[16,16,128]{2,1,0:T(8,128)(2,1)S(1)}, u32[]{:S(2)}, u32[]{:S(2)}) collective-permute-start(bf16[16,16,128]{2,1,0:T(8,128)(2,1)S(1)} %convert_element_type.12), channel_id=1, source_target_pairs={{0,4},{4,0},{8,12},{12,8},{1,5},{5,1},{9,13},{13,9},{2,6},{6,2},{1... | collective-permute-start | bytes 196616 | tf_op jit(solution)/shard_map/ppermute | solution.py:160
  11.8 12.8 %collective-permute-start.2 = (bf16[32,16,128]{2,1,0:T(8,128)(2,1)S(1)}, bf16[32,16,128]{2,1,0:T(8,128)(2,1)S(1)}, u32[]{:S(2)}, u32[]{:S(2)}) collective-permute-start(bf16[32,16,128]{2,1,0:T(8,128)(2,1)S(1)} %pad_maximum_fusion.1.refs_0_), channel_id=1, source_target_pairs={{0,1},{1,0},{2,3},{3,2},{4,5},{5,4},{6,7},{7,6},{8,9},{9,8},{10,11... | collective-permute-start | bytes 393224 | tf_op jit(solution)/shard_map/ppermute | solution.py:160
  15.1 12.4 %collective-permute-start.6 = (s32[1024]{0:T(1024)S(1)}, s32[1024]{0:T(1024)S(1)}, u32[]{:S(2)}, u32[]{:S(2)}) collective-permute-start(s32[1024]{0:T(1024)S(1)} %pad_add_fusion.1), channel_id=1, source_target_pairs={{0,2},{2,0},{1,3},{3,1},{4,6},{6,4},{5,7},{7,5},{8,10},{10,8},{9,1... | collective-permute-start | bytes 12296 | tf_op jit(solution)/shard_map/ppermute | solution.py:160
  27.4 1.4 collective-permute-start.3
  28.9 5.6 %collective-permute-start.4 = (f32[16,16,128]{2,1,0:T(8,128)S(1)}, f32[16,16,128]{2,1,0:T(8,128)S(1)}, u32[]{:S(2)}, u32[]{:S(2)}) collective-permute-start(f32[16,16,128]{2,1,0:T(8,128)S(1)} %add.93.own), channel_id=1, source_target_pairs={{0,2},{2,0},{1,3},{3,1},{4,6},{6,4},{5,7},{7,5},{8,10},{10,8},{9,1... | collective-permute-start | bytes 393224 | tf_op jit(solution)/shard_map/ppermute | solution.py:160
  37.4 1.6 %collective-permute-start.7 = (f32[32,16,128]{2,1,0:T(8,128)S(1)}, f32[32,16,128]{2,1,0:T(8,128)S(1)}, u32[]{:S(2)}, u32[]{:S(2)}) collective-permute-start(f32[32,16,128]{2,1,0:T(8,128)S(1)} %get-tuple-element.15), channel_id=1, source_target_pairs={{0,1},{1,0},{2,3},{3,2},{4,5},{5,4},{6,7},{7,6},{8,9},{9,8},{10,11... | collective-permute-start | bytes 786440 | tf_op jit(solution)/shard_map/ppermute | solution.py:160
  39.0 5.6 %collective-permute-start.8 = (f32[16,16,128]{2,1,0:T(8,128)S(1)}, f32[16,16,128]{2,1,0:T(8,128)S(1)}, u32[]{:S(2)}, u32[]{:S(2)}) collective-permute-start(f32[16,16,128]{2,1,0:T(8,128)S(1)} %slice.75), channel_id=1, source_target_pairs={{0,4},{4,0},{8,12},{12,8},{1,5},{5,1},{9,13},{13,9},{2,6},{6,2},{1... | collective-permute-start | bytes 393224 | tf_op jit(solution)/shard_map/ppermute | solution.py:160
  44.7 9.2 %collective-permute-start.9 = (f32[16,16,128]{2,1,0:T(8,128)S(1)}, f32[16,16,128]{2,1,0:T(8,128)S(1)}, u32[]{:S(2)}, u32[]{:S(2)}) collective-permute-start(f32[16,16,128]{2,1,0:T(8,128)S(1)} %slice_add_fusion.3), channel_id=1, source_target_pairs={{0,8},{4,12},{8,0},{12,4},{1,9},{5,13},{9,1},{13,5},{2,10},{6,14},... | collective-permute-start | bytes 393224 | tf_op jit(solution)/shard_map/ppermute | solution.py:160
  53.8 4.3 %collective-permute-start.10 = (bf16[16,16,128]{2,1,0:T(8,128)(2,1)S(1)}, bf16[16,16,128]{2,1,0:T(8,128)(2,1)S(1)}, u32[]{:S(2)}, u32[]{:S(2)}) collective-permute-start(bf16[16,16,128]{2,1,0:T(8,128)(2,1)S(1)} %fusion.1), channel_id=1, source_target_pairs={{0,4},{4,0},{8,12},{12,8},{1,5},{5,1},{9,13},{13,9},{2,6},{6,2},{1... | collective-permute-start | bytes 196616 | tf_op jit(solution)/shard_map/ppermute | solution.py:160
  58.2 1.4 collective-permute-start.11
  62.5 1.4 collective-permute-start.12
  63.9 5.6 %collective-permute-start.13 = (f32[16,16,128]{2,1,0:T(8,128)S(1)}, f32[16,16,128]{2,1,0:T(8,128)S(1)}, u32[]{:S(2)}, u32[]{:S(2)}) collective-permute-start(f32[16,16,128]{2,1,0:T(8,128)S(1)} %add.99.own), channel_id=1, source_target_pairs={{0,2},{2,0},{1,3},{3,1},{4,6},{6,4},{5,7},{7,5},{8,10},{10,8},{9,1... | collective-permute-start | bytes 393224 | tf_op jit(solution)/shard_map/ppermute | solution.py:160
  72.4 1.6 %collective-permute-start.14 = (f32[32,16,128]{2,1,0:T(8,128)S(1)}, f32[32,16,128]{2,1,0:T(8,128)S(1)}, u32[]{:S(2)}, u32[]{:S(2)}) collective-permute-start(f32[32,16,128]{2,1,0:T(8,128)S(1)} %get-tuple-element.17), channel_id=1, source_target_pairs={{0,1},{1,0},{2,3},{3,2},{4,5},{5,4},{6,7},{7,6},{8,9},{9,8},{10,11... | collective-permute-start | bytes 786440 | tf_op jit(solution)/shard_map/ppermute | solution.py:160
  74.1 5.6 %collective-permute-start.15 = (f32[16,16,128]{2,1,0:T(8,128)S(1)}, f32[16,16,128]{2,1,0:T(8,128)S(1)}, u32[]{:S(2)}, u32[]{:S(2)}) collective-permute-start(f32[16,16,128]{2,1,0:T(8,128)S(1)} %slice.77), channel_id=1, source_target_pairs={{0,4},{4,0},{8,12},{12,8},{1,5},{5,1},{9,13},{13,9},{2,6},{6,2},{1... | collective-permute-start | bytes 393224 | tf_op jit(solution)/shard_map/ppermute | solution.py:160
  79.7 8.5 %collective-permute-start.16 = (f32[16,16,128]{2,1,0:T(8,128)S(1)}, f32[16,16,128]{2,1,0:T(8,128)S(1)}, u32[]{:S(2)}, u32[]{:S(2)}) collective-permute-start(f32[16,16,128]{2,1,0:T(8,128)S(1)} %slice_add_fusion.2), channel_id=1, source_target_pairs={{0,8},{4,12},{8,0},{12,4},{1,9},{5,13},{9,1},{13,5},{2,10},{6,14},... | collective-permute-start | bytes 393224 | tf_op jit(solution)/shard_map/ppermute | solution.py:160
  88.2 4.3 %collective-permute-start.17 = (bf16[16,16,128]{2,1,0:T(8,128)(2,1)S(1)}, bf16[16,16,128]{2,1,0:T(8,128)(2,1)S(1)}, u32[]{:S(2)}, u32[]{:S(2)}) collective-permute-start(bf16[16,16,128]{2,1,0:T(8,128)(2,1)S(1)} %get-tuple-element.30), channel_id=1, source_target_pairs={{0,4},{4,0},{8,12},{12,8},{1,5},{5,1},{9,13},{13,9},{2,6},{6,2},{1... | collective-permute-start | bytes 196616 | tf_op jit(solution)/shard_map/ppermute | solution.py:160
  92.6 1.4 collective-permute-start.18
  96.9 1.4 collective-permute-start.19
  98.3 5.6 %collective-permute-start.20 = (f32[16,16,128]{2,1,0:T(8,128)S(1)}, f32[16,16,128]{2,1,0:T(8,128)S(1)}, u32[]{:S(2)}, u32[]{:S(2)}) collective-permute-start(f32[16,16,128]{2,1,0:T(8,128)S(1)} %add.103.own), channel_id=1, source_target_pairs={{0,2},{2,0},{1,3},{3,1},{4,6},{6,4},{5,7},{7,5},{8,10},{10,8},{9,1... | collective-permute-start | bytes 393224 | tf_op jit(solution)/shard_map/ppermute | solution.py:160
  106.8 1.6 %collective-permute-start.21 = (f32[32,16,128]{2,1,0:T(8,128)S(1)}, f32[32,16,128]{2,1,0:T(8,128)S(1)}, u32[]{:S(2)}, u32[]{:S(2)}) collective-permute-start(f32[32,16,128]{2,1,0:T(8,128)S(1)} %get-tuple-element.19), channel_id=1, source_target_pairs={{0,1},{1,0},{2,3},{3,2},{4,5},{5,4},{6,7},{7,6},{8,9},{9,8},{10,11... | collective-permute-start | bytes 786440 | tf_op jit(solution)/shard_map/ppermute | solution.py:160
  108.5 5.6 %collective-permute-start.22 = (f32[16,16,128]{2,1,0:T(8,128)S(1)}, f32[16,16,128]{2,1,0:T(8,128)S(1)}, u32[]{:S(2)}, u32[]{:S(2)}) collective-permute-start(f32[16,16,128]{2,1,0:T(8,128)S(1)} %slice.79), channel_id=1, source_target_pairs={{0,4},{4,0},{8,12},{12,8},{1,5},{5,1},{9,13},{13,9},{2,6},{6,2},{1... | collective-permute-start | bytes 393224 | tf_op jit(solution)/shard_map/ppermute | solution.py:160
  114.1 8.5 %collective-permute-start.23 = (f32[16,16,128]{2,1,0:T(8,128)S(1)}, f32[16,16,128]{2,1,0:T(8,128)S(1)}, u32[]{:S(2)}, u32[]{:S(2)}) collective-permute-start(f32[16,16,128]{2,1,0:T(8,128)S(1)} %slice_add_fusion.1), channel_id=1, source_target_pairs={{0,8},{4,12},{8,0},{12,4},{1,9},{5,13},{9,1},{13,5},{2,10},{6,14},... | collective-permute-start | bytes 393224 | tf_op jit(solution)/shard_map/ppermute | solution.py:160
  122.6 4.3 %collective-permute-start.24 = (bf16[16,16,128]{2,1,0:T(8,128)(2,1)S(1)}, bf16[16,16,128]{2,1,0:T(8,128)(2,1)S(1)}, u32[]{:S(2)}, u32[]{:S(2)}) collective-permute-start(bf16[16,16,128]{2,1,0:T(8,128)(2,1)S(1)} %fusion.2), channel_id=1, source_target_pairs={{0,4},{4,0},{8,12},{12,8},{1,5},{5,1},{9,13},{13,9},{2,6},{6,2},{1... | collective-permute-start | bytes 196616 | tf_op jit(solution)/shard_map/ppermute | solution.py:160
  127.0 1.4 collective-permute-start.25
  131.2 1.4 collective-permute-start.26
  132.7 5.6 %collective-permute-start.27 = (f32[16,16,128]{2,1,0:T(8,128)S(1)}, f32[16,16,128]{2,1,0:T(8,128)S(1)}, u32[]{:S(2)}, u32[]{:S(2)}) collective-permute-start(f32[16,16,128]{2,1,0:T(8,128)S(1)} %add.107.own), channel_id=1, source_target_pairs={{0,2},{2,0},{1,3},{3,1},{4,6},{6,4},{5,7},{7,5},{8,10},{10,8},{9,1... | collective-permute-start | bytes 393224 | tf_op jit(solution)/shard_map/ppermute | solution.py:160
  141.2 1.6 %collective-permute-start.28 = (f32[32,16,128]{2,1,0:T(8,128)S(1)}, f32[32,16,128]{2,1,0:T(8,128)S(1)}, u32[]{:S(2)}, u32[]{:S(2)}) collective-permute-start(f32[32,16,128]{2,1,0:T(8,128)S(1)} %get-tuple-element.21), channel_id=1, source_target_pairs={{0,1},{1,0},{2,3},{3,2},{4,5},{5,4},{6,7},{7,6},{8,9},{9,8},{10,11... | collective-permute-start | bytes 786440 | tf_op jit(solution)/shard_map/ppermute | solution.py:160
  142.8 5.6 %collective-permute-start.29 = (f32[16,16,128]{2,1,0:T(8,128)S(1)}, f32[16,16,128]{2,1,0:T(8,128)S(1)}, u32[]{:S(2)}, u32[]{:S(2)}) collective-permute-start(f32[16,16,128]{2,1,0:T(8,128)S(1)} %slice.81), channel_id=1, source_target_pairs={{0,4},{4,0},{8,12},{12,8},{1,5},{5,1},{9,13},{13,9},{2,6},{6,2},{1... | collective-permute-start | bytes 393224 | tf_op jit(solution)/shard_map/ppermute | solution.py:160
  148.5 8.5 %collective-permute-start.30 = (f32[16,16,128]{2,1,0:T(8,128)S(1)}, f32[16,16,128]{2,1,0:T(8,128)S(1)}, u32[]{:S(2)}, u32[]{:S(2)}) collective-permute-start(f32[16,16,128]{2,1,0:T(8,128)S(1)} %slice_add_fusion), channel_id=1, source_target_pairs={{0,8},{4,12},{8,0},{12,4},{1,9},{5,13},{9,1},{13,5},{2,10},{6,14},... | collective-permute-start | bytes 393224 | tf_op jit(solution)/shard_map/ppermute | solution.py:160
  157.0 1.6 %collective-permute-start.31 = (f32[2,16,16,128]{3,2,1,0:T(8,128)S(1)}, f32[2,16,16,128]{3,2,1,0:T(8,128)S(1)}, u32[]{:S(2)}, u32[]{:S(2)}) collective-permute-start(f32[2,16,16,128]{3,2,1,0:T(8,128)S(1)} %pad_maximum_fusion), channel_id=1, source_target_pairs={{0,1},{1,0},{2,3},{3,2},{4,5},{5,4},{6,7},{7,6},{8,9},{9,8},{10,11... | collective-permute-start | bytes 786440 | tf_op jit(solution)/shard_map/ppermute | solution.py:160

commit v2 on v1

--- a/solution.py
+++ b/solution.py
@@ -25,43 +25,57 @@
     return pltpu.with_memory_space_constraint(array, pltpu.VMEM)
 
 
-def load_kernel(pieces, stored, kept, turned, sems):
-    size = stored.shape[0] // pieces
+def load_kernel(place, cols, exps, live, stored, kept, turned, index, places, factor, sems):
+    z, core, n_vox = place[0], place[1], place[2]
+    rows, _, slots = cols.shape
+    columns = place[3]
+    own = columns // (2 * n_vox)
     copies = [
         pltpu.make_async_copy(
-            stored.at[pl.ds(i * size, size)], kept.at[pl.ds(i * size, size)], sems.at[i]
+            stored.at[pl.ds(b * slots, slots)], kept.at[pl.ds(b * slots, slots)], sems.at[b]
         )
-        for i in range(pieces)
+        for b in range(rows)
     ]
     for copy in copies:
         copy.start()
-    step = 8 if size % 8 == 0 else 1
-    for i, copy in enumerate(copies):
+    step = 8 if slots % 8 == 0 else 1
+    for b, copy in enumerate(copies):
         copy.wait()
 
-        def turn(t, carry, i=i):
+        def turn(t, carry, b=b):
             for u in range(step):
-                n = i * size + t * step + u
+                k = t * step + u
+                n = b * slots + k
                 turned[n] = kept[n].T
+                column, exponent = cols[b, 0, k], exps[b, 0, k]
+                piece, within = lax.div(column, own), lax.rem(column, own)
+                owner_core, owner_z = lax.rem(piece, 2), lax.div(piece, 2)
+                at = ((owner_core ^ core) * n_vox + (owner_z ^ z)) * own + within
+                used = core * slots + k < live[b, 0]
+                scale = jnp.where(exponent < 0, 0.5, jnp.where(exponent > 0, 2.0, 1.0))
+                places[n] = at
+                index[n] = jnp.where(used, (exponent + 1) * columns + at, 3 * columns)
+                factor[n] = jnp.where(used, scale, 0.0).astype(F32)
             return carry
 
-        lax.fori_loop(0, size // step, turn, 0)
-
-
-def load_matrix(tiles):
-    pieces = 16 if tiles.shape[0] % 16 == 0 else 1
+        lax.fori_loop(0, slots // step, turn, 0)
+
+
+def load_matrix(place, cols, exps, live, tiles):
+    rows, _, slots = cols.shape
     return pl.pallas_call(
-        functools.partial(load_kernel, pieces),
-        in_specs=[pl.BlockSpec(memory_space=pltpu.HBM)],
-        out_specs=[in_vmem(), in_vmem()],
-        out_shape=[pltpu.VMEM(tiles.shape, tiles.dtype)] * 2,
-        scratch_shapes=[pltpu.SemaphoreType.DMA((pieces,))],
+        load_kernel,
+        in_specs=[in_smem()] * 4 + [pl.BlockSpec(memory_space=pltpu.HBM)],
+        out_specs=[in_vmem()] * 2 + [in_smem()] * 3,
+        out_shape=[pltpu.VMEM(tiles.shape, tiles.dtype)] * 2
+        + [jax.ShapeDtypeStruct((rows * slots,), t) for t in (jnp.int32, jnp.int32, F32)],
+        scratch_shapes=[pltpu.SemaphoreType.DMA((rows,))],
         compiler_params=PARAMS,
         cost_estimate=pl.CostEstimate(
             flops=0, bytes_accessed=2 * tiles.size * 2, transcendentals=0
         ),
         name="load_matrix",
-    )(tiles)
+    )(place, cols, exps, live, tiles)
 
 
 def forward_kernel(slots, index, *refs):
@@ -156,10 +170,6 @@
     )(index, factor, own, other, levels, held(kept))
 
 
-def swap(array, axis, size, bit):
-    return lax.ppermute(array, axis, [(i, i ^ bit) for i in range(size)])
-
-
 def per_device(
     sizes,
     dose_blocks,
@@ -173,78 +183,84 @@
     lower_weight,
     initial_spot_weights,
 ):
-    n_vox, n_spot, n_rep = sizes
+    n_vox, n_spot = sizes
     z, x, core = (lax.axis_index(a) for a in ("vox", "spot", "rep"))
     rows, _, slots, width, _ = dose_blocks.shape
     weightings, _, chunk_spots = initial_spot_weights.shape
     chunk = chunk_spots // width
     columns = chunk * n_vox
-    vox_bits = n_vox.bit_length() - 1
-    top = 1 << (vox_bits - 1)
-
-    mine = core * top + z % top
-    places = block_cols[:, 0] ^ (mine * chunk)
-    position = core * slots + jnp.arange(slots, dtype=jnp.int32)
-    live = position[None, :] < live_counts
-    exps = block_exps[:, 0]
-    factor = jnp.where(live, jnp.where(exps < 0, 0.5, jnp.where(exps > 0, 2.0, 1.0)), 0.0)
-    factor = factor.astype(F32).reshape(-1)
-    forward_index = jnp.where(live, (exps + 1) * columns + places, 3 * columns).reshape(-1)
-    places = places.reshape(-1)
-
-    weights = initial_spot_weights[:, 0].reshape(weightings, chunk, width).transpose(1, 0, 2)
-    moves = []
-    for to_z in range(n_vox):
-        for to_core in range(2):
-            from_z, from_core = to_core * top + to_z % top, to_z // top
-            moves.append((from_z * 2 + from_core, to_z * 2 + to_core))
-    weights = lax.ppermute(weights, ("vox", "rep"), moves)
-
-    kept, turned = load_matrix(dose_blocks.reshape(rows * slots, width, width))
-
-    all_labels = labels
-    for axis, size, place in (("rep", n_rep, core), ("spot", n_spot, x)):
+    own = chunk // 2
+    initial = initial_spot_weights[:, 0].reshape(weightings, chunk, width)
+    weights = lax.dynamic_slice_in_dim(initial, core * own, own, 1).transpose(1, 0, 2)
+
+    def over_vox(arrays):
+        return [
+            lax.ppermute(a, "vox", [(i, i ^ d) for i in range(n_vox)])
+            for d, a in enumerate(arrays, 1)
+        ]
+
+    def over_rep(array):
+        return lax.ppermute(array, "rep", [(0, 1), (1, 0)])
+
+    place = jnp.stack([z, core, n_vox, columns]).astype(jnp.int32)
+    level_table = jnp.stack([upper_dose, upper_weight, lower_dose, lower_weight])
+    known = labels.astype(F32).reshape(-1, width)
+
+    def gather_weights(weights):
+        piece = weights.astype(BF16)
+        return [piece] + over_vox([piece] * (n_vox - 1))
+
+    pieces = gather_weights(weights)
+    kept, turned, index, places, factor = load_matrix(
+        place, block_cols, block_exps, live_counts, dose_blocks.reshape(rows * slots, width, width)
+    )
+
+    for step in range(ITERS):
+        near = jnp.concatenate(pieces, axis=0)
+        dose = forward(index, [near, over_rep(near)], turned, rows, slots)
+
+        exchanges = [("rep", 2, 1, core)]
         bit = 1
-        while bit < size:
-            got = swap(all_labels, axis, size, bit)
-            first = (place // bit) % 2 == 0
-            all_labels = jnp.concatenate(
-                [jnp.where(first, all_labels, got), jnp.where(first, got, all_labels)]
-            )
+        while bit < n_spot:
+            exchanges.append(("spot", n_spot, bit, x))
             bit *= 2
-    all_labels = all_labels.reshape(rows, 1, width)
-    table = jnp.stack([upper_dose, upper_weight, lower_dose, lower_weight], axis=0)
-    levels = jnp.zeros((4, rows, 1, width), F32)
-    for c in range(table.shape[1]):
-        levels = jnp.where(all_labels[None] == c, table[:, c][:, None, None, None], levels)
-
-    for step in range(ITERS):
-        piece = weights.astype(BF16)
-        pieces = [piece]
-        for bit in range(vox_bits - 1):
-            whole = jnp.concatenate(pieces, axis=0) if len(pieces) > 1 else piece
-            pieces = pieces + [swap(whole, "vox", n_vox, 1 << bit)]
-        whole = jnp.concatenate(pieces, axis=0) if len(pieces) > 1 else piece
-        pieces = [whole, swap(whole, "rep", n_rep, 1)]
-
-        dose = forward(forward_index, pieces, turned, rows, slots)
-        dose = dose + swap(dose, "rep", n_rep, 1)
-        bit = 1
-        while bit < n_spot // 2:
-            dose = dose + swap(dose, "spot", n_spot, bit)
-            bit *= 2
-        other = swap(dose, "spot", n_spot, bit)
-
-        far, near = backward(places, factor, dose, other, levels, kept, columns, slots)
-        part = near + swap(far, "rep", n_rep, 1)
-        for bit in reversed(range(vox_bits - 1)):
-            half = part.shape[0] // 2
-            part = part[:half] + swap(part[half:], "vox", n_vox, 1 << bit)
-        gradient = part + swap(part, "vox", n_vox, top)
+        for axis, size, bit, at in exchanges:
+            sent = dose
+            if step == 0:
+                n = known.shape[0]
+                tile = jnp.pad(known, ((0, weightings - n), (0, 0)))
+                sent = jnp.concatenate([dose, tile[None]], axis=0)
+            got = lax.ppermute(sent, axis, [(i, i ^ bit) for i in range(size)])
+            if step == 0:
+                theirs = got[rows, :n]
+                first = (at // bit) % 2 == 0
+                known = jnp.concatenate(
+                    [jnp.where(first, known, theirs), jnp.where(first, theirs, known)]
+                )
+                got = got[:rows]
+            if (axis, bit) != (exchanges[-1][0], exchanges[-1][2]):
+                dose = dose + got
+        if step == 0:
+            levels = jnp.zeros((4, rows, 1, width), F32)
+            for c in range(level_table.shape[1]):
+                value = level_table[:, c][:, None, None, None]
+                levels = jnp.where(known[None, :, None, :] == c, value, levels)
+
+        far, near = backward(places, factor, dose, got, levels, kept, columns, slots)
+        near = near + over_rep(far)
+        parts = over_vox([near[d * own : (d + 1) * own] for d in range(1, n_vox)])
+        gradient = near[:own]
+        for part in parts:
+            gradient = gradient + part
         weights = jnp.maximum(weights - 0.5 * gradient, 0.0)
-
-    both = jnp.stack([weights, gradient])
-    both = jnp.where(z // top == core, both, swap(both, "rep", n_rep, 1))
+        if step < ITERS - 1:
+            pieces = gather_weights(weights)
+
+    mine = jnp.stack([weights, gradient])
+    other = over_rep(mine)
+    both = jnp.concatenate(
+        [jnp.where(core == 0, mine, other), jnp.where(core == 0, other, mine)], axis=1
+    )
     both = both.transpose(0, 2, 1, 3).reshape(2, weightings, 1, chunk_spots)
     return both[0], both[1]
 
@@ -262,7 +278,7 @@
         P("groups"),
         P("groups", "spot", "vox"),
     )
-    sizes = tuple(mesh.shape[a] for a in ("vox", "spot", "rep"))
+    sizes = tuple(mesh.shape[a] for a in ("vox", "spot"))
     return jax.shard_map(
         functools.partial(per_device, sizes),
         mesh=mesh,

time: 160 us -> 168 us (1.050)
  waiting for transfers between devices: 92.5 us -> 68.8 us
  local copies, waits for them, and re-layouts: 3.05 us -> 23.1 us
  starting transfers between devices: 28.2 us -> 41.4 us
  other arithmetic: 5.2 us -> 1.58 us
  Pallas kernels: 30.2 us -> 32 us
    ppermute x32 -> x41, waiting for transfers between devices: 92.5 us -> 68.8 us  [the longest x24 36.5 us: over_vox(): lax.ppermute(a, 'vox', [(i, i ^ d) for i in range(n_vox)])]
    unnamed x0 -> x32, local copies, waits for them, and re-layouts: none -> 21.3 us
    ppermute x32 -> x41, starting transfers between devices: 28.2 us -> 41.4 us  [the longest x24 33.3 us: over_vox(): lax.ppermute(a, 'vox', [(i, i ^ d) for i in range(n_vox)])]
    pallas_call x1, Pallas kernels: 7.16 us -> 9 us  [load_matrix(): pl.pallas_call(load_kernel, in_specs=[in_smem()] * 4 + [pl.BlockSpec(memo...]
  transfers between devices with their start and end apart: 32 -> 41, of which waited for: 28 -> 36; matrix products, arithmetic and copies ran while one was open for 4% -> 1% of each run, Pallas kernels for 6% -> 5%
where the time goes in v2:
time: 168 us
  waiting for transfers between devices  68.8 us (41%)
  starting transfers between devices  41.4 us (25%)
  Pallas kernels  32 us (19%)
  local copies, waits for them, and re-layouts  23.1 us (14%)
    ppermute x24, waiting for transfers between devices, over_vox(): lax.ppermute(a, 'vox', [(i, i ^ d) for i in range(n_vox)])  36.5 us
    ppermute x24, starting transfers between devices, over_vox(): lax.ppermute(a, 'vox', [(i, i ^ d) for i in range(n_vox)])  33.3 us
    unnamed x32, local copies, waits for them, and re-layouts  21.3 us
    ppermute x8, waiting for transfers between devices, per_device(): got = lax.ppermute(sent, axis, [(i, i ^ bit) for i in range(size)])  20.9 us
    pallas_call x4, Pallas kernels, backward(): pl.pallas_call(functools.partial(backward_kernel, slots), in_specs=[in_sm...  11.6 us
    pallas_call x4, Pallas kernels, forward(): pl.pallas_call(functools.partial(forward_kernel, slots), in_specs=[in_sme...  11.5 us
    ppermute x9, waiting for transfers between devices, over_rep(): return lax.ppermute(array, 'rep', [(0, 1), (1, 0)])  11.4 us
    pallas_call x1, Pallas kernels, load_matrix(): pl.pallas_call(load_kernel, in_specs=[in_smem()] * 4 + [pl.BlockSpec(memo...  9 us
  transfers between devices with their start and end apart: 41, of which 36 were waited for; matrix products, arithmetic and copies ran while one was open for 1% of the time, Pallas kernels for 5%

profile of v2, /device:TPU:0, one launch (start us, length us, event | category | flops | bytes accessed | tf_op | source)
XLA Modules:
  0.0 167.9 jit_solution(7774835750293073157)
XLA Ops:
  1.6 5.1 %collective-permute-start.2 = (bf16[8,16,128]{2,1,0:T(8,128)(2,1)S(1)}, bf16[8,16,128]{2,1,0:T(8,128)(2,1)S(1)}, u32[]{:S(2)}, u32[]{:S(2)}) collective-permute-start(bf16[8,16,128]{2,1,0:T(8,128)(2,1)S(1)} %bitcast.53), channel_id=1, source_target_pairs={{0,12},{4,8},{8,4},{12,0},{1,13},{5,9},{9,5},{13,1},{2,14},{6,10},... | collective-permute-start | bytes 98312 | tf_op jit(solution)/shard_map/ppermute | solution.py:198
  8.6 2.9 %collective-permute-done.1 = bf16[8,16,128]{2,1,0:T(8,128)(2,1)S(1)} collective-permute-done((bf16[8,16,128]{2,1,0:T(8,128)(2,1)S(1)}, bf16[8,16,128]{2,1,0:T(8,128)(2,1)S(1)}, u32[]{:S(2)}, u32[]{:S(2)}) %collective-permute-start.1) | collective-permute-done | bytes 32800 | tf_op jit(solution)/shard_map/ppermute | solution.py:198
  13.8 9.0 %load_matrix.1 = (bf16[384,128,128]{2,1,0:T(8,128)(2,1)S(1)}, bf16[384,128,128]{2,1,0:T(8,128)(2,1)S(1)}, s32[384]{0:T(512)S(1)}, s32[384]{0:T(512)S(1)}, f32[384]{0:T(512)S(1)}) custom-call(s32[4]{0:T(128)S(1)} %pad_add_fusion.place, s32[16,1,24]{2,1,0:T(1,128)S(1)} %copy-done.5, s32[16,1,24]{2,1,0:T(1,128)S(1)} %copy-done.6, s32[16,1]{1,0:T(8,128)S(1)} %copy.14.live, ...), custom_call_target="tpu_custom_call" | custom-call | bytes 25165824 | tf_op jit(solution)/shard_map/load_matrix/pallas_call | solution.py:66
  22.9 4.6 %copy-done.1 = bf16[384,128,128]{2,1,0:T(8,128)(2,1)} copy-done((bf16[384,128,128]{2,1,0:T(8,128)(2,1)}, bf16[384,128,128]{2,1,0:T(8,128)(2,1)S(1)}, u32[]{:S(2)}) %copy-start.1) | copy-done | bytes 12582936
  27.4 2.9 %forward.4 = f32[16,16,128]{2,1,0:T(8,128)S(1)} custom-call(s32[384]{0:T(512)S(1)} %get-tuple-element.17.index, bf16[32,16,128]{2,1,0:T(8,128)(2,1)S(1)} %pad_maximum_fusion.2.refs_0_, bf16[32,16,128]{2,1,0:T(8,128)(2,1)S(1)} %collective-permute-done.3.refs_1_, bf16[384,128,128]{2,1,0:T(8,128)(2,1)S(1)} %get-tuple-element.18.refs_2_), custom_call_target="tpu_custom_call" | custom-call | tf_op jit(solution)/shard_map/forward/pallas_call | solution.py:111
  30.3 4.6 %copy-done.3 = bf16[384,128,128]{2,1,0:T(8,128)(2,1)} copy-done((bf16[384,128,128]{2,1,0:T(8,128)(2,1)}, bf16[384,128,128]{2,1,0:T(8,128)(2,1)S(1)}, u32[]{:S(2)}) %copy-start.3) | copy-done | bytes 12582936
  38.4 4.1 %collective-permute-done.5 = f32[17,16,128]{2,1,0:T(8,128)S(1)} collective-permute-done((f32[17,16,128]{2,1,0:T(8,128)S(1)}, f32[17,16,128]{2,1,0:T(8,128)S(1)}, u32[]{:S(2)}, u32[]{:S(2)}) %collective-permute-start.5) | collective-permute-done | bytes 139296 | tf_op jit(solution)/shard_map/ppermute | solution.py:233
  42.9 4.6 %copy-done.2 = bf16[384,128,128]{2,1,0:T(8,128)(2,1)S(1)} copy-done((bf16[384,128,128]{2,1,0:T(8,128)(2,1)S(1)}, bf16[384,128,128]{2,1,0:T(8,128)(2,1)}, u32[]{:S(2)}) %copy-start.2) | copy-done | bytes 12582936
  47.4 2.9 %slope_backward.4 = (f32[32,16,128]{2,1,0:T(8,128)S(1)}, f32[32,16,128]{2,1,0:T(8,128)S(1)}) custom-call(s32[384]{0:T(512)S(1)} %get-tuple-element.15.index, f32[384]{0:T(512)S(1)} %get-tuple-element.16.factor, f32[16,16,128]{2,1,0:T(8,128)S(1)} %slice_add_fusion.own, f32[16,16,128]{2,1,0:T(8,128)S(1)} %slice.124.other, ...), custom_call_target="tpu_custom_call" | custom-call | tf_op jit(solution)/shard_map/slope_backward/pallas_call | solution.py:159
  52.1 3.5 %collective-permute-start.9 = (f32[8,16,128]{2,1,0:T(8,128)S(1)}, f32[8,16,128]{2,1,0:T(8,128)S(1)}, u32[]{:S(2)}, u32[]{:S(2)}) collective-permute-start(f32[8,16,128]{2,1,0:T(8,128)S(1)} %get-tuple-element.58), channel_id=1, source_target_pairs={{0,12},{4,8},{8,4},{12,0},{1,13},{5,9},{9,5},{13,1},{2,14},{6,10},... | collective-permute-start | bytes 196616 | tf_op jit(solution)/shard_map/ppermute | solution.py:198
  56.3 3.5 %collective-permute-done.9 = f32[8,16,128]{2,1,0:T(8,128)S(1)} collective-permute-done((f32[8,16,128]{2,1,0:T(8,128)S(1)}, f32[8,16,128]{2,1,0:T(8,128)S(1)}, u32[]{:S(2)}, u32[]{:S(2)}) %collective-permute-start.9) | collective-permute-done | bytes 65568 | tf_op jit(solution)/shard_map/ppermute | solution.py:198
  59.9 2.0 %collective-permute-done.8 = f32[8,16,128]{2,1,0:T(8,128)S(1)} collective-permute-done((f32[8,16,128]{2,1,0:T(8,128)S(1)}, f32[8,16,128]{2,1,0:T(8,128)S(1)}, u32[]{:S(2)}, u32[]{:S(2)}) %collective-permute-start.8) | collective-permute-done | bytes 65568 | tf_op jit(solution)/shard_map/ppermute | solution.py:198
  63.6 2.7 %collective-permute-start.10 = (bf16[8,16,128]{2,1,0:T(8,128)(2,1)S(1)}, bf16[8,16,128]{2,1,0:T(8,128)(2,1)S(1)}, u32[]{:S(2)}, u32[]{:S(2)}) collective-permute-start(bf16[8,16,128]{2,1,0:T(8,128)(2,1)S(1)} %get-tuple-element.42), channel_id=1, source_target_pairs={{0,4},{4,0},{8,12},{12,8},{1,5},{5,1},{9,13},{13,9},{2,6},{6,2},{1... | collective-permute-start | bytes 98312 | tf_op jit(solution)/shard_map/ppermute | solution.py:198
  70.1 4.6 %copy-done.4 = bf16[384,128,128]{2,1,0:T(8,128)(2,1)S(1)} copy-done((bf16[384,128,128]{2,1,0:T(8,128)(2,1)S(1)}, bf16[384,128,128]{2,1,0:T(8,128)(2,1)}, u32[]{:S(2)}) %copy-start.4) | copy-done | bytes 12582936
  74.7 2.9 %forward.5 = f32[16,16,128]{2,1,0:T(8,128)S(1)} custom-call(s32[384]{0:T(512)S(1)} %get-tuple-element.17.index, bf16[32,16,128]{2,1,0:T(8,128)(2,1)S(1)} %pad_maximum_fusion.3.refs_0_, bf16[32,16,128]{2,1,0:T(8,128)(2,1)S(1)} %collective-permute-done.13.refs_1_, bf16[384,128,128]{2,1,0:T(8,128)(2,1)S(1)} %copy-done.4), custom_call_target="tpu_custom_call" | custom-call | tf_op jit(solution)/shard_map/forward/pallas_call | solution.py:111
  80.5 4.1 %collective-permute-done.15.other = f32[16,16,128]{2,1,0:T(8,128)S(1)} collective-permute-done((f32[16,16,128]{2,1,0:T(8,128)S(1)}, f32[16,16,128]{2,1,0:T(8,128)S(1)}, u32[]{:S(2)}, u32[]{:S(2)}) %collective-permute-start.15) | collective-permute-done | bytes 131104 | tf_op jit(solution)/shard_map/ppermute | solution.py:233
  84.6 2.9 %slope_backward.5 = (f32[32,16,128]{2,1,0:T(8,128)S(1)}, f32[32,16,128]{2,1,0:T(8,128)S(1)}) custom-call(s32[384]{0:T(512)S(1)} %get-tuple-element.15.index, f32[384]{0:T(512)S(1)} %get-tuple-element.16.factor, f32[16,16,128]{2,1,0:T(8,128)S(1)} %add.84.own, f32[16,16,128]{2,1,0:T(8,128)S(1)} %collective-permute-done.15.other, ...), custom_call_target="tpu_custom_call" | custom-call | tf_op jit(solution)/shard_map/slope_backward/pallas_call | solution.py:159
  93.5 3.8 %collective-permute-done.19 = f32[8,16,128]{2,1,0:T(8,128)S(1)} collective-permute-done((f32[8,16,128]{2,1,0:T(8,128)S(1)}, f32[8,16,128]{2,1,0:T(8,128)S(1)}, u32[]{:S(2)}, u32[]{:S(2)}) %collective-permute-start.19) | collective-permute-done | bytes 65568 | tf_op jit(solution)/shard_map/ppermute | solution.py:198
  97.3 2.0 %collective-permute-done.18 = f32[8,16,128]{2,1,0:T(8,128)S(1)} collective-permute-done((f32[8,16,128]{2,1,0:T(8,128)S(1)}, f32[8,16,128]{2,1,0:T(8,128)S(1)}, u32[]{:S(2)}, u32[]{:S(2)}) %collective-permute-start.18) | collective-permute-done | bytes 65568 | tf_op jit(solution)/shard_map/ppermute | solution.py:198
  99.3 1.9 %collective-permute-start.22 = (bf16[8,16,128]{2,1,0:T(8,128)(2,1)S(1)}, bf16[8,16,128]{2,1,0:T(8,128)(2,1)S(1)}, u32[]{:S(2)}, u32[]{:S(2)}) collective-permute-start(bf16[8,16,128]{2,1,0:T(8,128)(2,1)S(1)} %get-tuple-element.40), channel_id=1, source_target_pairs={{0,12},{4,8},{8,4},{12,0},{1,13},{5,9},{9,5},{13,1},{2,14},{6,10},... | collective-permute-start | bytes 98312 | tf_op jit(solution)/shard_map/ppermute | solution.py:198
  101.2 2.6 %collective-permute-start.20 = (bf16[8,16,128]{2,1,0:T(8,128)(2,1)S(1)}, bf16[8,16,128]{2,1,0:T(8,128)(2,1)S(1)}, u32[]{:S(2)}, u32[]{:S(2)}) collective-permute-start(bf16[8,16,128]{2,1,0:T(8,128)(2,1)S(1)} %get-tuple-element.40), channel_id=1, source_target_pairs={{0,4},{4,0},{8,12},{12,8},{1,5},{5,1},{9,13},{13,9},{2,6},{6,2},{1... | collective-permute-start | bytes 98312 | tf_op jit(solution)/shard_map/ppermute | solution.py:198
  107.5 2.9 %forward.6 = f32[16,16,128]{2,1,0:T(8,128)S(1)} custom-call(s32[384]{0:T(512)S(1)} %get-tuple-element.17.index, bf16[32,16,128]{2,1,0:T(8,128)(2,1)S(1)} %pad_maximum_fusion.4.refs_0_, bf16[32,16,128]{2,1,0:T(8,128)(2,1)S(1)} %collective-permute-done.23.refs_1_, bf16[384,128,128]{2,1,0:T(8,128)(2,1)S(1)} %copy-done.4), custom_call_target="tpu_custom_call" | custom-call | tf_op jit(solution)/shard_map/forward/pallas_call | solution.py:111
  113.4 4.1 %collective-permute-done.25.other = f32[16,16,128]{2,1,0:T(8,128)S(1)} collective-permute-done((f32[16,16,128]{2,1,0:T(8,128)S(1)}, f32[16,16,128]{2,1,0:T(8,128)S(1)}, u32[]{:S(2)}, u32[]{:S(2)}) %collective-permute-start.25) | collective-permute-done | bytes 131104 | tf_op jit(solution)/shard_map/ppermute | solution.py:233
  117.4 2.9 %slope_backward.6 = (f32[32,16,128]{2,1,0:T(8,128)S(1)}, f32[32,16,128]{2,1,0:T(8,128)S(1)}) custom-call(s32[384]{0:T(512)S(1)} %get-tuple-element.15.index, f32[384]{0:T(512)S(1)} %get-tuple-element.16.factor, f32[16,16,128]{2,1,0:T(8,128)S(1)} %add.89.own, f32[16,16,128]{2,1,0:T(8,128)S(1)} %collective-permute-done.25.other, ...), custom_call_target="tpu_custom_call" | custom-call | tf_op jit(solution)/shard_map/slope_backward/pallas_call | solution.py:159
  126.3 3.8 %collective-permute-done.29 = f32[8,16,128]{2,1,0:T(8,128)S(1)} collective-permute-done((f32[8,16,128]{2,1,0:T(8,128)S(1)}, f32[8,16,128]{2,1,0:T(8,128)S(1)}, u32[]{:S(2)}, u32[]{:S(2)}) %collective-permute-start.29) | collective-permute-done | bytes 65568 | tf_op jit(solution)/shard_map/ppermute | solution.py:198
  130.1 2.0 %collective-permute-done.28 = f32[8,16,128]{2,1,0:T(8,128)S(1)} collective-permute-done((f32[8,16,128]{2,1,0:T(8,128)S(1)}, f32[8,16,128]{2,1,0:T(8,128)S(1)}, u32[]{:S(2)}, u32[]{:S(2)}) %collective-permute-start.28) | collective-permute-done | bytes 65568 | tf_op jit(solution)/shard_map/ppermute | solution.py:198
  134.1 2.6 %collective-permute-start.30 = (bf16[8,16,128]{2,1,0:T(8,128)(2,1)S(1)}, bf16[8,16,128]{2,1,0:T(8,128)(2,1)S(1)}, u32[]{:S(2)}, u32[]{:S(2)}) collective-permute-start(bf16[8,16,128]{2,1,0:T(8,128)(2,1)S(1)} %get-tuple-element.38), channel_id=1, source_target_pairs={{0,4},{4,0},{8,12},{12,8},{1,5},{5,1},{9,13},{13,9},{2,6},{6,2},{1... | collective-permute-start | bytes 98312 | tf_op jit(solution)/shard_map/ppermute | solution.py:198
  140.4 2.9 %forward.7 = f32[16,16,128]{2,1,0:T(8,128)S(1)} custom-call(s32[384]{0:T(512)S(1)} %get-tuple-element.17.index, bf16[32,16,128]{2,1,0:T(8,128)(2,1)S(1)} %pad_maximum_fusion.5.refs_0_, bf16[32,16,128]{2,1,0:T(8,128)(2,1)S(1)} %collective-permute-done.33.refs_1_, bf16[384,128,128]{2,1,0:T(8,128)(2,1)S(1)} %copy-done.4), custom_call_target="tpu_custom_call" | custom-call | tf_op jit(solution)/shard_map/forward/pallas_call | solution.py:111
  146.3 4.1 %collective-permute-done.35.other = f32[16,16,128]{2,1,0:T(8,128)S(1)} collective-permute-done((f32[16,16,128]{2,1,0:T(8,128)S(1)}, f32[16,16,128]{2,1,0:T(8,128)S(1)}, u32[]{:S(2)}, u32[]{:S(2)}) %collective-permute-start.35) | collective-permute-done | bytes 131104 | tf_op jit(solution)/shard_map/ppermute | solution.py:233
  150.3 2.9 %slope_backward.7 = (f32[32,16,128]{2,1,0:T(8,128)S(1)}, f32[32,16,128]{2,1,0:T(8,128)S(1)}) custom-call(s32[384]{0:T(512)S(1)} %get-tuple-element.15.index, f32[384]{0:T(512)S(1)} %get-tuple-element.16.factor, f32[16,16,128]{2,1,0:T(8,128)S(1)} %add.94.own, f32[16,16,128]{2,1,0:T(8,128)S(1)} %collective-permute-done.35.other, ...), custom_call_target="tpu_custom_call" | custom-call | tf_op jit(solution)/shard_map/slope_backward/pallas_call | solution.py:159
  159.2 3.8 %collective-permute-done.39 = f32[8,16,128]{2,1,0:T(8,128)S(1)} collective-permute-done((f32[8,16,128]{2,1,0:T(8,128)S(1)}, f32[8,16,128]{2,1,0:T(8,128)S(1)}, u32[]{:S(2)}, u32[]{:S(2)}) %collective-permute-start.39) | collective-permute-done | bytes 65568 | tf_op jit(solution)/shard_map/ppermute | solution.py:198
  163.0 2.0 %collective-permute-done.38 = f32[8,16,128]{2,1,0:T(8,128)S(1)} collective-permute-done((f32[8,16,128]{2,1,0:T(8,128)S(1)}, f32[8,16,128]{2,1,0:T(8,128)S(1)}, u32[]{:S(2)}, u32[]{:S(2)}) %collective-permute-start.38) | collective-permute-done | bytes 65568 | tf_op jit(solution)/shard_map/ppermute | solution.py:198
  (133 shorter events, 56.1 us)
Async XLA Ops:
  1.6 7.0 %collective-permute-start.2 = (bf16[8,16,128]{2,1,0:T(8,128)(2,1)S(1)}, bf16[8,16,128]{2,1,0:T(8,128)(2,1)S(1)}, u32[]{:S(2)}, u32[]{:S(2)}) collective-permute-start(bf16[8,16,128]{2,1,0:T(8,128)(2,1)S(1)} %bitcast.53), channel_id=1, source_target_pairs={{0,12},{4,8},{8,4},{12,0},{1,13},{5,9},{9,5},{13,1},{2,14},{6,10},... | collective-permute-start | bytes 98312 | tf_op jit(solution)/shard_map/ppermute | solution.py:198
  6.7 4.8 %collective-permute-start.1 = (bf16[8,16,128]{2,1,0:T(8,128)(2,1)S(1)}, bf16[8,16,128]{2,1,0:T(8,128)(2,1)S(1)}, u32[]{:S(2)}, u32[]{:S(2)}) collective-permute-start(bf16[8,16,128]{2,1,0:T(8,128)(2,1)S(1)} %bitcast.54), channel_id=1, source_target_pairs={{0,8},{4,12},{8,0},{12,4},{1,9},{5,13},{9,1},{13,5},{2,10},{6,14},... | collective-permute-start | bytes 98312 | tf_op jit(solution)/shard_map/ppermute | solution.py:198
  6.7 4.8 %collective-permute-start = (bf16[8,16,128]{2,1,0:T(8,128)(2,1)S(1)}, bf16[8,16,128]{2,1,0:T(8,128)(2,1)S(1)}, u32[]{:S(2)}, u32[]{:S(2)}) collective-permute-start(bf16[8,16,128]{2,1,0:T(8,128)(2,1)S(1)} %bitcast.55), channel_id=1, source_target_pairs={{0,4},{4,0},{8,12},{12,8},{1,5},{5,1},{9,13},{13,9},{2,6},{6,2},{1... | collective-permute-start | bytes 98312 | tf_op jit(solution)/shard_map/ppermute | solution.py:198
  11.5 15.9 %collective-permute-start.3 = (bf16[32,16,128]{2,1,0:T(8,128)(2,1)S(1)}, bf16[32,16,128]{2,1,0:T(8,128)(2,1)S(1)}, u32[]{:S(2)}, u32[]{:S(2)}) collective-permute-start(bf16[32,16,128]{2,1,0:T(8,128)(2,1)S(1)} %pad_maximum_fusion.2.refs_0_), channel_id=1, source_target_pairs={{0,1},{1,0},{2,3},{3,2},{4,5},{5,4},{6,7},{7,6},{8,9},{9,8},{10,11... | collective-permute-start | bytes 393224 | tf_op jit(solution)/shard_map/ppermute | solution.py:203
  36.5 6.0 %collective-permute-start.5 = (f32[17,16,128]{2,1,0:T(8,128)S(1)}, f32[17,16,128]{2,1,0:T(8,128)S(1)}, u32[]{:S(2)}, u32[]{:S(2)}) collective-permute-start(f32[17,16,128]{2,1,0:T(8,128)S(1)} %pad_maximum_fusion.1), channel_id=1, source_target_pairs={{0,2},{2,0},{1,3},{3,1},{4,6},{6,4},{5,7},{7,5},{8,10},{10,8},{9,1... | collective-permute-start | bytes 417800 | tf_op jit(solution)/shard_map/ppermute | solution.py:233
  50.3 1.6 collective-permute-start.6
  52.0 4.3 %collective-permute-start.7 = (f32[8,16,128]{2,1,0:T(8,128)S(1)}, f32[8,16,128]{2,1,0:T(8,128)S(1)}, u32[]{:S(2)}, u32[]{:S(2)}) collective-permute-start(f32[8,16,128]{2,1,0:T(8,128)S(1)} %get-tuple-element.57), channel_id=1, source_target_pairs={{0,4},{4,0},{8,12},{12,8},{1,5},{5,1},{9,13},{13,9},{2,6},{6,2},{1... | collective-permute-start | bytes 196616 | tf_op jit(solution)/shard_map/ppermute | solution.py:198
  52.1 7.8 %collective-permute-start.9 = (f32[8,16,128]{2,1,0:T(8,128)S(1)}, f32[8,16,128]{2,1,0:T(8,128)S(1)}, u32[]{:S(2)}, u32[]{:S(2)}) collective-permute-start(f32[8,16,128]{2,1,0:T(8,128)S(1)} %get-tuple-element.58), channel_id=1, source_target_pairs={{0,12},{4,8},{8,4},{12,0},{1,13},{5,9},{9,5},{13,1},{2,14},{6,10},... | collective-permute-start | bytes 196616 | tf_op jit(solution)/shard_map/ppermute | solution.py:198
  55.5 6.3 %collective-permute-start.8 = (f32[8,16,128]{2,1,0:T(8,128)S(1)}, f32[8,16,128]{2,1,0:T(8,128)S(1)}, u32[]{:S(2)}, u32[]{:S(2)}) collective-permute-start(f32[8,16,128]{2,1,0:T(8,128)S(1)} %get-tuple-element.59), channel_id=1, source_target_pairs={{0,8},{4,12},{8,0},{12,4},{1,9},{5,13},{9,1},{13,5},{2,10},{6,14},... | collective-permute-start | bytes 196616 | tf_op jit(solution)/shard_map/ppermute | solution.py:198
  61.9 5.9 %collective-permute-start.12 = (bf16[8,16,128]{2,1,0:T(8,128)(2,1)S(1)}, bf16[8,16,128]{2,1,0:T(8,128)(2,1)S(1)}, u32[]{:S(2)}, u32[]{:S(2)}) collective-permute-start(bf16[8,16,128]{2,1,0:T(8,128)(2,1)S(1)} %get-tuple-element.42), channel_id=1, source_target_pairs={{0,12},{4,8},{8,4},{12,0},{1,13},{5,9},{9,5},{13,1},{2,14},{6,10},... | collective-permute-start | bytes 98312 | tf_op jit(solution)/shard_map/ppermute | solution.py:198
  63.6 5.0 %collective-permute-start.11 = (bf16[8,16,128]{2,1,0:T(8,128)(2,1)S(1)}, bf16[8,16,128]{2,1,0:T(8,128)(2,1)S(1)}, u32[]{:S(2)}, u32[]{:S(2)}) collective-permute-start(bf16[8,16,128]{2,1,0:T(8,128)(2,1)S(1)} %get-tuple-element.42), channel_id=1, source_target_pairs={{0,8},{4,12},{8,0},{12,4},{1,9},{5,13},{9,1},{13,5},{2,10},{6,14},... | collective-permute-start | bytes 98312 | tf_op jit(solution)/shard_map/ppermute | solution.py:198
  63.6 5.0 %collective-permute-start.10 = (bf16[8,16,128]{2,1,0:T(8,128)(2,1)S(1)}, bf16[8,16,128]{2,1,0:T(8,128)(2,1)S(1)}, u32[]{:S(2)}, u32[]{:S(2)}) collective-permute-start(bf16[8,16,128]{2,1,0:T(8,128)(2,1)S(1)} %get-tuple-element.42), channel_id=1, source_target_pairs={{0,4},{4,0},{8,12},{12,8},{1,5},{5,1},{9,13},{13,9},{2,6},{6,2},{1... | collective-permute-start | bytes 98312 | tf_op jit(solution)/shard_map/ppermute | solution.py:198
  79.0 5.6 %collective-permute-start.15 = (f32[16,16,128]{2,1,0:T(8,128)S(1)}, f32[16,16,128]{2,1,0:T(8,128)S(1)}, u32[]{:S(2)}, u32[]{:S(2)}) collective-permute-start(f32[16,16,128]{2,1,0:T(8,128)S(1)} %add.84.own), channel_id=1, source_target_pairs={{0,2},{2,0},{1,3},{3,1},{4,6},{6,4},{5,7},{7,5},{8,10},{10,8},{9,1... | collective-permute-start | bytes 393224 | tf_op jit(solution)/shard_map/ppermute | solution.py:233
  87.5 1.6 collective-permute-start.16
  89.2 4.3 %collective-permute-start.17 = (f32[8,16,128]{2,1,0:T(8,128)S(1)}, f32[8,16,128]{2,1,0:T(8,128)S(1)}, u32[]{:S(2)}, u32[]{:S(2)}) collective-permute-start(f32[8,16,128]{2,1,0:T(8,128)S(1)} %get-tuple-element.54), channel_id=1, source_target_pairs={{0,4},{4,0},{8,12},{12,8},{1,5},{5,1},{9,13},{13,9},{2,6},{6,2},{1... | collective-permute-start | bytes 196616 | tf_op jit(solution)/shard_map/ppermute | solution.py:198
  90.9 6.5 %collective-permute-start.19 = (f32[8,16,128]{2,1,0:T(8,128)S(1)}, f32[8,16,128]{2,1,0:T(8,128)S(1)}, u32[]{:S(2)}, u32[]{:S(2)}) collective-permute-start(f32[8,16,128]{2,1,0:T(8,128)S(1)} %get-tuple-element.55), channel_id=1, source_target_pairs={{0,12},{4,8},{8,4},{12,0},{1,13},{5,9},{9,5},{13,1},{2,14},{6,10},... | collective-permute-start | bytes 196616 | tf_op jit(solution)/shard_map/ppermute | solution.py:198
  92.5 6.8 %collective-permute-start.18 = (f32[8,16,128]{2,1,0:T(8,128)S(1)}, f32[8,16,128]{2,1,0:T(8,128)S(1)}, u32[]{:S(2)}, u32[]{:S(2)}) collective-permute-start(f32[8,16,128]{2,1,0:T(8,128)S(1)} %get-tuple-element.56), channel_id=1, source_target_pairs={{0,8},{4,12},{8,0},{12,4},{1,9},{5,13},{9,1},{13,5},{2,10},{6,14},... | collective-permute-start | bytes 196616 | tf_op jit(solution)/shard_map/ppermute | solution.py:198
  99.3 5.9 %collective-permute-start.22 = (bf16[8,16,128]{2,1,0:T(8,128)(2,1)S(1)}, bf16[8,16,128]{2,1,0:T(8,128)(2,1)S(1)}, u32[]{:S(2)}, u32[]{:S(2)}) collective-permute-start(bf16[8,16,128]{2,1,0:T(8,128)(2,1)S(1)} %get-tuple-element.40), channel_id=1, source_target_pairs={{0,12},{4,8},{8,4},{12,0},{1,13},{5,9},{9,5},{13,1},{2,14},{6,10},... | collective-permute-start | bytes 98312 | tf_op jit(solution)/shard_map/ppermute | solution.py:198
  101.2 4.8 %collective-permute-start.21 = (bf16[8,16,128]{2,1,0:T(8,128)(2,1)S(1)}, bf16[8,16,128]{2,1,0:T(8,128)(2,1)S(1)}, u32[]{:S(2)}, u32[]{:S(2)}) collective-permute-start(bf16[8,16,128]{2,1,0:T(8,128)(2,1)S(1)} %get-tuple-element.40), channel_id=1, source_target_pairs={{0,8},{4,12},{8,0},{12,4},{1,9},{5,13},{9,1},{13,5},{2,10},{6,14},... | collective-permute-start | bytes 98312 | tf_op jit(solution)/shard_map/ppermute | solution.py:198
  101.2 4.8 %collective-permute-start.20 = (bf16[8,16,128]{2,1,0:T(8,128)(2,1)S(1)}, bf16[8,16,128]{2,1,0:T(8,128)(2,1)S(1)}, u32[]{:S(2)}, u32[]{:S(2)}) collective-permute-start(bf16[8,16,128]{2,1,0:T(8,128)(2,1)S(1)} %get-tuple-element.40), channel_id=1, source_target_pairs={{0,4},{4,0},{8,12},{12,8},{1,5},{5,1},{9,13},{13,9},{2,6},{6,2},{1... | collective-permute-start | bytes 98312 | tf_op jit(solution)/shard_map/ppermute | solution.py:198
  111.8 5.6 %collective-permute-start.25 = (f32[16,16,128]{2,1,0:T(8,128)S(1)}, f32[16,16,128]{2,1,0:T(8,128)S(1)}, u32[]{:S(2)}, u32[]{:S(2)}) collective-permute-start(f32[16,16,128]{2,1,0:T(8,128)S(1)} %add.89.own), channel_id=1, source_target_pairs={{0,2},{2,0},{1,3},{3,1},{4,6},{6,4},{5,7},{7,5},{8,10},{10,8},{9,1... | collective-permute-start | bytes 393224 | tf_op jit(solution)/shard_map/ppermute | solution.py:233
  120.3 1.6 collective-permute-start.26
  122.0 4.3 %collective-permute-start.27 = (f32[8,16,128]{2,1,0:T(8,128)S(1)}, f32[8,16,128]{2,1,0:T(8,128)S(1)}, u32[]{:S(2)}, u32[]{:S(2)}) collective-permute-start(f32[8,16,128]{2,1,0:T(8,128)S(1)} %get-tuple-element.51), channel_id=1, source_target_pairs={{0,4},{4,0},{8,12},{12,8},{1,5},{5,1},{9,13},{13,9},{2,6},{6,2},{1... | collective-permute-start | bytes 196616 | tf_op jit(solution)/shard_map/ppermute | solution.py:198
  123.7 6.5 %collective-permute-start.29 = (f32[8,16,128]{2,1,0:T(8,128)S(1)}, f32[8,16,128]{2,1,0:T(8,128)S(1)}, u32[]{:S(2)}, u32[]{:S(2)}) collective-permute-start(f32[8,16,128]{2,1,0:T(8,128)S(1)} %get-tuple-element.52), channel_id=1, source_target_pairs={{0,12},{4,8},{8,4},{12,0},{1,13},{5,9},{9,5},{13,1},{2,14},{6,10},... | collective-permute-start | bytes 196616 | tf_op jit(solution)/shard_map/ppermute | solution.py:198
  125.5 6.6 %collective-permute-start.28 = (f32[8,16,128]{2,1,0:T(8,128)S(1)}, f32[8,16,128]{2,1,0:T(8,128)S(1)}, u32[]{:S(2)}, u32[]{:S(2)}) collective-permute-start(f32[8,16,128]{2,1,0:T(8,128)S(1)} %get-tuple-element.53), channel_id=1, source_target_pairs={{0,8},{4,12},{8,0},{12,4},{1,9},{5,13},{9,1},{13,5},{2,10},{6,14},... | collective-permute-start | bytes 196616 | tf_op jit(solution)/shard_map/ppermute | solution.py:198
  132.2 5.8 %collective-permute-start.32 = (bf16[8,16,128]{2,1,0:T(8,128)(2,1)S(1)}, bf16[8,16,128]{2,1,0:T(8,128)(2,1)S(1)}, u32[]{:S(2)}, u32[]{:S(2)}) collective-permute-start(bf16[8,16,128]{2,1,0:T(8,128)(2,1)S(1)} %get-tuple-element.38), channel_id=1, source_target_pairs={{0,12},{4,8},{8,4},{12,0},{1,13},{5,9},{9,5},{13,1},{2,14},{6,10},... | collective-permute-start | bytes 98312 | tf_op jit(solution)/shard_map/ppermute | solution.py:198
  134.1 4.9 %collective-permute-start.31 = (bf16[8,16,128]{2,1,0:T(8,128)(2,1)S(1)}, bf16[8,16,128]{2,1,0:T(8,128)(2,1)S(1)}, u32[]{:S(2)}, u32[]{:S(2)}) collective-permute-start(bf16[8,16,128]{2,1,0:T(8,128)(2,1)S(1)} %get-tuple-element.38), channel_id=1, source_target_pairs={{0,8},{4,12},{8,0},{12,4},{1,9},{5,13},{9,1},{13,5},{2,10},{6,14},... | collective-permute-start | bytes 98312 | tf_op jit(solution)/shard_map/ppermute | solution.py:198
  134.1 4.9 %collective-permute-start.30 = (bf16[8,16,128]{2,1,0:T(8,128)(2,1)S(1)}, bf16[8,16,128]{2,1,0:T(8,128)(2,1)S(1)}, u32[]{:S(2)}, u32[]{:S(2)}) collective-permute-start(bf16[8,16,128]{2,1,0:T(8,128)(2,1)S(1)} %get-tuple-element.38), channel_id=1, source_target_pairs={{0,4},{4,0},{8,12},{12,8},{1,5},{5,1},{9,13},{13,9},{2,6},{6,2},{1... | collective-permute-start | bytes 98312 | tf_op jit(solution)/shard_map/ppermute | solution.py:198
  144.7 5.6 %collective-permute-start.35 = (f32[16,16,128]{2,1,0:T(8,128)S(1)}, f32[16,16,128]{2,1,0:T(8,128)S(1)}, u32[]{:S(2)}, u32[]{:S(2)}) collective-permute-start(f32[16,16,128]{2,1,0:T(8,128)S(1)} %add.94.own), channel_id=1, source_target_pairs={{0,2},{2,0},{1,3},{3,1},{4,6},{6,4},{5,7},{7,5},{8,10},{10,8},{9,1... | collective-permute-start | bytes 393224 | tf_op jit(solution)/shard_map/ppermute | solution.py:233
  154.9 4.3 %collective-permute-start.37 = (f32[8,16,128]{2,1,0:T(8,128)S(1)}, f32[8,16,128]{2,1,0:T(8,128)S(1)}, u32[]{:S(2)}, u32[]{:S(2)}) collective-permute-start(f32[8,16,128]{2,1,0:T(8,128)S(1)} %get-tuple-element.48), channel_id=1, source_target_pairs={{0,4},{4,0},{8,12},{12,8},{1,5},{5,1},{9,13},{13,9},{2,6},{6,2},{1... | collective-permute-start | bytes 196616 | tf_op jit(solution)/shard_map/ppermute | solution.py:198
  156.5 6.5 %collective-permute-start.39 = (f32[8,16,128]{2,1,0:T(8,128)S(1)}, f32[8,16,128]{2,1,0:T(8,128)S(1)}, u32[]{:S(2)}, u32[]{:S(2)}) collective-permute-start(f32[8,16,128]{2,1,0:T(8,128)S(1)} %get-tuple-element.49), channel_id=1, source_target_pairs={{0,12},{4,8},{8,4},{12,0},{1,13},{5,9},{9,5},{13,1},{2,14},{6,10},... | collective-permute-start | bytes 196616 | tf_op jit(solution)/shard_map/ppermute | solution.py:198
  158.3 6.6 %collective-permute-start.38 = (f32[8,16,128]{2,1,0:T(8,128)S(1)}, f32[8,16,128]{2,1,0:T(8,128)S(1)}, u32[]{:S(2)}, u32[]{:S(2)}) collective-permute-start(f32[8,16,128]{2,1,0:T(8,128)S(1)} %get-tuple-element.50), channel_id=1, source_target_pairs={{0,8},{4,12},{8,0},{12,4},{1,9},{5,13},{9,1},{13,5},{2,10},{6,14},... | collective-permute-start | bytes 196616 | tf_op jit(solution)/shard_map/ppermute | solution.py:198
  (24 other events, 243.6 us)

commit v3 on v2

--- a/solution.py
+++ b/solution.py
@@ -10,7 +10,7 @@
 ITERS = 4
 F32 = jnp.float32
 BF16 = jnp.bfloat16
-PARAMS = pltpu.CompilerParams(vmem_limit_bytes=20 * 2**20)
+PARAMS = pltpu.CompilerParams(vmem_limit_bytes=8 * 2**20)
 
 
 def in_vmem():
@@ -25,14 +25,14 @@
     return pltpu.with_memory_space_constraint(array, pltpu.VMEM)
 
 
-def load_kernel(place, cols, exps, live, stored, kept, turned, index, places, factor, sems):
-    z, core, n_vox = place[0], place[1], place[2]
-    rows, _, slots = cols.shape
-    columns = place[3]
+def load_kernel(n_vox, columns, row0, me, cols, exps, live, stored, kept, turned, index, places, factor, sems):
+    z, core = me[0], me[1]
+    slots = cols.shape[2]
+    rows = kept.shape[0] // slots
     own = columns // (2 * n_vox)
     copies = [
         pltpu.make_async_copy(
-            stored.at[pl.ds(b * slots, slots)], kept.at[pl.ds(b * slots, slots)], sems.at[b]
+            stored.at[pl.ds((row0 + b) * slots, slots)], kept.at[pl.ds(b * slots, slots)], sems.at[b]
         )
         for b in range(rows)
     ]
@@ -41,17 +41,17 @@
     step = 8 if slots % 8 == 0 else 1
     for b, copy in enumerate(copies):
         copy.wait()
-
-        def turn(t, carry, b=b):
+        used_slots = live[row0 + b, 0] - core * slots
+
+        def turn(t, carry, b=b, used_slots=used_slots):
             for u in range(step):
                 k = t * step + u
                 n = b * slots + k
                 turned[n] = kept[n].T
-                column, exponent = cols[b, 0, k], exps[b, 0, k]
-                piece, within = lax.div(column, own), lax.rem(column, own)
-                owner_core, owner_z = lax.rem(piece, 2), lax.div(piece, 2)
-                at = ((owner_core ^ core) * n_vox + (owner_z ^ z)) * own + within
-                used = core * slots + k < live[b, 0]
+                column, exponent = cols[row0 + b, 0, k], exps[row0 + b, 0, k]
+                piece, within = column // own, column % own
+                at = (((piece % 2) ^ core) * n_vox + ((piece // 2) ^ z)) * own + within
+                used = k < used_slots
                 scale = jnp.where(exponent < 0, 0.5, jnp.where(exponent > 0, 2.0, 1.0))
                 places[n] = at
                 index[n] = jnp.where(used, (exponent + 1) * columns + at, 3 * columns)
@@ -61,21 +61,22 @@
         lax.fori_loop(0, slots // step, turn, 0)
 
 
-def load_matrix(place, cols, exps, live, tiles):
-    rows, _, slots = cols.shape
+def load_matrix(n_vox, columns, row0, rows, me, cols, exps, live, tiles):
+    slots = cols.shape[2]
+    shape = (rows * slots,) + tiles.shape[1:]
     return pl.pallas_call(
-        load_kernel,
+        functools.partial(load_kernel, n_vox, columns, row0),
         in_specs=[in_smem()] * 4 + [pl.BlockSpec(memory_space=pltpu.HBM)],
         out_specs=[in_vmem()] * 2 + [in_smem()] * 3,
-        out_shape=[pltpu.VMEM(tiles.shape, tiles.dtype)] * 2
-        + [jax.ShapeDtypeStruct((rows * slots,), t) for t in (jnp.int32, jnp.int32, F32)],
+        out_shape=[pltpu.VMEM(shape, tiles.dtype)] * 2
+        + [jax.ShapeDtypeStruct(shape[:1], t) for t in (jnp.int32, jnp.int32, F32)],
         scratch_shapes=[pltpu.SemaphoreType.DMA((rows,))],
         compiler_params=PARAMS,
         cost_estimate=pl.CostEstimate(
-            flops=0, bytes_accessed=2 * tiles.size * 2, transcendentals=0
+            flops=0, bytes_accessed=8 * rows * slots * tiles.shape[1] * tiles.shape[2], transcendentals=0
         ),
         name="load_matrix",
-    )(place, cols, exps, live, tiles)
+    )(me, *(pltpu.with_memory_space_constraint(a, pltpu.HBM) for a in (cols, exps, live, tiles)))
 
 
 def forward_kernel(slots, index, *refs):
@@ -115,18 +116,24 @@
         out_shape=jax.ShapeDtypeStruct((rows, weightings, width), F32),
         scratch_shapes=[pltpu.VMEM((3 * columns + 1, weightings, width), BF16)],
         compiler_params=PARAMS,
+        cost_estimate=pl.CostEstimate(
+            flops=2 * rows * slots * weightings * width * width,
+            bytes_accessed=2 * rows * slots * width * width,
+            transcendentals=0,
+        ),
         name="forward",
     )(index, *pieces, held(turned))
 
 
-def backward_kernel(slots, index, factor, own, other, levels, kept, far, near, slope, total):
+def backward_kernel(slots, first, last, index, factor, own, other, levels, kept, *refs):
+    *before, slope, total = refs
     dose = own[...] + other[...]
     upper_dose, upper_weight, lower_dose, lower_weight = (levels[i] for i in range(4))
     slope[...] = (
         upper_weight * jax.nn.sigmoid(4.0 * (dose - upper_dose))
         - lower_weight * jax.nn.sigmoid(4.0 * (lower_dose - dose))
     ).astype(BF16)
-    total[...] = jnp.zeros_like(total)
+    total[...] = jnp.zeros_like(total) if first else before.pop(0)[...]
     rows = own.shape[0]
     width = kept.shape[-1]
     unroll = 4 if rows % 4 == 0 else 1
@@ -148,26 +155,36 @@
         return carry
 
     lax.fori_loop(0, rows // unroll, some_rows, 0)
-    half = near.shape[0]
-    near[...] = total[:half]
-    far[...] = total[half:]
-
-
-def backward(index, factor, own, other, levels, kept, columns, slots):
+    if last:
+        far, near = before
+        half = near.shape[0]
+        near[...] = total[:half]
+        far[...] = total[half:]
+    else:
+        before[0][...] = total[...]
+
+
+def backward(index, factor, own, other, levels, kept, columns, slots, total, last):
     rows, weightings, width = own.shape
-    half = (columns // 2, weightings, width)
+    first = total is None
+    out = [(columns // 2, weightings, width)] * 2 if last else [(columns, weightings, width)]
     return pl.pallas_call(
-        functools.partial(backward_kernel, slots),
-        in_specs=[in_smem()] * 2 + [in_vmem()] * 4,
-        out_specs=[in_vmem()] * 2,
-        out_shape=[jax.ShapeDtypeStruct(half, F32)] * 2,
+        functools.partial(backward_kernel, slots, first, last),
+        in_specs=[in_smem()] * 2 + [in_vmem()] * (4 if first else 5),
+        out_specs=[in_vmem()] * len(out),
+        out_shape=[jax.ShapeDtypeStruct(shape, F32) for shape in out],
         scratch_shapes=[
             pltpu.VMEM((rows, weightings, width), BF16),
             pltpu.VMEM((columns, weightings, width), F32),
         ],
         compiler_params=PARAMS,
+        cost_estimate=pl.CostEstimate(
+            flops=2 * rows * slots * weightings * width * width,
+            bytes_accessed=2 * rows * slots * width * width,
+            transcendentals=0,
+        ),
         name="slope_backward",
-    )(index, factor, own, other, levels, held(kept))
+    )(index, factor, own, other, levels, held(kept), *([] if first else [total]))
 
 
 def per_device(
@@ -202,55 +219,86 @@
     def over_rep(array):
         return lax.ppermute(array, "rep", [(0, 1), (1, 0)])
 
-    place = jnp.stack([z, core, n_vox, columns]).astype(jnp.int32)
+    me = jnp.stack([z, core]).astype(jnp.int32)
     level_table = jnp.stack([upper_dose, upper_weight, lower_dose, lower_weight])
     known = labels.astype(F32).reshape(-1, width)
+    tiles = dose_blocks.reshape(rows * slots, width, width)
+    halves = 2 if rows % 2 == 0 else 1
+    some = rows // halves
+
+    def load(h):
+        return load_matrix(
+            n_vox, columns, h * some, some, me, block_cols, block_exps, live_counts, tiles
+        )
 
     def gather_weights(weights):
         piece = weights.astype(BF16)
         return [piece] + over_vox([piece] * (n_vox - 1))
 
+    exchanges = [("rep", 2, 1, core)]
+    bit = 1
+    while bit < n_spot:
+        exchanges.append(("spot", n_spot, bit, x))
+        bit *= 2
+
     pieces = gather_weights(weights)
-    kept, turned, index, places, factor = load_matrix(
-        place, block_cols, block_exps, live_counts, dose_blocks.reshape(rows * slots, width, width)
-    )
+    parts = [load(0)]
+    pieces, first_part = lax.optimization_barrier((pieces, parts[0][2:]))
+    parts[0] = [*parts[0][:2], *first_part]
+    parts += [load(h) for h in range(1, halves)]
 
     for step in range(ITERS):
         near = jnp.concatenate(pieces, axis=0)
-        dose = forward(index, [near, over_rep(near)], turned, rows, slots)
-
-        exchanges = [("rep", 2, 1, core)]
-        bit = 1
-        while bit < n_spot:
-            exchanges.append(("spot", n_spot, bit, x))
-            bit *= 2
-        for axis, size, bit, at in exchanges:
-            sent = dose
-            if step == 0:
-                n = known.shape[0]
-                tile = jnp.pad(known, ((0, weightings - n), (0, 0)))
-                sent = jnp.concatenate([dose, tile[None]], axis=0)
-            got = lax.ppermute(sent, axis, [(i, i ^ bit) for i in range(size)])
-            if step == 0:
-                theirs = got[rows, :n]
-                first = (at // bit) % 2 == 0
-                known = jnp.concatenate(
-                    [jnp.where(first, known, theirs), jnp.where(first, theirs, known)]
-                )
-                got = got[:rows]
-            if (axis, bit) != (exchanges[-1][0], exchanges[-1][2]):
-                dose = dose + got
+        weight_halves = [near, over_rep(near)]
+        doses = [forward(index, weight_halves, turned, some, slots) for _, turned, index, _, _ in parts]
+
+        own_doses, other_doses = [], []
+        for h, dose in enumerate(doses):
+            with_labels = step == 0 and h == 0
+            for axis, size, bit, at in exchanges:
+                sent = dose
+                if with_labels:
+                    n = known.shape[0]
+                    tile = jnp.pad(known, ((0, weightings - n), (0, 0)))
+                    sent = jnp.concatenate([dose, tile[None]], axis=0)
+                got = lax.ppermute(sent, axis, [(i, i ^ bit) for i in range(size)])
+                if with_labels:
+                    theirs = got[some, :n]
+                    first = (at // bit) % 2 == 0
+                    known = jnp.concatenate(
+                        [jnp.where(first, known, theirs), jnp.where(first, theirs, known)]
+                    )
+                    got = got[:some]
+                if (axis, bit) != (exchanges[-1][0], exchanges[-1][2]):
+                    dose = dose + got
+            own_doses.append(dose)
+            other_doses.append(got)
         if step == 0:
             levels = jnp.zeros((4, rows, 1, width), F32)
             for c in range(level_table.shape[1]):
                 value = level_table[:, c][:, None, None, None]
                 levels = jnp.where(known[None, :, None, :] == c, value, levels)
 
-        far, near = backward(places, factor, dose, got, levels, kept, columns, slots)
+        total = None
+        for h, (kept, _, _, places, factor) in enumerate(parts):
+            result = backward(
+                places,
+                factor,
+                own_doses[h],
+                other_doses[h],
+                levels[:, h * some : (h + 1) * some],
+                kept,
+                columns,
+                slots,
+                total,
+                h == halves - 1,
+            )
+            total = result[0]
+        far, near = result
         near = near + over_rep(far)
-        parts = over_vox([near[d * own : (d + 1) * own] for d in range(1, n_vox)])
+        received = over_vox([near[d * own : (d + 1) * own] for d in range(1, n_vox)])
         gradient = near[:own]
-        for part in parts:
+        for part in received:
             gradient = gradient + part
         weights = jnp.maximum(weights - 0.5 * gradient, 0.0)
         if step < ITERS - 1:

time: 168 us -> 166 us (0.988)
  waiting for transfers between devices: 68.8 us -> 52 us
  Pallas kernels: 32 us -> 41.7 us
  starting transfers between devices: 41.4 us -> 49.2 us
  local copies, waits for them, and re-layouts: 23.1 us -> 20.7 us
    ppermute x8 -> x16, waiting for transfers between devices: 20.9 us -> 6.96 us  [per_device(): got = lax.ppermute(sent, axis, [(i, i ^ bit) for i in range(size)])]
    pallas_call x5 -> x10, Pallas kernels: 20.6 us -> 27.6 us  [the longest x8 14 us: backward(): pl.pallas_call(functools.partial(backward_kernel, slots, first, last), in...]
    ppermute x8 -> x16, starting transfers between devices: 7.39 us -> 14.2 us  [per_device(): got = lax.ppermute(sent, axis, [(i, i ^ bit) for i in range(size)])]
    ppermute x24, waiting for transfers between devices: 36.5 us -> 33.6 us  [over_vox(): lax.ppermute(a, 'vox', [(i, i ^ d) for i in range(n_vox)])]
    pallas_call x4 -> x8, Pallas kernels: 11.5 us -> 14.1 us  [forward(): pl.pallas_call(functools.partial(forward_kernel, slots), in_specs=[in_sme...]
    unnamed x32 -> x41, local copies, waits for them, and re-layouts: 21.3 us -> 18.9 us
  transfers between devices with their start and end apart: 41 -> 49, of which waited for: 36 -> 32; matrix products, arithmetic and copies ran while one was open for 1% -> 1% of each run, Pallas kernels for 5% -> 17%
where the time goes in v3:
time: 166 us
  waiting for transfers between devices  52 us (31%)
  starting transfers between devices  49.2 us (30%)
  Pallas kernels  41.7 us (25%)
  local copies, waits for them, and re-layouts  20.7 us (12%)
    ppermute x24, starting transfers between devices, over_vox(): lax.ppermute(a, 'vox', [(i, i ^ d) for i in range(n_vox)])  34.3 us
    ppermute x24, waiting for transfers between devices, over_vox(): lax.ppermute(a, 'vox', [(i, i ^ d) for i in range(n_vox)])  33.6 us
    unnamed x41, local copies, waits for them, and re-layouts  18.9 us
    ppermute x16, starting transfers between devices, per_device(): got = lax.ppermute(sent, axis, [(i, i ^ bit) for i in range(size)])  14.2 us
    pallas_call x8, Pallas kernels, forward(): pl.pallas_call(functools.partial(forward_kernel, slots), in_specs=[in_sme...  14.1 us
    pallas_call x8, Pallas kernels, backward(): pl.pallas_call(functools.partial(backward_kernel, slots, first, last), in...  14 us
    pallas_call x2, Pallas kernels, load_matrix(): pl.pallas_call(functools.partial(load_kernel, n_vox, columns, row0), in_s...  13.6 us
    ppermute x9, waiting for transfers between devices, over_rep(): return lax.ppermute(array, 'rep', [(0, 1), (1, 0)])  11.4 us
  transfers between devices with their start and end apart: 49, of which 32 were waited for; matrix products, arithmetic and copies ran while one was open for 1% of the time, Pallas kernels for 17%

profile of v3, /device:TPU:0, one launch (start us, length us, event | category | flops | bytes accessed | tf_op | source)
XLA Modules:
  0.0 165.7 jit_solution(17200105642801061160)
XLA Ops:
  1.6 5.1 %collective-permute-start.2 = (bf16[8,16,128]{2,1,0:T(8,128)(2,1)S(1)}, bf16[8,16,128]{2,1,0:T(8,128)(2,1)S(1)}, u32[]{:S(2)}, u32[]{:S(2)}) collective-permute-start(bf16[8,16,128]{2,1,0:T(8,128)(2,1)S(1)} %bitcast.54), channel_id=1, source_target_pairs={{0,12},{4,8},{8,4},{12,0},{1,13},{5,9},{9,5},{13,1},{2,14},{6,10},... | collective-permute-start | bytes 98312 | tf_op jit(solution)/shard_map/ppermute | solution.py:215
  8.7 6.9 %load_matrix.3 = (bf16[192,128,128]{2,1,0:T(8,128)(2,1)S(1)}, bf16[192,128,128]{2,1,0:T(8,128)(2,1)S(1)}, s32[192]{0:T(256)S(1)}, s32[192]{0:T(256)S(1)}, f32[192]{0:T(256)S(1)}) custom-call(s32[2]{0:T(128)S(1)} %pad_add_fusion.me, s32[16,1,24]{2,1,0:T(1,128)} %cols.3, s32[16,1,24]{2,1,0:T(1,128)} %exps.3, s32[16,1]{1,0:T(8,128)} %copy.15.live, ...), custom_call_target="tpu_custom_call" | custom-call | bytes 25165824 | tf_op jit(solution)/shard_map/load_matrix/pallas_call | solution.py:67
  15.6 2.6 %copy-done.1 = bf16[192,128,128]{2,1,0:T(8,128)(2,1)} copy-done((bf16[192,128,128]{2,1,0:T(8,128)(2,1)}, bf16[192,128,128]{2,1,0:T(8,128)(2,1)S(1)}, u32[]{:S(2)}) %copy-start.1) | copy-done | bytes 6291480
  18.2 2.7 %copy-done.5 = bf16[192,128,128]{2,1,0:T(8,128)(2,1)} copy-done((bf16[192,128,128]{2,1,0:T(8,128)(2,1)}, bf16[192,128,128]{2,1,0:T(8,128)(2,1)S(1)}, u32[]{:S(2)}) %copy-start.5) | copy-done | bytes 6291480
  21.1 6.8 %load_matrix.2 = (bf16[192,128,128]{2,1,0:T(8,128)(2,1)S(1)}, bf16[192,128,128]{2,1,0:T(8,128)(2,1)S(1)}, s32[192]{0:T(256)S(1)}, s32[192]{0:T(256)S(1)}, f32[192]{0:T(256)S(1)}) custom-call(s32[2]{0:T(128)S(1)} %pad_add_fusion.me, s32[16,1,24]{2,1,0:T(1,128)} %cols.3, s32[16,1,24]{2,1,0:T(1,128)} %exps.3, s32[16,1]{1,0:T(8,128)} %copy.15.live, ...), custom_call_target="tpu_custom_call" | custom-call | bytes 25165824 | tf_op jit(solution)/shard_map/load_matrix/pallas_call | solution.py:67
  27.9 2.6 %copy-done.3 = bf16[192,128,128]{2,1,0:T(8,128)(2,1)} copy-done((bf16[192,128,128]{2,1,0:T(8,128)(2,1)}, bf16[192,128,128]{2,1,0:T(8,128)(2,1)S(1)}, u32[]{:S(2)}) %copy-start.3) | copy-done | bytes 6291480
  30.4 2.7 %copy-done.7 = bf16[192,128,128]{2,1,0:T(8,128)(2,1)} copy-done((bf16[192,128,128]{2,1,0:T(8,128)(2,1)}, bf16[192,128,128]{2,1,0:T(8,128)(2,1)S(1)}, u32[]{:S(2)}) %copy-start.7) | copy-done | bytes 6291480
  33.2 2.8 %copy-done.6 = bf16[192,128,128]{2,1,0:T(8,128)(2,1)S(1)} copy-done((bf16[192,128,128]{2,1,0:T(8,128)(2,1)S(1)}, bf16[192,128,128]{2,1,0:T(8,128)(2,1)}, u32[]{:S(2)}) %copy-start.6) | copy-done | bytes 6291480
  43.7 1.9 %collective-permute-done.7 = f32[9,16,128]{2,1,0:T(8,128)S(1)} collective-permute-done((f32[9,16,128]{2,1,0:T(8,128)S(1)}, f32[9,16,128]{2,1,0:T(8,128)S(1)}, u32[]{:S(2)}, u32[]{:S(2)}) %collective-permute-start.7) | collective-permute-done | bytes 73760 | tf_op jit(solution)/shard_map/ppermute | solution.py:264
  45.9 2.8 %copy-done.2 = bf16[192,128,128]{2,1,0:T(8,128)(2,1)S(1)} copy-done((bf16[192,128,128]{2,1,0:T(8,128)(2,1)S(1)}, bf16[192,128,128]{2,1,0:T(8,128)(2,1)}, u32[]{:S(2)}) %copy-start.2) | copy-done | bytes 6291480
  55.5 2.4 %collective-permute-start.11 = (f32[8,16,128]{2,1,0:T(8,128)S(1)}, f32[8,16,128]{2,1,0:T(8,128)S(1)}, u32[]{:S(2)}, u32[]{:S(2)}) collective-permute-start(f32[8,16,128]{2,1,0:T(8,128)S(1)} %get-tuple-element.82), channel_id=1, source_target_pairs={{0,12},{4,8},{8,4},{12,0},{1,13},{5,9},{9,5},{13,1},{2,14},{6,10},... | collective-permute-start | bytes 196616 | tf_op jit(solution)/shard_map/ppermute | solution.py:215
  58.4 3.5 %collective-permute-done.11 = f32[8,16,128]{2,1,0:T(8,128)S(1)} collective-permute-done((f32[8,16,128]{2,1,0:T(8,128)S(1)}, f32[8,16,128]{2,1,0:T(8,128)S(1)}, u32[]{:S(2)}, u32[]{:S(2)}) %collective-permute-start.11) | collective-permute-done | bytes 65568 | tf_op jit(solution)/shard_map/ppermute | solution.py:215
  62.0 2.8 %collective-permute-done.10 = f32[8,16,128]{2,1,0:T(8,128)S(1)} collective-permute-done((f32[8,16,128]{2,1,0:T(8,128)S(1)}, f32[8,16,128]{2,1,0:T(8,128)S(1)}, u32[]{:S(2)}, u32[]{:S(2)}) %collective-permute-start.10) | collective-permute-done | bytes 65568 | tf_op jit(solution)/shard_map/ppermute | solution.py:215
  64.8 2.7 %collective-permute-start.14 = (bf16[8,16,128]{2,1,0:T(8,128)(2,1)S(1)}, bf16[8,16,128]{2,1,0:T(8,128)(2,1)S(1)}, u32[]{:S(2)}, u32[]{:S(2)}) collective-permute-start(bf16[8,16,128]{2,1,0:T(8,128)(2,1)S(1)} %get-tuple-element.66), channel_id=1, source_target_pairs={{0,12},{4,8},{8,4},{12,0},{1,13},{5,9},{9,5},{13,1},{2,14},{6,10},... | collective-permute-start | bytes 98312 | tf_op jit(solution)/shard_map/ppermute | solution.py:215
  67.5 1.8 %collective-permute-start.12 = (bf16[8,16,128]{2,1,0:T(8,128)(2,1)S(1)}, bf16[8,16,128]{2,1,0:T(8,128)(2,1)S(1)}, u32[]{:S(2)}, u32[]{:S(2)}) collective-permute-start(bf16[8,16,128]{2,1,0:T(8,128)(2,1)S(1)} %get-tuple-element.66), channel_id=1, source_target_pairs={{0,4},{4,0},{8,12},{12,8},{1,5},{5,1},{9,13},{13,9},{2,6},{6,2},{1... | collective-permute-start | bytes 98312 | tf_op jit(solution)/shard_map/ppermute | solution.py:215
  77.9 1.9 %collective-permute-start.19 = (f32[8,16,128]{2,1,0:T(8,128)S(1)}, f32[8,16,128]{2,1,0:T(8,128)S(1)}, u32[]{:S(2)}, u32[]{:S(2)}) collective-permute-start(f32[8,16,128]{2,1,0:T(8,128)S(1)} %add.98.own), channel_id=1, source_target_pairs={{0,2},{2,0},{1,3},{3,1},{4,6},{6,4},{5,7},{7,5},{8,10},{10,8},{9,1... | collective-permute-start | bytes 196616 | tf_op jit(solution)/shard_map/ppermute | solution.py:264
  88.6 2.6 %collective-permute-start.23 = (f32[8,16,128]{2,1,0:T(8,128)S(1)}, f32[8,16,128]{2,1,0:T(8,128)S(1)}, u32[]{:S(2)}, u32[]{:S(2)}) collective-permute-start(f32[8,16,128]{2,1,0:T(8,128)S(1)} %get-tuple-element.79), channel_id=1, source_target_pairs={{0,12},{4,8},{8,4},{12,0},{1,13},{5,9},{9,5},{13,1},{2,14},{6,10},... | collective-permute-start | bytes 196616 | tf_op jit(solution)/shard_map/ppermute | solution.py:215
  91.9 3.5 %collective-permute-done.23 = f32[8,16,128]{2,1,0:T(8,128)S(1)} collective-permute-done((f32[8,16,128]{2,1,0:T(8,128)S(1)}, f32[8,16,128]{2,1,0:T(8,128)S(1)}, u32[]{:S(2)}, u32[]{:S(2)}) %collective-permute-start.23) | collective-permute-done | bytes 65568 | tf_op jit(solution)/shard_map/ppermute | solution.py:215
  95.5 2.1 %collective-permute-done.22 = f32[8,16,128]{2,1,0:T(8,128)S(1)} collective-permute-done((f32[8,16,128]{2,1,0:T(8,128)S(1)}, f32[8,16,128]{2,1,0:T(8,128)S(1)}, u32[]{:S(2)}, u32[]{:S(2)}) %collective-permute-start.22) | collective-permute-done | bytes 65568 | tf_op jit(solution)/shard_map/ppermute | solution.py:215
  97.7 2.1 %collective-permute-start.26 = (bf16[8,16,128]{2,1,0:T(8,128)(2,1)S(1)}, bf16[8,16,128]{2,1,0:T(8,128)(2,1)S(1)}, u32[]{:S(2)}, u32[]{:S(2)}) collective-permute-start(bf16[8,16,128]{2,1,0:T(8,128)(2,1)S(1)} %get-tuple-element.64), channel_id=1, source_target_pairs={{0,12},{4,8},{8,4},{12,0},{1,13},{5,9},{9,5},{13,1},{2,14},{6,10},... | collective-permute-start | bytes 98312 | tf_op jit(solution)/shard_map/ppermute | solution.py:215
  99.7 2.4 %collective-permute-start.24 = (bf16[8,16,128]{2,1,0:T(8,128)(2,1)S(1)}, bf16[8,16,128]{2,1,0:T(8,128)(2,1)S(1)}, u32[]{:S(2)}, u32[]{:S(2)}) collective-permute-start(bf16[8,16,128]{2,1,0:T(8,128)(2,1)S(1)} %get-tuple-element.64), channel_id=1, source_target_pairs={{0,4},{4,0},{8,12},{12,8},{1,5},{5,1},{9,13},{13,9},{2,6},{6,2},{1... | collective-permute-start | bytes 98312 | tf_op jit(solution)/shard_map/ppermute | solution.py:215
  107.9 1.9 %forward.12 = f32[8,16,128]{2,1,0:T(8,128)S(1)} custom-call(s32[192]{0:T(256)S(1)} %get-tuple-element.29.index, bf16[32,16,128]{2,1,0:T(8,128)(2,1)S(1)} %pad_maximum_fusion.1.refs_0_, bf16[32,16,128]{2,1,0:T(8,128)(2,1)S(1)} %collective-permute-done.27.refs_1_, bf16[192,128,128]{2,1,0:T(8,128)(2,1)S(1)} %copy-done.8), custom_call_target="tpu_custom_call" | custom-call | flops 100663296 | bytes 6291456 | tf_op jit(solution)/shard_map/forward/pallas_call | solution.py:112
  110.3 2.2 %collective-permute-start.31 = (f32[8,16,128]{2,1,0:T(8,128)S(1)}, f32[8,16,128]{2,1,0:T(8,128)S(1)}, u32[]{:S(2)}, u32[]{:S(2)}) collective-permute-start(f32[8,16,128]{2,1,0:T(8,128)S(1)} %add.104.own), channel_id=1, source_target_pairs={{0,2},{2,0},{1,3},{3,1},{4,6},{6,4},{5,7},{7,5},{8,10},{10,8},{9,1... | collective-permute-start | bytes 196616 | tf_op jit(solution)/shard_map/ppermute | solution.py:264
  121.8 2.0 %collective-permute-start.35 = (f32[8,16,128]{2,1,0:T(8,128)S(1)}, f32[8,16,128]{2,1,0:T(8,128)S(1)}, u32[]{:S(2)}, u32[]{:S(2)}) collective-permute-start(f32[8,16,128]{2,1,0:T(8,128)S(1)} %get-tuple-element.76), channel_id=1, source_target_pairs={{0,12},{4,8},{8,4},{12,0},{1,13},{5,9},{9,5},{13,1},{2,14},{6,10},... | collective-permute-start | bytes 196616 | tf_op jit(solution)/shard_map/ppermute | solution.py:215
  124.6 3.7 %collective-permute-done.35 = f32[8,16,128]{2,1,0:T(8,128)S(1)} collective-permute-done((f32[8,16,128]{2,1,0:T(8,128)S(1)}, f32[8,16,128]{2,1,0:T(8,128)S(1)}, u32[]{:S(2)}, u32[]{:S(2)}) %collective-permute-start.35) | collective-permute-done | bytes 65568 | tf_op jit(solution)/shard_map/ppermute | solution.py:215
  128.3 2.0 %collective-permute-done.34 = f32[8,16,128]{2,1,0:T(8,128)S(1)} collective-permute-done((f32[8,16,128]{2,1,0:T(8,128)S(1)}, f32[8,16,128]{2,1,0:T(8,128)S(1)}, u32[]{:S(2)}, u32[]{:S(2)}) %collective-permute-start.34) | collective-permute-done | bytes 65568 | tf_op jit(solution)/shard_map/ppermute | solution.py:215
  130.3 2.1 %collective-permute-start.38 = (bf16[8,16,128]{2,1,0:T(8,128)(2,1)S(1)}, bf16[8,16,128]{2,1,0:T(8,128)(2,1)S(1)}, u32[]{:S(2)}, u32[]{:S(2)}) collective-permute-start(bf16[8,16,128]{2,1,0:T(8,128)(2,1)S(1)} %get-tuple-element.62), channel_id=1, source_target_pairs={{0,12},{4,8},{8,4},{12,0},{1,13},{5,9},{9,5},{13,1},{2,14},{6,10},... | collective-permute-start | bytes 98312 | tf_op jit(solution)/shard_map/ppermute | solution.py:215
  132.4 2.4 %collective-permute-start.36 = (bf16[8,16,128]{2,1,0:T(8,128)(2,1)S(1)}, bf16[8,16,128]{2,1,0:T(8,128)(2,1)S(1)}, u32[]{:S(2)}, u32[]{:S(2)}) collective-permute-start(bf16[8,16,128]{2,1,0:T(8,128)(2,1)S(1)} %get-tuple-element.62), channel_id=1, source_target_pairs={{0,4},{4,0},{8,12},{12,8},{1,5},{5,1},{9,13},{13,9},{2,6},{6,2},{1... | collective-permute-start | bytes 98312 | tf_op jit(solution)/shard_map/ppermute | solution.py:215
  142.8 2.2 %collective-permute-start.43 = (f32[8,16,128]{2,1,0:T(8,128)S(1)}, f32[8,16,128]{2,1,0:T(8,128)S(1)}, u32[]{:S(2)}, u32[]{:S(2)}) collective-permute-start(f32[8,16,128]{2,1,0:T(8,128)S(1)} %add.110.own), channel_id=1, source_target_pairs={{0,2},{2,0},{1,3},{3,1},{4,6},{6,4},{5,7},{7,5},{8,10},{10,8},{9,1... | collective-permute-start | bytes 196616 | tf_op jit(solution)/shard_map/ppermute | solution.py:264
  154.3 2.0 %collective-permute-start.47 = (f32[8,16,128]{2,1,0:T(8,128)S(1)}, f32[8,16,128]{2,1,0:T(8,128)S(1)}, u32[]{:S(2)}, u32[]{:S(2)}) collective-permute-start(f32[8,16,128]{2,1,0:T(8,128)S(1)} %get-tuple-element.73), channel_id=1, source_target_pairs={{0,12},{4,8},{8,4},{12,0},{1,13},{5,9},{9,5},{13,1},{2,14},{6,10},... | collective-permute-start | bytes 196616 | tf_op jit(solution)/shard_map/ppermute | solution.py:215
  157.0 3.7 %collective-permute-done.47 = f32[8,16,128]{2,1,0:T(8,128)S(1)} collective-permute-done((f32[8,16,128]{2,1,0:T(8,128)S(1)}, f32[8,16,128]{2,1,0:T(8,128)S(1)}, u32[]{:S(2)}, u32[]{:S(2)}) %collective-permute-start.47) | collective-permute-done | bytes 65568 | tf_op jit(solution)/shard_map/ppermute | solution.py:215
  160.7 2.0 %collective-permute-done.46 = f32[8,16,128]{2,1,0:T(8,128)S(1)} collective-permute-done((f32[8,16,128]{2,1,0:T(8,128)S(1)}, f32[8,16,128]{2,1,0:T(8,128)S(1)}, u32[]{:S(2)}, u32[]{:S(2)}) %collective-permute-start.46) | collective-permute-done | bytes 65568 | tf_op jit(solution)/shard_map/ppermute | solution.py:215
  (173 shorter events, 73.7 us)
Async XLA Ops:
  1.6 19.4 %collective-permute-start.2 = (bf16[8,16,128]{2,1,0:T(8,128)(2,1)S(1)}, bf16[8,16,128]{2,1,0:T(8,128)(2,1)S(1)}, u32[]{:S(2)}, u32[]{:S(2)}) collective-permute-start(bf16[8,16,128]{2,1,0:T(8,128)(2,1)S(1)} %bitcast.54), channel_id=1, source_target_pairs={{0,12},{4,8},{8,4},{12,0},{1,13},{5,9},{9,5},{13,1},{2,14},{6,10},... | collective-permute-start | bytes 98312 | tf_op jit(solution)/shard_map/ppermute | solution.py:215
  6.7 14.2 %collective-permute-start.1 = (bf16[8,16,128]{2,1,0:T(8,128)(2,1)S(1)}, bf16[8,16,128]{2,1,0:T(8,128)(2,1)S(1)}, u32[]{:S(2)}, u32[]{:S(2)}) collective-permute-start(bf16[8,16,128]{2,1,0:T(8,128)(2,1)S(1)} %bitcast.55), channel_id=1, source_target_pairs={{0,8},{4,12},{8,0},{12,4},{1,9},{5,13},{9,1},{13,5},{2,10},{6,14},... | collective-permute-start | bytes 98312 | tf_op jit(solution)/shard_map/ppermute | solution.py:215
  6.7 14.2 %collective-permute-start = (bf16[8,16,128]{2,1,0:T(8,128)(2,1)S(1)}, bf16[8,16,128]{2,1,0:T(8,128)(2,1)S(1)}, u32[]{:S(2)}, u32[]{:S(2)}) collective-permute-start(bf16[8,16,128]{2,1,0:T(8,128)(2,1)S(1)} %bitcast.56), channel_id=1, source_target_pairs={{0,4},{4,0},{8,12},{12,8},{1,5},{5,1},{9,13},{13,9},{2,6},{6,2},{1... | collective-permute-start | bytes 98312 | tf_op jit(solution)/shard_map/ppermute | solution.py:215
  21.0 12.2 %collective-permute-start.3 = (bf16[32,16,128]{2,1,0:T(8,128)(2,1)S(1)}, bf16[32,16,128]{2,1,0:T(8,128)(2,1)S(1)}, u32[]{:S(2)}, u32[]{:S(2)}) collective-permute-start(bf16[32,16,128]{2,1,0:T(8,128)(2,1)S(1)} %constant_dynamic-update-slice_fusion.refs_0_), channel_id=1, source_target_pairs={{0,1},{1,0},{2,3},{3,2},{4,5},{5,4},{6,7},{7,6},{8,9},{9,8},{10,11... | collective-permute-start | bytes 393224 | tf_op jit(solution)/shard_map/ppermute | solution.py:220
  41.1 4.4 %collective-permute-start.7 = (f32[9,16,128]{2,1,0:T(8,128)S(1)}, f32[9,16,128]{2,1,0:T(8,128)S(1)}, u32[]{:S(2)}, u32[]{:S(2)}) collective-permute-start(f32[9,16,128]{2,1,0:T(8,128)S(1)} %pad_maximum_fusion.5), channel_id=1, source_target_pairs={{0,2},{2,0},{1,3},{3,1},{4,6},{6,4},{5,7},{7,5},{8,10},{10,8},{9,1... | collective-permute-start | bytes 221192 | tf_op jit(solution)/shard_map/ppermute | solution.py:264
  43.1 7.3 %collective-permute-start.5 = (f32[8,16,128]{2,1,0:T(8,128)S(1)}, f32[8,16,128]{2,1,0:T(8,128)S(1)}, u32[]{:S(2)}, u32[]{:S(2)}) collective-permute-start(f32[8,16,128]{2,1,0:T(8,128)S(1)} %add.89.own), channel_id=1, source_target_pairs={{0,2},{2,0},{1,3},{3,1},{4,6},{6,4},{5,7},{7,5},{8,10},{10,8},{9,1... | collective-permute-start | bytes 196616 | tf_op jit(solution)/shard_map/ppermute | solution.py:264
  53.9 4.6 %collective-permute-start.9 = (f32[8,16,128]{2,1,0:T(8,128)S(1)}, f32[8,16,128]{2,1,0:T(8,128)S(1)}, u32[]{:S(2)}, u32[]{:S(2)}) collective-permute-start(f32[8,16,128]{2,1,0:T(8,128)S(1)} %get-tuple-element.81), channel_id=1, source_target_pairs={{0,4},{4,0},{8,12},{12,8},{1,5},{5,1},{9,13},{13,9},{2,6},{6,2},{1... | collective-permute-start | bytes 196616 | tf_op jit(solution)/shard_map/ppermute | solution.py:215
  55.5 6.5 %collective-permute-start.11 = (f32[8,16,128]{2,1,0:T(8,128)S(1)}, f32[8,16,128]{2,1,0:T(8,128)S(1)}, u32[]{:S(2)}, u32[]{:S(2)}) collective-permute-start(f32[8,16,128]{2,1,0:T(8,128)S(1)} %get-tuple-element.82), channel_id=1, source_target_pairs={{0,12},{4,8},{8,4},{12,0},{1,13},{5,9},{9,5},{13,1},{2,14},{6,10},... | collective-permute-start | bytes 196616 | tf_op jit(solution)/shard_map/ppermute | solution.py:215
  57.9 6.8 %collective-permute-start.10 = (f32[8,16,128]{2,1,0:T(8,128)S(1)}, f32[8,16,128]{2,1,0:T(8,128)S(1)}, u32[]{:S(2)}, u32[]{:S(2)}) collective-permute-start(f32[8,16,128]{2,1,0:T(8,128)S(1)} %get-tuple-element.83), channel_id=1, source_target_pairs={{0,8},{4,12},{8,0},{12,4},{1,9},{5,13},{9,1},{13,5},{2,10},{6,14},... | collective-permute-start | bytes 196616 | tf_op jit(solution)/shard_map/ppermute | solution.py:215
  64.8 5.8 %collective-permute-start.14 = (bf16[8,16,128]{2,1,0:T(8,128)(2,1)S(1)}, bf16[8,16,128]{2,1,0:T(8,128)(2,1)S(1)}, u32[]{:S(2)}, u32[]{:S(2)}) collective-permute-start(bf16[8,16,128]{2,1,0:T(8,128)(2,1)S(1)} %get-tuple-element.66), channel_id=1, source_target_pairs={{0,12},{4,8},{8,4},{12,0},{1,13},{5,9},{9,5},{13,1},{2,14},{6,10},... | collective-permute-start | bytes 98312 | tf_op jit(solution)/shard_map/ppermute | solution.py:215
  67.5 4.8 %collective-permute-start.13 = (bf16[8,16,128]{2,1,0:T(8,128)(2,1)S(1)}, bf16[8,16,128]{2,1,0:T(8,128)(2,1)S(1)}, u32[]{:S(2)}, u32[]{:S(2)}) collective-permute-start(bf16[8,16,128]{2,1,0:T(8,128)(2,1)S(1)} %get-tuple-element.66), channel_id=1, source_target_pairs={{0,8},{4,12},{8,0},{12,4},{1,9},{5,13},{9,1},{13,5},{2,10},{6,14},... | collective-permute-start | bytes 98312 | tf_op jit(solution)/shard_map/ppermute | solution.py:215
  67.5 4.8 %collective-permute-start.12 = (bf16[8,16,128]{2,1,0:T(8,128)(2,1)S(1)}, bf16[8,16,128]{2,1,0:T(8,128)(2,1)S(1)}, u32[]{:S(2)}, u32[]{:S(2)}) collective-permute-start(bf16[8,16,128]{2,1,0:T(8,128)(2,1)S(1)} %get-tuple-element.66), channel_id=1, source_target_pairs={{0,4},{4,0},{8,12},{12,8},{1,5},{5,1},{9,13},{13,9},{2,6},{6,2},{1... | collective-permute-start | bytes 98312 | tf_op jit(solution)/shard_map/ppermute | solution.py:215
  77.9 4.4 %collective-permute-start.19 = (f32[8,16,128]{2,1,0:T(8,128)S(1)}, f32[8,16,128]{2,1,0:T(8,128)S(1)}, u32[]{:S(2)}, u32[]{:S(2)}) collective-permute-start(f32[8,16,128]{2,1,0:T(8,128)S(1)} %add.98.own), channel_id=1, source_target_pairs={{0,2},{2,0},{1,3},{3,1},{4,6},{6,4},{5,7},{7,5},{8,10},{10,8},{9,1... | collective-permute-start | bytes 196616 | tf_op jit(solution)/shard_map/ppermute | solution.py:264
  79.9 4.3 %collective-permute-start.17 = (f32[8,16,128]{2,1,0:T(8,128)S(1)}, f32[8,16,128]{2,1,0:T(8,128)S(1)}, u32[]{:S(2)}, u32[]{:S(2)}) collective-permute-start(f32[8,16,128]{2,1,0:T(8,128)S(1)} %add.97.own), channel_id=1, source_target_pairs={{0,2},{2,0},{1,3},{3,1},{4,6},{6,4},{5,7},{7,5},{8,10},{10,8},{9,1... | collective-permute-start | bytes 196616 | tf_op jit(solution)/shard_map/ppermute | solution.py:264
  87.6 4.3 %collective-permute-start.21 = (f32[8,16,128]{2,1,0:T(8,128)S(1)}, f32[8,16,128]{2,1,0:T(8,128)S(1)}, u32[]{:S(2)}, u32[]{:S(2)}) collective-permute-start(f32[8,16,128]{2,1,0:T(8,128)S(1)} %get-tuple-element.78), channel_id=1, source_target_pairs={{0,4},{4,0},{8,12},{12,8},{1,5},{5,1},{9,13},{13,9},{2,6},{6,2},{1... | collective-permute-start | bytes 196616 | tf_op jit(solution)/shard_map/ppermute | solution.py:215
  88.6 6.9 %collective-permute-start.23 = (f32[8,16,128]{2,1,0:T(8,128)S(1)}, f32[8,16,128]{2,1,0:T(8,128)S(1)}, u32[]{:S(2)}, u32[]{:S(2)}) collective-permute-start(f32[8,16,128]{2,1,0:T(8,128)S(1)} %get-tuple-element.79), channel_id=1, source_target_pairs={{0,12},{4,8},{8,4},{12,0},{1,13},{5,9},{9,5},{13,1},{2,14},{6,10},... | collective-permute-start | bytes 196616 | tf_op jit(solution)/shard_map/ppermute | solution.py:215
  91.2 6.5 %collective-permute-start.22 = (f32[8,16,128]{2,1,0:T(8,128)S(1)}, f32[8,16,128]{2,1,0:T(8,128)S(1)}, u32[]{:S(2)}, u32[]{:S(2)}) collective-permute-start(f32[8,16,128]{2,1,0:T(8,128)S(1)} %get-tuple-element.80), channel_id=1, source_target_pairs={{0,8},{4,12},{8,0},{12,4},{1,9},{5,13},{9,1},{13,5},{2,10},{6,14},... | collective-permute-start | bytes 196616 | tf_op jit(solution)/shard_map/ppermute | solution.py:215
  97.7 5.9 %collective-permute-start.26 = (bf16[8,16,128]{2,1,0:T(8,128)(2,1)S(1)}, bf16[8,16,128]{2,1,0:T(8,128)(2,1)S(1)}, u32[]{:S(2)}, u32[]{:S(2)}) collective-permute-start(bf16[8,16,128]{2,1,0:T(8,128)(2,1)S(1)} %get-tuple-element.64), channel_id=1, source_target_pairs={{0,12},{4,8},{8,4},{12,0},{1,13},{5,9},{9,5},{13,1},{2,14},{6,10},... | collective-permute-start | bytes 98312 | tf_op jit(solution)/shard_map/ppermute | solution.py:215
  99.7 4.8 %collective-permute-start.25 = (bf16[8,16,128]{2,1,0:T(8,128)(2,1)S(1)}, bf16[8,16,128]{2,1,0:T(8,128)(2,1)S(1)}, u32[]{:S(2)}, u32[]{:S(2)}) collective-permute-start(bf16[8,16,128]{2,1,0:T(8,128)(2,1)S(1)} %get-tuple-element.64), channel_id=1, source_target_pairs={{0,8},{4,12},{8,0},{12,4},{1,9},{5,13},{9,1},{13,5},{2,10},{6,14},... | collective-permute-start | bytes 98312 | tf_op jit(solution)/shard_map/ppermute | solution.py:215
  99.7 4.8 %collective-permute-start.24 = (bf16[8,16,128]{2,1,0:T(8,128)(2,1)S(1)}, bf16[8,16,128]{2,1,0:T(8,128)(2,1)S(1)}, u32[]{:S(2)}, u32[]{:S(2)}) collective-permute-start(bf16[8,16,128]{2,1,0:T(8,128)(2,1)S(1)} %get-tuple-element.64), channel_id=1, source_target_pairs={{0,4},{4,0},{8,12},{12,8},{1,5},{5,1},{9,13},{13,9},{2,6},{6,2},{1... | collective-permute-start | bytes 98312 | tf_op jit(solution)/shard_map/ppermute | solution.py:215
  110.3 4.6 %collective-permute-start.31 = (f32[8,16,128]{2,1,0:T(8,128)S(1)}, f32[8,16,128]{2,1,0:T(8,128)S(1)}, u32[]{:S(2)}, u32[]{:S(2)}) collective-permute-start(f32[8,16,128]{2,1,0:T(8,128)S(1)} %add.104.own), channel_id=1, source_target_pairs={{0,2},{2,0},{1,3},{3,1},{4,6},{6,4},{5,7},{7,5},{8,10},{10,8},{9,1... | collective-permute-start | bytes 196616 | tf_op jit(solution)/shard_map/ppermute | solution.py:264
  112.5 4.3 %collective-permute-start.29 = (f32[8,16,128]{2,1,0:T(8,128)S(1)}, f32[8,16,128]{2,1,0:T(8,128)S(1)}, u32[]{:S(2)}, u32[]{:S(2)}) collective-permute-start(f32[8,16,128]{2,1,0:T(8,128)S(1)} %add.103.own), channel_id=1, source_target_pairs={{0,2},{2,0},{1,3},{3,1},{4,6},{6,4},{5,7},{7,5},{8,10},{10,8},{9,1... | collective-permute-start | bytes 196616 | tf_op jit(solution)/shard_map/ppermute | solution.py:264
  121.8 6.5 %collective-permute-start.35 = (f32[8,16,128]{2,1,0:T(8,128)S(1)}, f32[8,16,128]{2,1,0:T(8,128)S(1)}, u32[]{:S(2)}, u32[]{:S(2)}) collective-permute-start(f32[8,16,128]{2,1,0:T(8,128)S(1)} %get-tuple-element.76), channel_id=1, source_target_pairs={{0,12},{4,8},{8,4},{12,0},{1,13},{5,9},{9,5},{13,1},{2,14},{6,10},... | collective-permute-start | bytes 196616 | tf_op jit(solution)/shard_map/ppermute | solution.py:215
  123.8 6.5 %collective-permute-start.34 = (f32[8,16,128]{2,1,0:T(8,128)S(1)}, f32[8,16,128]{2,1,0:T(8,128)S(1)}, u32[]{:S(2)}, u32[]{:S(2)}) collective-permute-start(f32[8,16,128]{2,1,0:T(8,128)S(1)} %get-tuple-element.77), channel_id=1, source_target_pairs={{0,8},{4,12},{8,0},{12,4},{1,9},{5,13},{9,1},{13,5},{2,10},{6,14},... | collective-permute-start | bytes 196616 | tf_op jit(solution)/shard_map/ppermute | solution.py:215
  130.3 5.9 %collective-permute-start.38 = (bf16[8,16,128]{2,1,0:T(8,128)(2,1)S(1)}, bf16[8,16,128]{2,1,0:T(8,128)(2,1)S(1)}, u32[]{:S(2)}, u32[]{:S(2)}) collective-permute-start(bf16[8,16,128]{2,1,0:T(8,128)(2,1)S(1)} %get-tuple-element.62), channel_id=1, source_target_pairs={{0,12},{4,8},{8,4},{12,0},{1,13},{5,9},{9,5},{13,1},{2,14},{6,10},... | collective-permute-start | bytes 98312 | tf_op jit(solution)/shard_map/ppermute | solution.py:215
  132.4 4.8 %collective-permute-start.37 = (bf16[8,16,128]{2,1,0:T(8,128)(2,1)S(1)}, bf16[8,16,128]{2,1,0:T(8,128)(2,1)S(1)}, u32[]{:S(2)}, u32[]{:S(2)}) collective-permute-start(bf16[8,16,128]{2,1,0:T(8,128)(2,1)S(1)} %get-tuple-element.62), channel_id=1, source_target_pairs={{0,8},{4,12},{8,0},{12,4},{1,9},{5,13},{9,1},{13,5},{2,10},{6,14},... | collective-permute-start | bytes 98312 | tf_op jit(solution)/shard_map/ppermute | solution.py:215
  132.4 4.8 %collective-permute-start.36 = (bf16[8,16,128]{2,1,0:T(8,128)(2,1)S(1)}, bf16[8,16,128]{2,1,0:T(8,128)(2,1)S(1)}, u32[]{:S(2)}, u32[]{:S(2)}) collective-permute-start(bf16[8,16,128]{2,1,0:T(8,128)(2,1)S(1)} %get-tuple-element.62), channel_id=1, source_target_pairs={{0,4},{4,0},{8,12},{12,8},{1,5},{5,1},{9,13},{13,9},{2,6},{6,2},{1... | collective-permute-start | bytes 98312 | tf_op jit(solution)/shard_map/ppermute | solution.py:215
  142.8 4.6 %collective-permute-start.43 = (f32[8,16,128]{2,1,0:T(8,128)S(1)}, f32[8,16,128]{2,1,0:T(8,128)S(1)}, u32[]{:S(2)}, u32[]{:S(2)}) collective-permute-start(f32[8,16,128]{2,1,0:T(8,128)S(1)} %add.110.own), channel_id=1, source_target_pairs={{0,2},{2,0},{1,3},{3,1},{4,6},{6,4},{5,7},{7,5},{8,10},{10,8},{9,1... | collective-permute-start | bytes 196616 | tf_op jit(solution)/shard_map/ppermute | solution.py:264
  145.0 4.3 %collective-permute-start.41 = (f32[8,16,128]{2,1,0:T(8,128)S(1)}, f32[8,16,128]{2,1,0:T(8,128)S(1)}, u32[]{:S(2)}, u32[]{:S(2)}) collective-permute-start(f32[8,16,128]{2,1,0:T(8,128)S(1)} %add.109.own), channel_id=1, source_target_pairs={{0,2},{2,0},{1,3},{3,1},{4,6},{6,4},{5,7},{7,5},{8,10},{10,8},{9,1... | collective-permute-start | bytes 196616 | tf_op jit(solution)/shard_map/ppermute | solution.py:264
  152.7 4.3 %collective-permute-start.45 = (f32[8,16,128]{2,1,0:T(8,128)S(1)}, f32[8,16,128]{2,1,0:T(8,128)S(1)}, u32[]{:S(2)}, u32[]{:S(2)}) collective-permute-start(f32[8,16,128]{2,1,0:T(8,128)S(1)} %get-tuple-element.72), channel_id=1, source_target_pairs={{0,4},{4,0},{8,12},{12,8},{1,5},{5,1},{9,13},{13,9},{2,6},{6,2},{1... | collective-permute-start | bytes 196616 | tf_op jit(solution)/shard_map/ppermute | solution.py:215
  154.3 6.5 %collective-permute-start.47 = (f32[8,16,128]{2,1,0:T(8,128)S(1)}, f32[8,16,128]{2,1,0:T(8,128)S(1)}, u32[]{:S(2)}, u32[]{:S(2)}) collective-permute-start(f32[8,16,128]{2,1,0:T(8,128)S(1)} %get-tuple-element.73), channel_id=1, source_target_pairs={{0,12},{4,8},{8,4},{12,0},{1,13},{5,9},{9,5},{13,1},{2,14},{6,10},... | collective-permute-start | bytes 196616 | tf_op jit(solution)/shard_map/ppermute | solution.py:215
  156.3 6.5 %collective-permute-start.46 = (f32[8,16,128]{2,1,0:T(8,128)S(1)}, f32[8,16,128]{2,1,0:T(8,128)S(1)}, u32[]{:S(2)}, u32[]{:S(2)}) collective-permute-start(f32[8,16,128]{2,1,0:T(8,128)S(1)} %get-tuple-element.74), channel_id=1, source_target_pairs={{0,8},{4,12},{8,0},{12,4},{1,9},{5,13},{9,1},{13,5},{2,10},{6,14},... | collective-permute-start | bytes 196616 | tf_op jit(solution)/shard_map/ppermute | solution.py:215
  (35 other events, 188.6 us)

commit v4 on v3

--- a/solution.py
+++ b/solution.py
@@ -10,7 +10,7 @@
 ITERS = 4
 F32 = jnp.float32
 BF16 = jnp.bfloat16
-PARAMS = pltpu.CompilerParams(vmem_limit_bytes=8 * 2**20)
+PARAMS = pltpu.CompilerParams(vmem_limit_bytes=16 * 2**20)
 
 
 def in_vmem():
@@ -25,58 +25,75 @@
     return pltpu.with_memory_space_constraint(array, pltpu.VMEM)
 
 
-def load_kernel(n_vox, columns, row0, me, cols, exps, live, stored, kept, turned, index, places, factor, sems):
+def index_kernel(n_vox, columns, steps, me, cols, exps, live, index, places, factor, sides):
     z, core = me[0], me[1]
     slots = cols.shape[2]
-    rows = kept.shape[0] // slots
     own = columns // (2 * n_vox)
+    column, exponent = cols[:, 0, :], exps[:, 0, :]
+    piece, within = lax.div(column, own), lax.rem(column, own)
+    place = ((lax.rem(piece, 2) ^ core) * n_vox + (lax.div(piece, 2) ^ z)) * own + within
+    position = core * slots + lax.broadcasted_iota(jnp.int32, column.shape, 1)
+    used = position < live[...]
+    scale = jnp.where(exponent < 0, 0.5, jnp.where(exponent > 0, 2.0, 1.0))
+    places[...] = place
+    index[...] = jnp.where(used, (exponent + 1) * columns + place, 3 * columns)
+    factor[...] = jnp.where(used, scale, 0.0).astype(F32)
+    for e, (at, bit) in enumerate(steps):
+        first = jnp.where((me[at] & bit) == 0, 1.0, 0.0).astype(F32)
+        sides[e] = jnp.full(sides.shape[1:], first)
+
+
+def indices(n_vox, columns, steps, me, cols, exps, live):
+    rows, _, slots = cols.shape
+    return pl.pallas_call(
+        functools.partial(index_kernel, n_vox, columns, steps),
+        in_specs=[in_smem()] + [in_vmem()] * 3,
+        out_specs=[in_vmem()] * 4,
+        out_shape=[jax.ShapeDtypeStruct((rows, slots), t) for t in (jnp.int32, jnp.int32, F32)]
+        + [jax.ShapeDtypeStruct((len(steps), 8, 128), F32)],
+        compiler_params=PARAMS,
+        name="indices",
+    )(me, cols, exps, live)
+
+
+def load_kernel(first, stored, after, kept, turned, sems):
+    pieces = sems.shape[0]
+    size = kept.shape[0] // pieces
     copies = [
         pltpu.make_async_copy(
-            stored.at[pl.ds((row0 + b) * slots, slots)], kept.at[pl.ds(b * slots, slots)], sems.at[b]
+            stored.at[pl.ds(first + i * size, size)], kept.at[pl.ds(i * size, size)], sems.at[i]
         )
-        for b in range(rows)
+        for i in range(pieces)
     ]
     for copy in copies:
         copy.start()
-    step = 8 if slots % 8 == 0 else 1
-    for b, copy in enumerate(copies):
+    step = 8 if size % 8 == 0 else 1
+    for i, copy in enumerate(copies):
         copy.wait()
-        used_slots = live[row0 + b, 0] - core * slots
-
-        def turn(t, carry, b=b, used_slots=used_slots):
+
+        def turn(t, carry, i=i):
             for u in range(step):
-                k = t * step + u
-                n = b * slots + k
+                n = i * size + t * step + u
                 turned[n] = kept[n].T
-                column, exponent = cols[row0 + b, 0, k], exps[row0 + b, 0, k]
-                piece, within = column // own, column % own
-                at = (((piece % 2) ^ core) * n_vox + ((piece // 2) ^ z)) * own + within
-                used = k < used_slots
-                scale = jnp.where(exponent < 0, 0.5, jnp.where(exponent > 0, 2.0, 1.0))
-                places[n] = at
-                index[n] = jnp.where(used, (exponent + 1) * columns + at, 3 * columns)
-                factor[n] = jnp.where(used, scale, 0.0).astype(F32)
             return carry
 
-        lax.fori_loop(0, slots // step, turn, 0)
-
-
-def load_matrix(n_vox, columns, row0, rows, me, cols, exps, live, tiles):
-    slots = cols.shape[2]
-    shape = (rows * slots,) + tiles.shape[1:]
+        lax.fori_loop(0, size // step, turn, 0)
+
+
+def load_matrix(first, count, pieces, tiles, after):
+    shape = (count,) + tiles.shape[1:]
     return pl.pallas_call(
-        functools.partial(load_kernel, n_vox, columns, row0),
-        in_specs=[in_smem()] * 4 + [pl.BlockSpec(memory_space=pltpu.HBM)],
-        out_specs=[in_vmem()] * 2 + [in_smem()] * 3,
-        out_shape=[pltpu.VMEM(shape, tiles.dtype)] * 2
-        + [jax.ShapeDtypeStruct(shape[:1], t) for t in (jnp.int32, jnp.int32, F32)],
-        scratch_shapes=[pltpu.SemaphoreType.DMA((rows,))],
+        functools.partial(load_kernel, first),
+        in_specs=[pl.BlockSpec(memory_space=pltpu.HBM), in_vmem()],
+        out_specs=[in_vmem()] * 2,
+        out_shape=[pltpu.VMEM(shape, tiles.dtype)] * 2,
+        scratch_shapes=[pltpu.SemaphoreType.DMA((pieces,))],
         compiler_params=PARAMS,
         cost_estimate=pl.CostEstimate(
-            flops=0, bytes_accessed=8 * rows * slots * tiles.shape[1] * tiles.shape[2], transcendentals=0
+            flops=0, bytes_accessed=8 * count * tiles.shape[1] * tiles.shape[2], transcendentals=0
         ),
         name="load_matrix",
-    )(me, *(pltpu.with_memory_space_constraint(a, pltpu.HBM) for a in (cols, exps, live, tiles)))
+    )(pltpu.with_memory_space_constraint(tiles, pltpu.HBM), after)
 
 
 def forward_kernel(slots, index, *refs):
@@ -97,7 +114,7 @@
     def some_rows(t, carry):
         for u in range(unroll):
             b = t * unroll + u
-            left = jnp.concatenate([scaled[index[b * slots + k]] for k in range(slots)], axis=1)
+            left = jnp.concatenate([scaled[index[b, k]] for k in range(slots)], axis=1)
             right = turned[pl.ds(b * slots, slots)]
             right = right.reshape(slots * right.shape[1], right.shape[2])
             dose[b] = jnp.dot(left, right, preferred_element_type=F32)
@@ -147,11 +164,11 @@
                 places = [b * slots + k0 + k for k in range(group)]
                 right = jnp.concatenate([kept[p] for p in places], axis=1)
                 product = jnp.dot(left, right, preferred_element_type=F32)
-                columns = [index[p] for p in places]
+                columns = [index[b, k0 + k] for k in range(group)]
                 old = [total[c] for c in columns]
-                for k, p in enumerate(places):
+                for k in range(group):
                     part = product[:, k * width : (k + 1) * width]
-                    total[columns[k]] = old[k] + part * factor[p]
+                    total[columns[k]] = old[k] + part * factor[b, k0 + k]
         return carry
 
     lax.fori_loop(0, rows // unroll, some_rows, 0)
@@ -219,33 +236,35 @@
     def over_rep(array):
         return lax.ppermute(array, "rep", [(0, 1), (1, 0)])
 
-    me = jnp.stack([z, core]).astype(jnp.int32)
+    me = jnp.stack([z, core, x]).astype(jnp.int32)
     level_table = jnp.stack([upper_dose, upper_weight, lower_dose, lower_weight])
     known = labels.astype(F32).reshape(-1, width)
     tiles = dose_blocks.reshape(rows * slots, width, width)
     halves = 2 if rows % 2 == 0 else 1
     some = rows // halves
 
-    def load(h):
-        return load_matrix(
-            n_vox, columns, h * some, some, me, block_cols, block_exps, live_counts, tiles
-        )
-
     def gather_weights(weights):
         piece = weights.astype(BF16)
         return [piece] + over_vox([piece] * (n_vox - 1))
 
-    exchanges = [("rep", 2, 1, core)]
+    exchanges = [("rep", 2, 1)]
     bit = 1
     while bit < n_spot:
-        exchanges.append(("spot", n_spot, bit, x))
+        exchanges.append(("spot", n_spot, bit))
         bit *= 2
 
     pieces = gather_weights(weights)
-    parts = [load(0)]
-    pieces, first_part = lax.optimization_barrier((pieces, parts[0][2:]))
-    parts[0] = [*parts[0][:2], *first_part]
-    parts += [load(h) for h in range(1, halves)]
+    steps = [(1 if axis == "rep" else 2, bit) for axis, _, bit in exchanges]
+    index, places, factor, sides = indices(
+        n_vox, columns, steps, me, block_cols, block_exps, live_counts
+    )
+    count = some * slots
+    loaded = [load_matrix(0, count, some, tiles, index)]
+    pieces, loaded[0] = lax.optimization_barrier((pieces, loaded[0]))
+    loaded += [load_matrix(h * count, count, some, tiles, index) for h in range(1, halves)]
+    parts = []
+    for h, (kept, turned) in enumerate(loaded):
+        parts.append((kept, turned, *(a[h * some : (h + 1) * some] for a in (index, places, factor))))
 
     for step in range(ITERS):
         near = jnp.concatenate(pieces, axis=0)
@@ -255,7 +274,7 @@
         own_doses, other_doses = [], []
         for h, dose in enumerate(doses):
             with_labels = step == 0 and h == 0
-            for axis, size, bit, at in exchanges:
+            for e, (axis, size, bit) in enumerate(exchanges):
                 sent = dose
                 if with_labels:
                     n = known.shape[0]
@@ -264,12 +283,12 @@
                 got = lax.ppermute(sent, axis, [(i, i ^ bit) for i in range(size)])
                 if with_labels:
                     theirs = got[some, :n]
-                    first = (at // bit) % 2 == 0
+                    first = sides[e, :1] > 0
                     known = jnp.concatenate(
                         [jnp.where(first, known, theirs), jnp.where(first, theirs, known)]
                     )
                     got = got[:some]
-                if (axis, bit) != (exchanges[-1][0], exchanges[-1][2]):
+                if e < len(exchanges) - 1:
                     dose = dose + got
             own_doses.append(dose)
             other_doses.append(got)
@@ -306,8 +325,9 @@
 
     mine = jnp.stack([weights, gradient])
     other = over_rep(mine)
+    first = sides[0, :1] > 0
     both = jnp.concatenate(
-        [jnp.where(core == 0, mine, other), jnp.where(core == 0, other, mine)], axis=1
+        [jnp.where(first, mine, other), jnp.where(first, other, mine)], axis=1
     )
     both = both.transpose(0, 2, 1, 3).reshape(2, weightings, 1, chunk_spots)
     return both[0], both[1]

time: 166 us -> 146 us (0.88)
  local copies, waits for them, and re-layouts: 20.7 us -> 4.9 us
  Pallas kernels: 41.7 us -> 38.2 us
    unnamed x41 -> x21, local copies, waits for them, and re-layouts: 18.9 us -> 3.1 us
    pallas_call x2 -> x3, Pallas kernels: 13.6 us -> 8.93 us  [the longest x2 8.3 us: load_matrix(): pl.pallas_call(functools.partial(load_kernel, first), in_specs=[pl.BlockS...]
  transfers between devices with their start and end apart: 49 -> 49, of which waited for: 32 -> 32; matrix products, arithmetic and copies ran while one was open for 1% -> 1% of each run, Pallas kernels for 17% -> 16%
where the time goes in v4:
time: 146 us
  waiting for transfers between devices  51.7 us (35%)
  starting transfers between devices  49.1 us (34%)
  Pallas kernels  38.2 us (26%)
  local copies, waits for them, and re-layouts  4.9 us (3%)
    ppermute x24, starting transfers between devices, over_vox(): lax.ppermute(a, 'vox', [(i, i ^ d) for i in range(n_vox)])  34.1 us
    ppermute x24, waiting for transfers between devices, over_vox(): lax.ppermute(a, 'vox', [(i, i ^ d) for i in range(n_vox)])  33.6 us
    pallas_call x8, Pallas kernels, backward(): pl.pallas_call(functools.partial(backward_kernel, slots, first, last), in...  14.9 us
    pallas_call x8, Pallas kernels, forward(): pl.pallas_call(functools.partial(forward_kernel, slots), in_specs=[in_sme...  14.4 us
    ppermute x16, starting transfers between devices, per_device(): got = lax.ppermute(sent, axis, [(i, i ^ bit) for i in range(size)])  14.3 us
    ppermute x9, waiting for transfers between devices, over_rep(): return lax.ppermute(array, 'rep', [(0, 1), (1, 0)])  11.4 us
    pallas_call x2, Pallas kernels, load_matrix(): pl.pallas_call(functools.partial(load_kernel, first), in_specs=[pl.BlockS...  8.3 us
    ppermute x16, waiting for transfers between devices, per_device(): got = lax.ppermute(sent, axis, [(i, i ^ bit) for i in range(size)])  6.65 us
  transfers between devices with their start and end apart: 49, of which 32 were waited for; matrix products, arithmetic and copies ran while one was open for 1% of the time, Pallas kernels for 16%

profile of v4, /device:TPU:0, one launch (start us, length us, event | category | flops | bytes accessed | tf_op | source)
XLA Modules:
  0.0 146.0 jit_solution(8773664078845148570)
XLA Ops:
  1.6 5.1 %collective-permute-start.2 = (bf16[8,16,128]{2,1,0:T(8,128)(2,1)S(1)}, bf16[8,16,128]{2,1,0:T(8,128)(2,1)S(1)}, u32[]{:S(2)}, u32[]{:S(2)}) collective-permute-start(bf16[8,16,128]{2,1,0:T(8,128)(2,1)S(1)} %bitcast.55), channel_id=1, source_target_pairs={{0,12},{4,8},{8,4},{12,0},{1,13},{5,9},{9,5},{13,1},{2,14},{6,10},... | collective-permute-start | bytes 98312 | tf_op jit(solution)/shard_map/ppermute | solution.py:232
  10.2 4.2 %load_matrix.2 = (bf16[192,128,128]{2,1,0:T(8,128)(2,1)S(1)}, bf16[192,128,128]{2,1,0:T(8,128)(2,1)S(1)}) custom-call(bf16[384,128,128]{2,1,0:T(8,128)(2,1)} %bitcast.51, s32[16,24]{1,0:T(8,128)S(1)} %get-tuple-element.27.after), custom_call_target="tpu_custom_call" | custom-call | bytes 25165824 | tf_op jit(solution)/shard_map/load_matrix/pallas_call | solution.py:85
  14.6 4.2 %load_matrix.3 = (bf16[192,128,128]{2,1,0:T(8,128)(2,1)S(1)}, bf16[192,128,128]{2,1,0:T(8,128)(2,1)S(1)}) custom-call(bf16[384,128,128]{2,1,0:T(8,128)(2,1)} %bitcast.52, s32[16,24]{1,0:T(8,128)S(1)} %get-tuple-element.27.after), custom_call_target="tpu_custom_call" | custom-call | bytes 25165824 | tf_op jit(solution)/shard_map/load_matrix/pallas_call | solution.py:85
  26.0 1.9 %collective-permute-done.7 = f32[9,16,128]{2,1,0:T(8,128)S(1)} collective-permute-done((f32[9,16,128]{2,1,0:T(8,128)S(1)}, f32[9,16,128]{2,1,0:T(8,128)S(1)}, u32[]{:S(2)}, u32[]{:S(2)}) %collective-permute-start.7) | collective-permute-done | bytes 73760 | tf_op jit(solution)/shard_map/ppermute | solution.py:283
  28.2 1.9 %slope_backward.8.refs_0_ = f32[64,16,128]{2,1,0:T(8,128)S(1)} custom-call(s32[8,24]{1,0:T(8,128)S(1)} %get-tuple-element.86.index, f32[8,24]{1,0:T(8,128)S(1)} %get-tuple-element.84.factor, f32[8,16,128]{2,1,0:T(8,128)S(1)} %slice_add_fusion.4.own, f32[8,16,128]{2,1,0:T(8,128)S(1)} %slice.173.other, f32[4,8,1,128]{3,2,1,0:T(1,128)S(1)} %get-tuple-element.82.levels, ...), custom_call_target="tpu_custom_call" | custom-call | flops 100663296 | bytes 6291456 | tf_op jit(solution)/shard_map/slope_backward/pallas_call | solution.py:188
  30.1 1.8 %slope_backward.9 = (f32[32,16,128]{2,1,0:T(8,128)S(1)}, f32[32,16,128]{2,1,0:T(8,128)S(1)}) custom-call(s32[8,24]{1,0:T(8,128)S(1)} %get-tuple-element.87.index, f32[8,24]{1,0:T(8,128)S(1)} %get-tuple-element.85.factor, f32[8,16,128]{2,1,0:T(8,128)S(1)} %add.80.own, f32[8,16,128]{2,1,0:T(8,128)S(1)} %collective-permute-done.5.other, ...), custom_call_target="tpu_custom_call" | custom-call | flops 100663296 | bytes 6291456 | tf_op jit(solution)/shard_map/slope_backward/pallas_call | solution.py:188
  35.1 2.4 %collective-permute-start.11 = (f32[8,16,128]{2,1,0:T(8,128)S(1)}, f32[8,16,128]{2,1,0:T(8,128)S(1)}, u32[]{:S(2)}, u32[]{:S(2)}) collective-permute-start(f32[8,16,128]{2,1,0:T(8,128)S(1)} %get-tuple-element.76), channel_id=1, source_target_pairs={{0,12},{4,8},{8,4},{12,0},{1,13},{5,9},{9,5},{13,1},{2,14},{6,10},... | collective-permute-start | bytes 196616 | tf_op jit(solution)/shard_map/ppermute | solution.py:232
  38.0 3.5 %collective-permute-done.11 = f32[8,16,128]{2,1,0:T(8,128)S(1)} collective-permute-done((f32[8,16,128]{2,1,0:T(8,128)S(1)}, f32[8,16,128]{2,1,0:T(8,128)S(1)}, u32[]{:S(2)}, u32[]{:S(2)}) %collective-permute-start.11) | collective-permute-done | bytes 65568 | tf_op jit(solution)/shard_map/ppermute | solution.py:232
  41.5 2.8 %collective-permute-done.10 = f32[8,16,128]{2,1,0:T(8,128)S(1)} collective-permute-done((f32[8,16,128]{2,1,0:T(8,128)S(1)}, f32[8,16,128]{2,1,0:T(8,128)S(1)}, u32[]{:S(2)}, u32[]{:S(2)}) %collective-permute-start.10) | collective-permute-done | bytes 65568 | tf_op jit(solution)/shard_map/ppermute | solution.py:232
  44.4 2.7 %collective-permute-start.14 = (bf16[8,16,128]{2,1,0:T(8,128)(2,1)S(1)}, bf16[8,16,128]{2,1,0:T(8,128)(2,1)S(1)}, u32[]{:S(2)}, u32[]{:S(2)}) collective-permute-start(bf16[8,16,128]{2,1,0:T(8,128)(2,1)S(1)} %get-tuple-element.60), channel_id=1, source_target_pairs={{0,12},{4,8},{8,4},{12,0},{1,13},{5,9},{9,5},{13,1},{2,14},{6,10},... | collective-permute-start | bytes 98312 | tf_op jit(solution)/shard_map/ppermute | solution.py:232
  57.6 2.0 %collective-permute-start.19 = (f32[8,16,128]{2,1,0:T(8,128)S(1)}, f32[8,16,128]{2,1,0:T(8,128)S(1)}, u32[]{:S(2)}, u32[]{:S(2)}) collective-permute-start(f32[8,16,128]{2,1,0:T(8,128)S(1)} %add.87.own), channel_id=1, source_target_pairs={{0,2},{2,0},{1,3},{3,1},{4,6},{6,4},{5,7},{7,5},{8,10},{10,8},{9,1... | collective-permute-start | bytes 196616 | tf_op jit(solution)/shard_map/ppermute | solution.py:283
  62.0 1.8 %slope_backward.10.refs_0_ = f32[64,16,128]{2,1,0:T(8,128)S(1)} custom-call(s32[8,24]{1,0:T(8,128)S(1)} %get-tuple-element.86.index, f32[8,24]{1,0:T(8,128)S(1)} %get-tuple-element.84.factor, f32[8,16,128]{2,1,0:T(8,128)S(1)} %add.87.own, f32[8,16,128]{2,1,0:T(8,128)S(1)} %collective-permute-done.19.other, f32[4,8,1,128]{3,2,1,0:T(1,128)S(1)} %get-tuple-element.82.levels, ...), custom_call_target="tpu_custom_call" | custom-call | flops 100663296 | bytes 6291456 | tf_op jit(solution)/shard_map/slope_backward/pallas_call | solution.py:188
  63.9 1.8 %slope_backward.11 = (f32[32,16,128]{2,1,0:T(8,128)S(1)}, f32[32,16,128]{2,1,0:T(8,128)S(1)}) custom-call(s32[8,24]{1,0:T(8,128)S(1)} %get-tuple-element.87.index, f32[8,24]{1,0:T(8,128)S(1)} %get-tuple-element.85.factor, f32[8,16,128]{2,1,0:T(8,128)S(1)} %add.86.own, f32[8,16,128]{2,1,0:T(8,128)S(1)} %collective-permute-done.17.other, ...), custom_call_target="tpu_custom_call" | custom-call | flops 100663296 | bytes 6291456 | tf_op jit(solution)/shard_map/slope_backward/pallas_call | solution.py:188
  68.4 2.6 %collective-permute-start.23 = (f32[8,16,128]{2,1,0:T(8,128)S(1)}, f32[8,16,128]{2,1,0:T(8,128)S(1)}, u32[]{:S(2)}, u32[]{:S(2)}) collective-permute-start(f32[8,16,128]{2,1,0:T(8,128)S(1)} %get-tuple-element.73), channel_id=1, source_target_pairs={{0,12},{4,8},{8,4},{12,0},{1,13},{5,9},{9,5},{13,1},{2,14},{6,10},... | collective-permute-start | bytes 196616 | tf_op jit(solution)/shard_map/ppermute | solution.py:232
  71.7 3.6 %collective-permute-done.23 = f32[8,16,128]{2,1,0:T(8,128)S(1)} collective-permute-done((f32[8,16,128]{2,1,0:T(8,128)S(1)}, f32[8,16,128]{2,1,0:T(8,128)S(1)}, u32[]{:S(2)}, u32[]{:S(2)}) %collective-permute-start.23) | collective-permute-done | bytes 65568 | tf_op jit(solution)/shard_map/ppermute | solution.py:232
  75.3 2.1 %collective-permute-done.22 = f32[8,16,128]{2,1,0:T(8,128)S(1)} collective-permute-done((f32[8,16,128]{2,1,0:T(8,128)S(1)}, f32[8,16,128]{2,1,0:T(8,128)S(1)}, u32[]{:S(2)}, u32[]{:S(2)}) %collective-permute-start.22) | collective-permute-done | bytes 65568 | tf_op jit(solution)/shard_map/ppermute | solution.py:232
  77.5 2.1 %collective-permute-start.26 = (bf16[8,16,128]{2,1,0:T(8,128)(2,1)S(1)}, bf16[8,16,128]{2,1,0:T(8,128)(2,1)S(1)}, u32[]{:S(2)}, u32[]{:S(2)}) collective-permute-start(bf16[8,16,128]{2,1,0:T(8,128)(2,1)S(1)} %get-tuple-element.58), channel_id=1, source_target_pairs={{0,12},{4,8},{8,4},{12,0},{1,13},{5,9},{9,5},{13,1},{2,14},{6,10},... | collective-permute-start | bytes 98312 | tf_op jit(solution)/shard_map/ppermute | solution.py:232
  79.5 2.4 %collective-permute-start.24 = (bf16[8,16,128]{2,1,0:T(8,128)(2,1)S(1)}, bf16[8,16,128]{2,1,0:T(8,128)(2,1)S(1)}, u32[]{:S(2)}, u32[]{:S(2)}) collective-permute-start(bf16[8,16,128]{2,1,0:T(8,128)(2,1)S(1)} %get-tuple-element.58), channel_id=1, source_target_pairs={{0,4},{4,0},{8,12},{12,8},{1,5},{5,1},{9,13},{13,9},{2,6},{6,2},{1... | collective-permute-start | bytes 98312 | tf_op jit(solution)/shard_map/ppermute | solution.py:232
  90.0 2.3 %collective-permute-start.31 = (f32[8,16,128]{2,1,0:T(8,128)S(1)}, f32[8,16,128]{2,1,0:T(8,128)S(1)}, u32[]{:S(2)}, u32[]{:S(2)}) collective-permute-start(f32[8,16,128]{2,1,0:T(8,128)S(1)} %add.93.own), channel_id=1, source_target_pairs={{0,2},{2,0},{1,3},{3,1},{4,6},{6,4},{5,7},{7,5},{8,10},{10,8},{9,1... | collective-permute-start | bytes 196616 | tf_op jit(solution)/shard_map/ppermute | solution.py:283
  94.7 1.8 %slope_backward.12.refs_0_ = f32[64,16,128]{2,1,0:T(8,128)S(1)} custom-call(s32[8,24]{1,0:T(8,128)S(1)} %get-tuple-element.86.index, f32[8,24]{1,0:T(8,128)S(1)} %get-tuple-element.84.factor, f32[8,16,128]{2,1,0:T(8,128)S(1)} %add.93.own, f32[8,16,128]{2,1,0:T(8,128)S(1)} %collective-permute-done.31.other, f32[4,8,1,128]{3,2,1,0:T(1,128)S(1)} %get-tuple-element.82.levels, ...), custom_call_target="tpu_custom_call" | custom-call | flops 100663296 | bytes 6291456 | tf_op jit(solution)/shard_map/slope_backward/pallas_call | solution.py:188
  96.7 2.0 %slope_backward.13 = (f32[32,16,128]{2,1,0:T(8,128)S(1)}, f32[32,16,128]{2,1,0:T(8,128)S(1)}) custom-call(s32[8,24]{1,0:T(8,128)S(1)} %get-tuple-element.87.index, f32[8,24]{1,0:T(8,128)S(1)} %get-tuple-element.85.factor, f32[8,16,128]{2,1,0:T(8,128)S(1)} %add.92.own, f32[8,16,128]{2,1,0:T(8,128)S(1)} %collective-permute-done.29.other, ...), custom_call_target="tpu_custom_call" | custom-call | flops 100663296 | bytes 6291456 | tf_op jit(solution)/shard_map/slope_backward/pallas_call | solution.py:188
  101.9 2.0 %collective-permute-start.35 = (f32[8,16,128]{2,1,0:T(8,128)S(1)}, f32[8,16,128]{2,1,0:T(8,128)S(1)}, u32[]{:S(2)}, u32[]{:S(2)}) collective-permute-start(f32[8,16,128]{2,1,0:T(8,128)S(1)} %get-tuple-element.70), channel_id=1, source_target_pairs={{0,12},{4,8},{8,4},{12,0},{1,13},{5,9},{9,5},{13,1},{2,14},{6,10},... | collective-permute-start | bytes 196616 | tf_op jit(solution)/shard_map/ppermute | solution.py:232
  104.7 3.7 %collective-permute-done.35 = f32[8,16,128]{2,1,0:T(8,128)S(1)} collective-permute-done((f32[8,16,128]{2,1,0:T(8,128)S(1)}, f32[8,16,128]{2,1,0:T(8,128)S(1)}, u32[]{:S(2)}, u32[]{:S(2)}) %collective-permute-start.35) | collective-permute-done | bytes 65568 | tf_op jit(solution)/shard_map/ppermute | solution.py:232
  108.3 2.0 %collective-permute-done.34 = f32[8,16,128]{2,1,0:T(8,128)S(1)} collective-permute-done((f32[8,16,128]{2,1,0:T(8,128)S(1)}, f32[8,16,128]{2,1,0:T(8,128)S(1)}, u32[]{:S(2)}, u32[]{:S(2)}) %collective-permute-start.34) | collective-permute-done | bytes 65568 | tf_op jit(solution)/shard_map/ppermute | solution.py:232
  110.4 2.1 %collective-permute-start.38 = (bf16[8,16,128]{2,1,0:T(8,128)(2,1)S(1)}, bf16[8,16,128]{2,1,0:T(8,128)(2,1)S(1)}, u32[]{:S(2)}, u32[]{:S(2)}) collective-permute-start(bf16[8,16,128]{2,1,0:T(8,128)(2,1)S(1)} %get-tuple-element.56), channel_id=1, source_target_pairs={{0,12},{4,8},{8,4},{12,0},{1,13},{5,9},{9,5},{13,1},{2,14},{6,10},... | collective-permute-start | bytes 98312 | tf_op jit(solution)/shard_map/ppermute | solution.py:232
  112.4 2.4 %collective-permute-start.36 = (bf16[8,16,128]{2,1,0:T(8,128)(2,1)S(1)}, bf16[8,16,128]{2,1,0:T(8,128)(2,1)S(1)}, u32[]{:S(2)}, u32[]{:S(2)}) collective-permute-start(bf16[8,16,128]{2,1,0:T(8,128)(2,1)S(1)} %get-tuple-element.56), channel_id=1, source_target_pairs={{0,4},{4,0},{8,12},{12,8},{1,5},{5,1},{9,13},{13,9},{2,6},{6,2},{1... | collective-permute-start | bytes 98312 | tf_op jit(solution)/shard_map/ppermute | solution.py:232
  123.0 2.3 %collective-permute-start.43 = (f32[8,16,128]{2,1,0:T(8,128)S(1)}, f32[8,16,128]{2,1,0:T(8,128)S(1)}, u32[]{:S(2)}, u32[]{:S(2)}) collective-permute-start(f32[8,16,128]{2,1,0:T(8,128)S(1)} %add.99.own), channel_id=1, source_target_pairs={{0,2},{2,0},{1,3},{3,1},{4,6},{6,4},{5,7},{7,5},{8,10},{10,8},{9,1... | collective-permute-start | bytes 196616 | tf_op jit(solution)/shard_map/ppermute | solution.py:283
  127.6 1.8 %slope_backward.14.refs_0_ = f32[64,16,128]{2,1,0:T(8,128)S(1)} custom-call(s32[8,24]{1,0:T(8,128)S(1)} %get-tuple-element.86.index, f32[8,24]{1,0:T(8,128)S(1)} %get-tuple-element.84.factor, f32[8,16,128]{2,1,0:T(8,128)S(1)} %add.99.own, f32[8,16,128]{2,1,0:T(8,128)S(1)} %collective-permute-done.43.other, f32[4,8,1,128]{3,2,1,0:T(1,128)S(1)} %get-tuple-element.82.levels, ...), custom_call_target="tpu_custom_call" | custom-call | flops 100663296 | bytes 6291456 | tf_op jit(solution)/shard_map/slope_backward/pallas_call | solution.py:188
  129.6 1.8 %slope_backward.15 = (f32[32,16,128]{2,1,0:T(8,128)S(1)}, f32[32,16,128]{2,1,0:T(8,128)S(1)}) custom-call(s32[8,24]{1,0:T(8,128)S(1)} %get-tuple-element.87.index, f32[8,24]{1,0:T(8,128)S(1)} %get-tuple-element.85.factor, f32[8,16,128]{2,1,0:T(8,128)S(1)} %add.98.own, f32[8,16,128]{2,1,0:T(8,128)S(1)} %collective-permute-done.41.other, ...), custom_call_target="tpu_custom_call" | custom-call | flops 100663296 | bytes 6291456 | tf_op jit(solution)/shard_map/slope_backward/pallas_call | solution.py:188
  134.6 2.0 %collective-permute-start.47 = (f32[8,16,128]{2,1,0:T(8,128)S(1)}, f32[8,16,128]{2,1,0:T(8,128)S(1)}, u32[]{:S(2)}, u32[]{:S(2)}) collective-permute-start(f32[8,16,128]{2,1,0:T(8,128)S(1)} %get-tuple-element.67), channel_id=1, source_target_pairs={{0,12},{4,8},{8,4},{12,0},{1,13},{5,9},{9,5},{13,1},{2,14},{6,10},... | collective-permute-start | bytes 196616 | tf_op jit(solution)/shard_map/ppermute | solution.py:232
  137.4 3.7 %collective-permute-done.47 = f32[8,16,128]{2,1,0:T(8,128)S(1)} collective-permute-done((f32[8,16,128]{2,1,0:T(8,128)S(1)}, f32[8,16,128]{2,1,0:T(8,128)S(1)}, u32[]{:S(2)}, u32[]{:S(2)}) %collective-permute-start.47) | collective-permute-done | bytes 65568 | tf_op jit(solution)/shard_map/ppermute | solution.py:232
  141.1 2.0 %collective-permute-done.46 = f32[8,16,128]{2,1,0:T(8,128)S(1)} collective-permute-done((f32[8,16,128]{2,1,0:T(8,128)S(1)}, f32[8,16,128]{2,1,0:T(8,128)S(1)}, u32[]{:S(2)}, u32[]{:S(2)}) %collective-permute-start.46) | collective-permute-done | bytes 65568 | tf_op jit(solution)/shard_map/ppermute | solution.py:232
  (156 shorter events, 64.1 us)
Async XLA Ops:
  1.6 12.8 %collective-permute-start.2 = (bf16[8,16,128]{2,1,0:T(8,128)(2,1)S(1)}, bf16[8,16,128]{2,1,0:T(8,128)(2,1)S(1)}, u32[]{:S(2)}, u32[]{:S(2)}) collective-permute-start(bf16[8,16,128]{2,1,0:T(8,128)(2,1)S(1)} %bitcast.55), channel_id=1, source_target_pairs={{0,12},{4,8},{8,4},{12,0},{1,13},{5,9},{9,5},{13,1},{2,14},{6,10},... | collective-permute-start | bytes 98312 | tf_op jit(solution)/shard_map/ppermute | solution.py:232
  6.7 7.7 %collective-permute-start.1 = (bf16[8,16,128]{2,1,0:T(8,128)(2,1)S(1)}, bf16[8,16,128]{2,1,0:T(8,128)(2,1)S(1)}, u32[]{:S(2)}, u32[]{:S(2)}) collective-permute-start(bf16[8,16,128]{2,1,0:T(8,128)(2,1)S(1)} %bitcast.56), channel_id=1, source_target_pairs={{0,8},{4,12},{8,0},{12,4},{1,9},{5,13},{9,1},{13,5},{2,10},{6,14},... | collective-permute-start | bytes 98312 | tf_op jit(solution)/shard_map/ppermute | solution.py:232
  6.7 7.7 %collective-permute-start = (bf16[8,16,128]{2,1,0:T(8,128)(2,1)S(1)}, bf16[8,16,128]{2,1,0:T(8,128)(2,1)S(1)}, u32[]{:S(2)}, u32[]{:S(2)}) collective-permute-start(bf16[8,16,128]{2,1,0:T(8,128)(2,1)S(1)} %bitcast.57), channel_id=1, source_target_pairs={{0,4},{4,0},{8,12},{12,8},{1,5},{5,1},{9,13},{13,9},{2,6},{6,2},{1... | collective-permute-start | bytes 98312 | tf_op jit(solution)/shard_map/ppermute | solution.py:232
  23.2 4.7 %collective-permute-start.7 = (f32[9,16,128]{2,1,0:T(8,128)S(1)}, f32[9,16,128]{2,1,0:T(8,128)S(1)}, u32[]{:S(2)}, u32[]{:S(2)}) collective-permute-start(f32[9,16,128]{2,1,0:T(8,128)S(1)} %pad_maximum_fusion.5), channel_id=1, source_target_pairs={{0,2},{2,0},{1,3},{3,1},{4,6},{6,4},{5,7},{7,5},{8,10},{10,8},{9,1... | collective-permute-start | bytes 221192 | tf_op jit(solution)/shard_map/ppermute | solution.py:283
  25.2 4.9 %collective-permute-start.5 = (f32[8,16,128]{2,1,0:T(8,128)S(1)}, f32[8,16,128]{2,1,0:T(8,128)S(1)}, u32[]{:S(2)}, u32[]{:S(2)}) collective-permute-start(f32[8,16,128]{2,1,0:T(8,128)S(1)} %add.80.own), channel_id=1, source_target_pairs={{0,2},{2,0},{1,3},{3,1},{4,6},{6,4},{5,7},{7,5},{8,10},{10,8},{9,1... | collective-permute-start | bytes 196616 | tf_op jit(solution)/shard_map/ppermute | solution.py:283
  33.6 4.4 %collective-permute-start.9 = (f32[8,16,128]{2,1,0:T(8,128)S(1)}, f32[8,16,128]{2,1,0:T(8,128)S(1)}, u32[]{:S(2)}, u32[]{:S(2)}) collective-permute-start(f32[8,16,128]{2,1,0:T(8,128)S(1)} %get-tuple-element.75), channel_id=1, source_target_pairs={{0,4},{4,0},{8,12},{12,8},{1,5},{5,1},{9,13},{13,9},{2,6},{6,2},{1... | collective-permute-start | bytes 196616 | tf_op jit(solution)/shard_map/ppermute | solution.py:232
  35.1 6.5 %collective-permute-start.11 = (f32[8,16,128]{2,1,0:T(8,128)S(1)}, f32[8,16,128]{2,1,0:T(8,128)S(1)}, u32[]{:S(2)}, u32[]{:S(2)}) collective-permute-start(f32[8,16,128]{2,1,0:T(8,128)S(1)} %get-tuple-element.76), channel_id=1, source_target_pairs={{0,12},{4,8},{8,4},{12,0},{1,13},{5,9},{9,5},{13,1},{2,14},{6,10},... | collective-permute-start | bytes 196616 | tf_op jit(solution)/shard_map/ppermute | solution.py:232
  37.5 6.8 %collective-permute-start.10 = (f32[8,16,128]{2,1,0:T(8,128)S(1)}, f32[8,16,128]{2,1,0:T(8,128)S(1)}, u32[]{:S(2)}, u32[]{:S(2)}) collective-permute-start(f32[8,16,128]{2,1,0:T(8,128)S(1)} %get-tuple-element.77), channel_id=1, source_target_pairs={{0,8},{4,12},{8,0},{12,4},{1,9},{5,13},{9,1},{13,5},{2,10},{6,14},... | collective-permute-start | bytes 196616 | tf_op jit(solution)/shard_map/ppermute | solution.py:232
  44.4 5.8 %collective-permute-start.14 = (bf16[8,16,128]{2,1,0:T(8,128)(2,1)S(1)}, bf16[8,16,128]{2,1,0:T(8,128)(2,1)S(1)}, u32[]{:S(2)}, u32[]{:S(2)}) collective-permute-start(bf16[8,16,128]{2,1,0:T(8,128)(2,1)S(1)} %get-tuple-element.60), channel_id=1, source_target_pairs={{0,12},{4,8},{8,4},{12,0},{1,13},{5,9},{9,5},{13,1},{2,14},{6,10},... | collective-permute-start | bytes 98312 | tf_op jit(solution)/shard_map/ppermute | solution.py:232
  47.1 4.8 %collective-permute-start.13 = (bf16[8,16,128]{2,1,0:T(8,128)(2,1)S(1)}, bf16[8,16,128]{2,1,0:T(8,128)(2,1)S(1)}, u32[]{:S(2)}, u32[]{:S(2)}) collective-permute-start(bf16[8,16,128]{2,1,0:T(8,128)(2,1)S(1)} %get-tuple-element.60), channel_id=1, source_target_pairs={{0,8},{4,12},{8,0},{12,4},{1,9},{5,13},{9,1},{13,5},{2,10},{6,14},... | collective-permute-start | bytes 98312 | tf_op jit(solution)/shard_map/ppermute | solution.py:232
  47.1 4.8 %collective-permute-start.12 = (bf16[8,16,128]{2,1,0:T(8,128)(2,1)S(1)}, bf16[8,16,128]{2,1,0:T(8,128)(2,1)S(1)}, u32[]{:S(2)}, u32[]{:S(2)}) collective-permute-start(bf16[8,16,128]{2,1,0:T(8,128)(2,1)S(1)} %get-tuple-element.60), channel_id=1, source_target_pairs={{0,4},{4,0},{8,12},{12,8},{1,5},{5,1},{9,13},{13,9},{2,6},{6,2},{1... | collective-permute-start | bytes 98312 | tf_op jit(solution)/shard_map/ppermute | solution.py:232
  57.6 4.4 %collective-permute-start.19 = (f32[8,16,128]{2,1,0:T(8,128)S(1)}, f32[8,16,128]{2,1,0:T(8,128)S(1)}, u32[]{:S(2)}, u32[]{:S(2)}) collective-permute-start(f32[8,16,128]{2,1,0:T(8,128)S(1)} %add.87.own), channel_id=1, source_target_pairs={{0,2},{2,0},{1,3},{3,1},{4,6},{6,4},{5,7},{7,5},{8,10},{10,8},{9,1... | collective-permute-start | bytes 196616 | tf_op jit(solution)/shard_map/ppermute | solution.py:283
  59.6 4.3 %collective-permute-start.17 = (f32[8,16,128]{2,1,0:T(8,128)S(1)}, f32[8,16,128]{2,1,0:T(8,128)S(1)}, u32[]{:S(2)}, u32[]{:S(2)}) collective-permute-start(f32[8,16,128]{2,1,0:T(8,128)S(1)} %add.86.own), channel_id=1, source_target_pairs={{0,2},{2,0},{1,3},{3,1},{4,6},{6,4},{5,7},{7,5},{8,10},{10,8},{9,1... | collective-permute-start | bytes 196616 | tf_op jit(solution)/shard_map/ppermute | solution.py:283
  67.4 4.3 %collective-permute-start.21 = (f32[8,16,128]{2,1,0:T(8,128)S(1)}, f32[8,16,128]{2,1,0:T(8,128)S(1)}, u32[]{:S(2)}, u32[]{:S(2)}) collective-permute-start(f32[8,16,128]{2,1,0:T(8,128)S(1)} %get-tuple-element.72), channel_id=1, source_target_pairs={{0,4},{4,0},{8,12},{12,8},{1,5},{5,1},{9,13},{13,9},{2,6},{6,2},{1... | collective-permute-start | bytes 196616 | tf_op jit(solution)/shard_map/ppermute | solution.py:232
  68.4 6.9 %collective-permute-start.23 = (f32[8,16,128]{2,1,0:T(8,128)S(1)}, f32[8,16,128]{2,1,0:T(8,128)S(1)}, u32[]{:S(2)}, u32[]{:S(2)}) collective-permute-start(f32[8,16,128]{2,1,0:T(8,128)S(1)} %get-tuple-element.73), channel_id=1, source_target_pairs={{0,12},{4,8},{8,4},{12,0},{1,13},{5,9},{9,5},{13,1},{2,14},{6,10},... | collective-permute-start | bytes 196616 | tf_op jit(solution)/shard_map/ppermute | solution.py:232
  71.0 6.5 %collective-permute-start.22 = (f32[8,16,128]{2,1,0:T(8,128)S(1)}, f32[8,16,128]{2,1,0:T(8,128)S(1)}, u32[]{:S(2)}, u32[]{:S(2)}) collective-permute-start(f32[8,16,128]{2,1,0:T(8,128)S(1)} %get-tuple-element.74), channel_id=1, source_target_pairs={{0,8},{4,12},{8,0},{12,4},{1,9},{5,13},{9,1},{13,5},{2,10},{6,14},... | collective-permute-start | bytes 196616 | tf_op jit(solution)/shard_map/ppermute | solution.py:232
  77.5 5.9 %collective-permute-start.26 = (bf16[8,16,128]{2,1,0:T(8,128)(2,1)S(1)}, bf16[8,16,128]{2,1,0:T(8,128)(2,1)S(1)}, u32[]{:S(2)}, u32[]{:S(2)}) collective-permute-start(bf16[8,16,128]{2,1,0:T(8,128)(2,1)S(1)} %get-tuple-element.58), channel_id=1, source_target_pairs={{0,12},{4,8},{8,4},{12,0},{1,13},{5,9},{9,5},{13,1},{2,14},{6,10},... | collective-permute-start | bytes 98312 | tf_op jit(solution)/shard_map/ppermute | solution.py:232
  79.5 4.8 %collective-permute-start.25 = (bf16[8,16,128]{2,1,0:T(8,128)(2,1)S(1)}, bf16[8,16,128]{2,1,0:T(8,128)(2,1)S(1)}, u32[]{:S(2)}, u32[]{:S(2)}) collective-permute-start(bf16[8,16,128]{2,1,0:T(8,128)(2,1)S(1)} %get-tuple-element.58), channel_id=1, source_target_pairs={{0,8},{4,12},{8,0},{12,4},{1,9},{5,13},{9,1},{13,5},{2,10},{6,14},... | collective-permute-start | bytes 98312 | tf_op jit(solution)/shard_map/ppermute | solution.py:232
  79.5 4.8 %collective-permute-start.24 = (bf16[8,16,128]{2,1,0:T(8,128)(2,1)S(1)}, bf16[8,16,128]{2,1,0:T(8,128)(2,1)S(1)}, u32[]{:S(2)}, u32[]{:S(2)}) collective-permute-start(bf16[8,16,128]{2,1,0:T(8,128)(2,1)S(1)} %get-tuple-element.58), channel_id=1, source_target_pairs={{0,4},{4,0},{8,12},{12,8},{1,5},{5,1},{9,13},{13,9},{2,6},{6,2},{1... | collective-permute-start | bytes 98312 | tf_op jit(solution)/shard_map/ppermute | solution.py:232
  90.0 4.7 %collective-permute-start.31 = (f32[8,16,128]{2,1,0:T(8,128)S(1)}, f32[8,16,128]{2,1,0:T(8,128)S(1)}, u32[]{:S(2)}, u32[]{:S(2)}) collective-permute-start(f32[8,16,128]{2,1,0:T(8,128)S(1)} %add.93.own), channel_id=1, source_target_pairs={{0,2},{2,0},{1,3},{3,1},{4,6},{6,4},{5,7},{7,5},{8,10},{10,8},{9,1... | collective-permute-start | bytes 196616 | tf_op jit(solution)/shard_map/ppermute | solution.py:283
  92.3 4.3 %collective-permute-start.29 = (f32[8,16,128]{2,1,0:T(8,128)S(1)}, f32[8,16,128]{2,1,0:T(8,128)S(1)}, u32[]{:S(2)}, u32[]{:S(2)}) collective-permute-start(f32[8,16,128]{2,1,0:T(8,128)S(1)} %add.92.own), channel_id=1, source_target_pairs={{0,2},{2,0},{1,3},{3,1},{4,6},{6,4},{5,7},{7,5},{8,10},{10,8},{9,1... | collective-permute-start | bytes 196616 | tf_op jit(solution)/shard_map/ppermute | solution.py:283
  100.3 4.3 %collective-permute-start.33 = (f32[8,16,128]{2,1,0:T(8,128)S(1)}, f32[8,16,128]{2,1,0:T(8,128)S(1)}, u32[]{:S(2)}, u32[]{:S(2)}) collective-permute-start(f32[8,16,128]{2,1,0:T(8,128)S(1)} %get-tuple-element.69), channel_id=1, source_target_pairs={{0,4},{4,0},{8,12},{12,8},{1,5},{5,1},{9,13},{13,9},{2,6},{6,2},{1... | collective-permute-start | bytes 196616 | tf_op jit(solution)/shard_map/ppermute | solution.py:232
  101.9 6.5 %collective-permute-start.35 = (f32[8,16,128]{2,1,0:T(8,128)S(1)}, f32[8,16,128]{2,1,0:T(8,128)S(1)}, u32[]{:S(2)}, u32[]{:S(2)}) collective-permute-start(f32[8,16,128]{2,1,0:T(8,128)S(1)} %get-tuple-element.70), channel_id=1, source_target_pairs={{0,12},{4,8},{8,4},{12,0},{1,13},{5,9},{9,5},{13,1},{2,14},{6,10},... | collective-permute-start | bytes 196616 | tf_op jit(solution)/shard_map/ppermute | solution.py:232
  103.9 6.5 %collective-permute-start.34 = (f32[8,16,128]{2,1,0:T(8,128)S(1)}, f32[8,16,128]{2,1,0:T(8,128)S(1)}, u32[]{:S(2)}, u32[]{:S(2)}) collective-permute-start(f32[8,16,128]{2,1,0:T(8,128)S(1)} %get-tuple-element.71), channel_id=1, source_target_pairs={{0,8},{4,12},{8,0},{12,4},{1,9},{5,13},{9,1},{13,5},{2,10},{6,14},... | collective-permute-start | bytes 196616 | tf_op jit(solution)/shard_map/ppermute | solution.py:232
  110.4 5.9 %collective-permute-start.38 = (bf16[8,16,128]{2,1,0:T(8,128)(2,1)S(1)}, bf16[8,16,128]{2,1,0:T(8,128)(2,1)S(1)}, u32[]{:S(2)}, u32[]{:S(2)}) collective-permute-start(bf16[8,16,128]{2,1,0:T(8,128)(2,1)S(1)} %get-tuple-element.56), channel_id=1, source_target_pairs={{0,12},{4,8},{8,4},{12,0},{1,13},{5,9},{9,5},{13,1},{2,14},{6,10},... | collective-permute-start | bytes 98312 | tf_op jit(solution)/shard_map/ppermute | solution.py:232
  112.4 4.8 %collective-permute-start.37 = (bf16[8,16,128]{2,1,0:T(8,128)(2,1)S(1)}, bf16[8,16,128]{2,1,0:T(8,128)(2,1)S(1)}, u32[]{:S(2)}, u32[]{:S(2)}) collective-permute-start(bf16[8,16,128]{2,1,0:T(8,128)(2,1)S(1)} %get-tuple-element.56), channel_id=1, source_target_pairs={{0,8},{4,12},{8,0},{12,4},{1,9},{5,13},{9,1},{13,5},{2,10},{6,14},... | collective-permute-start | bytes 98312 | tf_op jit(solution)/shard_map/ppermute | solution.py:232
  112.4 4.8 %collective-permute-start.36 = (bf16[8,16,128]{2,1,0:T(8,128)(2,1)S(1)}, bf16[8,16,128]{2,1,0:T(8,128)(2,1)S(1)}, u32[]{:S(2)}, u32[]{:S(2)}) collective-permute-start(bf16[8,16,128]{2,1,0:T(8,128)(2,1)S(1)} %get-tuple-element.56), channel_id=1, source_target_pairs={{0,4},{4,0},{8,12},{12,8},{1,5},{5,1},{9,13},{13,9},{2,6},{6,2},{1... | collective-permute-start | bytes 98312 | tf_op jit(solution)/shard_map/ppermute | solution.py:232
  123.0 4.7 %collective-permute-start.43 = (f32[8,16,128]{2,1,0:T(8,128)S(1)}, f32[8,16,128]{2,1,0:T(8,128)S(1)}, u32[]{:S(2)}, u32[]{:S(2)}) collective-permute-start(f32[8,16,128]{2,1,0:T(8,128)S(1)} %add.99.own), channel_id=1, source_target_pairs={{0,2},{2,0},{1,3},{3,1},{4,6},{6,4},{5,7},{7,5},{8,10},{10,8},{9,1... | collective-permute-start | bytes 196616 | tf_op jit(solution)/shard_map/ppermute | solution.py:283
  125.2 4.3 %collective-permute-start.41 = (f32[8,16,128]{2,1,0:T(8,128)S(1)}, f32[8,16,128]{2,1,0:T(8,128)S(1)}, u32[]{:S(2)}, u32[]{:S(2)}) collective-permute-start(f32[8,16,128]{2,1,0:T(8,128)S(1)} %add.98.own), channel_id=1, source_target_pairs={{0,2},{2,0},{1,3},{3,1},{4,6},{6,4},{5,7},{7,5},{8,10},{10,8},{9,1... | collective-permute-start | bytes 196616 | tf_op jit(solution)/shard_map/ppermute | solution.py:283
  133.1 4.3 %collective-permute-start.45 = (f32[8,16,128]{2,1,0:T(8,128)S(1)}, f32[8,16,128]{2,1,0:T(8,128)S(1)}, u32[]{:S(2)}, u32[]{:S(2)}) collective-permute-start(f32[8,16,128]{2,1,0:T(8,128)S(1)} %get-tuple-element.66), channel_id=1, source_target_pairs={{0,4},{4,0},{8,12},{12,8},{1,5},{5,1},{9,13},{13,9},{2,6},{6,2},{1... | collective-permute-start | bytes 196616 | tf_op jit(solution)/shard_map/ppermute | solution.py:232
  134.6 6.5 %collective-permute-start.47 = (f32[8,16,128]{2,1,0:T(8,128)S(1)}, f32[8,16,128]{2,1,0:T(8,128)S(1)}, u32[]{:S(2)}, u32[]{:S(2)}) collective-permute-start(f32[8,16,128]{2,1,0:T(8,128)S(1)} %get-tuple-element.67), channel_id=1, source_target_pairs={{0,12},{4,8},{8,4},{12,0},{1,13},{5,9},{9,5},{13,1},{2,14},{6,10},... | collective-permute-start | bytes 196616 | tf_op jit(solution)/shard_map/ppermute | solution.py:232
  136.6 6.5 %collective-permute-start.46 = (f32[8,16,128]{2,1,0:T(8,128)S(1)}, f32[8,16,128]{2,1,0:T(8,128)S(1)}, u32[]{:S(2)}, u32[]{:S(2)}) collective-permute-start(f32[8,16,128]{2,1,0:T(8,128)S(1)} %get-tuple-element.68), channel_id=1, source_target_pairs={{0,8},{4,12},{8,0},{12,4},{1,9},{5,13},{9,1},{13,5},{2,10},{6,14},... | collective-permute-start | bytes 196616 | tf_op jit(solution)/shard_map/ppermute | solution.py:232
  (25 other events, 52.6 us)

commit v5 on v2

v5 whole, which is shorter than its diff:
```python
import functools

import jax
import jax.numpy as jnp
from jax import lax
from jax.experimental import pallas as pl
from jax.experimental.pallas import tpu as pltpu
from jax.sharding import PartitionSpec as P

ITERS = 4
F32 = jnp.float32
BF16 = jnp.bfloat16
PARAMS = pltpu.CompilerParams(vmem_limit_bytes=16 * 2**20)


def in_vmem():
    return pl.BlockSpec(memory_space=pltpu.VMEM)


def in_smem():
    return pl.BlockSpec(memory_space=pltpu.SMEM)


def held(array):
    return pltpu.with_memory_space_constraint(array, pltpu.VMEM)


def index_kernel(n_vox, columns, runs, steps, me, cols, exps, live, *outs):
    z, core = me[0], me[1]
    rows, _, slots = cols.shape
    own = columns // (2 * n_vox)
    column, exponent = cols[:, 0, :], exps[:, 0, :]
    piece, within = lax.div(column, own), lax.rem(column, own)
    place = ((lax.rem(piece, 2) ^ core) * n_vox + (lax.div(piece, 2) ^ z)) * own + within
    scale = jnp.where(exponent < 0, 0.5, jnp.where(exponent > 0, 2.0, 1.0))
    scaled = (exponent + 1) * columns + place
    position = core * slots + lax.broadcasted_iota(jnp.int32, (1, slots), 1)
    n = rows // (2 * runs)
    for half in range(2):
        index, places, factor = outs[3 * half : 3 * half + 3]
        for r in range(rows // 2):
            first = 2 * n * (r // n) + r % n
            low, high = (first, first + n) if half == 0 else (first + n, first)

            def row(array):
                return jnp.where(core == 0, array[low : low + 1], array[high : high + 1])

            used = position < jnp.where(core == 0, live[low], live[high])
            places[r : r + 1] = row(place)
            index[r : r + 1] = jnp.where(used, row(scaled), 3 * columns)
            factor[r : r + 1] = jnp.where(used, row(scale), 0.0).astype(F32)
    sides = outs[-1]
    for e, (at, bit) in enumerate(steps):
        side = jnp.where((me[at] & bit) == 0, 1.0, 0.0).astype(F32)
        sides[e] = jnp.full(sides.shape[1:], side)


def indices(n_vox, columns, runs, steps, me, cols, exps, live):
    rows, _, slots = cols.shape
    out = [jax.ShapeDtypeStruct((rows // 2, slots), t) for t in (jnp.int32, jnp.int32, F32)] * 2
    out.append(jax.ShapeDtypeStruct((len(steps), 8, 128), F32))
    return pl.pallas_call(
        functools.partial(index_kernel, n_vox, columns, runs, steps),
        in_specs=[in_smem()] + [in_vmem()] * 2 + [in_smem()],
        out_specs=[in_vmem()] * len(out),
        out_shape=out,
        compiler_params=PARAMS,
        name="indices",
    )(me, *(pltpu.with_memory_space_constraint(a, pltpu.HBM) for a in (cols, exps)), live)


def turn_kernel(kept, after, turned):
    count = kept.shape[0]
    step = 8 if count % 8 == 0 else 1

    def some(t, carry):
        for u in range(step):
            turned[t * step + u] = kept[t * step + u].T
        return carry

    lax.fori_loop(0, count // step, some, 0)


def turn(kept, after):
    return pl.pallas_call(
        turn_kernel,
        in_specs=[in_vmem(), pl.BlockSpec(memory_space=pl.ANY)],
        out_specs=in_vmem(),
        out_shape=pltpu.VMEM(kept.shape, kept.dtype),
        compiler_params=PARAMS,
        cost_estimate=pl.CostEstimate(flops=0, bytes_accessed=4 * kept.size, transcendentals=0),
        name="turn",
    )(held(kept), after)


def scale_weights(pieces, scaled):
    columns = (scaled.shape[0] - 1) // 3
    at = 0
    for piece in pieces:
        n = piece.shape[0]
        values = piece[...]
        scaled[at : at + n] = values * BF16(0.5)
        scaled[columns + at : columns + at + n] = values
        scaled[2 * columns + at : 2 * columns + at + n] = values * BF16(2.0)
        at += n
    scaled[3 * columns] = jnp.zeros(scaled.shape[1:], BF16)


def row_copies(mine, runs, slots, me, stored, kept, sems):
    rows = sems.shape[0]
    n = rows // runs
    half = me[1] if mine else 1 - me[1]
    return [
        pltpu.make_async_copy(
            stored.at[pl.ds(((2 * (b // n) + half) * n + b % n) * slots, slots)],
            kept.at[pl.ds(b * slots, slots)],
            sems.at[b],
        )
        for b in range(rows)
    ]


def load_kernel(slots, runs, me, stored, after, kept, sems):
    copies = row_copies(False, runs, slots, me, stored, kept, sems)
    for copy in copies:
        copy.start()
    for copy in copies:
        copy.wait()


def load_others(rows, runs, me, tiles, after):
    shape = (tiles.shape[0] // 2,) + tiles.shape[1:]
    return pl.pallas_call(
        functools.partial(load_kernel, tiles.shape[0] // rows, runs),
        in_specs=[in_smem(), pl.BlockSpec(memory_space=pltpu.HBM), in_vmem()],
        out_specs=in_vmem(),
        out_shape=pltpu.VMEM(shape, tiles.dtype),
        scratch_shapes=[pltpu.SemaphoreType.DMA((rows // 2,))],
        compiler_params=PARAMS,
        cost_estimate=pl.CostEstimate(flops=0, bytes_accessed=2 * tiles.size, transcendentals=0),
        name="load_others",
    )(me, pltpu.with_memory_space_constraint(tiles, pltpu.HBM), after)


def first_forward_kernel(slots, runs, me, index_others, index_mine, *refs):
    pieces, (kept_others, stored, given, dose, kept_mine, scaled, sems) = refs[:-7], refs[-7:]
    copies = row_copies(True, runs, slots, me, stored, kept_mine, sems)
    for copy in copies:
        copy.start()
    scale_weights(pieces, scaled)
    rows = dose.shape[0]
    unroll = 4 if rows % 4 == 0 else 1
    for index, kept, out in ((index_others, kept_others, given), (index_mine, kept_mine, dose)):
        for t in range(rows // unroll):
            if kept is kept_mine:
                for u in range(unroll):
                    copies[t * unroll + u].wait()
            for u in range(unroll):
                b = t * unroll + u
                left = jnp.concatenate([scaled[index[b, k]] for k in range(slots)], axis=1)
                right = jnp.concatenate([kept[b * slots + k] for k in range(slots)], axis=1)
                out[b] = lax.dot_general(
                    left, right, (((1,), (1,)), ((), ())), preferred_element_type=F32
                )


def forward_kernel(slots, index, *refs):
    pieces, turned, dose, scaled = refs[:-3], refs[-3], refs[-2], refs[-1]
    scale_weights(pieces, scaled)
    rows = dose.shape[0]
    unroll = 4 if rows % 4 == 0 else 1

    def some_rows(t, carry):
        for u in range(unroll):
            b = t * unroll + u
            left = jnp.concatenate([scaled[index[b, k]] for k in range(slots)], axis=1)
            right = turned[pl.ds(b * slots, slots)]
            right = right.reshape(slots * right.shape[1], right.shape[2])
            dose[b] = jnp.dot(left, right, preferred_element_type=F32)
        return carry

    lax.fori_loop(0, rows // unroll, some_rows, 0)


def work_of(rows, slots, weightings, width):
    return pl.CostEstimate(
        flops=2 * rows * slots * weightings * width * width,
        bytes_accessed=2 * rows * slots * width * width,
        transcendentals=0,
    )


def forward(index, pieces, turned):
    columns = sum(p.shape[0] for p in pieces)
    weightings, width = pieces[0].shape[1:]
    rows, slots = index.shape
    return pl.pallas_call(
        functools.partial(forward_kernel, slots),
        in_specs=[in_smem()] + [in_vmem()] * (len(pieces) + 1),
        out_specs=in_vmem(),
        out_shape=jax.ShapeDtypeStruct((rows, weightings, width), F32),
        scratch_shapes=[pltpu.VMEM((3 * columns + 1, weightings, width), BF16)],
        compiler_params=PARAMS,
        cost_estimate=work_of(rows, slots, weightings, width),
        name="forward",
    )(index, *pieces, held(turned))


def first_forward(runs, me, index_others, index_mine, pieces, kept_others, tiles):
    columns = sum(p.shape[0] for p in pieces)
    weightings, width = pieces[0].shape[1:]
    rows, slots = index_mine.shape
    part = jax.ShapeDtypeStruct((rows, weightings, width), F32)
    return pl.pallas_call(
        functools.partial(first_forward_kernel, slots, runs),
        in_specs=[in_smem()] * 3
        + [in_vmem()] * (len(pieces) + 1)
        + [pl.BlockSpec(memory_space=pltpu.HBM)],
        out_specs=[in_vmem()] * 3,
        out_shape=[part, part, pltpu.VMEM((rows * slots, width, width), BF16)],
        scratch_shapes=[
            pltpu.VMEM((3 * columns + 1, weightings, width), BF16),
            pltpu.SemaphoreType.DMA((rows,)),
        ],
        compiler_params=PARAMS,
        cost_estimate=work_of(2 * rows, slots, weightings, width),
        name="first_forward",
    )(
        me,
        index_others,
        index_mine,
        *pieces,
        held(kept_others),
        pltpu.with_memory_space_constraint(tiles, pltpu.HBM),
    )


def backward_kernel(slots, mine, index, factor, slope, kept, *refs):
    *before, total = refs
    total[...] = jnp.zeros_like(total) if mine else before.pop(0)[...]
    width = kept.shape[-1]
    group = 12 if slots % 12 == 0 else 1
    rows = slope.shape[0]
    unroll = 4 if rows % 4 == 0 else 1

    def some_rows(t, carry):
        for u in range(unroll):
            b = t * unroll + u
            left = slope[b]
            for k0 in range(0, slots, group):
                right = jnp.concatenate([kept[b * slots + k0 + k] for k in range(group)], axis=1)
                product = jnp.dot(left, right, preferred_element_type=F32)
                columns = [index[b, k0 + k] for k in range(group)]
                old = [total[c] for c in columns]
                for k in range(group):
                    part = product[:, k * width : (k + 1) * width]
                    total[columns[k]] = old[k] + part * factor[b, k0 + k]
        return carry

    lax.fori_loop(0, rows // unroll, some_rows, 0)
    if mine:
        before[0][...] = total[...]
    else:
        far, near = before
        half = near.shape[0]
        near[...] = total[:half]
        far[...] = total[half:]


def backward(mine, index, factor, slope, kept, columns, *total):
    half_rows, weightings, width = slope.shape
    slots = index.shape[1]
    out = [(columns, weightings, width)] if mine else [(columns // 2, weightings, width)] * 2
    return pl.pallas_call(
        functools.partial(backward_kernel, slots, mine),
        in_specs=[in_smem()] * 2 + [in_vmem()] * (2 + len(total)),
        out_specs=[in_vmem()] * len(out),
        out_shape=[jax.ShapeDtypeStruct(shape, F32) for shape in out],
        scratch_shapes=[pltpu.VMEM((columns, weightings, width), F32)],
        compiler_params=PARAMS,
        cost_estimate=work_of(half_rows, slots, weightings, width),
        name="backward",
    )(index, factor, slope, held(kept), *total)


def per_device(
    sizes,
    dose_blocks,
    block_cols,
    block_exps,
    live_counts,
    labels,
    upper_dose,
    upper_weight,
    lower_dose,
    lower_weight,
    initial_spot_weights,
):
    n_vox, n_spot = sizes
    z, x, core = (lax.axis_index(a) for a in ("vox", "spot", "rep"))
    rows, _, slots, width, _ = dose_blocks.shape
    weightings, _, chunk_spots = initial_spot_weights.shape
    chunk = chunk_spots // width
    columns = chunk * n_vox
    own = chunk // 2
    initial = initial_spot_weights[:, 0].reshape(weightings, chunk, width)
    weights = lax.dynamic_slice_in_dim(initial, core * own, own, 1).transpose(1, 0, 2)

    def over_vox(arrays):
        return [
            lax.ppermute(a, "vox", [(i, i ^ d) for i in range(n_vox)])
            for d, a in enumerate(arrays, 1)
        ]

    def over_rep(array):
        return lax.ppermute(array, "rep", [(0, 1), (1, 0)])

    me = jnp.stack([z, core, x]).astype(jnp.int32)
    level_table = jnp.stack([upper_dose, upper_weight, lower_dose, lower_weight])
    known = labels.astype(F32).reshape(-1, width)
    tiles = dose_blocks.reshape(rows * slots, width, width)

    def gather_weights(weights):
        piece = weights.astype(BF16)
        return [piece] + over_vox([piece] * (n_vox - 1))

    bits = [1 << i for i in range(n_spot.bit_length() - 1)]
    *tables, sides = indices(
        n_vox,
        columns,
        n_spot,
        [(1, 1)] + [(2, bit) for bit in bits],
        me,
        block_cols,
        block_exps,
        live_counts.reshape(rows),
    )
    mine, others = tables[:3], tables[3:]
    pieces = gather_weights(weights)
    kept_others = load_others(rows, n_spot, me, tiles, sides)
    pieces, kept_others = lax.optimization_barrier((pieces, kept_others))

    for step in range(ITERS):
        near = jnp.concatenate(pieces, axis=0)
        weight_halves = [near, over_rep(near)]
        if step == 0:
            given, dose, kept_mine = first_forward(
                n_spot, me, others[0], mine[0], weight_halves, kept_others, tiles
            )
        else:
            given = forward(others[0], weight_halves, turned_others)
            dose = forward(mine[0], weight_halves, turned_mine)
        dose = dose + over_rep(given)
        for e, bit in enumerate(bits, 1):
            sent = dose
            if step == 0:
                n = known.shape[0]
                tile = jnp.pad(known, ((0, weightings - n), (0, 0)))
                sent = jnp.concatenate([dose, tile[None]], axis=0)
            got = lax.ppermute(sent, "spot", [(i, i ^ bit) for i in range(n_spot)])
            if step == 0:
                theirs = got[rows // 2, :n]
                first = sides[e, :1] > 0
                known = jnp.concatenate(
                    [jnp.where(first, known, theirs), jnp.where(first, theirs, known)]
                )
                got = got[: rows // 2]
            dose = dose + got
        if step == 0:
            levels = jnp.zeros((4, rows // 2, 1, width), F32)
            for c in range(level_table.shape[1]):
                value = level_table[:, c][:, None, None, None]
                levels = jnp.where(known[None, :, None, :] == c, value, levels)
        slope = (
            levels[1] * jax.nn.sigmoid(4.0 * (dose - levels[0]))
            - levels[3] * jax.nn.sigmoid(4.0 * (levels[2] - dose))
        ).astype(BF16)
        (total,) = backward(True, *mine[1:], slope, kept_mine, columns)
        far, near = backward(False, *others[1:], over_rep(slope), kept_others, columns, total)
        near = near + over_rep(far)
        received = over_vox([near[d * own : (d + 1) * own] for d in range(1, n_vox)])
        if step == 0:
            turned = [turn(kept_others, near), turn(kept_mine, near)]
            received, turned = lax.optimization_barrier((received, turned))
            turned_others, turned_mine = turned
        gradient = near[:own]
        for part in received:
            gradient = gradient + part
        weights = jnp.maximum(weights - 0.5 * gradient, 0.0)
        if step < ITERS - 1:
            pieces = gather_weights(weights)

    mine = jnp.stack([weights, gradient])
    other = over_rep(mine)
    first = sides[0, :1] > 0
    both = jnp.concatenate(
        [jnp.where(first, mine, other), jnp.where(first, other, mine)], axis=1
    )
    both = both.transpose(0, 2, 1, 3).reshape(2, weightings, 1, chunk_spots)
    return both[0], both[1]


def solution(mesh):
    placed = (
        P(("groups", "vox"), "spot", "rep", None, None),
        P(("groups", "vox"), "spot", "rep"),
        P(("groups", "vox"), "spot", "rep"),
        P(("groups", "vox"), "spot"),
        P(("groups", "vox", "spot", "rep")),
        P("groups"),
        P("groups"),
        P("groups"),
        P("groups"),
        P("groups", "spot", "vox"),
    )
    sizes = tuple(mesh.shape[a] for a in ("vox", "spot"))
    return jax.shard_map(
        functools.partial(per_device, sizes),
        mesh=mesh,
        in_specs=placed,
        out_specs=(P("groups", "spot", "vox"), P("groups", "spot", "vox")),
        check_vma=False,
    )
```

time: 168 us -> 144 us (0.86)
  local copies, waits for them, and re-layouts: 23.1 us -> 3.4 us
  waiting for transfers between devices: 68.8 us -> 52.3 us
  Pallas kernels: 32 us -> 41.7 us
  starting transfers between devices: 41.4 us -> 44.4 us
    unnamed x32 -> x18, local copies, waits for them, and re-layouts: 21.3 us -> 1.62 us
    pallas_call x5 -> x13, Pallas kernels: 20.6 us -> 30.9 us  [the longest x8 14.8 us: backward(): pl.pallas_call(functools.partial(backward_kernel, slots, mine), in_specs=...]
    ppermute x8 -> x4, waiting for transfers between devices: 20.9 us -> 11 us  [per_device(): got = lax.ppermute(sent, 'spot', [(i, i ^ bit) for i in range(n_spot)])]
    ppermute x24, waiting for transfers between devices: 36.5 us -> 28.9 us  [over_vox(): lax.ppermute(a, 'vox', [(i, i ^ d) for i in range(n_vox)])]
    ppermute x9 -> x17, starting transfers between devices: 0.65 us -> 3.73 us  [over_rep(): return lax.ppermute(array, 'rep', [(0, 1), (1, 0)])]
    ppermute x9 -> x17, waiting for transfers between devices: 11.4 us -> 12.4 us  [over_rep(): return lax.ppermute(array, 'rep', [(0, 1), (1, 0)])]
    ppermute x8 -> x4, starting transfers between devices: 7.39 us -> 6.43 us  [per_device(): got = lax.ppermute(sent, 'spot', [(i, i ^ bit) for i in range(n_spot)])]
    pallas_call x4 -> x6, Pallas kernels: 11.5 us -> 10.8 us  [forward(): pl.pallas_call(functools.partial(forward_kernel, slots), in_specs=[in_sme...]
  transfers between devices with their start and end apart: 41 -> 45, of which waited for: 36 -> 30; matrix products, arithmetic and copies ran while one was open for 1% -> 0% of each run, Pallas kernels for 5% -> 16%
where the time goes in v5:
time: 144 us
  waiting for transfers between devices  52.3 us (36%)
  starting transfers between devices  44.4 us (31%)
  Pallas kernels  41.7 us (29%)
  local copies, waits for them, and re-layouts  3.4 us (2%)
    ppermute x24, starting transfers between devices, over_vox(): lax.ppermute(a, 'vox', [(i, i ^ d) for i in range(n_vox)])  34.3 us
    ppermute x24, waiting for transfers between devices, over_vox(): lax.ppermute(a, 'vox', [(i, i ^ d) for i in range(n_vox)])  28.9 us
    pallas_call x8, Pallas kernels, backward(): pl.pallas_call(functools.partial(backward_kernel, slots, mine), in_specs=...  14.8 us
    ppermute x17, waiting for transfers between devices, over_rep(): return lax.ppermute(array, 'rep', [(0, 1), (1, 0)])  12.4 us
    ppermute x4, waiting for transfers between devices, per_device(): got = lax.ppermute(sent, 'spot', [(i, i ^ bit) for i in range(n_spot)])  11 us
    pallas_call x6, Pallas kernels, forward(): pl.pallas_call(functools.partial(forward_kernel, slots), in_specs=[in_sme...  10.8 us
    ppermute x4, starting transfers between devices, per_device(): got = lax.ppermute(sent, 'spot', [(i, i ^ bit) for i in range(n_spot)])  6.43 us
    pallas_call x1, Pallas kernels, first_forward(): pl.pallas_call(functools.partial(first_forward_kernel, slots, runs), in_s...  6.04 us
  transfers between devices with their start and end apart: 45, of which 30 were waited for; matrix products, arithmetic and copies ran while one was open for 0% of the time, Pallas kernels for 16%

profile of v5, /device:TPU:0, one launch (start us, length us, event | category | flops | bytes accessed | tf_op | source)
XLA Modules:
  0.0 143.9 jit_solution(12594674490754440236)
XLA Ops:
  1.6 5.1 %collective-permute-start.2 = (bf16[8,16,128]{2,1,0:T(8,128)(2,1)S(1)}, bf16[8,16,128]{2,1,0:T(8,128)(2,1)S(1)}, u32[]{:S(2)}, u32[]{:S(2)}) collective-permute-start(bf16[8,16,128]{2,1,0:T(8,128)(2,1)S(1)} %bitcast.57), channel_id=1, source_target_pairs={{0,12},{4,8},{8,4},{12,0},{1,13},{5,9},{9,5},{13,1},{2,14},{6,10},... | collective-permute-start | bytes 98312 | tf_op jit(solution)/shard_map/ppermute | solution.py:311
  8.9 3.4 %load_others.1.refs_2_.kept = bf16[192,128,128]{2,1,0:T(8,128)(2,1)S(1)} custom-call(s32[3]{0:T(128)S(1)} %pad_add_fusion.me, bf16[384,128,128]{2,1,0:T(8,128)(2,1)} %bitcast.53, f32[2,8,128]{2,1,0:T(8,128)S(1)} %get-tuple-element.30.after), custom_call_target="tpu_custom_call" | custom-call | bytes 12582912 | tf_op jit(solution)/shard_map/load_others/pallas_call | solution.py:133
  13.8 6.0 %first_forward.1 = (f32[8,16,128]{2,1,0:T(8,128)S(1)}, f32[8,16,128]{2,1,0:T(8,128)S(1)}, bf16[192,128,128]{2,1,0:T(8,128)(2,1)S(1)}) custom-call(s32[3]{0:T(128)S(1)} %pad_add_fusion.me, s32[8,24]{1,0:T(8,128)S(1)} %get-tuple-element.33.index_others.index, s32[8,24]{1,0:T(8,128)S(1)} %get-tuple-element.34.index_mine.index, ...), custom_call_target="tpu_custom_call" | custom-call | flops 201326592 | bytes 12582912 | tf_op jit(solution)/shard_map/first_forward/pallas_call | solution.py:214
  23.2 2.4 %collective-permute-done.5 = f32[9,16,128]{2,1,0:T(8,128)S(1)} collective-permute-done((f32[9,16,128]{2,1,0:T(8,128)S(1)}, f32[9,16,128]{2,1,0:T(8,128)S(1)}, u32[]{:S(2)}, u32[]{:S(2)}) %collective-permute-start.5) | collective-permute-done | bytes 73760 | tf_op jit(solution)/shard_map/ppermute | solution.py:360
  25.9 2.0 %backward.8.refs_0_ = f32[64,16,128]{2,1,0:T(8,128)S(1)} custom-call(s32[8,24]{1,0:T(8,128)S(1)} %get-tuple-element.42.index, f32[8,24]{1,0:T(8,128)S(1)} %get-tuple-element.43.factor, bf16[8,16,128]{2,1,0:T(8,128)(2,1)S(1)} %subtract_convert_fusion.3.slope, bf16[192,128,128]{2,1,0:T(8,128)(2,1)S(1)} %get-tuple-element.44.kept), custom_call_target="tpu_custom_call" | custom-call | flops 100663296 | bytes 6291456 | tf_op jit(solution)/shard_map/backward/pallas_call | solution.py:274
  27.9 1.8 %backward.9 = (f32[32,16,128]{2,1,0:T(8,128)S(1)}, f32[32,16,128]{2,1,0:T(8,128)S(1)}) custom-call(s32[8,24]{1,0:T(8,128)S(1)} %get-tuple-element.31.index, f32[8,24]{1,0:T(8,128)S(1)} %get-tuple-element.32.factor, bf16[8,16,128]{2,1,0:T(8,128)(2,1)S(1)} %collective-permute-done.6.slope, bf16[192,128,128]{2,1,0:T(8,128)(2,1)S(1)} %load_others.1.refs_2_.kept, ...), custom_call_target="tpu_custom_call" | custom-call | flops 100663296 | bytes 6291456 | tf_op jit(solution)/shard_map/backward/pallas_call | solution.py:274
  31.6 3.8 %collective-permute-start.10 = (f32[8,16,128]{2,1,0:T(8,128)S(1)}, f32[8,16,128]{2,1,0:T(8,128)S(1)}, u32[]{:S(2)}, u32[]{:S(2)}) collective-permute-start(f32[8,16,128]{2,1,0:T(8,128)S(1)} %get-tuple-element.87), channel_id=1, source_target_pairs={{0,12},{4,8},{8,4},{12,0},{1,13},{5,9},{9,5},{13,1},{2,14},{6,10},... | collective-permute-start | bytes 196616 | tf_op jit(solution)/shard_map/ppermute | solution.py:311
  36.0 2.9 %turn.3.refs_2_ = bf16[192,128,128]{2,1,0:T(8,128)(2,1)S(1)} custom-call(bf16[192,128,128]{2,1,0:T(8,128)(2,1)S(1)} %get-tuple-element.44.kept, f32[32,16,128]{2,1,0:T(8,128)S(1)} %add.106.after), custom_call_target="tpu_custom_call" | custom-call | bytes 12582912 | tf_op jit(solution)/shard_map/turn/pallas_call | solution.py:85
  39.0 2.9 %turn.2.refs_2_ = bf16[192,128,128]{2,1,0:T(8,128)(2,1)S(1)} custom-call(bf16[192,128,128]{2,1,0:T(8,128)(2,1)S(1)} %load_others.1.refs_2_.kept, f32[32,16,128]{2,1,0:T(8,128)S(1)} %add.106.after), custom_call_target="tpu_custom_call" | custom-call | bytes 12582912 | tf_op jit(solution)/shard_map/turn/pallas_call | solution.py:85
  42.0 3.8 %collective-permute-start.13 = (bf16[8,16,128]{2,1,0:T(8,128)(2,1)S(1)}, bf16[8,16,128]{2,1,0:T(8,128)(2,1)S(1)}, u32[]{:S(2)}, u32[]{:S(2)}) collective-permute-start(bf16[8,16,128]{2,1,0:T(8,128)(2,1)S(1)} %get-tuple-element.72), channel_id=1, source_target_pairs={{0,12},{4,8},{8,4},{12,0},{1,13},{5,9},{9,5},{13,1},{2,14},{6,10},... | collective-permute-start | bytes 98312 | tf_op jit(solution)/shard_map/ppermute | solution.py:311
  48.2 2.5 %collective-permute-done.12 = bf16[8,16,128]{2,1,0:T(8,128)(2,1)S(1)} collective-permute-done((bf16[8,16,128]{2,1,0:T(8,128)(2,1)S(1)}, bf16[8,16,128]{2,1,0:T(8,128)(2,1)S(1)}, u32[]{:S(2)}, u32[]{:S(2)}) %collective-permute-start.12) | collective-permute-done | bytes 32800 | tf_op jit(solution)/shard_map/ppermute | solution.py:311
  54.1 1.8 %forward.6 = f32[8,16,128]{2,1,0:T(8,128)S(1)} custom-call(s32[8,24]{1,0:T(8,128)S(1)} %get-tuple-element.34.index_mine.index, bf16[32,16,128]{2,1,0:T(8,128)(2,1)S(1)} %pad_maximum_fusion.refs_0_, bf16[32,16,128]{2,1,0:T(8,128)(2,1)S(1)} %collective-permute-done.14.refs_1_, bf16[192,128,128]{2,1,0:T(8,128)(2,1)S(1)} %turn.3.refs_2_), custom_call_target="tpu_custom_call" | custom-call | flops 100663296 | bytes 6291456 | tf_op jit(solution)/shard_map/forward/pallas_call | solution.py:197
  57.5 2.9 %collective-permute-done.16 = f32[8,16,128]{2,1,0:T(8,128)S(1)} collective-permute-done((f32[8,16,128]{2,1,0:T(8,128)S(1)}, f32[8,16,128]{2,1,0:T(8,128)S(1)}, u32[]{:S(2)}, u32[]{:S(2)}) %collective-permute-start.16) | collective-permute-done | bytes 65568 | tf_op jit(solution)/shard_map/ppermute | solution.py:360
  60.5 1.8 %backward.10.refs_0_ = f32[64,16,128]{2,1,0:T(8,128)S(1)} custom-call(s32[8,24]{1,0:T(8,128)S(1)} %get-tuple-element.42.index, f32[8,24]{1,0:T(8,128)S(1)} %get-tuple-element.43.factor, bf16[8,16,128]{2,1,0:T(8,128)(2,1)S(1)} %subtract_convert_fusion.2.slope, bf16[192,128,128]{2,1,0:T(8,128)(2,1)S(1)} %get-tuple-element.44.kept), custom_call_target="tpu_custom_call" | custom-call | flops 100663296 | bytes 6291456 | tf_op jit(solution)/shard_map/backward/pallas_call | solution.py:274
  62.3 1.8 %backward.11 = (f32[32,16,128]{2,1,0:T(8,128)S(1)}, f32[32,16,128]{2,1,0:T(8,128)S(1)}) custom-call(s32[8,24]{1,0:T(8,128)S(1)} %get-tuple-element.31.index, f32[8,24]{1,0:T(8,128)S(1)} %get-tuple-element.32.factor, bf16[8,16,128]{2,1,0:T(8,128)(2,1)S(1)} %collective-permute-done.17.slope, bf16[192,128,128]{2,1,0:T(8,128)(2,1)S(1)} %load_others.1.refs_2_.kept, ...), custom_call_target="tpu_custom_call" | custom-call | flops 100663296 | bytes 6291456 | tf_op jit(solution)/shard_map/backward/pallas_call | solution.py:274
  66.0 3.5 %collective-permute-start.21 = (f32[8,16,128]{2,1,0:T(8,128)S(1)}, f32[8,16,128]{2,1,0:T(8,128)S(1)}, u32[]{:S(2)}, u32[]{:S(2)}) collective-permute-start(f32[8,16,128]{2,1,0:T(8,128)S(1)} %get-tuple-element.85), channel_id=1, source_target_pairs={{0,12},{4,8},{8,4},{12,0},{1,13},{5,9},{9,5},{13,1},{2,14},{6,10},... | collective-permute-start | bytes 196616 | tf_op jit(solution)/shard_map/ppermute | solution.py:311
  70.4 3.5 %collective-permute-done.21 = f32[8,16,128]{2,1,0:T(8,128)S(1)} collective-permute-done((f32[8,16,128]{2,1,0:T(8,128)S(1)}, f32[8,16,128]{2,1,0:T(8,128)S(1)}, u32[]{:S(2)}, u32[]{:S(2)}) %collective-permute-start.21) | collective-permute-done | bytes 65568 | tf_op jit(solution)/shard_map/ppermute | solution.py:311
  73.9 2.2 %collective-permute-done.20 = f32[8,16,128]{2,1,0:T(8,128)S(1)} collective-permute-done((f32[8,16,128]{2,1,0:T(8,128)S(1)}, f32[8,16,128]{2,1,0:T(8,128)S(1)}, u32[]{:S(2)}, u32[]{:S(2)}) %collective-permute-start.20) | collective-permute-done | bytes 65568 | tf_op jit(solution)/shard_map/ppermute | solution.py:311
  77.8 2.7 %collective-permute-start.22 = (bf16[8,16,128]{2,1,0:T(8,128)(2,1)S(1)}, bf16[8,16,128]{2,1,0:T(8,128)(2,1)S(1)}, u32[]{:S(2)}, u32[]{:S(2)}) collective-permute-start(bf16[8,16,128]{2,1,0:T(8,128)(2,1)S(1)} %get-tuple-element.70), channel_id=1, source_target_pairs={{0,4},{4,0},{8,12},{12,8},{1,5},{5,1},{9,13},{13,9},{2,6},{6,2},{1... | collective-permute-start | bytes 98312 | tf_op jit(solution)/shard_map/ppermute | solution.py:311
  86.2 1.8 %forward.8 = f32[8,16,128]{2,1,0:T(8,128)S(1)} custom-call(s32[8,24]{1,0:T(8,128)S(1)} %get-tuple-element.34.index_mine.index, bf16[32,16,128]{2,1,0:T(8,128)(2,1)S(1)} %pad_maximum_fusion.1.refs_0_, bf16[32,16,128]{2,1,0:T(8,128)(2,1)S(1)} %collective-permute-done.25.refs_1_, bf16[192,128,128]{2,1,0:T(8,128)(2,1)S(1)} %turn.3.refs_2_), custom_call_target="tpu_custom_call" | custom-call | flops 100663296 | bytes 6291456 | tf_op jit(solution)/shard_map/forward/pallas_call | solution.py:197
  89.7 2.8 %collective-permute-done.27 = f32[8,16,128]{2,1,0:T(8,128)S(1)} collective-permute-done((f32[8,16,128]{2,1,0:T(8,128)S(1)}, f32[8,16,128]{2,1,0:T(8,128)S(1)}, u32[]{:S(2)}, u32[]{:S(2)}) %collective-permute-start.27) | collective-permute-done | bytes 65568 | tf_op jit(solution)/shard_map/ppermute | solution.py:360
  92.6 1.8 %backward.12.refs_0_ = f32[64,16,128]{2,1,0:T(8,128)S(1)} custom-call(s32[8,24]{1,0:T(8,128)S(1)} %get-tuple-element.42.index, f32[8,24]{1,0:T(8,128)S(1)} %get-tuple-element.43.factor, bf16[8,16,128]{2,1,0:T(8,128)(2,1)S(1)} %subtract_convert_fusion.1.slope, bf16[192,128,128]{2,1,0:T(8,128)(2,1)S(1)} %get-tuple-element.44.kept), custom_call_target="tpu_custom_call" | custom-call | flops 100663296 | bytes 6291456 | tf_op jit(solution)/shard_map/backward/pallas_call | solution.py:274
  94.5 1.8 %backward.13 = (f32[32,16,128]{2,1,0:T(8,128)S(1)}, f32[32,16,128]{2,1,0:T(8,128)S(1)}) custom-call(s32[8,24]{1,0:T(8,128)S(1)} %get-tuple-element.31.index, f32[8,24]{1,0:T(8,128)S(1)} %get-tuple-element.32.factor, bf16[8,16,128]{2,1,0:T(8,128)(2,1)S(1)} %collective-permute-done.28.slope, bf16[192,128,128]{2,1,0:T(8,128)(2,1)S(1)} %load_others.1.refs_2_.kept, ...), custom_call_target="tpu_custom_call" | custom-call | flops 100663296 | bytes 6291456 | tf_op jit(solution)/shard_map/backward/pallas_call | solution.py:274
  102.5 3.9 %collective-permute-done.32 = f32[8,16,128]{2,1,0:T(8,128)S(1)} collective-permute-done((f32[8,16,128]{2,1,0:T(8,128)S(1)}, f32[8,16,128]{2,1,0:T(8,128)S(1)}, u32[]{:S(2)}, u32[]{:S(2)}) %collective-permute-start.32) | collective-permute-done | bytes 65568 | tf_op jit(solution)/shard_map/ppermute | solution.py:311
  106.5 2.0 %collective-permute-done.31 = f32[8,16,128]{2,1,0:T(8,128)S(1)} collective-permute-done((f32[8,16,128]{2,1,0:T(8,128)S(1)}, f32[8,16,128]{2,1,0:T(8,128)S(1)}, u32[]{:S(2)}, u32[]{:S(2)}) %collective-permute-start.31) | collective-permute-done | bytes 65568 | tf_op jit(solution)/shard_map/ppermute | solution.py:311
  110.3 2.7 %collective-permute-start.33 = (bf16[8,16,128]{2,1,0:T(8,128)(2,1)S(1)}, bf16[8,16,128]{2,1,0:T(8,128)(2,1)S(1)}, u32[]{:S(2)}, u32[]{:S(2)}) collective-permute-start(bf16[8,16,128]{2,1,0:T(8,128)(2,1)S(1)} %get-tuple-element.68), channel_id=1, source_target_pairs={{0,4},{4,0},{8,12},{12,8},{1,5},{5,1},{9,13},{13,9},{2,6},{6,2},{1... | collective-permute-start | bytes 98312 | tf_op jit(solution)/shard_map/ppermute | solution.py:311
  118.8 1.8 %forward.10 = f32[8,16,128]{2,1,0:T(8,128)S(1)} custom-call(s32[8,24]{1,0:T(8,128)S(1)} %get-tuple-element.34.index_mine.index, bf16[32,16,128]{2,1,0:T(8,128)(2,1)S(1)} %pad_maximum_fusion.2.refs_0_, bf16[32,16,128]{2,1,0:T(8,128)(2,1)S(1)} %collective-permute-done.36.refs_1_, bf16[192,128,128]{2,1,0:T(8,128)(2,1)S(1)} %turn.3.refs_2_), custom_call_target="tpu_custom_call" | custom-call | flops 100663296 | bytes 6291456 | tf_op jit(solution)/shard_map/forward/pallas_call | solution.py:197
  122.2 2.8 %collective-permute-done.38 = f32[8,16,128]{2,1,0:T(8,128)S(1)} collective-permute-done((f32[8,16,128]{2,1,0:T(8,128)S(1)}, f32[8,16,128]{2,1,0:T(8,128)S(1)}, u32[]{:S(2)}, u32[]{:S(2)}) %collective-permute-start.38) | collective-permute-done | bytes 65568 | tf_op jit(solution)/shard_map/ppermute | solution.py:360
  125.2 1.8 %backward.14.refs_0_ = f32[64,16,128]{2,1,0:T(8,128)S(1)} custom-call(s32[8,24]{1,0:T(8,128)S(1)} %get-tuple-element.42.index, f32[8,24]{1,0:T(8,128)S(1)} %get-tuple-element.43.factor, bf16[8,16,128]{2,1,0:T(8,128)(2,1)S(1)} %subtract_convert_fusion.slope, bf16[192,128,128]{2,1,0:T(8,128)(2,1)S(1)} %get-tuple-element.44.kept), custom_call_target="tpu_custom_call" | custom-call | flops 100663296 | bytes 6291456 | tf_op jit(solution)/shard_map/backward/pallas_call | solution.py:274
  127.0 1.8 %backward.15 = (f32[32,16,128]{2,1,0:T(8,128)S(1)}, f32[32,16,128]{2,1,0:T(8,128)S(1)}) custom-call(s32[8,24]{1,0:T(8,128)S(1)} %get-tuple-element.31.index, f32[8,24]{1,0:T(8,128)S(1)} %get-tuple-element.32.factor, bf16[8,16,128]{2,1,0:T(8,128)(2,1)S(1)} %collective-permute-done.39.slope, bf16[192,128,128]{2,1,0:T(8,128)(2,1)S(1)} %load_others.1.refs_2_.kept, ...), custom_call_target="tpu_custom_call" | custom-call | flops 100663296 | bytes 6291456 | tf_op jit(solution)/shard_map/backward/pallas_call | solution.py:274
  135.1 3.9 %collective-permute-done.43 = f32[8,16,128]{2,1,0:T(8,128)S(1)} collective-permute-done((f32[8,16,128]{2,1,0:T(8,128)S(1)}, f32[8,16,128]{2,1,0:T(8,128)S(1)}, u32[]{:S(2)}, u32[]{:S(2)}) %collective-permute-start.43) | collective-permute-done | bytes 65568 | tf_op jit(solution)/shard_map/ppermute | solution.py:311
  139.0 2.0 %collective-permute-done.42 = f32[8,16,128]{2,1,0:T(8,128)S(1)} collective-permute-done((f32[8,16,128]{2,1,0:T(8,128)S(1)}, f32[8,16,128]{2,1,0:T(8,128)S(1)}, u32[]{:S(2)}, u32[]{:S(2)}) %collective-permute-start.42) | collective-permute-done | bytes 65568 | tf_op jit(solution)/shard_map/ppermute | solution.py:311
  (137 shorter events, 54.6 us)
Async XLA Ops:
  1.6 10.7 %collective-permute-start.2 = (bf16[8,16,128]{2,1,0:T(8,128)(2,1)S(1)}, bf16[8,16,128]{2,1,0:T(8,128)(2,1)S(1)}, u32[]{:S(2)}, u32[]{:S(2)}) collective-permute-start(bf16[8,16,128]{2,1,0:T(8,128)(2,1)S(1)} %bitcast.57), channel_id=1, source_target_pairs={{0,12},{4,8},{8,4},{12,0},{1,13},{5,9},{9,5},{13,1},{2,14},{6,10},... | collective-permute-start | bytes 98312 | tf_op jit(solution)/shard_map/ppermute | solution.py:311
  6.7 5.6 %collective-permute-start.1 = (bf16[8,16,128]{2,1,0:T(8,128)(2,1)S(1)}, bf16[8,16,128]{2,1,0:T(8,128)(2,1)S(1)}, u32[]{:S(2)}, u32[]{:S(2)}) collective-permute-start(bf16[8,16,128]{2,1,0:T(8,128)(2,1)S(1)} %bitcast.58), channel_id=1, source_target_pairs={{0,8},{4,12},{8,0},{12,4},{1,9},{5,13},{9,1},{13,5},{2,10},{6,14},... | collective-permute-start | bytes 98312 | tf_op jit(solution)/shard_map/ppermute | solution.py:311
  6.7 5.7 %collective-permute-start = (bf16[8,16,128]{2,1,0:T(8,128)(2,1)S(1)}, bf16[8,16,128]{2,1,0:T(8,128)(2,1)S(1)}, u32[]{:S(2)}, u32[]{:S(2)}) collective-permute-start(bf16[8,16,128]{2,1,0:T(8,128)(2,1)S(1)} %bitcast.59), channel_id=1, source_target_pairs={{0,4},{4,0},{8,12},{12,8},{1,5},{5,1},{9,13},{13,9},{2,6},{6,2},{1... | collective-permute-start | bytes 98312 | tf_op jit(solution)/shard_map/ppermute | solution.py:311
  21.2 4.4 %collective-permute-start.5 = (f32[9,16,128]{2,1,0:T(8,128)S(1)}, f32[9,16,128]{2,1,0:T(8,128)S(1)}, u32[]{:S(2)}, u32[]{:S(2)}) collective-permute-start(f32[9,16,128]{2,1,0:T(8,128)S(1)} %pad_maximum_fusion.4), channel_id=1, source_target_pairs={{0,2},{2,0},{1,3},{3,1},{4,6},{6,4},{5,7},{7,5},{8,10},{10,8},{9,1... | collective-permute-start | bytes 221192 | tf_op jit(solution)/shard_map/ppermute | solution.py:360
  25.8 2.1 %collective-permute-start.6 = (bf16[8,16,128]{2,1,0:T(8,128)(2,1)S(1)}, bf16[8,16,128]{2,1,0:T(8,128)(2,1)S(1)}, u32[]{:S(2)}, u32[]{:S(2)}) collective-permute-start(bf16[8,16,128]{2,1,0:T(8,128)(2,1)S(1)} %subtract_convert_fusion.3.slope), channel_id=1, source_target_pairs={{0,1},{1,0},{2,3},{3,2},{4,5},{5,4},{6,7},{7,6},{8,9},{9,8},{10,11... | collective-permute-start | bytes 98312 | tf_op jit(solution)/shard_map/ppermute | solution.py:316
  31.6 10.4 %collective-permute-start.10 = (f32[8,16,128]{2,1,0:T(8,128)S(1)}, f32[8,16,128]{2,1,0:T(8,128)S(1)}, u32[]{:S(2)}, u32[]{:S(2)}) collective-permute-start(f32[8,16,128]{2,1,0:T(8,128)S(1)} %get-tuple-element.87), channel_id=1, source_target_pairs={{0,12},{4,8},{8,4},{12,0},{1,13},{5,9},{9,5},{13,1},{2,14},{6,10},... | collective-permute-start | bytes 196616 | tf_op jit(solution)/shard_map/ppermute | solution.py:311
  35.4 6.5 %collective-permute-start.9 = (f32[8,16,128]{2,1,0:T(8,128)S(1)}, f32[8,16,128]{2,1,0:T(8,128)S(1)}, u32[]{:S(2)}, u32[]{:S(2)}) collective-permute-start(f32[8,16,128]{2,1,0:T(8,128)S(1)} %get-tuple-element.88), channel_id=1, source_target_pairs={{0,8},{4,12},{8,0},{12,4},{1,9},{5,13},{9,1},{13,5},{2,10},{6,14},... | collective-permute-start | bytes 196616 | tf_op jit(solution)/shard_map/ppermute | solution.py:311
  35.4 6.5 %collective-permute-start.8 = (f32[8,16,128]{2,1,0:T(8,128)S(1)}, f32[8,16,128]{2,1,0:T(8,128)S(1)}, u32[]{:S(2)}, u32[]{:S(2)}) collective-permute-start(f32[8,16,128]{2,1,0:T(8,128)S(1)} %get-tuple-element.89), channel_id=1, source_target_pairs={{0,4},{4,0},{8,12},{12,8},{1,5},{5,1},{9,13},{13,9},{2,6},{6,2},{1... | collective-permute-start | bytes 196616 | tf_op jit(solution)/shard_map/ppermute | solution.py:311
  42.0 6.2 %collective-permute-start.13 = (bf16[8,16,128]{2,1,0:T(8,128)(2,1)S(1)}, bf16[8,16,128]{2,1,0:T(8,128)(2,1)S(1)}, u32[]{:S(2)}, u32[]{:S(2)}) collective-permute-start(bf16[8,16,128]{2,1,0:T(8,128)(2,1)S(1)} %get-tuple-element.72), channel_id=1, source_target_pairs={{0,12},{4,8},{8,4},{12,0},{1,13},{5,9},{9,5},{13,1},{2,14},{6,10},... | collective-permute-start | bytes 98312 | tf_op jit(solution)/shard_map/ppermute | solution.py:311
  45.8 4.8 %collective-permute-start.12 = (bf16[8,16,128]{2,1,0:T(8,128)(2,1)S(1)}, bf16[8,16,128]{2,1,0:T(8,128)(2,1)S(1)}, u32[]{:S(2)}, u32[]{:S(2)}) collective-permute-start(bf16[8,16,128]{2,1,0:T(8,128)(2,1)S(1)} %get-tuple-element.72), channel_id=1, source_target_pairs={{0,8},{4,12},{8,0},{12,4},{1,9},{5,13},{9,1},{13,5},{2,10},{6,14},... | collective-permute-start | bytes 98312 | tf_op jit(solution)/shard_map/ppermute | solution.py:311
  45.8 4.8 %collective-permute-start.11 = (bf16[8,16,128]{2,1,0:T(8,128)(2,1)S(1)}, bf16[8,16,128]{2,1,0:T(8,128)(2,1)S(1)}, u32[]{:S(2)}, u32[]{:S(2)}) collective-permute-start(bf16[8,16,128]{2,1,0:T(8,128)(2,1)S(1)} %get-tuple-element.72), channel_id=1, source_target_pairs={{0,4},{4,0},{8,12},{12,8},{1,5},{5,1},{9,13},{13,9},{2,6},{6,2},{1... | collective-permute-start | bytes 98312 | tf_op jit(solution)/shard_map/ppermute | solution.py:311
  53.8 2.0 %collective-permute-start.15 = (f32[8,16,128]{2,1,0:T(8,128)S(1)}, f32[8,16,128]{2,1,0:T(8,128)S(1)}, u32[]{:S(2)}, u32[]{:S(2)}) collective-permute-start(f32[8,16,128]{2,1,0:T(8,128)S(1)} %forward.7), channel_id=1, source_target_pairs={{0,1},{1,0},{2,3},{3,2},{4,5},{5,4},{6,7},{7,6},{8,9},{9,8},{10,11... | collective-permute-start | bytes 196616 | tf_op jit(solution)/shard_map/ppermute | solution.py:316
  55.9 4.4 %collective-permute-start.16 = (f32[8,16,128]{2,1,0:T(8,128)S(1)}, f32[8,16,128]{2,1,0:T(8,128)S(1)}, u32[]{:S(2)}, u32[]{:S(2)}) collective-permute-start(f32[8,16,128]{2,1,0:T(8,128)S(1)} %add.110), channel_id=1, source_target_pairs={{0,2},{2,0},{1,3},{3,1},{4,6},{6,4},{5,7},{7,5},{8,10},{10,8},{9,1... | collective-permute-start | bytes 196616 | tf_op jit(solution)/shard_map/ppermute | solution.py:360
  65.9 4.4 %collective-permute-start.19 = (f32[8,16,128]{2,1,0:T(8,128)S(1)}, f32[8,16,128]{2,1,0:T(8,128)S(1)}, u32[]{:S(2)}, u32[]{:S(2)}) collective-permute-start(f32[8,16,128]{2,1,0:T(8,128)S(1)} %get-tuple-element.84), channel_id=1, source_target_pairs={{0,4},{4,0},{8,12},{12,8},{1,5},{5,1},{9,13},{13,9},{2,6},{6,2},{1... | collective-permute-start | bytes 196616 | tf_op jit(solution)/shard_map/ppermute | solution.py:311
  66.0 7.9 %collective-permute-start.21 = (f32[8,16,128]{2,1,0:T(8,128)S(1)}, f32[8,16,128]{2,1,0:T(8,128)S(1)}, u32[]{:S(2)}, u32[]{:S(2)}) collective-permute-start(f32[8,16,128]{2,1,0:T(8,128)S(1)} %get-tuple-element.85), channel_id=1, source_target_pairs={{0,12},{4,8},{8,4},{12,0},{1,13},{5,9},{9,5},{13,1},{2,14},{6,10},... | collective-permute-start | bytes 196616 | tf_op jit(solution)/shard_map/ppermute | solution.py:311
  69.5 6.5 %collective-permute-start.20 = (f32[8,16,128]{2,1,0:T(8,128)S(1)}, f32[8,16,128]{2,1,0:T(8,128)S(1)}, u32[]{:S(2)}, u32[]{:S(2)}) collective-permute-start(f32[8,16,128]{2,1,0:T(8,128)S(1)} %get-tuple-element.86), channel_id=1, source_target_pairs={{0,8},{4,12},{8,0},{12,4},{1,9},{5,13},{9,1},{13,5},{2,10},{6,14},... | collective-permute-start | bytes 196616 | tf_op jit(solution)/shard_map/ppermute | solution.py:311
  76.1 5.9 %collective-permute-start.24 = (bf16[8,16,128]{2,1,0:T(8,128)(2,1)S(1)}, bf16[8,16,128]{2,1,0:T(8,128)(2,1)S(1)}, u32[]{:S(2)}, u32[]{:S(2)}) collective-permute-start(bf16[8,16,128]{2,1,0:T(8,128)(2,1)S(1)} %get-tuple-element.70), channel_id=1, source_target_pairs={{0,12},{4,8},{8,4},{12,0},{1,13},{5,9},{9,5},{13,1},{2,14},{6,10},... | collective-permute-start | bytes 98312 | tf_op jit(solution)/shard_map/ppermute | solution.py:311
  77.8 5.0 %collective-permute-start.23 = (bf16[8,16,128]{2,1,0:T(8,128)(2,1)S(1)}, bf16[8,16,128]{2,1,0:T(8,128)(2,1)S(1)}, u32[]{:S(2)}, u32[]{:S(2)}) collective-permute-start(bf16[8,16,128]{2,1,0:T(8,128)(2,1)S(1)} %get-tuple-element.70), channel_id=1, source_target_pairs={{0,8},{4,12},{8,0},{12,4},{1,9},{5,13},{9,1},{13,5},{2,10},{6,14},... | collective-permute-start | bytes 98312 | tf_op jit(solution)/shard_map/ppermute | solution.py:311
  77.8 5.0 %collective-permute-start.22 = (bf16[8,16,128]{2,1,0:T(8,128)(2,1)S(1)}, bf16[8,16,128]{2,1,0:T(8,128)(2,1)S(1)}, u32[]{:S(2)}, u32[]{:S(2)}) collective-permute-start(bf16[8,16,128]{2,1,0:T(8,128)(2,1)S(1)} %get-tuple-element.70), channel_id=1, source_target_pairs={{0,4},{4,0},{8,12},{12,8},{1,5},{5,1},{9,13},{13,9},{2,6},{6,2},{1... | collective-permute-start | bytes 98312 | tf_op jit(solution)/shard_map/ppermute | solution.py:311
  86.0 2.0 %collective-permute-start.26 = (f32[8,16,128]{2,1,0:T(8,128)S(1)}, f32[8,16,128]{2,1,0:T(8,128)S(1)}, u32[]{:S(2)}, u32[]{:S(2)}) collective-permute-start(f32[8,16,128]{2,1,0:T(8,128)S(1)} %forward.9), channel_id=1, source_target_pairs={{0,1},{1,0},{2,3},{3,2},{4,5},{5,4},{6,7},{7,6},{8,9},{9,8},{10,11... | collective-permute-start | bytes 196616 | tf_op jit(solution)/shard_map/ppermute | solution.py:316
  88.1 4.4 %collective-permute-start.27 = (f32[8,16,128]{2,1,0:T(8,128)S(1)}, f32[8,16,128]{2,1,0:T(8,128)S(1)}, u32[]{:S(2)}, u32[]{:S(2)}) collective-permute-start(f32[8,16,128]{2,1,0:T(8,128)S(1)} %add.118), channel_id=1, source_target_pairs={{0,2},{2,0},{1,3},{3,1},{4,6},{6,4},{5,7},{7,5},{8,10},{10,8},{9,1... | collective-permute-start | bytes 196616 | tf_op jit(solution)/shard_map/ppermute | solution.py:360
  98.1 4.4 %collective-permute-start.30 = (f32[8,16,128]{2,1,0:T(8,128)S(1)}, f32[8,16,128]{2,1,0:T(8,128)S(1)}, u32[]{:S(2)}, u32[]{:S(2)}) collective-permute-start(f32[8,16,128]{2,1,0:T(8,128)S(1)} %get-tuple-element.81), channel_id=1, source_target_pairs={{0,4},{4,0},{8,12},{12,8},{1,5},{5,1},{9,13},{13,9},{2,6},{6,2},{1... | collective-permute-start | bytes 196616 | tf_op jit(solution)/shard_map/ppermute | solution.py:311
  99.8 6.7 %collective-permute-start.32 = (f32[8,16,128]{2,1,0:T(8,128)S(1)}, f32[8,16,128]{2,1,0:T(8,128)S(1)}, u32[]{:S(2)}, u32[]{:S(2)}) collective-permute-start(f32[8,16,128]{2,1,0:T(8,128)S(1)} %get-tuple-element.82), channel_id=1, source_target_pairs={{0,12},{4,8},{8,4},{12,0},{1,13},{5,9},{9,5},{13,1},{2,14},{6,10},... | collective-permute-start | bytes 196616 | tf_op jit(solution)/shard_map/ppermute | solution.py:311
  101.5 7.0 %collective-permute-start.31 = (f32[8,16,128]{2,1,0:T(8,128)S(1)}, f32[8,16,128]{2,1,0:T(8,128)S(1)}, u32[]{:S(2)}, u32[]{:S(2)}) collective-permute-start(f32[8,16,128]{2,1,0:T(8,128)S(1)} %get-tuple-element.83), channel_id=1, source_target_pairs={{0,8},{4,12},{8,0},{12,4},{1,9},{5,13},{9,1},{13,5},{2,10},{6,14},... | collective-permute-start | bytes 196616 | tf_op jit(solution)/shard_map/ppermute | solution.py:311
  108.5 5.8 %collective-permute-start.35 = (bf16[8,16,128]{2,1,0:T(8,128)(2,1)S(1)}, bf16[8,16,128]{2,1,0:T(8,128)(2,1)S(1)}, u32[]{:S(2)}, u32[]{:S(2)}) collective-permute-start(bf16[8,16,128]{2,1,0:T(8,128)(2,1)S(1)} %get-tuple-element.68), channel_id=1, source_target_pairs={{0,12},{4,8},{8,4},{12,0},{1,13},{5,9},{9,5},{13,1},{2,14},{6,10},... | collective-permute-start | bytes 98312 | tf_op jit(solution)/shard_map/ppermute | solution.py:311
  110.3 4.9 %collective-permute-start.34 = (bf16[8,16,128]{2,1,0:T(8,128)(2,1)S(1)}, bf16[8,16,128]{2,1,0:T(8,128)(2,1)S(1)}, u32[]{:S(2)}, u32[]{:S(2)}) collective-permute-start(bf16[8,16,128]{2,1,0:T(8,128)(2,1)S(1)} %get-tuple-element.68), channel_id=1, source_target_pairs={{0,8},{4,12},{8,0},{12,4},{1,9},{5,13},{9,1},{13,5},{2,10},{6,14},... | collective-permute-start | bytes 98312 | tf_op jit(solution)/shard_map/ppermute | solution.py:311
  110.3 5.0 %collective-permute-start.33 = (bf16[8,16,128]{2,1,0:T(8,128)(2,1)S(1)}, bf16[8,16,128]{2,1,0:T(8,128)(2,1)S(1)}, u32[]{:S(2)}, u32[]{:S(2)}) collective-permute-start(bf16[8,16,128]{2,1,0:T(8,128)(2,1)S(1)} %get-tuple-element.68), channel_id=1, source_target_pairs={{0,4},{4,0},{8,12},{12,8},{1,5},{5,1},{9,13},{13,9},{2,6},{6,2},{1... | collective-permute-start | bytes 98312 | tf_op jit(solution)/shard_map/ppermute | solution.py:311
  118.6 2.0 %collective-permute-start.37 = (f32[8,16,128]{2,1,0:T(8,128)S(1)}, f32[8,16,128]{2,1,0:T(8,128)S(1)}, u32[]{:S(2)}, u32[]{:S(2)}) collective-permute-start(f32[8,16,128]{2,1,0:T(8,128)S(1)} %forward.11), channel_id=1, source_target_pairs={{0,1},{1,0},{2,3},{3,2},{4,5},{5,4},{6,7},{7,6},{8,9},{9,8},{10,11... | collective-permute-start | bytes 196616 | tf_op jit(solution)/shard_map/ppermute | solution.py:316
  120.6 4.4 %collective-permute-start.38 = (f32[8,16,128]{2,1,0:T(8,128)S(1)}, f32[8,16,128]{2,1,0:T(8,128)S(1)}, u32[]{:S(2)}, u32[]{:S(2)}) collective-permute-start(f32[8,16,128]{2,1,0:T(8,128)S(1)} %add.126), channel_id=1, source_target_pairs={{0,2},{2,0},{1,3},{3,1},{4,6},{6,4},{5,7},{7,5},{8,10},{10,8},{9,1... | collective-permute-start | bytes 196616 | tf_op jit(solution)/shard_map/ppermute | solution.py:360
  130.6 4.4 %collective-permute-start.41 = (f32[8,16,128]{2,1,0:T(8,128)S(1)}, f32[8,16,128]{2,1,0:T(8,128)S(1)}, u32[]{:S(2)}, u32[]{:S(2)}) collective-permute-start(f32[8,16,128]{2,1,0:T(8,128)S(1)} %get-tuple-element.78), channel_id=1, source_target_pairs={{0,4},{4,0},{8,12},{12,8},{1,5},{5,1},{9,13},{13,9},{2,6},{6,2},{1... | collective-permute-start | bytes 196616 | tf_op jit(solution)/shard_map/ppermute | solution.py:311
  132.3 6.7 %collective-permute-start.43 = (f32[8,16,128]{2,1,0:T(8,128)S(1)}, f32[8,16,128]{2,1,0:T(8,128)S(1)}, u32[]{:S(2)}, u32[]{:S(2)}) collective-permute-start(f32[8,16,128]{2,1,0:T(8,128)S(1)} %get-tuple-element.79), channel_id=1, source_target_pairs={{0,12},{4,8},{8,4},{12,0},{1,13},{5,9},{9,5},{13,1},{2,14},{6,10},... | collective-permute-start | bytes 196616 | tf_op jit(solution)/shard_map/ppermute | solution.py:311
  134.0 7.0 %collective-permute-start.42 = (f32[8,16,128]{2,1,0:T(8,128)S(1)}, f32[8,16,128]{2,1,0:T(8,128)S(1)}, u32[]{:S(2)}, u32[]{:S(2)}) collective-permute-start(f32[8,16,128]{2,1,0:T(8,128)S(1)} %get-tuple-element.80), channel_id=1, source_target_pairs={{0,8},{4,12},{8,0},{12,4},{1,9},{5,13},{9,1},{13,5},{2,10},{6,14},... | collective-permute-start | bytes 196616 | tf_op jit(solution)/shard_map/ppermute | solution.py:311
  (20 other events, 51.3 us)

commit v6 on v5

--- a/solution.py
+++ b/solution.py
@@ -36,19 +36,19 @@
     scaled = (exponent + 1) * columns + place
     position = core * slots + lax.broadcasted_iota(jnp.int32, (1, slots), 1)
     n = rows // (2 * runs)
-    for half in range(2):
-        index, places, factor = outs[3 * half : 3 * half + 3]
-        for r in range(rows // 2):
-            first = 2 * n * (r // n) + r % n
-            low, high = (first, first + n) if half == 0 else (first + n, first)
-
-            def row(array):
-                return jnp.where(core == 0, array[low : low + 1], array[high : high + 1])
-
-            used = position < jnp.where(core == 0, live[low], live[high])
-            places[r : r + 1] = row(place)
-            index[r : r + 1] = jnp.where(used, row(scaled), 3 * columns)
-            factor[r : r + 1] = jnp.where(used, row(scale), 0.0).astype(F32)
+    index, places, factor = outs[:3]
+    for r in range(rows):
+        half, t = divmod(r, rows // 2)
+        first = 2 * n * (t // n) + t % n
+        low, high = (first, first + n) if half == 0 else (first + n, first)
+
+        def row(array):
+            return jnp.where(core == 0, array[low : low + 1], array[high : high + 1])
+
+        used = position < jnp.where(core == 0, live[low], live[high])
+        places[r : r + 1] = row(place)
+        index[r : r + 1] = jnp.where(used, row(scaled), 3 * columns)
+        factor[r : r + 1] = jnp.where(used, row(scale), 0.0).astype(F32)
     sides = outs[-1]
     for e, (at, bit) in enumerate(steps):
         side = jnp.where((me[at] & bit) == 0, 1.0, 0.0).astype(F32)
@@ -57,7 +57,7 @@
 
 def indices(n_vox, columns, runs, steps, me, cols, exps, live):
     rows, _, slots = cols.shape
-    out = [jax.ShapeDtypeStruct((rows // 2, slots), t) for t in (jnp.int32, jnp.int32, F32)] * 2
+    out = [jax.ShapeDtypeStruct((rows, slots), t) for t in (jnp.int32, jnp.int32, F32)]
     out.append(jax.ShapeDtypeStruct((len(steps), 8, 128), F32))
     return pl.pallas_call(
         functools.partial(index_kernel, n_vox, columns, runs, steps),
@@ -67,6 +67,34 @@
         compiler_params=PARAMS,
         name="indices",
     )(me, *(pltpu.with_memory_space_constraint(a, pltpu.HBM) for a in (cols, exps)), live)
+
+
+RUN = 4
+
+
+def cut_of(slots):
+    return 2 * slots // 3
+
+
+def sort_slots(index, places, factor, columns):
+    rows, slots = index.shape
+    here = jnp.arange(slots, dtype=jnp.int32)
+    dead = factor == 0
+    kind = jnp.where(dead, 2, jnp.where(places >= columns // 2, 0, 1))
+    key = kind * slots + here
+    rank = jnp.sum((key[:, None, :] < key[:, :, None]).astype(jnp.int32), axis=-1)
+    chosen = rank[:, None, :] == here[None, :, None]
+
+    def pick(array):
+        return jnp.sum(jnp.where(chosen, array[:, None, :], 0), axis=-1)
+
+    row = jnp.arange(rows, dtype=jnp.int32)[:, None] % (rows // 2)
+    slot = pick(row * slots + here)
+    places = pick(jnp.where(dead, columns + rank, places))
+    others = jnp.sum((kind == 0).astype(jnp.int32), axis=1)
+    over = jnp.max(others.reshape(-1, RUN), axis=1, keepdims=True) > cut_of(slots)
+    over = jnp.broadcast_to(over.astype(jnp.int32), (rows // RUN, 128))
+    return slot, pick(index), places, pick(factor), over
 
 
 def turn_kernel(kept, after, turned):
@@ -104,6 +132,11 @@
         scaled[2 * columns + at : 2 * columns + at + n] = values * BF16(2.0)
         at += n
     scaled[3 * columns] = jnp.zeros(scaled.shape[1:], BF16)
+
+
+def row_operands(chosen, b, slot, index, scaled, blocks):
+    left = jnp.concatenate([scaled[index[b, k]] for k in chosen], axis=1)
+    return left, [blocks[slot[b, k]] for k in chosen]
 
 
 def row_copies(mine, runs, slots, me, stored, kept, sems):
@@ -120,66 +153,120 @@
     ]
 
 
-def load_kernel(slots, runs, me, stored, after, kept, sems):
+def load_kernel(runs, count, me, stored, *refs):
+    tables, kept, me_out, outs, sems, table_sems = (
+        refs[:count],
+        refs[count],
+        refs[count + 1],
+        refs[count + 2 : 2 * count + 2],
+        refs[-2],
+        refs[-1],
+    )
+    slots = tables[0].shape[1]
     copies = row_copies(False, runs, slots, me, stored, kept, sems)
+    copies += [
+        pltpu.make_async_copy(table, out, table_sems.at[i])
+        for i, (table, out) in enumerate(zip(tables, outs, strict=True))
+    ]
     for copy in copies:
         copy.start()
+    for i in range(me.shape[0]):
+        me_out[i] = me[i]
     for copy in copies:
         copy.wait()
 
 
-def load_others(rows, runs, me, tiles, after):
+def load_others(runs, me, tables, tiles):
+    rows = tables[0].shape[0]
     shape = (tiles.shape[0] // 2,) + tiles.shape[1:]
     return pl.pallas_call(
-        functools.partial(load_kernel, tiles.shape[0] // rows, runs),
-        in_specs=[in_smem(), pl.BlockSpec(memory_space=pltpu.HBM), in_vmem()],
-        out_specs=in_vmem(),
-        out_shape=pltpu.VMEM(shape, tiles.dtype),
-        scratch_shapes=[pltpu.SemaphoreType.DMA((rows // 2,))],
+        functools.partial(load_kernel, runs, len(tables)),
+        in_specs=[in_smem(), pl.BlockSpec(memory_space=pltpu.HBM)] + [in_vmem()] * len(tables),
+        out_specs=[in_vmem()] + [in_smem()] * (len(tables) + 1),
+        out_shape=[pltpu.VMEM(shape, tiles.dtype)]
+        + [pltpu.SMEM(t.shape, t.dtype) for t in (me, *tables)],
+        scratch_shapes=[
+            pltpu.SemaphoreType.DMA((rows // 2,)),
+            pltpu.SemaphoreType.DMA((len(tables),)),
+        ],
         compiler_params=PARAMS,
         cost_estimate=pl.CostEstimate(flops=0, bytes_accessed=2 * tiles.size, transcendentals=0),
         name="load_others",
-    )(me, pltpu.with_memory_space_constraint(tiles, pltpu.HBM), after)
-
-
-def first_forward_kernel(slots, runs, me, index_others, index_mine, *refs):
+    )(me, pltpu.with_memory_space_constraint(tiles, pltpu.HBM), *tables)
+
+
+def first_forward_kernel(runs, me, slot, index, *refs):
     pieces, (kept_others, stored, given, dose, kept_mine, scaled, sems) = refs[:-7], refs[-7:]
+    slots = slot.shape[1]
     copies = row_copies(True, runs, slots, me, stored, kept_mine, sems)
     for copy in copies:
         copy.start()
     scale_weights(pieces, scaled)
     rows = dose.shape[0]
-    unroll = 4 if rows % 4 == 0 else 1
-    for index, kept, out in ((index_others, kept_others, given), (index_mine, kept_mine, dose)):
-        for t in range(rows // unroll):
+    for kept, out, row0 in ((kept_others, given, rows), (kept_mine, dose, 0)):
+        for t in range(0, rows, RUN):
             if kept is kept_mine:
-                for u in range(unroll):
-                    copies[t * unroll + u].wait()
-            for u in range(unroll):
-                b = t * unroll + u
-                left = jnp.concatenate([scaled[index[b, k]] for k in range(slots)], axis=1)
-                right = jnp.concatenate([kept[b * slots + k] for k in range(slots)], axis=1)
+                for b in range(t, t + RUN):
+                    copies[b].wait()
+            for b in range(t, t + RUN):
+                left, blocks = row_operands(range(slots), row0 + b, slot, index, scaled, kept)
+                right = jnp.concatenate(blocks, axis=1)
                 out[b] = lax.dot_general(
                     left, right, (((1,), (1,)), ((), ())), preferred_element_type=F32
                 )
 
 
-def forward_kernel(slots, index, *refs):
-    pieces, turned, dose, scaled = refs[:-3], refs[-3], refs[-2], refs[-1]
-    scale_weights(pieces, scaled)
-    rows = dose.shape[0]
-    unroll = 4 if rows % 4 == 0 else 1
-
-    def some_rows(t, carry):
-        for u in range(unroll):
-            b = t * unroll + u
-            left = jnp.concatenate([scaled[index[b, k]] for k in range(slots)], axis=1)
-            right = turned[pl.ds(b * slots, slots)]
-            right = right.reshape(slots * right.shape[1], right.shape[2])
-            dose[b] = jnp.dot(left, right, preferred_element_type=F32)
+def row_dose(chosen, b, slot, index, scaled, turned):
+    left, blocks = row_operands(chosen, b, slot, index, scaled, turned)
+    return jnp.dot(left, jnp.concatenate(blocks, axis=0), preferred_element_type=F32)
+
+
+def near_forward_kernel(slot, index, over, near, turned_mine, turned_others, dose, scaled):
+    scale_weights([near], scaled)
+    rows, slots = slot.shape
+    last = range(cut_of(slots), slots)
+    for turned, row0 in ((turned_mine, 0), (turned_others, rows // 2)):
+
+        def run(t, carry, turned=turned, row0=row0):
+            b0 = row0 + t * RUN
+            skip = over[b0 // RUN, 0] > 0
+
+            @pl.when(skip)
+            def _():
+                for u in range(RUN):
+                    dose[b0 + u] = jnp.zeros(dose.shape[1:], F32)
+
+            @pl.when(jnp.logical_not(skip))
+            def _():
+                for u in range(RUN):
+                    dose[b0 + u] = row_dose(last, b0 + u, slot, index, scaled, turned)
+
+            return carry
+
+        lax.fori_loop(0, rows // 2 // RUN, run, 0)
+
+
+def forward_kernel(row0, slot, index, over, near, far, turned, part, dose, scaled):
+    scale_weights([near, far], scaled)
+    slots = slot.shape[1]
+    cut = cut_of(slots)
+
+    def run(t, carry):
+        b0 = row0 + t * RUN
+        for u in range(RUN):
+            value = row_dose(range(cut), b0 + u, slot, index, scaled, turned)
+            dose[t * RUN + u] = part[b0 + u] + value
+
+        @pl.when(over[b0 // RUN, 0] > 0)
+        def _():
+            for u in range(RUN):
+                dose[t * RUN + u] += row_dose(
+                    range(cut, slots), b0 + u, slot, index, scaled, turned
+                )
+
         return carry
 
-    lax.fori_loop(0, rows // unroll, some_rows, 0)
+    lax.fori_loop(0, dose.shape[0] // RUN, run, 0)
 
 
 def work_of(rows, slots, weightings, width):
@@ -190,29 +277,44 @@
     )
 
 
-def forward(index, pieces, turned):
+def near_forward(tables, near, turned_mine, turned_others):
+    half, weightings, width = near.shape
+    rows, slots = tables[0].shape
+    return pl.pallas_call(
+        near_forward_kernel,
+        in_specs=[in_smem()] * 3 + [in_vmem()] * 3,
+        out_specs=in_vmem(),
+        out_shape=jax.ShapeDtypeStruct((rows, weightings, width), F32),
+        scratch_shapes=[pltpu.VMEM((6 * half + 1, weightings, width), BF16)],
+        compiler_params=PARAMS,
+        cost_estimate=work_of(rows, slots - cut_of(slots), weightings, width),
+        name="near_forward",
+    )(*tables[:2], tables[4], near, held(turned_mine), held(turned_others))
+
+
+def forward(row0, tables, near, far, turned, part):
+    half, weightings, width = near.shape
+    rows, slots = tables[0].shape
+    return pl.pallas_call(
+        functools.partial(forward_kernel, row0),
+        in_specs=[in_smem()] * 3 + [in_vmem()] * 4,
+        out_specs=in_vmem(),
+        out_shape=jax.ShapeDtypeStruct((rows // 2, weightings, width), F32),
+        scratch_shapes=[pltpu.VMEM((6 * half + 1, weightings, width), BF16)],
+        compiler_params=PARAMS,
+        cost_estimate=work_of(rows // 2, cut_of(slots), weightings, width),
+        name="forward",
+    )(*tables[:2], tables[4], near, far, held(turned), part)
+
+
+def first_forward(runs, me, tables, pieces, kept_others, tiles):
     columns = sum(p.shape[0] for p in pieces)
     weightings, width = pieces[0].shape[1:]
-    rows, slots = index.shape
-    return pl.pallas_call(
-        functools.partial(forward_kernel, slots),
-        in_specs=[in_smem()] + [in_vmem()] * (len(pieces) + 1),
-        out_specs=in_vmem(),
-        out_shape=jax.ShapeDtypeStruct((rows, weightings, width), F32),
-        scratch_shapes=[pltpu.VMEM((3 * columns + 1, weightings, width), BF16)],
-        compiler_params=PARAMS,
-        cost_estimate=work_of(rows, slots, weightings, width),
-        name="forward",
-    )(index, *pieces, held(turned))
-
-
-def first_forward(runs, me, index_others, index_mine, pieces, kept_others, tiles):
-    columns = sum(p.shape[0] for p in pieces)
-    weightings, width = pieces[0].shape[1:]
-    rows, slots = index_mine.shape
+    rows, slots = tables[0].shape
+    rows //= 2
     part = jax.ShapeDtypeStruct((rows, weightings, width), F32)
     return pl.pallas_call(
-        functools.partial(first_forward_kernel, slots, runs),
+        functools.partial(first_forward_kernel, runs),
         in_specs=[in_smem()] * 3
         + [in_vmem()] * (len(pieces) + 1)
         + [pl.BlockSpec(memory_space=pltpu.HBM)],
@@ -227,60 +329,111 @@
         name="first_forward",
     )(
         me,
-        index_others,
-        index_mine,
+        *tables[:2],
         *pieces,
         held(kept_others),
         pltpu.with_memory_space_constraint(tiles, pltpu.HBM),
     )
 
 
-def backward_kernel(slots, mine, index, factor, slope, kept, *refs):
+def add_row(chosen, b, tables, left, kept, total):
+    slot, places, factor = tables
+    width = kept.shape[-1]
+    group = 8 if len(chosen) % 8 == 0 else 1
+    for k0 in range(0, len(chosen), group):
+        some = chosen[k0 : k0 + group]
+        right = jnp.concatenate([kept[slot[b, k]] for k in some], axis=1)
+        product = jnp.dot(left, right, preferred_element_type=F32)
+        at = [places[b, k] for k in some]
+        old = [total[p] for p in at]
+        for i, k in enumerate(some):
+            total[at[i]] = old[i] + product[:, i * width : (i + 1) * width] * factor[b, k]
+
+
+def backward_kernel(mine, row0, slot, places, factor, over, slope, kept, *refs):
     *before, total = refs
-    total[...] = jnp.zeros_like(total) if mine else before.pop(0)[...]
-    width = kept.shape[-1]
-    group = 12 if slots % 12 == 0 else 1
-    rows = slope.shape[0]
-    unroll = 4 if rows % 4 == 0 else 1
-
-    def some_rows(t, carry):
-        for u in range(unroll):
-            b = t * unroll + u
-            left = slope[b]
-            for k0 in range(0, slots, group):
-                right = jnp.concatenate([kept[b * slots + k0 + k] for k in range(group)], axis=1)
-                product = jnp.dot(left, right, preferred_element_type=F32)
-                columns = [index[b, k0 + k] for k in range(group)]
-                old = [total[c] for c in columns]
-                for k in range(group):
-                    part = product[:, k * width : (k + 1) * width]
-                    total[columns[k]] = old[k] + part * factor[b, k0 + k]
+    columns = total.shape[0] - slot.shape[1]
+    total[columns:] = jnp.zeros_like(total[columns:])
+    total[:columns] = jnp.zeros_like(total[:columns]) if mine else before.pop(0)[...]
+    tables = (slot, places, factor)
+    slots = slot.shape[1]
+    cut = cut_of(slots)
+
+    def run(t, carry):
+        b0 = row0 + t * RUN
+        for u in range(RUN):
+            add_row(range(cut), b0 + u, tables, slope[t * RUN + u], kept, total)
+
+        @pl.when(over[b0 // RUN, 0] > 0)
+        def _():
+            for u in range(RUN):
+                add_row(range(cut, slots), b0 + u, tables, slope[t * RUN + u], kept, total)
+
         return carry
 
-    lax.fori_loop(0, rows // unroll, some_rows, 0)
+    lax.fori_loop(0, slope.shape[0] // RUN, run, 0)
     if mine:
-        before[0][...] = total[...]
+        before[0][...] = total[:columns]
     else:
         far, near = before
-        half = near.shape[0]
-        near[...] = total[:half]
-        far[...] = total[half:]
-
-
-def backward(mine, index, factor, slope, kept, columns, *total):
+        near[...] = total[: columns // 2]
+        far[...] = total[columns // 2 : columns]
+
+
+def near_backward_kernel(
+    slot, places, factor, over, slope_mine, slope_others, kept_mine, kept_others, near, out, total
+):
+    half = near.shape[0]
+    total[:half] = near[...]
+    total[2 * half :] = jnp.zeros_like(total[2 * half :])
+    tables = (slot, places, factor)
+    rows, slots = slot.shape
+    last = range(cut_of(slots), slots)
+    for slope, kept, row0 in ((slope_mine, kept_mine, 0), (slope_others, kept_others, rows // 2)):
+
+        def run(t, carry, slope=slope, kept=kept, row0=row0):
+            b0 = row0 + t * RUN
+
+            @pl.when(over[b0 // RUN, 0] == 0)
+            def _():
+                for u in range(RUN):
+                    add_row(last, b0 + u, tables, slope[t * RUN + u], kept, total)
+
+            return carry
+
+        lax.fori_loop(0, rows // 2 // RUN, run, 0)
+    out[...] = total[:half]
+
+
+def backward(mine, row0, tables, slope, kept, columns, *total):
     half_rows, weightings, width = slope.shape
-    slots = index.shape[1]
+    slots = tables[0].shape[1]
     out = [(columns, weightings, width)] if mine else [(columns // 2, weightings, width)] * 2
     return pl.pallas_call(
-        functools.partial(backward_kernel, slots, mine),
-        in_specs=[in_smem()] * 2 + [in_vmem()] * (2 + len(total)),
+        functools.partial(backward_kernel, mine, row0),
+        in_specs=[in_smem()] * 4 + [in_vmem()] * (2 + len(total)),
         out_specs=[in_vmem()] * len(out),
         out_shape=[jax.ShapeDtypeStruct(shape, F32) for shape in out],
-        scratch_shapes=[pltpu.VMEM((columns, weightings, width), F32)],
-        compiler_params=PARAMS,
-        cost_estimate=work_of(half_rows, slots, weightings, width),
+        scratch_shapes=[pltpu.VMEM((columns + slots, weightings, width), F32)],
+        compiler_params=PARAMS,
+        cost_estimate=work_of(half_rows, cut_of(slots), weightings, width),
         name="backward",
-    )(index, factor, slope, held(kept), *total)
+    )(tables[0], *tables[2:], slope, held(kept), *total)
+
+
+def near_backward(tables, slope_mine, slope_others, kept_mine, kept_others, near):
+    half, weightings, width = near.shape
+    rows, slots = tables[0].shape
+    return pl.pallas_call(
+        near_backward_kernel,
+        in_specs=[in_smem()] * 4 + [in_vmem()] * 5,
+        out_specs=in_vmem(),
+        out_shape=jax.ShapeDtypeStruct(near.shape, F32),
+        scratch_shapes=[pltpu.VMEM((2 * half + slots, weightings, width), F32)],
+        compiler_params=PARAMS,
+        cost_estimate=work_of(rows, slots - cut_of(slots), weightings, width),
+        name="near_backward",
+    )(tables[0], *tables[2:], slope_mine, slope_others, held(kept_mine), held(kept_others), near)
 
 
 def per_device(
@@ -325,7 +478,7 @@
         return [piece] + over_vox([piece] * (n_vox - 1))
 
     bits = [1 << i for i in range(n_spot.bit_length() - 1)]
-    *tables, sides = indices(
+    *unsorted, sides = indices(
         n_vox,
         columns,
         n_spot,
@@ -335,21 +488,22 @@
         block_exps,
         live_counts.reshape(rows),
     )
-    mine, others = tables[:3], tables[3:]
+    tables = sort_slots(*unsorted, columns)
     pieces = gather_weights(weights)
-    kept_others = load_others(rows, n_spot, me, tiles, sides)
+    kept_others, me, *tables = load_others(n_spot, me, tables, tiles)
     pieces, kept_others = lax.optimization_barrier((pieces, kept_others))
 
     for step in range(ITERS):
         near = jnp.concatenate(pieces, axis=0)
-        weight_halves = [near, over_rep(near)]
+        other_half = over_rep(near)
         if step == 0:
             given, dose, kept_mine = first_forward(
-                n_spot, me, others[0], mine[0], weight_halves, kept_others, tiles
+                n_spot, me, tables, [near, other_half], kept_others, tiles
             )
         else:
-            given = forward(others[0], weight_halves, turned_others)
-            dose = forward(mine[0], weight_halves, turned_mine)
+            part = near_forward(tables, near, turned_mine, turned_others)
+            given = forward(rows // 2, tables, near, other_half, turned_others, part)
+            dose = forward(0, tables, near, other_half, turned_mine, part)
         dose = dose + over_rep(given)
         for e, bit in enumerate(bits, 1):
             sent = dose
@@ -375,9 +529,11 @@
             levels[1] * jax.nn.sigmoid(4.0 * (dose - levels[0]))
             - levels[3] * jax.nn.sigmoid(4.0 * (levels[2] - dose))
         ).astype(BF16)
-        (total,) = backward(True, *mine[1:], slope, kept_mine, columns)
-        far, near = backward(False, *others[1:], over_rep(slope), kept_others, columns, total)
-        near = near + over_rep(far)
+        slope_others = over_rep(slope)
+        (total,) = backward(True, 0, tables, slope, kept_mine, columns)
+        far, near = backward(False, rows // 2, tables, slope_others, kept_others, columns, total)
+        theirs = over_rep(far)
+        near = near_backward(tables, slope, slope_others, kept_mine, kept_others, near) + theirs
         received = over_vox([near[d * own : (d + 1) * own] for d in range(1, n_vox)])
         if step == 0:
             turned = [turn(kept_others, near), turn(kept_mine, near)]

time: 144 us -> 134 us (0.931)
  waiting for transfers between devices: 52.3 us -> 43.9 us
  Pallas kernels: 41.7 us -> 36.3 us
  other arithmetic: 0.84 us -> 2.61 us
    ppermute x17, waiting for transfers between devices: 12.4 us -> 6.05 us  [over_rep(): return lax.ppermute(array, 'rep', [(0, 1), (1, 0)])]
    pallas_call x16 -> x23, Pallas kernels: 35 us -> 29.7 us  [the longest x8 7.41 us: backward(): pl.pallas_call(functools.partial(backward_kernel, mine, row0), in_specs=[...]
    ppermute x4, starting transfers between devices: 6.43 us -> 8.27 us  [per_device(): got = lax.ppermute(sent, 'spot', [(i, i ^ bit) for i in range(n_spot)])]
    reduce_sum x0 -> x4, other arithmetic: none -> 1.57 us  [the longest x2 1.02 us: pick(): return jnp.sum(jnp.where(chosen, array[:, None, :], 0), axis=-1)]
  transfers between devices with their start and end apart: 45 -> 45, of which waited for: 30 -> 34; matrix products, arithmetic and copies ran while one was open for 0% -> 2% of each run, Pallas kernels for 16% -> 18%
where the time goes in v6:
time: 134 us; the launch traced here: 133 us
  starting transfers between devices  45.7 us (34%)
  waiting for transfers between devices  43.9 us (33%)
  Pallas kernels  36.3 us (27%)
  local copies, waits for them, and re-layouts  3.55 us (3%)
  other arithmetic  2.61 us (2%)
    ppermute x24, starting transfers between devices, over_vox(): lax.ppermute(a, 'vox', [(i, i ^ d) for i in range(n_vox)])  34.2 us
    ppermute x24, waiting for transfers between devices, over_vox(): lax.ppermute(a, 'vox', [(i, i ^ d) for i in range(n_vox)])  28.2 us
    ppermute x4, waiting for transfers between devices, per_device(): got = lax.ppermute(sent, 'spot', [(i, i ^ bit) for i in range(n_spot)])  9.72 us
    ppermute x4, starting transfers between devices, per_device(): got = lax.ppermute(sent, 'spot', [(i, i ^ bit) for i in range(n_spot)])  8.27 us
    pallas_call x8, Pallas kernels, backward(): pl.pallas_call(functools.partial(backward_kernel, mine, row0), in_specs=[...  7.41 us
    ppermute x17, waiting for transfers between devices, over_rep(): return lax.ppermute(array, 'rep', [(0, 1), (1, 0)])  6.05 us
    pallas_call x2, Pallas kernels, turn(): pl.pallas_call(turn_kernel, in_specs=[in_vmem(), pl.BlockSpec(memory_spac...  5.86 us
    pallas_call x1, Pallas kernels, first_forward(): pl.pallas_call(functools.partial(first_forward_kernel, runs), in_specs=[i...  5.39 us
  transfers between devices with their start and end apart: 45, of which 34 were waited for; matrix products, arithmetic and copies ran while one was open for 2% of the time, Pallas kernels for 18%

profile of v6, /device:TPU:0, one launch (start us, length us, event | category | flops | bytes accessed | tf_op | source)
XLA Modules:
  0.0 133.3 jit_solution(125285927537396036)
XLA Ops:
  1.6 5.1 %collective-permute-start.2 = (bf16[8,16,128]{2,1,0:T(8,128)(2,1)S(1)}, bf16[8,16,128]{2,1,0:T(8,128)(2,1)S(1)}, u32[]{:S(2)}, u32[]{:S(2)}) collective-permute-start(bf16[8,16,128]{2,1,0:T(8,128)(2,1)S(1)} %bitcast.57), channel_id=1, source_target_pairs={{0,12},{4,8},{8,4},{12,0},{1,13},{5,9},{9,5},{13,1},{2,14},{6,10},... | collective-permute-start | bytes 98312 | tf_op jit(solution)/shard_map/ppermute | solution.py:464
  10.9 3.5 %load_others.1 = (bf16[192,128,128]{2,1,0:T(8,128)(2,1)S(1)}, s32[3]{0:T(128)S(4)}, s32[16,24]{1,0:T(8,128)S(4)}, s32[16,24]{1,0:T(8,128)S(4)}, s32[16,24]{1,0:T...) custom-call(s32[3]{0:T(128)S(1)} %pad_add_fusion.me, bf16[384,128,128]{2,1,0:T(8,128)(2,1)} %bitcast.53, ...), custom_call_target="tpu_custom_call" | custom-call | bytes 12582912 | tf_op jit(solution)/shard_map/load_others/pallas_call | solution.py:182
  15.9 5.4 %first_forward.1 = (f32[8,16,128]{2,1,0:T(8,128)S(1)}, f32[8,16,128]{2,1,0:T(8,128)S(1)}, bf16[192,128,128]{2,1,0:T(8,128)(2,1)S(1)}) custom-call(s32[3]{0:T(128)S(4)} %get-tuple-element.42.me, s32[16,24]{1,0:T(8,128)S(4)} %get-tuple-element.38.slot, s32[16,24]{1,0:T(8,128)S(4)} %get-tuple-element.43.index, ...), custom_call_target="tpu_custom_call" | custom-call | flops 201326592 | bytes 12582912 | tf_op jit(solution)/shard_map/first_forward/pallas_call | solution.py:316
  22.6 1.7 %collective-permute-start.5 = (f32[9,16,128]{2,1,0:T(8,128)S(1)}, f32[9,16,128]{2,1,0:T(8,128)S(1)}, u32[]{:S(2)}, u32[]{:S(2)}) collective-permute-start(f32[9,16,128]{2,1,0:T(8,128)S(1)} %pad_maximum_fusion.4), channel_id=1, source_target_pairs={{0,2},{2,0},{1,3},{3,1},{4,6},{6,4},{5,7},{7,5},{8,10},{10,8},{9,1... | collective-permute-start | bytes 221192 | tf_op jit(solution)/shard_map/ppermute | solution.py:514
  24.6 2.4 %collective-permute-done.5 = f32[9,16,128]{2,1,0:T(8,128)S(1)} collective-permute-done((f32[9,16,128]{2,1,0:T(8,128)S(1)}, f32[9,16,128]{2,1,0:T(8,128)S(1)}, u32[]{:S(2)}, u32[]{:S(2)}) %collective-permute-start.5) | collective-permute-done | bytes 73760 | tf_op jit(solution)/shard_map/ppermute | solution.py:514
  31.1 3.8 %collective-permute-start.10 = (f32[8,16,128]{2,1,0:T(8,128)S(1)}, f32[8,16,128]{2,1,0:T(8,128)S(1)}, u32[]{:S(2)}, u32[]{:S(2)}) collective-permute-start(f32[8,16,128]{2,1,0:T(8,128)S(1)} %get-tuple-element.101), channel_id=1, source_target_pairs={{0,12},{4,8},{8,4},{12,0},{1,13},{5,9},{9,5},{13,1},{2,14},{6,10},... | collective-permute-start | bytes 196616 | tf_op jit(solution)/shard_map/ppermute | solution.py:464
  35.6 2.9 %turn.3.turned_mine.turned = bf16[192,128,128]{2,1,0:T(8,128)(2,1)S(1)} custom-call(bf16[192,128,128]{2,1,0:T(8,128)(2,1)S(1)} %get-tuple-element.52.kept.kept_mine, f32[32,16,128]{2,1,0:T(8,128)S(1)} %add.156.after), custom_call_target="tpu_custom_call" | custom-call | bytes 12582912 | tf_op jit(solution)/shard_map/turn/pallas_call | solution.py:113
  38.5 2.9 %turn.2.turned_others.turned = bf16[192,128,128]{2,1,0:T(8,128)(2,1)S(1)} custom-call(bf16[192,128,128]{2,1,0:T(8,128)(2,1)S(1)} %get-tuple-element.49.refs_2_.kept.kept_others, f32[32,16,128]{2,1,0:T(8,128)S(1)} %add.156.after), custom_call_target="tpu_custom_call" | custom-call | bytes 12582912 | tf_op jit(solution)/shard_map/turn/pallas_call | solution.py:113
  41.5 3.8 %collective-permute-start.13 = (bf16[8,16,128]{2,1,0:T(8,128)(2,1)S(1)}, bf16[8,16,128]{2,1,0:T(8,128)(2,1)S(1)}, u32[]{:S(2)}, u32[]{:S(2)}) collective-permute-start(bf16[8,16,128]{2,1,0:T(8,128)(2,1)S(1)} %get-tuple-element.83), channel_id=1, source_target_pairs={{0,12},{4,8},{8,4},{12,0},{1,13},{5,9},{9,5},{13,1},{2,14},{6,10},... | collective-permute-start | bytes 98312 | tf_op jit(solution)/shard_map/ppermute | solution.py:464
  46.0 1.7 %collective-permute-done.13 = bf16[8,16,128]{2,1,0:T(8,128)(2,1)S(1)} collective-permute-done((bf16[8,16,128]{2,1,0:T(8,128)(2,1)S(1)}, bf16[8,16,128]{2,1,0:T(8,128)(2,1)S(1)}, u32[]{:S(2)}, u32[]{:S(2)}) %collective-permute-start.13) | collective-permute-done | bytes 32800 | tf_op jit(solution)/shard_map/ppermute | solution.py:464
  47.7 2.5 %collective-permute-done.12 = bf16[8,16,128]{2,1,0:T(8,128)(2,1)S(1)} collective-permute-done((bf16[8,16,128]{2,1,0:T(8,128)(2,1)S(1)}, bf16[8,16,128]{2,1,0:T(8,128)(2,1)S(1)}, u32[]{:S(2)}, u32[]{:S(2)}) %collective-permute-start.12) | collective-permute-done | bytes 32800 | tf_op jit(solution)/shard_map/ppermute | solution.py:464
  53.8 2.0 %collective-permute-start.16 = (f32[8,16,128]{2,1,0:T(8,128)S(1)}, f32[8,16,128]{2,1,0:T(8,128)S(1)}, u32[]{:S(2)}, u32[]{:S(2)}) collective-permute-start(f32[8,16,128]{2,1,0:T(8,128)S(1)} %add.160), channel_id=1, source_target_pairs={{0,2},{2,0},{1,3},{3,1},{4,6},{6,4},{5,7},{7,5},{8,10},{10,8},{9,1... | collective-permute-start | bytes 196616 | tf_op jit(solution)/shard_map/ppermute | solution.py:514
  55.8 2.4 %collective-permute-done.16 = f32[8,16,128]{2,1,0:T(8,128)S(1)} collective-permute-done((f32[8,16,128]{2,1,0:T(8,128)S(1)}, f32[8,16,128]{2,1,0:T(8,128)S(1)}, u32[]{:S(2)}, u32[]{:S(2)}) %collective-permute-start.16) | collective-permute-done | bytes 65568 | tf_op jit(solution)/shard_map/ppermute | solution.py:514
  62.2 3.4 %collective-permute-start.21 = (f32[8,16,128]{2,1,0:T(8,128)S(1)}, f32[8,16,128]{2,1,0:T(8,128)S(1)}, u32[]{:S(2)}, u32[]{:S(2)}) collective-permute-start(f32[8,16,128]{2,1,0:T(8,128)S(1)} %get-tuple-element.99), channel_id=1, source_target_pairs={{0,12},{4,8},{8,4},{12,0},{1,13},{5,9},{9,5},{13,1},{2,14},{6,10},... | collective-permute-start | bytes 196616 | tf_op jit(solution)/shard_map/ppermute | solution.py:464
  66.5 3.5 %collective-permute-done.21 = f32[8,16,128]{2,1,0:T(8,128)S(1)} collective-permute-done((f32[8,16,128]{2,1,0:T(8,128)S(1)}, f32[8,16,128]{2,1,0:T(8,128)S(1)}, u32[]{:S(2)}, u32[]{:S(2)}) %collective-permute-start.21) | collective-permute-done | bytes 65568 | tf_op jit(solution)/shard_map/ppermute | solution.py:464
  70.0 2.1 %collective-permute-done.20 = f32[8,16,128]{2,1,0:T(8,128)S(1)} collective-permute-done((f32[8,16,128]{2,1,0:T(8,128)S(1)}, f32[8,16,128]{2,1,0:T(8,128)S(1)}, u32[]{:S(2)}, u32[]{:S(2)}) %collective-permute-start.20) | collective-permute-done | bytes 65568 | tf_op jit(solution)/shard_map/ppermute | solution.py:464
  72.1 1.8 %collective-permute-start.24 = (bf16[8,16,128]{2,1,0:T(8,128)(2,1)S(1)}, bf16[8,16,128]{2,1,0:T(8,128)(2,1)S(1)}, u32[]{:S(2)}, u32[]{:S(2)}) collective-permute-start(bf16[8,16,128]{2,1,0:T(8,128)(2,1)S(1)} %get-tuple-element.81), channel_id=1, source_target_pairs={{0,12},{4,8},{8,4},{12,0},{1,13},{5,9},{9,5},{13,1},{2,14},{6,10},... | collective-permute-start | bytes 98312 | tf_op jit(solution)/shard_map/ppermute | solution.py:464
  73.8 2.7 %collective-permute-start.22 = (bf16[8,16,128]{2,1,0:T(8,128)(2,1)S(1)}, bf16[8,16,128]{2,1,0:T(8,128)(2,1)S(1)}, u32[]{:S(2)}, u32[]{:S(2)}) collective-permute-start(bf16[8,16,128]{2,1,0:T(8,128)(2,1)S(1)} %get-tuple-element.81), channel_id=1, source_target_pairs={{0,4},{4,0},{8,12},{12,8},{1,5},{5,1},{9,13},{13,9},{2,6},{6,2},{1... | collective-permute-start | bytes 98312 | tf_op jit(solution)/shard_map/ppermute | solution.py:464
  82.5 2.2 %collective-permute-start.27 = (f32[8,16,128]{2,1,0:T(8,128)S(1)}, f32[8,16,128]{2,1,0:T(8,128)S(1)}, u32[]{:S(2)}, u32[]{:S(2)}) collective-permute-start(f32[8,16,128]{2,1,0:T(8,128)S(1)} %add.168), channel_id=1, source_target_pairs={{0,2},{2,0},{1,3},{3,1},{4,6},{6,4},{5,7},{7,5},{8,10},{10,8},{9,1... | collective-permute-start | bytes 196616 | tf_op jit(solution)/shard_map/ppermute | solution.py:514
  84.7 2.4 %collective-permute-done.27 = f32[8,16,128]{2,1,0:T(8,128)S(1)} collective-permute-done((f32[8,16,128]{2,1,0:T(8,128)S(1)}, f32[8,16,128]{2,1,0:T(8,128)S(1)}, u32[]{:S(2)}, u32[]{:S(2)}) %collective-permute-start.27) | collective-permute-done | bytes 65568 | tf_op jit(solution)/shard_map/ppermute | solution.py:514
  91.1 1.6 %collective-permute-start.30 = (f32[8,16,128]{2,1,0:T(8,128)S(1)}, f32[8,16,128]{2,1,0:T(8,128)S(1)}, u32[]{:S(2)}, u32[]{:S(2)}) collective-permute-start(f32[8,16,128]{2,1,0:T(8,128)S(1)} %get-tuple-element.95), channel_id=1, source_target_pairs={{0,4},{4,0},{8,12},{12,8},{1,5},{5,1},{9,13},{13,9},{2,6},{6,2},{1... | collective-permute-start | bytes 196616 | tf_op jit(solution)/shard_map/ppermute | solution.py:464
  92.7 1.7 %collective-permute-start.32 = (f32[8,16,128]{2,1,0:T(8,128)S(1)}, f32[8,16,128]{2,1,0:T(8,128)S(1)}, u32[]{:S(2)}, u32[]{:S(2)}) collective-permute-start(f32[8,16,128]{2,1,0:T(8,128)S(1)} %get-tuple-element.96), channel_id=1, source_target_pairs={{0,12},{4,8},{8,4},{12,0},{1,13},{5,9},{9,5},{13,1},{2,14},{6,10},... | collective-permute-start | bytes 196616 | tf_op jit(solution)/shard_map/ppermute | solution.py:464
  95.5 3.8 %collective-permute-done.32 = f32[8,16,128]{2,1,0:T(8,128)S(1)} collective-permute-done((f32[8,16,128]{2,1,0:T(8,128)S(1)}, f32[8,16,128]{2,1,0:T(8,128)S(1)}, u32[]{:S(2)}, u32[]{:S(2)}) %collective-permute-start.32) | collective-permute-done | bytes 65568 | tf_op jit(solution)/shard_map/ppermute | solution.py:464
  99.3 2.0 %collective-permute-done.31 = f32[8,16,128]{2,1,0:T(8,128)S(1)} collective-permute-done((f32[8,16,128]{2,1,0:T(8,128)S(1)}, f32[8,16,128]{2,1,0:T(8,128)S(1)}, u32[]{:S(2)}, u32[]{:S(2)}) %collective-permute-start.31) | collective-permute-done | bytes 65568 | tf_op jit(solution)/shard_map/ppermute | solution.py:464
  101.3 1.9 %collective-permute-start.35 = (bf16[8,16,128]{2,1,0:T(8,128)(2,1)S(1)}, bf16[8,16,128]{2,1,0:T(8,128)(2,1)S(1)}, u32[]{:S(2)}, u32[]{:S(2)}) collective-permute-start(bf16[8,16,128]{2,1,0:T(8,128)(2,1)S(1)} %get-tuple-element.79), channel_id=1, source_target_pairs={{0,12},{4,8},{8,4},{12,0},{1,13},{5,9},{9,5},{13,1},{2,14},{6,10},... | collective-permute-start | bytes 98312 | tf_op jit(solution)/shard_map/ppermute | solution.py:464
  103.2 2.6 %collective-permute-start.33 = (bf16[8,16,128]{2,1,0:T(8,128)(2,1)S(1)}, bf16[8,16,128]{2,1,0:T(8,128)(2,1)S(1)}, u32[]{:S(2)}, u32[]{:S(2)}) collective-permute-start(bf16[8,16,128]{2,1,0:T(8,128)(2,1)S(1)} %get-tuple-element.79), channel_id=1, source_target_pairs={{0,4},{4,0},{8,12},{12,8},{1,5},{5,1},{9,13},{13,9},{2,6},{6,2},{1... | collective-permute-start | bytes 98312 | tf_op jit(solution)/shard_map/ppermute | solution.py:464
  105.8 1.4 %collective-permute-done.35 = bf16[8,16,128]{2,1,0:T(8,128)(2,1)S(1)} collective-permute-done((bf16[8,16,128]{2,1,0:T(8,128)(2,1)S(1)}, bf16[8,16,128]{2,1,0:T(8,128)(2,1)S(1)}, u32[]{:S(2)}, u32[]{:S(2)}) %collective-permute-start.35) | collective-permute-done | bytes 32800 | tf_op jit(solution)/shard_map/ppermute | solution.py:464
  111.7 2.3 %collective-permute-start.38 = (f32[8,16,128]{2,1,0:T(8,128)S(1)}, f32[8,16,128]{2,1,0:T(8,128)S(1)}, u32[]{:S(2)}, u32[]{:S(2)}) collective-permute-start(f32[8,16,128]{2,1,0:T(8,128)S(1)} %add.176), channel_id=1, source_target_pairs={{0,2},{2,0},{1,3},{3,1},{4,6},{6,4},{5,7},{7,5},{8,10},{10,8},{9,1... | collective-permute-start | bytes 196616 | tf_op jit(solution)/shard_map/ppermute | solution.py:514
  114.0 2.4 %collective-permute-done.38 = f32[8,16,128]{2,1,0:T(8,128)S(1)} collective-permute-done((f32[8,16,128]{2,1,0:T(8,128)S(1)}, f32[8,16,128]{2,1,0:T(8,128)S(1)}, u32[]{:S(2)}, u32[]{:S(2)}) %collective-permute-start.38) | collective-permute-done | bytes 65568 | tf_op jit(solution)/shard_map/ppermute | solution.py:514
  121.8 2.0 %collective-permute-start.43 = (f32[8,16,128]{2,1,0:T(8,128)S(1)}, f32[8,16,128]{2,1,0:T(8,128)S(1)}, u32[]{:S(2)}, u32[]{:S(2)}) collective-permute-start(f32[8,16,128]{2,1,0:T(8,128)S(1)} %get-tuple-element.93), channel_id=1, source_target_pairs={{0,12},{4,8},{8,4},{12,0},{1,13},{5,9},{9,5},{13,1},{2,14},{6,10},... | collective-permute-start | bytes 196616 | tf_op jit(solution)/shard_map/ppermute | solution.py:464
  124.7 3.6 %collective-permute-done.43 = f32[8,16,128]{2,1,0:T(8,128)S(1)} collective-permute-done((f32[8,16,128]{2,1,0:T(8,128)S(1)}, f32[8,16,128]{2,1,0:T(8,128)S(1)}, u32[]{:S(2)}, u32[]{:S(2)}) %collective-permute-start.43) | collective-permute-done | bytes 65568 | tf_op jit(solution)/shard_map/ppermute | solution.py:464
  128.3 2.1 %collective-permute-done.42 = f32[8,16,128]{2,1,0:T(8,128)S(1)} collective-permute-done((f32[8,16,128]{2,1,0:T(8,128)S(1)}, f32[8,16,128]{2,1,0:T(8,128)S(1)}, u32[]{:S(2)}, u32[]{:S(2)}) %collective-permute-start.42) | collective-permute-done | bytes 65568 | tf_op jit(solution)/shard_map/ppermute | solution.py:464
  (155 shorter events, 46.5 us)
Async XLA Ops:
  1.6 12.8 %collective-permute-start.2 = (bf16[8,16,128]{2,1,0:T(8,128)(2,1)S(1)}, bf16[8,16,128]{2,1,0:T(8,128)(2,1)S(1)}, u32[]{:S(2)}, u32[]{:S(2)}) collective-permute-start(bf16[8,16,128]{2,1,0:T(8,128)(2,1)S(1)} %bitcast.57), channel_id=1, source_target_pairs={{0,12},{4,8},{8,4},{12,0},{1,13},{5,9},{9,5},{13,1},{2,14},{6,10},... | collective-permute-start | bytes 98312 | tf_op jit(solution)/shard_map/ppermute | solution.py:464
  6.7 7.7 %collective-permute-start.1 = (bf16[8,16,128]{2,1,0:T(8,128)(2,1)S(1)}, bf16[8,16,128]{2,1,0:T(8,128)(2,1)S(1)}, u32[]{:S(2)}, u32[]{:S(2)}) collective-permute-start(bf16[8,16,128]{2,1,0:T(8,128)(2,1)S(1)} %bitcast.58), channel_id=1, source_target_pairs={{0,8},{4,12},{8,0},{12,4},{1,9},{5,13},{9,1},{13,5},{2,10},{6,14},... | collective-permute-start | bytes 98312 | tf_op jit(solution)/shard_map/ppermute | solution.py:464
  6.7 7.7 %collective-permute-start = (bf16[8,16,128]{2,1,0:T(8,128)(2,1)S(1)}, bf16[8,16,128]{2,1,0:T(8,128)(2,1)S(1)}, u32[]{:S(2)}, u32[]{:S(2)}) collective-permute-start(bf16[8,16,128]{2,1,0:T(8,128)(2,1)S(1)} %bitcast.59), channel_id=1, source_target_pairs={{0,4},{4,0},{8,12},{12,8},{1,5},{5,1},{9,13},{13,9},{2,6},{6,2},{1... | collective-permute-start | bytes 98312 | tf_op jit(solution)/shard_map/ppermute | solution.py:464
  22.6 4.4 %collective-permute-start.5 = (f32[9,16,128]{2,1,0:T(8,128)S(1)}, f32[9,16,128]{2,1,0:T(8,128)S(1)}, u32[]{:S(2)}, u32[]{:S(2)}) collective-permute-start(f32[9,16,128]{2,1,0:T(8,128)S(1)} %pad_maximum_fusion.4), channel_id=1, source_target_pairs={{0,2},{2,0},{1,3},{3,1},{4,6},{6,4},{5,7},{7,5},{8,10},{10,8},{9,1... | collective-permute-start | bytes 221192 | tf_op jit(solution)/shard_map/ppermute | solution.py:514
  29.4 1.6 %collective-permute-start.7 = (f32[32,16,128]{2,1,0:T(8,128)S(1)}, f32[32,16,128]{2,1,0:T(8,128)S(1)}, u32[]{:S(2)}, u32[]{:S(2)}) collective-permute-start(f32[32,16,128]{2,1,0:T(8,128)S(1)} %get-tuple-element.54), channel_id=1, source_target_pairs={{0,1},{1,0},{2,3},{3,2},{4,5},{5,4},{6,7},{7,6},{8,9},{9,8},{10,11... | collective-permute-start | bytes 786440 | tf_op jit(solution)/shard_map/ppermute | solution.py:469
  31.1 10.4 %collective-permute-start.10 = (f32[8,16,128]{2,1,0:T(8,128)S(1)}, f32[8,16,128]{2,1,0:T(8,128)S(1)}, u32[]{:S(2)}, u32[]{:S(2)}) collective-permute-start(f32[8,16,128]{2,1,0:T(8,128)S(1)} %get-tuple-element.101), channel_id=1, source_target_pairs={{0,12},{4,8},{8,4},{12,0},{1,13},{5,9},{9,5},{13,1},{2,14},{6,10},... | collective-permute-start | bytes 196616 | tf_op jit(solution)/shard_map/ppermute | solution.py:464
  34.9 6.5 %collective-permute-start.9 = (f32[8,16,128]{2,1,0:T(8,128)S(1)}, f32[8,16,128]{2,1,0:T(8,128)S(1)}, u32[]{:S(2)}, u32[]{:S(2)}) collective-permute-start(f32[8,16,128]{2,1,0:T(8,128)S(1)} %get-tuple-element.102), channel_id=1, source_target_pairs={{0,8},{4,12},{8,0},{12,4},{1,9},{5,13},{9,1},{13,5},{2,10},{6,14},... | collective-permute-start | bytes 196616 | tf_op jit(solution)/shard_map/ppermute | solution.py:464
  34.9 6.5 %collective-permute-start.8 = (f32[8,16,128]{2,1,0:T(8,128)S(1)}, f32[8,16,128]{2,1,0:T(8,128)S(1)}, u32[]{:S(2)}, u32[]{:S(2)}) collective-permute-start(f32[8,16,128]{2,1,0:T(8,128)S(1)} %get-tuple-element.103), channel_id=1, source_target_pairs={{0,4},{4,0},{8,12},{12,8},{1,5},{5,1},{9,13},{13,9},{2,6},{6,2},{1... | collective-permute-start | bytes 196616 | tf_op jit(solution)/shard_map/ppermute | solution.py:464
  41.5 6.2 %collective-permute-start.13 = (bf16[8,16,128]{2,1,0:T(8,128)(2,1)S(1)}, bf16[8,16,128]{2,1,0:T(8,128)(2,1)S(1)}, u32[]{:S(2)}, u32[]{:S(2)}) collective-permute-start(bf16[8,16,128]{2,1,0:T(8,128)(2,1)S(1)} %get-tuple-element.83), channel_id=1, source_target_pairs={{0,12},{4,8},{8,4},{12,0},{1,13},{5,9},{9,5},{13,1},{2,14},{6,10},... | collective-permute-start | bytes 98312 | tf_op jit(solution)/shard_map/ppermute | solution.py:464
  45.3 4.8 %collective-permute-start.12 = (bf16[8,16,128]{2,1,0:T(8,128)(2,1)S(1)}, bf16[8,16,128]{2,1,0:T(8,128)(2,1)S(1)}, u32[]{:S(2)}, u32[]{:S(2)}) collective-permute-start(bf16[8,16,128]{2,1,0:T(8,128)(2,1)S(1)} %get-tuple-element.83), channel_id=1, source_target_pairs={{0,8},{4,12},{8,0},{12,4},{1,9},{5,13},{9,1},{13,5},{2,10},{6,14},... | collective-permute-start | bytes 98312 | tf_op jit(solution)/shard_map/ppermute | solution.py:464
  45.3 4.8 %collective-permute-start.11 = (bf16[8,16,128]{2,1,0:T(8,128)(2,1)S(1)}, bf16[8,16,128]{2,1,0:T(8,128)(2,1)S(1)}, u32[]{:S(2)}, u32[]{:S(2)}) collective-permute-start(bf16[8,16,128]{2,1,0:T(8,128)(2,1)S(1)} %get-tuple-element.83), channel_id=1, source_target_pairs={{0,4},{4,0},{8,12},{12,8},{1,5},{5,1},{9,13},{13,9},{2,6},{6,2},{1... | collective-permute-start | bytes 98312 | tf_op jit(solution)/shard_map/ppermute | solution.py:464
  53.8 4.4 %collective-permute-start.16 = (f32[8,16,128]{2,1,0:T(8,128)S(1)}, f32[8,16,128]{2,1,0:T(8,128)S(1)}, u32[]{:S(2)}, u32[]{:S(2)}) collective-permute-start(f32[8,16,128]{2,1,0:T(8,128)S(1)} %add.160), channel_id=1, source_target_pairs={{0,2},{2,0},{1,3},{3,1},{4,6},{6,4},{5,7},{7,5},{8,10},{10,8},{9,1... | collective-permute-start | bytes 196616 | tf_op jit(solution)/shard_map/ppermute | solution.py:514
  60.5 1.6 %collective-permute-start.18 = (f32[32,16,128]{2,1,0:T(8,128)S(1)}, f32[32,16,128]{2,1,0:T(8,128)S(1)}, u32[]{:S(2)}, u32[]{:S(2)}) collective-permute-start(f32[32,16,128]{2,1,0:T(8,128)S(1)} %get-tuple-element.61), channel_id=1, source_target_pairs={{0,1},{1,0},{2,3},{3,2},{4,5},{5,4},{6,7},{7,6},{8,9},{9,8},{10,11... | collective-permute-start | bytes 786440 | tf_op jit(solution)/shard_map/ppermute | solution.py:469
  62.1 4.3 %collective-permute-start.19 = (f32[8,16,128]{2,1,0:T(8,128)S(1)}, f32[8,16,128]{2,1,0:T(8,128)S(1)}, u32[]{:S(2)}, u32[]{:S(2)}) collective-permute-start(f32[8,16,128]{2,1,0:T(8,128)S(1)} %get-tuple-element.98), channel_id=1, source_target_pairs={{0,4},{4,0},{8,12},{12,8},{1,5},{5,1},{9,13},{13,9},{2,6},{6,2},{1... | collective-permute-start | bytes 196616 | tf_op jit(solution)/shard_map/ppermute | solution.py:464
  62.2 7.8 %collective-permute-start.21 = (f32[8,16,128]{2,1,0:T(8,128)S(1)}, f32[8,16,128]{2,1,0:T(8,128)S(1)}, u32[]{:S(2)}, u32[]{:S(2)}) collective-permute-start(f32[8,16,128]{2,1,0:T(8,128)S(1)} %get-tuple-element.99), channel_id=1, source_target_pairs={{0,12},{4,8},{8,4},{12,0},{1,13},{5,9},{9,5},{13,1},{2,14},{6,10},... | collective-permute-start | bytes 196616 | tf_op jit(solution)/shard_map/ppermute | solution.py:464
  65.6 6.5 %collective-permute-start.20 = (f32[8,16,128]{2,1,0:T(8,128)S(1)}, f32[8,16,128]{2,1,0:T(8,128)S(1)}, u32[]{:S(2)}, u32[]{:S(2)}) collective-permute-start(f32[8,16,128]{2,1,0:T(8,128)S(1)} %get-tuple-element.100), channel_id=1, source_target_pairs={{0,8},{4,12},{8,0},{12,4},{1,9},{5,13},{9,1},{13,5},{2,10},{6,14},... | collective-permute-start | bytes 196616 | tf_op jit(solution)/shard_map/ppermute | solution.py:464
  72.1 5.8 %collective-permute-start.24 = (bf16[8,16,128]{2,1,0:T(8,128)(2,1)S(1)}, bf16[8,16,128]{2,1,0:T(8,128)(2,1)S(1)}, u32[]{:S(2)}, u32[]{:S(2)}) collective-permute-start(bf16[8,16,128]{2,1,0:T(8,128)(2,1)S(1)} %get-tuple-element.81), channel_id=1, source_target_pairs={{0,12},{4,8},{8,4},{12,0},{1,13},{5,9},{9,5},{13,1},{2,14},{6,10},... | collective-permute-start | bytes 98312 | tf_op jit(solution)/shard_map/ppermute | solution.py:464
  73.8 5.0 %collective-permute-start.23 = (bf16[8,16,128]{2,1,0:T(8,128)(2,1)S(1)}, bf16[8,16,128]{2,1,0:T(8,128)(2,1)S(1)}, u32[]{:S(2)}, u32[]{:S(2)}) collective-permute-start(bf16[8,16,128]{2,1,0:T(8,128)(2,1)S(1)} %get-tuple-element.81), channel_id=1, source_target_pairs={{0,8},{4,12},{8,0},{12,4},{1,9},{5,13},{9,1},{13,5},{2,10},{6,14},... | collective-permute-start | bytes 98312 | tf_op jit(solution)/shard_map/ppermute | solution.py:464
  73.8 5.0 %collective-permute-start.22 = (bf16[8,16,128]{2,1,0:T(8,128)(2,1)S(1)}, bf16[8,16,128]{2,1,0:T(8,128)(2,1)S(1)}, u32[]{:S(2)}, u32[]{:S(2)}) collective-permute-start(bf16[8,16,128]{2,1,0:T(8,128)(2,1)S(1)} %get-tuple-element.81), channel_id=1, source_target_pairs={{0,4},{4,0},{8,12},{12,8},{1,5},{5,1},{9,13},{13,9},{2,6},{6,2},{1... | collective-permute-start | bytes 98312 | tf_op jit(solution)/shard_map/ppermute | solution.py:464
  82.5 4.7 %collective-permute-start.27 = (f32[8,16,128]{2,1,0:T(8,128)S(1)}, f32[8,16,128]{2,1,0:T(8,128)S(1)}, u32[]{:S(2)}, u32[]{:S(2)}) collective-permute-start(f32[8,16,128]{2,1,0:T(8,128)S(1)} %add.168), channel_id=1, source_target_pairs={{0,2},{2,0},{1,3},{3,1},{4,6},{6,4},{5,7},{7,5},{8,10},{10,8},{9,1... | collective-permute-start | bytes 196616 | tf_op jit(solution)/shard_map/ppermute | solution.py:514
  89.4 1.6 %collective-permute-start.29 = (f32[32,16,128]{2,1,0:T(8,128)S(1)}, f32[32,16,128]{2,1,0:T(8,128)S(1)}, u32[]{:S(2)}, u32[]{:S(2)}) collective-permute-start(f32[32,16,128]{2,1,0:T(8,128)S(1)} %get-tuple-element.63), channel_id=1, source_target_pairs={{0,1},{1,0},{2,3},{3,2},{4,5},{5,4},{6,7},{7,6},{8,9},{9,8},{10,11... | collective-permute-start | bytes 786440 | tf_op jit(solution)/shard_map/ppermute | solution.py:469
  91.1 4.4 %collective-permute-start.30 = (f32[8,16,128]{2,1,0:T(8,128)S(1)}, f32[8,16,128]{2,1,0:T(8,128)S(1)}, u32[]{:S(2)}, u32[]{:S(2)}) collective-permute-start(f32[8,16,128]{2,1,0:T(8,128)S(1)} %get-tuple-element.95), channel_id=1, source_target_pairs={{0,4},{4,0},{8,12},{12,8},{1,5},{5,1},{9,13},{13,9},{2,6},{6,2},{1... | collective-permute-start | bytes 196616 | tf_op jit(solution)/shard_map/ppermute | solution.py:464
  92.7 6.6 %collective-permute-start.32 = (f32[8,16,128]{2,1,0:T(8,128)S(1)}, f32[8,16,128]{2,1,0:T(8,128)S(1)}, u32[]{:S(2)}, u32[]{:S(2)}) collective-permute-start(f32[8,16,128]{2,1,0:T(8,128)S(1)} %get-tuple-element.96), channel_id=1, source_target_pairs={{0,12},{4,8},{8,4},{12,0},{1,13},{5,9},{9,5},{13,1},{2,14},{6,10},... | collective-permute-start | bytes 196616 | tf_op jit(solution)/shard_map/ppermute | solution.py:464
  94.4 6.9 %collective-permute-start.31 = (f32[8,16,128]{2,1,0:T(8,128)S(1)}, f32[8,16,128]{2,1,0:T(8,128)S(1)}, u32[]{:S(2)}, u32[]{:S(2)}) collective-permute-start(f32[8,16,128]{2,1,0:T(8,128)S(1)} %get-tuple-element.97), channel_id=1, source_target_pairs={{0,8},{4,12},{8,0},{12,4},{1,9},{5,13},{9,1},{13,5},{2,10},{6,14},... | collective-permute-start | bytes 196616 | tf_op jit(solution)/shard_map/ppermute | solution.py:464
  101.3 5.9 %collective-permute-start.35 = (bf16[8,16,128]{2,1,0:T(8,128)(2,1)S(1)}, bf16[8,16,128]{2,1,0:T(8,128)(2,1)S(1)}, u32[]{:S(2)}, u32[]{:S(2)}) collective-permute-start(bf16[8,16,128]{2,1,0:T(8,128)(2,1)S(1)} %get-tuple-element.79), channel_id=1, source_target_pairs={{0,12},{4,8},{8,4},{12,0},{1,13},{5,9},{9,5},{13,1},{2,14},{6,10},... | collective-permute-start | bytes 98312 | tf_op jit(solution)/shard_map/ppermute | solution.py:464
  103.2 4.8 %collective-permute-start.34 = (bf16[8,16,128]{2,1,0:T(8,128)(2,1)S(1)}, bf16[8,16,128]{2,1,0:T(8,128)(2,1)S(1)}, u32[]{:S(2)}, u32[]{:S(2)}) collective-permute-start(bf16[8,16,128]{2,1,0:T(8,128)(2,1)S(1)} %get-tuple-element.79), channel_id=1, source_target_pairs={{0,8},{4,12},{8,0},{12,4},{1,9},{5,13},{9,1},{13,5},{2,10},{6,14},... | collective-permute-start | bytes 98312 | tf_op jit(solution)/shard_map/ppermute | solution.py:464
  103.2 4.8 %collective-permute-start.33 = (bf16[8,16,128]{2,1,0:T(8,128)(2,1)S(1)}, bf16[8,16,128]{2,1,0:T(8,128)(2,1)S(1)}, u32[]{:S(2)}, u32[]{:S(2)}) collective-permute-start(bf16[8,16,128]{2,1,0:T(8,128)(2,1)S(1)} %get-tuple-element.79), channel_id=1, source_target_pairs={{0,4},{4,0},{8,12},{12,8},{1,5},{5,1},{9,13},{13,9},{2,6},{6,2},{1... | collective-permute-start | bytes 98312 | tf_op jit(solution)/shard_map/ppermute | solution.py:464
  111.7 4.8 %collective-permute-start.38 = (f32[8,16,128]{2,1,0:T(8,128)S(1)}, f32[8,16,128]{2,1,0:T(8,128)S(1)}, u32[]{:S(2)}, u32[]{:S(2)}) collective-permute-start(f32[8,16,128]{2,1,0:T(8,128)S(1)} %add.176), channel_id=1, source_target_pairs={{0,2},{2,0},{1,3},{3,1},{4,6},{6,4},{5,7},{7,5},{8,10},{10,8},{9,1... | collective-permute-start | bytes 196616 | tf_op jit(solution)/shard_map/ppermute | solution.py:514
  118.7 1.6 %collective-permute-start.40 = (f32[32,16,128]{2,1,0:T(8,128)S(1)}, f32[32,16,128]{2,1,0:T(8,128)S(1)}, u32[]{:S(2)}, u32[]{:S(2)}) collective-permute-start(f32[32,16,128]{2,1,0:T(8,128)S(1)} %get-tuple-element.65), channel_id=1, source_target_pairs={{0,1},{1,0},{2,3},{3,2},{4,5},{5,4},{6,7},{7,6},{8,9},{9,8},{10,11... | collective-permute-start | bytes 786440 | tf_op jit(solution)/shard_map/ppermute | solution.py:469
  120.4 4.3 %collective-permute-start.41 = (f32[8,16,128]{2,1,0:T(8,128)S(1)}, f32[8,16,128]{2,1,0:T(8,128)S(1)}, u32[]{:S(2)}, u32[]{:S(2)}) collective-permute-start(f32[8,16,128]{2,1,0:T(8,128)S(1)} %get-tuple-element.92), channel_id=1, source_target_pairs={{0,4},{4,0},{8,12},{12,8},{1,5},{5,1},{9,13},{13,9},{2,6},{6,2},{1... | collective-permute-start | bytes 196616 | tf_op jit(solution)/shard_map/ppermute | solution.py:464
  121.8 6.5 %collective-permute-start.43 = (f32[8,16,128]{2,1,0:T(8,128)S(1)}, f32[8,16,128]{2,1,0:T(8,128)S(1)}, u32[]{:S(2)}, u32[]{:S(2)}) collective-permute-start(f32[8,16,128]{2,1,0:T(8,128)S(1)} %get-tuple-element.93), channel_id=1, source_target_pairs={{0,12},{4,8},{8,4},{12,0},{1,13},{5,9},{9,5},{13,1},{2,14},{6,10},... | collective-permute-start | bytes 196616 | tf_op jit(solution)/shard_map/ppermute | solution.py:464
  123.8 6.6 %collective-permute-start.42 = (f32[8,16,128]{2,1,0:T(8,128)S(1)}, f32[8,16,128]{2,1,0:T(8,128)S(1)}, u32[]{:S(2)}, u32[]{:S(2)}) collective-permute-start(f32[8,16,128]{2,1,0:T(8,128)S(1)} %get-tuple-element.94), channel_id=1, source_target_pairs={{0,8},{4,12},{8,0},{12,4},{1,9},{5,13},{9,1},{13,5},{2,10},{6,14},... | collective-permute-start | bytes 196616 | tf_op jit(solution)/shard_map/ppermute | solution.py:464
  (20 other events, 45.1 us)

commit v7 on v6

--- a/solution.py
+++ b/solution.py
@@ -25,76 +25,89 @@
     return pltpu.with_memory_space_constraint(array, pltpu.VMEM)
 
 
-def index_kernel(n_vox, columns, runs, steps, me, cols, exps, live, *outs):
+RUN = 4
+
+
+def cut_of(slots):
+    return 2 * slots // 3
+
+
+def index_kernel(n_vox, columns, runs, steps, me, cols, exps, live, after, *refs):
+    outs, sides, packed, *tables, sems = refs[:5], *refs[5:]
     z, core = me[0], me[1]
     rows, _, slots = cols.shape
     own = columns // (2 * n_vox)
     column, exponent = cols[:, 0, :], exps[:, 0, :]
     piece, within = lax.div(column, own), lax.rem(column, own)
     place = ((lax.rem(piece, 2) ^ core) * n_vox + (lax.div(piece, 2) ^ z)) * own + within
-    scale = jnp.where(exponent < 0, 0.5, jnp.where(exponent > 0, 2.0, 1.0))
-    scaled = (exponent + 1) * columns + place
+    both = place * 4 + exponent + 1
     position = core * slots + lax.broadcasted_iota(jnp.int32, (1, slots), 1)
     n = rows // (2 * runs)
-    index, places, factor = outs[:3]
     for r in range(rows):
         half, t = divmod(r, rows // 2)
         first = 2 * n * (t // n) + t % n
         low, high = (first, first + n) if half == 0 else (first + n, first)
-
-        def row(array):
-            return jnp.where(core == 0, array[low : low + 1], array[high : high + 1])
-
+        row = jnp.where(core == 0, both[low : low + 1], both[high : high + 1])
         used = position < jnp.where(core == 0, live[low], live[high])
-        places[r : r + 1] = row(place)
-        index[r : r + 1] = jnp.where(used, row(scaled), 3 * columns)
-        factor[r : r + 1] = jnp.where(used, row(scale), 0.0).astype(F32)
-    sides = outs[-1]
+        packed[r : r + 1] = jnp.where(used, row, 3)
+
+    both = packed[...]
+    here = lax.broadcasted_iota(jnp.int32, (rows, slots), 1)
+    dead = lax.rem(both, 4) == 3
+    kind = jnp.where(dead, 2, jnp.where(both >= 2 * columns, 0, 1))
+    key = kind * slots + here
+    rank = jnp.zeros_like(key)
+    for k in range(slots):
+        rank = rank + jnp.where(key[:, k : k + 1] < key, 1, 0)
+    both = jnp.where(dead, (columns + rank) * 4 + 3, both) * 64 + here
+    ordered = jnp.zeros_like(key)
+    for k in range(slots):
+        ordered = ordered + jnp.where(rank[:, k : k + 1] == here, both[:, k : k + 1], 0)
+    kind, place = lax.rem(lax.div(ordered, 64), 4), lax.div(ordered, 256)
+    slot, index, places, factor, over = tables
+    in_half = lax.rem(lax.broadcasted_iota(jnp.int32, (rows, slots), 0), rows // 2)
+    slot[...] = in_half * slots + lax.rem(ordered, 64)
+    index[...] = jnp.where(kind == 3, 3 * columns, kind * columns + place)
+    places[...] = place
+    factor[...] = jnp.where(
+        kind == 3, 0.0, jnp.where(kind == 0, 0.5, jnp.where(kind == 2, 2.0, 1.0))
+    ).astype(F32)
+    others = jnp.where((kind != 3) & (place >= columns // 2), 1.0, 0.0).astype(F32)
+    others = jnp.sum(others, axis=1, keepdims=True)
+    for r in range(rows // RUN):
+        most = jnp.max(others[r * RUN : (r + 1) * RUN], axis=0, keepdims=True)
+        most = jnp.broadcast_to(most, (1, over.shape[1]))
+        over[r : r + 1] = jnp.where(most > cut_of(slots), 1, 0)
+    copies = [
+        pltpu.make_async_copy(table, out, sems.at[i])
+        for i, (table, out) in enumerate(zip(tables, outs, strict=True))
+    ]
+    for copy in copies:
+        copy.start()
     for e, (at, bit) in enumerate(steps):
         side = jnp.where((me[at] & bit) == 0, 1.0, 0.0).astype(F32)
         sides[e] = jnp.full(sides.shape[1:], side)
-
-
-def indices(n_vox, columns, runs, steps, me, cols, exps, live):
+    for copy in copies:
+        copy.wait()
+
+
+def indices(n_vox, columns, runs, steps, me, cols, exps, live, after):
     rows, _, slots = cols.shape
-    out = [jax.ShapeDtypeStruct((rows, slots), t) for t in (jnp.int32, jnp.int32, F32)]
-    out.append(jax.ShapeDtypeStruct((len(steps), 8, 128), F32))
+    shapes = [((rows, slots), t) for t in (jnp.int32, jnp.int32, jnp.int32, F32)]
+    shapes.append(((rows // RUN, 128), jnp.int32))
     return pl.pallas_call(
         functools.partial(index_kernel, n_vox, columns, runs, steps),
-        in_specs=[in_smem()] + [in_vmem()] * 2 + [in_smem()],
-        out_specs=[in_vmem()] * len(out),
-        out_shape=out,
-        compiler_params=PARAMS,
+        in_specs=[in_smem()] + [in_vmem()] * 2 + [in_smem(), pl.BlockSpec(memory_space=pl.ANY)],
+        out_specs=[in_smem()] * 5 + [in_vmem()],
+        out_shape=[pltpu.SMEM(*shape) for shape in shapes]
+        + [jax.ShapeDtypeStruct((len(steps), 8, 128), F32)],
+        scratch_shapes=[pltpu.VMEM((rows, slots), jnp.int32)]
+        + [pltpu.VMEM(*shape) for shape in shapes]
+        + [pltpu.SemaphoreType.DMA((len(shapes),))],
+        compiler_params=PARAMS,
+        cost_estimate=pl.CostEstimate(flops=0, bytes_accessed=2**21, transcendentals=0),
         name="indices",
-    )(me, *(pltpu.with_memory_space_constraint(a, pltpu.HBM) for a in (cols, exps)), live)
-
-
-RUN = 4
-
-
-def cut_of(slots):
-    return 2 * slots // 3
-
-
-def sort_slots(index, places, factor, columns):
-    rows, slots = index.shape
-    here = jnp.arange(slots, dtype=jnp.int32)
-    dead = factor == 0
-    kind = jnp.where(dead, 2, jnp.where(places >= columns // 2, 0, 1))
-    key = kind * slots + here
-    rank = jnp.sum((key[:, None, :] < key[:, :, None]).astype(jnp.int32), axis=-1)
-    chosen = rank[:, None, :] == here[None, :, None]
-
-    def pick(array):
-        return jnp.sum(jnp.where(chosen, array[:, None, :], 0), axis=-1)
-
-    row = jnp.arange(rows, dtype=jnp.int32)[:, None] % (rows // 2)
-    slot = pick(row * slots + here)
-    places = pick(jnp.where(dead, columns + rank, places))
-    others = jnp.sum((kind == 0).astype(jnp.int32), axis=1)
-    over = jnp.max(others.reshape(-1, RUN), axis=1, keepdims=True) > cut_of(slots)
-    over = jnp.broadcast_to(over.astype(jnp.int32), (rows // RUN, 128))
-    return slot, pick(index), places, pick(factor), over
+    )(me, *(pltpu.with_memory_space_constraint(a, pltpu.HBM) for a in (cols, exps)), live, after)
 
 
 def turn_kernel(kept, after, turned):
@@ -153,21 +166,8 @@
     ]
 
 
-def load_kernel(runs, count, me, stored, *refs):
-    tables, kept, me_out, outs, sems, table_sems = (
-        refs[:count],
-        refs[count],
-        refs[count + 1],
-        refs[count + 2 : 2 * count + 2],
-        refs[-2],
-        refs[-1],
-    )
-    slots = tables[0].shape[1]
+def load_kernel(runs, slots, me, stored, kept, me_out, sems):
     copies = row_copies(False, runs, slots, me, stored, kept, sems)
-    copies += [
-        pltpu.make_async_copy(table, out, table_sems.at[i])
-        for i, (table, out) in enumerate(zip(tables, outs, strict=True))
-    ]
     for copy in copies:
         copy.start()
     for i in range(me.shape[0]):
@@ -176,23 +176,18 @@
         copy.wait()
 
 
-def load_others(runs, me, tables, tiles):
-    rows = tables[0].shape[0]
+def load_others(runs, rows, me, tiles):
     shape = (tiles.shape[0] // 2,) + tiles.shape[1:]
     return pl.pallas_call(
-        functools.partial(load_kernel, runs, len(tables)),
-        in_specs=[in_smem(), pl.BlockSpec(memory_space=pltpu.HBM)] + [in_vmem()] * len(tables),
-        out_specs=[in_vmem()] + [in_smem()] * (len(tables) + 1),
-        out_shape=[pltpu.VMEM(shape, tiles.dtype)]
-        + [pltpu.SMEM(t.shape, t.dtype) for t in (me, *tables)],
-        scratch_shapes=[
-            pltpu.SemaphoreType.DMA((rows // 2,)),
-            pltpu.SemaphoreType.DMA((len(tables),)),
-        ],
+        functools.partial(load_kernel, runs, tiles.shape[0] // rows),
+        in_specs=[in_smem(), pl.BlockSpec(memory_space=pltpu.HBM)],
+        out_specs=[in_vmem(), in_smem()],
+        out_shape=[pltpu.VMEM(shape, tiles.dtype), pltpu.SMEM(me.shape, me.dtype)],
+        scratch_shapes=[pltpu.SemaphoreType.DMA((rows // 2,))],
         compiler_params=PARAMS,
         cost_estimate=pl.CostEstimate(flops=0, bytes_accessed=2 * tiles.size, transcendentals=0),
         name="load_others",
-    )(me, pltpu.with_memory_space_constraint(tiles, pltpu.HBM), *tables)
+    )(me, pltpu.with_memory_space_constraint(tiles, pltpu.HBM))
 
 
 def first_forward_kernel(runs, me, slot, index, *refs):
@@ -470,7 +465,6 @@
 
     me = jnp.stack([z, core, x]).astype(jnp.int32)
     level_table = jnp.stack([upper_dose, upper_weight, lower_dose, lower_weight])
-    known = labels.astype(F32).reshape(-1, width)
     tiles = dose_blocks.reshape(rows * slots, width, width)
 
     def gather_weights(weights):
@@ -478,28 +472,26 @@
         return [piece] + over_vox([piece] * (n_vox - 1))
 
     bits = [1 << i for i in range(n_spot.bit_length() - 1)]
-    *unsorted, sides = indices(
-        n_vox,
-        columns,
-        n_spot,
-        [(1, 1)] + [(2, bit) for bit in bits],
-        me,
-        block_cols,
-        block_exps,
-        live_counts.reshape(rows),
+    pieces = gather_weights(weights)
+    kept_others, me = load_others(n_spot, rows, me, tiles)
+    pieces, kept_others = lax.optimization_barrier((pieces, kept_others))
+    steps = [(1, 1)] + [(2, bit) for bit in bits]
+    near = jnp.concatenate(pieces, axis=0)
+    live = live_counts.reshape(rows)
+    *tables, sides = indices(
+        n_vox, columns, n_spot, steps, me, block_cols, block_exps, live, near
     )
-    tables = sort_slots(*unsorted, columns)
-    pieces = gather_weights(weights)
-    kept_others, me, *tables = load_others(n_spot, me, tables, tiles)
-    pieces, kept_others = lax.optimization_barrier((pieces, kept_others))
 
     for step in range(ITERS):
-        near = jnp.concatenate(pieces, axis=0)
+        if step > 0:
+            near = jnp.concatenate(pieces, axis=0)
         other_half = over_rep(near)
         if step == 0:
             given, dose, kept_mine = first_forward(
                 n_spot, me, tables, [near, other_half], kept_others, tiles
             )
+            labels, given = lax.optimization_barrier((labels, given))
+            known = labels.astype(F32).reshape(-1, width)
         else:
             part = near_forward(tables, near, turned_mine, turned_others)
             given = forward(rows // 2, tables, near, other_half, turned_others, part)
@@ -536,15 +528,19 @@
         near = near_backward(tables, slope, slope_others, kept_mine, kept_others, near) + theirs
         received = over_vox([near[d * own : (d + 1) * own] for d in range(1, n_vox)])
         if step == 0:
-            turned = [turn(kept_others, near), turn(kept_mine, near)]
-            received, turned = lax.optimization_barrier((received, turned))
-            turned_others, turned_mine = turned
+            turned_mine = turn(kept_mine, near)
+            received, turned_mine = lax.optimization_barrier((received, turned_mine))
+        else:
+            received = lax.optimization_barrier(received)
         gradient = near[:own]
         for part in received:
             gradient = gradient + part
         weights = jnp.maximum(weights - 0.5 * gradient, 0.0)
         if step < ITERS - 1:
             pieces = gather_weights(weights)
+            if step == 0:
+                turned_others = turn(kept_others, pieces[0])
+                pieces, turned_others = lax.optimization_barrier((pieces, turned_others))
 
     mine = jnp.stack([weights, gradient])
     other = over_rep(mine)

time: 134 us -> 128 us (0.955)
  waiting for transfers between devices: 43.9 us -> 41 us
  other arithmetic: 2.61 us -> 0.81 us
  Pallas kernels: 36.3 us -> 37.8 us
    ppermute x24, waiting for transfers between devices: 28.2 us -> 22.7 us  [over_vox(): lax.ppermute(a, 'vox', [(i, i ^ d) for i in range(n_vox)])]
    ppermute x4, starting transfers between devices: 8.27 us -> 4.53 us  [per_device(): got = lax.ppermute(sent, 'spot', [(i, i ^ bit) for i in range(n_spot)])]
    ppermute x4, waiting for transfers between devices: 9.72 us -> 13 us  [per_device(): got = lax.ppermute(sent, 'spot', [(i, i ^ bit) for i in range(n_spot)])]
    ppermute x24, starting transfers between devices: 34.2 us -> 36.9 us  [over_vox(): lax.ppermute(a, 'vox', [(i, i ^ d) for i in range(n_vox)])]
    reduce_sum x4 -> x0, other arithmetic: 1.57 us -> none  [the longest x2 1.02 us: pick(): return jnp.sum(jnp.where(chosen, array[:, None, :], 0), axis=-1)]
    pallas_call x1, Pallas kernels: 0.81 us -> 2.31 us  [indices(): pl.pallas_call(functools.partial(index_kernel, n_vox, columns, runs, step...]
  transfers between devices with their start and end apart: 45 -> 45, of which waited for: 34 -> 25; matrix products, arithmetic and copies ran while one was open for 2% -> 0% of each run, Pallas kernels for 18% -> 20%
where the time goes in v7:
time: 128 us
  starting transfers between devices  44.7 us (35%)
  waiting for transfers between devices  41 us (32%)
  Pallas kernels  37.8 us (30%)
  local copies, waits for them, and re-layouts  2.79 us (2%)
    ppermute x24, starting transfers between devices, over_vox(): lax.ppermute(a, 'vox', [(i, i ^ d) for i in range(n_vox)])  36.9 us
    ppermute x24, waiting for transfers between devices, over_vox(): lax.ppermute(a, 'vox', [(i, i ^ d) for i in range(n_vox)])  22.7 us
    ppermute x4, waiting for transfers between devices, per_device(): got = lax.ppermute(sent, 'spot', [(i, i ^ bit) for i in range(n_spot)])  13 us
    pallas_call x8, Pallas kernels, backward(): pl.pallas_call(functools.partial(backward_kernel, mine, row0), in_specs=[...  8.41 us
    pallas_call x6, Pallas kernels, forward(): pl.pallas_call(functools.partial(forward_kernel, row0), in_specs=[in_smem...  6.1 us
    pallas_call x2, Pallas kernels, turn(): pl.pallas_call(turn_kernel, in_specs=[in_vmem(), pl.BlockSpec(memory_spac...  5.85 us
    pallas_call x1, Pallas kernels, first_forward(): pl.pallas_call(functools.partial(first_forward_kernel, runs), in_specs=[i...  5.39 us
    ppermute x17, waiting for transfers between devices, over_rep(): return lax.ppermute(array, 'rep', [(0, 1), (1, 0)])  5.27 us
  transfers between devices with their start and end apart: 45, of which 25 were waited for; matrix products, arithmetic and copies ran while one was open for 0% of the time, Pallas kernels for 20%

profile of v7, /device:TPU:0, one launch (start us, length us, event | category | flops | bytes accessed | tf_op | source)
XLA Modules:
  0.0 128.4 jit_solution(18328956024910403770)
XLA Ops:
  1.6 5.1 %collective-permute-start.2 = (bf16[8,16,128]{2,1,0:T(8,128)(2,1)S(1)}, bf16[8,16,128]{2,1,0:T(8,128)(2,1)S(1)}, u32[]{:S(2)}, u32[]{:S(2)}) collective-permute-start(bf16[8,16,128]{2,1,0:T(8,128)(2,1)S(1)} %bitcast.57), channel_id=1, source_target_pairs={{0,12},{4,8},{8,4},{12,0},{1,13},{5,9},{9,5},{13,1},{2,14},{6,10},... | collective-permute-start | bytes 98312 | tf_op jit(solution)/shard_map/ppermute | solution.py:459
  7.4 3.4 %load_others.1 = (bf16[192,128,128]{2,1,0:T(8,128)(2,1)S(1)}, s32[3]{0:T(128)S(4)}) custom-call(s32[3]{0:T(128)S(1)} %pad_add_fusion.me, bf16[384,128,128]{2,1,0:T(8,128)(2,1)} %bitcast.53), custom_call_target="tpu_custom_call" | custom-call | bytes 12582912 | tf_op jit(solution)/shard_map/load_others/pallas_call | solution.py:181
  12.0 2.3 %indices.1 = (s32[16,24]{1,0:T(8,128)S(4)}, s32[16,24]{1,0:T(8,128)S(4)}, s32[16,24]{1,0:T(8,128)S(4)}, f32[16,24]{1,0:T(8,128)S(4)}, s32[4,128]{1,0:T(4,128)S(4)}, /*index=5*/f32[2,8,128]{2,1,0:T(8,128)S(1)}) custom-call(s32[3]{0:T(128)S(4)} %get-tuple-element.46.me, s32[16,1,24]{2,1,0:T(1,128)} %cols.1, s32[16,1,24]{2,1,0:T(1,128)} %exps.1, ...), custom_call_target="tpu_custom_call" | custom-call | bytes 2097152 | tf_op jit(solution)/shard_map/indices/pallas_call | solution.py:98
  14.3 5.4 %first_forward.1 = (f32[8,16,128]{2,1,0:T(8,128)S(1)}, f32[8,16,128]{2,1,0:T(8,128)S(1)}, bf16[192,128,128]{2,1,0:T(8,128)(2,1)S(1)}) custom-call(s32[3]{0:T(128)S(4)} %get-tuple-element.46.me, s32[16,24]{1,0:T(8,128)S(4)} %get-tuple-element.53.slot, s32[16,24]{1,0:T(8,128)S(4)} %get-tuple-element.57.index, ...), custom_call_target="tpu_custom_call" | custom-call | flops 201326592 | bytes 12582912 | tf_op jit(solution)/shard_map/first_forward/pallas_call | solution.py:311
  22.8 3.0 %collective-permute-done.5 = f32[9,16,128]{2,1,0:T(8,128)S(1)} collective-permute-done((f32[9,16,128]{2,1,0:T(8,128)S(1)}, f32[9,16,128]{2,1,0:T(8,128)S(1)}, u32[]{:S(2)}, u32[]{:S(2)}) %collective-permute-start.5) | collective-permute-done | bytes 73760 | tf_op jit(solution)/shard_map/ppermute | solution.py:506
  30.0 3.1 %collective-permute-start.10 = (f32[8,16,128]{2,1,0:T(8,128)S(1)}, f32[8,16,128]{2,1,0:T(8,128)S(1)}, u32[]{:S(2)}, u32[]{:S(2)}) collective-permute-start(f32[8,16,128]{2,1,0:T(8,128)S(1)} %get-tuple-element.119), channel_id=1, source_target_pairs={{0,12},{4,8},{8,4},{12,0},{1,13},{5,9},{9,5},{13,1},{2,14},{6,10},... | collective-permute-start | bytes 196616 | tf_op jit(solution)/shard_map/ppermute | solution.py:459
  34.4 2.9 %turn.2.turned_mine.turned = bf16[192,128,128]{2,1,0:T(8,128)(2,1)S(1)} custom-call(bf16[192,128,128]{2,1,0:T(8,128)(2,1)S(1)} %get-tuple-element.63.kept.kept_mine, f32[32,16,128]{2,1,0:T(8,128)S(1)} %add.106.after), custom_call_target="tpu_custom_call" | custom-call | bytes 12582912 | tf_op jit(solution)/shard_map/turn/pallas_call | solution.py:126
  37.4 1.6 %collective-permute-done.9 = f32[8,16,128]{2,1,0:T(8,128)S(1)} collective-permute-done((f32[8,16,128]{2,1,0:T(8,128)S(1)}, f32[8,16,128]{2,1,0:T(8,128)S(1)}, u32[]{:S(2)}, u32[]{:S(2)}) %collective-permute-start.9) | collective-permute-done | bytes 65568 | tf_op jit(solution)/shard_map/ppermute | solution.py:459
  39.1 2.6 %collective-permute-start.13 = (bf16[8,16,128]{2,1,0:T(8,128)(2,1)S(1)}, bf16[8,16,128]{2,1,0:T(8,128)(2,1)S(1)}, u32[]{:S(2)}, u32[]{:S(2)}) collective-permute-start(bf16[8,16,128]{2,1,0:T(8,128)(2,1)S(1)} %get-tuple-element.69.after), channel_id=1, source_target_pairs={{0,12},{4,8},{8,4},{12,0},{1,13},{5,9},{9,5},{13,1},{2,14},{6,10},... | collective-permute-start | bytes 98312 | tf_op jit(solution)/shard_map/ppermute | solution.py:459
  41.8 1.7 %collective-permute-start.11 = (bf16[8,16,128]{2,1,0:T(8,128)(2,1)S(1)}, bf16[8,16,128]{2,1,0:T(8,128)(2,1)S(1)}, u32[]{:S(2)}, u32[]{:S(2)}) collective-permute-start(bf16[8,16,128]{2,1,0:T(8,128)(2,1)S(1)} %get-tuple-element.69.after), channel_id=1, source_target_pairs={{0,4},{4,0},{8,12},{12,8},{1,5},{5,1},{9,13},{13,9},{2,6},{6,2},{1... | collective-permute-start | bytes 98312 | tf_op jit(solution)/shard_map/ppermute | solution.py:459
  43.5 2.9 %turn.3.turned_others.turned = bf16[192,128,128]{2,1,0:T(8,128)(2,1)S(1)} custom-call(bf16[192,128,128]{2,1,0:T(8,128)(2,1)S(1)} %get-tuple-element.58.refs_2_.kept.kept_others, bf16[8,16,128]{2,1,0:T(8,128)(2,1)S(1)} %get-tuple-element.69.after), custom_call_target="tpu_custom_call" | custom-call | bytes 12582912 | tf_op jit(solution)/shard_map/turn/pallas_call | solution.py:126
  51.7 3.0 %collective-permute-done.16 = f32[8,16,128]{2,1,0:T(8,128)S(1)} collective-permute-done((f32[8,16,128]{2,1,0:T(8,128)S(1)}, f32[8,16,128]{2,1,0:T(8,128)S(1)}, u32[]{:S(2)}, u32[]{:S(2)}) %collective-permute-start.16) | collective-permute-done | bytes 65568 | tf_op jit(solution)/shard_map/ppermute | solution.py:506
  58.6 2.4 %collective-permute-start.21 = (f32[8,16,128]{2,1,0:T(8,128)S(1)}, f32[8,16,128]{2,1,0:T(8,128)S(1)}, u32[]{:S(2)}, u32[]{:S(2)}) collective-permute-start(f32[8,16,128]{2,1,0:T(8,128)S(1)} %get-tuple-element.116), channel_id=1, source_target_pairs={{0,12},{4,8},{8,4},{12,0},{1,13},{5,9},{9,5},{13,1},{2,14},{6,10},... | collective-permute-start | bytes 196616 | tf_op jit(solution)/shard_map/ppermute | solution.py:459
  61.4 1.7 %collective-permute-start.19 = (f32[8,16,128]{2,1,0:T(8,128)S(1)}, f32[8,16,128]{2,1,0:T(8,128)S(1)}, u32[]{:S(2)}, u32[]{:S(2)}) collective-permute-start(f32[8,16,128]{2,1,0:T(8,128)S(1)} %get-tuple-element.118), channel_id=1, source_target_pairs={{0,4},{4,0},{8,12},{12,8},{1,5},{5,1},{9,13},{13,9},{2,6},{6,2},{1... | collective-permute-start | bytes 196616 | tf_op jit(solution)/shard_map/ppermute | solution.py:459
  63.0 2.1 %collective-permute-done.21 = f32[8,16,128]{2,1,0:T(8,128)S(1)} collective-permute-done((f32[8,16,128]{2,1,0:T(8,128)S(1)}, f32[8,16,128]{2,1,0:T(8,128)S(1)}, u32[]{:S(2)}, u32[]{:S(2)}) %collective-permute-start.21) | collective-permute-done | bytes 65568 | tf_op jit(solution)/shard_map/ppermute | solution.py:459
  65.2 2.7 %collective-permute-done.20 = f32[8,16,128]{2,1,0:T(8,128)S(1)} collective-permute-done((f32[8,16,128]{2,1,0:T(8,128)S(1)}, f32[8,16,128]{2,1,0:T(8,128)S(1)}, u32[]{:S(2)}, u32[]{:S(2)}) %collective-permute-start.20) | collective-permute-done | bytes 65568 | tf_op jit(solution)/shard_map/ppermute | solution.py:459
  67.9 2.6 %collective-permute-start.24 = (bf16[8,16,128]{2,1,0:T(8,128)(2,1)S(1)}, bf16[8,16,128]{2,1,0:T(8,128)(2,1)S(1)}, u32[]{:S(2)}, u32[]{:S(2)}) collective-permute-start(bf16[8,16,128]{2,1,0:T(8,128)(2,1)S(1)} %get-tuple-element.102), channel_id=1, source_target_pairs={{0,12},{4,8},{8,4},{12,0},{1,13},{5,9},{9,5},{13,1},{2,14},{6,10},... | collective-permute-start | bytes 98312 | tf_op jit(solution)/shard_map/ppermute | solution.py:459
  70.4 1.9 %collective-permute-start.22 = (bf16[8,16,128]{2,1,0:T(8,128)(2,1)S(1)}, bf16[8,16,128]{2,1,0:T(8,128)(2,1)S(1)}, u32[]{:S(2)}, u32[]{:S(2)}) collective-permute-start(bf16[8,16,128]{2,1,0:T(8,128)(2,1)S(1)} %get-tuple-element.102), channel_id=1, source_target_pairs={{0,4},{4,0},{8,12},{12,8},{1,5},{5,1},{9,13},{13,9},{2,6},{6,2},{1... | collective-permute-start | bytes 98312 | tf_op jit(solution)/shard_map/ppermute | solution.py:459
  73.7 1.6 %collective-permute-done.23 = bf16[8,16,128]{2,1,0:T(8,128)(2,1)S(1)} collective-permute-done((bf16[8,16,128]{2,1,0:T(8,128)(2,1)S(1)}, bf16[8,16,128]{2,1,0:T(8,128)(2,1)S(1)}, u32[]{:S(2)}, u32[]{:S(2)}) %collective-permute-start.23) | collective-permute-done | bytes 32800 | tf_op jit(solution)/shard_map/ppermute | solution.py:459
  80.0 3.4 %collective-permute-done.27 = f32[8,16,128]{2,1,0:T(8,128)S(1)} collective-permute-done((f32[8,16,128]{2,1,0:T(8,128)S(1)}, f32[8,16,128]{2,1,0:T(8,128)S(1)}, u32[]{:S(2)}, u32[]{:S(2)}) %collective-permute-start.27) | collective-permute-done | bytes 65568 | tf_op jit(solution)/shard_map/ppermute | solution.py:506
  87.3 1.7 %collective-permute-start.32 = (f32[8,16,128]{2,1,0:T(8,128)S(1)}, f32[8,16,128]{2,1,0:T(8,128)S(1)}, u32[]{:S(2)}, u32[]{:S(2)}) collective-permute-start(f32[8,16,128]{2,1,0:T(8,128)S(1)} %get-tuple-element.113), channel_id=1, source_target_pairs={{0,12},{4,8},{8,4},{12,0},{1,13},{5,9},{9,5},{13,1},{2,14},{6,10},... | collective-permute-start | bytes 196616 | tf_op jit(solution)/shard_map/ppermute | solution.py:459
  90.1 1.6 %collective-permute-start.30 = (f32[8,16,128]{2,1,0:T(8,128)S(1)}, f32[8,16,128]{2,1,0:T(8,128)S(1)}, u32[]{:S(2)}, u32[]{:S(2)}) collective-permute-start(f32[8,16,128]{2,1,0:T(8,128)S(1)} %get-tuple-element.115), channel_id=1, source_target_pairs={{0,4},{4,0},{8,12},{12,8},{1,5},{5,1},{9,13},{13,9},{2,6},{6,2},{1... | collective-permute-start | bytes 196616 | tf_op jit(solution)/shard_map/ppermute | solution.py:459
  91.8 2.2 %collective-permute-done.32 = f32[8,16,128]{2,1,0:T(8,128)S(1)} collective-permute-done((f32[8,16,128]{2,1,0:T(8,128)S(1)}, f32[8,16,128]{2,1,0:T(8,128)S(1)}, u32[]{:S(2)}, u32[]{:S(2)}) %collective-permute-start.32) | collective-permute-done | bytes 65568 | tf_op jit(solution)/shard_map/ppermute | solution.py:459
  94.0 2.7 %collective-permute-done.31 = f32[8,16,128]{2,1,0:T(8,128)S(1)} collective-permute-done((f32[8,16,128]{2,1,0:T(8,128)S(1)}, f32[8,16,128]{2,1,0:T(8,128)S(1)}, u32[]{:S(2)}, u32[]{:S(2)}) %collective-permute-start.31) | collective-permute-done | bytes 65568 | tf_op jit(solution)/shard_map/ppermute | solution.py:459
  96.7 2.6 %collective-permute-start.35 = (bf16[8,16,128]{2,1,0:T(8,128)(2,1)S(1)}, bf16[8,16,128]{2,1,0:T(8,128)(2,1)S(1)}, u32[]{:S(2)}, u32[]{:S(2)}) collective-permute-start(bf16[8,16,128]{2,1,0:T(8,128)(2,1)S(1)} %get-tuple-element.100), channel_id=1, source_target_pairs={{0,12},{4,8},{8,4},{12,0},{1,13},{5,9},{9,5},{13,1},{2,14},{6,10},... | collective-permute-start | bytes 98312 | tf_op jit(solution)/shard_map/ppermute | solution.py:459
  99.3 1.9 %collective-permute-start.33 = (bf16[8,16,128]{2,1,0:T(8,128)(2,1)S(1)}, bf16[8,16,128]{2,1,0:T(8,128)(2,1)S(1)}, u32[]{:S(2)}, u32[]{:S(2)}) collective-permute-start(bf16[8,16,128]{2,1,0:T(8,128)(2,1)S(1)} %get-tuple-element.100), channel_id=1, source_target_pairs={{0,4},{4,0},{8,12},{12,8},{1,5},{5,1},{9,13},{13,9},{2,6},{6,2},{1... | collective-permute-start | bytes 98312 | tf_op jit(solution)/shard_map/ppermute | solution.py:459
  102.5 1.6 %collective-permute-done.34 = bf16[8,16,128]{2,1,0:T(8,128)(2,1)S(1)} collective-permute-done((bf16[8,16,128]{2,1,0:T(8,128)(2,1)S(1)}, bf16[8,16,128]{2,1,0:T(8,128)(2,1)S(1)}, u32[]{:S(2)}, u32[]{:S(2)}) %collective-permute-start.34) | collective-permute-done | bytes 32800 | tf_op jit(solution)/shard_map/ppermute | solution.py:459
  108.7 3.6 %collective-permute-done.38 = f32[8,16,128]{2,1,0:T(8,128)S(1)} collective-permute-done((f32[8,16,128]{2,1,0:T(8,128)S(1)}, f32[8,16,128]{2,1,0:T(8,128)S(1)}, u32[]{:S(2)}, u32[]{:S(2)}) %collective-permute-start.38) | collective-permute-done | bytes 65568 | tf_op jit(solution)/shard_map/ppermute | solution.py:506
  116.1 1.6 %collective-permute-start.43 = (f32[8,16,128]{2,1,0:T(8,128)S(1)}, f32[8,16,128]{2,1,0:T(8,128)S(1)}, u32[]{:S(2)}, u32[]{:S(2)}) collective-permute-start(f32[8,16,128]{2,1,0:T(8,128)S(1)} %get-tuple-element.110), channel_id=1, source_target_pairs={{0,12},{4,8},{8,4},{12,0},{1,13},{5,9},{9,5},{13,1},{2,14},{6,10},... | collective-permute-start | bytes 196616 | tf_op jit(solution)/shard_map/ppermute | solution.py:459
  119.0 1.6 %collective-permute-start.41 = (f32[8,16,128]{2,1,0:T(8,128)S(1)}, f32[8,16,128]{2,1,0:T(8,128)S(1)}, u32[]{:S(2)}, u32[]{:S(2)}) collective-permute-start(f32[8,16,128]{2,1,0:T(8,128)S(1)} %get-tuple-element.112), channel_id=1, source_target_pairs={{0,4},{4,0},{8,12},{12,8},{1,5},{5,1},{9,13},{13,9},{2,6},{6,2},{1... | collective-permute-start | bytes 196616 | tf_op jit(solution)/shard_map/ppermute | solution.py:459
  120.6 2.1 %collective-permute-done.43 = f32[8,16,128]{2,1,0:T(8,128)S(1)} collective-permute-done((f32[8,16,128]{2,1,0:T(8,128)S(1)}, f32[8,16,128]{2,1,0:T(8,128)S(1)}, u32[]{:S(2)}, u32[]{:S(2)}) %collective-permute-start.43) | collective-permute-done | bytes 65568 | tf_op jit(solution)/shard_map/ppermute | solution.py:459
  122.7 2.7 %collective-permute-done.42 = f32[8,16,128]{2,1,0:T(8,128)S(1)} collective-permute-done((f32[8,16,128]{2,1,0:T(8,128)S(1)}, f32[8,16,128]{2,1,0:T(8,128)S(1)}, u32[]{:S(2)}, u32[]{:S(2)}) %collective-permute-start.42) | collective-permute-done | bytes 65568 | tf_op jit(solution)/shard_map/ppermute | solution.py:459
  (147 shorter events, 45.8 us)
Async XLA Ops:
  1.6 9.3 %collective-permute-start.2 = (bf16[8,16,128]{2,1,0:T(8,128)(2,1)S(1)}, bf16[8,16,128]{2,1,0:T(8,128)(2,1)S(1)}, u32[]{:S(2)}, u32[]{:S(2)}) collective-permute-start(bf16[8,16,128]{2,1,0:T(8,128)(2,1)S(1)} %bitcast.57), channel_id=1, source_target_pairs={{0,12},{4,8},{8,4},{12,0},{1,13},{5,9},{9,5},{13,1},{2,14},{6,10},... | collective-permute-start | bytes 98312 | tf_op jit(solution)/shard_map/ppermute | solution.py:459
  6.7 4.8 %collective-permute-start.1 = (bf16[8,16,128]{2,1,0:T(8,128)(2,1)S(1)}, bf16[8,16,128]{2,1,0:T(8,128)(2,1)S(1)}, u32[]{:S(2)}, u32[]{:S(2)}) collective-permute-start(bf16[8,16,128]{2,1,0:T(8,128)(2,1)S(1)} %bitcast.58), channel_id=1, source_target_pairs={{0,8},{4,12},{8,0},{12,4},{1,9},{5,13},{9,1},{13,5},{2,10},{6,14},... | collective-permute-start | bytes 98312 | tf_op jit(solution)/shard_map/ppermute | solution.py:459
  6.7 4.8 %collective-permute-start = (bf16[8,16,128]{2,1,0:T(8,128)(2,1)S(1)}, bf16[8,16,128]{2,1,0:T(8,128)(2,1)S(1)}, u32[]{:S(2)}, u32[]{:S(2)}) collective-permute-start(bf16[8,16,128]{2,1,0:T(8,128)(2,1)S(1)} %bitcast.59), channel_id=1, source_target_pairs={{0,4},{4,0},{8,12},{12,8},{1,5},{5,1},{9,13},{13,9},{2,6},{6,2},{1... | collective-permute-start | bytes 98312 | tf_op jit(solution)/shard_map/ppermute | solution.py:459
  11.5 2.8 %collective-permute-start.3 = (bf16[32,16,128]{2,1,0:T(8,128)(2,1)S(1)}, bf16[32,16,128]{2,1,0:T(8,128)(2,1)S(1)}, u32[]{:S(2)}, u32[]{:S(2)}) collective-permute-start(bf16[32,16,128]{2,1,0:T(8,128)(2,1)S(1)} %constant_dynamic-update-slice_fusion.after.refs_0_), channel_id=1, source_target_pairs={{0,1},{1,0},{2,3},{3,2},{4,5},{5,4},{6,7},{7,6},{8,9},{9,8},{10,11... | collective-permute-start | bytes 393224 | tf_op jit(solution)/shard_map/ppermute | solution.py:464
  21.2 4.6 %collective-permute-start.5 = (f32[9,16,128]{2,1,0:T(8,128)S(1)}, f32[9,16,128]{2,1,0:T(8,128)S(1)}, u32[]{:S(2)}, u32[]{:S(2)}) collective-permute-start(f32[9,16,128]{2,1,0:T(8,128)S(1)} %pad_maximum_fusion.3), channel_id=1, source_target_pairs={{0,2},{2,0},{1,3},{3,1},{4,6},{6,4},{5,7},{7,5},{8,10},{10,8},{9,1... | collective-permute-start | bytes 221192 | tf_op jit(solution)/shard_map/ppermute | solution.py:506
  28.3 1.6 %collective-permute-start.7 = (f32[32,16,128]{2,1,0:T(8,128)S(1)}, f32[32,16,128]{2,1,0:T(8,128)S(1)}, u32[]{:S(2)}, u32[]{:S(2)}) collective-permute-start(f32[32,16,128]{2,1,0:T(8,128)S(1)} %get-tuple-element.65), channel_id=1, source_target_pairs={{0,1},{1,0},{2,3},{3,2},{4,5},{5,4},{6,7},{7,6},{8,9},{9,8},{10,11... | collective-permute-start | bytes 786440 | tf_op jit(solution)/shard_map/ppermute | solution.py:464
  30.0 7.4 %collective-permute-start.10 = (f32[8,16,128]{2,1,0:T(8,128)S(1)}, f32[8,16,128]{2,1,0:T(8,128)S(1)}, u32[]{:S(2)}, u32[]{:S(2)}) collective-permute-start(f32[8,16,128]{2,1,0:T(8,128)S(1)} %get-tuple-element.119), channel_id=1, source_target_pairs={{0,12},{4,8},{8,4},{12,0},{1,13},{5,9},{9,5},{13,1},{2,14},{6,10},... | collective-permute-start | bytes 196616 | tf_op jit(solution)/shard_map/ppermute | solution.py:459
  33.1 5.9 %collective-permute-start.9 = (f32[8,16,128]{2,1,0:T(8,128)S(1)}, f32[8,16,128]{2,1,0:T(8,128)S(1)}, u32[]{:S(2)}, u32[]{:S(2)}) collective-permute-start(f32[8,16,128]{2,1,0:T(8,128)S(1)} %get-tuple-element.120), channel_id=1, source_target_pairs={{0,8},{4,12},{8,0},{12,4},{1,9},{5,13},{9,1},{13,5},{2,10},{6,14},... | collective-permute-start | bytes 196616 | tf_op jit(solution)/shard_map/ppermute | solution.py:459
  33.1 6.0 %collective-permute-start.8 = (f32[8,16,128]{2,1,0:T(8,128)S(1)}, f32[8,16,128]{2,1,0:T(8,128)S(1)}, u32[]{:S(2)}, u32[]{:S(2)}) collective-permute-start(f32[8,16,128]{2,1,0:T(8,128)S(1)} %get-tuple-element.121), channel_id=1, source_target_pairs={{0,4},{4,0},{8,12},{12,8},{1,5},{5,1},{9,13},{13,9},{2,6},{6,2},{1... | collective-permute-start | bytes 196616 | tf_op jit(solution)/shard_map/ppermute | solution.py:459
  39.1 7.4 %collective-permute-start.13 = (bf16[8,16,128]{2,1,0:T(8,128)(2,1)S(1)}, bf16[8,16,128]{2,1,0:T(8,128)(2,1)S(1)}, u32[]{:S(2)}, u32[]{:S(2)}) collective-permute-start(bf16[8,16,128]{2,1,0:T(8,128)(2,1)S(1)} %get-tuple-element.69.after), channel_id=1, source_target_pairs={{0,12},{4,8},{8,4},{12,0},{1,13},{5,9},{9,5},{13,1},{2,14},{6,10},... | collective-permute-start | bytes 98312 | tf_op jit(solution)/shard_map/ppermute | solution.py:459
  41.7 4.8 %collective-permute-start.12 = (bf16[8,16,128]{2,1,0:T(8,128)(2,1)S(1)}, bf16[8,16,128]{2,1,0:T(8,128)(2,1)S(1)}, u32[]{:S(2)}, u32[]{:S(2)}) collective-permute-start(bf16[8,16,128]{2,1,0:T(8,128)(2,1)S(1)} %get-tuple-element.69.after), channel_id=1, source_target_pairs={{0,8},{4,12},{8,0},{12,4},{1,9},{5,13},{9,1},{13,5},{2,10},{6,14},... | collective-permute-start | bytes 98312 | tf_op jit(solution)/shard_map/ppermute | solution.py:459
  41.8 4.7 %collective-permute-start.11 = (bf16[8,16,128]{2,1,0:T(8,128)(2,1)S(1)}, bf16[8,16,128]{2,1,0:T(8,128)(2,1)S(1)}, u32[]{:S(2)}, u32[]{:S(2)}) collective-permute-start(bf16[8,16,128]{2,1,0:T(8,128)(2,1)S(1)} %get-tuple-element.69.after), channel_id=1, source_target_pairs={{0,4},{4,0},{8,12},{12,8},{1,5},{5,1},{9,13},{13,9},{2,6},{6,2},{1... | collective-permute-start | bytes 98312 | tf_op jit(solution)/shard_map/ppermute | solution.py:459
  50.4 4.3 %collective-permute-start.16 = (f32[8,16,128]{2,1,0:T(8,128)S(1)}, f32[8,16,128]{2,1,0:T(8,128)S(1)}, u32[]{:S(2)}, u32[]{:S(2)}) collective-permute-start(f32[8,16,128]{2,1,0:T(8,128)S(1)} %add.110), channel_id=1, source_target_pairs={{0,2},{2,0},{1,3},{3,1},{4,6},{6,4},{5,7},{7,5},{8,10},{10,8},{9,1... | collective-permute-start | bytes 196616 | tf_op jit(solution)/shard_map/ppermute | solution.py:506
  56.9 1.6 %collective-permute-start.18 = (f32[32,16,128]{2,1,0:T(8,128)S(1)}, f32[32,16,128]{2,1,0:T(8,128)S(1)}, u32[]{:S(2)}, u32[]{:S(2)}) collective-permute-start(f32[32,16,128]{2,1,0:T(8,128)S(1)} %get-tuple-element.76), channel_id=1, source_target_pairs={{0,1},{1,0},{2,3},{3,2},{4,5},{5,4},{6,7},{7,6},{8,9},{9,8},{10,11... | collective-permute-start | bytes 786440 | tf_op jit(solution)/shard_map/ppermute | solution.py:464
  58.6 6.6 %collective-permute-start.21 = (f32[8,16,128]{2,1,0:T(8,128)S(1)}, f32[8,16,128]{2,1,0:T(8,128)S(1)}, u32[]{:S(2)}, u32[]{:S(2)}) collective-permute-start(f32[8,16,128]{2,1,0:T(8,128)S(1)} %get-tuple-element.116), channel_id=1, source_target_pairs={{0,12},{4,8},{8,4},{12,0},{1,13},{5,9},{9,5},{13,1},{2,14},{6,10},... | collective-permute-start | bytes 196616 | tf_op jit(solution)/shard_map/ppermute | solution.py:459
  61.0 6.8 %collective-permute-start.20 = (f32[8,16,128]{2,1,0:T(8,128)S(1)}, f32[8,16,128]{2,1,0:T(8,128)S(1)}, u32[]{:S(2)}, u32[]{:S(2)}) collective-permute-start(f32[8,16,128]{2,1,0:T(8,128)S(1)} %get-tuple-element.117), channel_id=1, source_target_pairs={{0,8},{4,12},{8,0},{12,4},{1,9},{5,13},{9,1},{13,5},{2,10},{6,14},... | collective-permute-start | bytes 196616 | tf_op jit(solution)/shard_map/ppermute | solution.py:459
  61.4 6.5 %collective-permute-start.19 = (f32[8,16,128]{2,1,0:T(8,128)S(1)}, f32[8,16,128]{2,1,0:T(8,128)S(1)}, u32[]{:S(2)}, u32[]{:S(2)}) collective-permute-start(f32[8,16,128]{2,1,0:T(8,128)S(1)} %get-tuple-element.118), channel_id=1, source_target_pairs={{0,4},{4,0},{8,12},{12,8},{1,5},{5,1},{9,13},{13,9},{2,6},{6,2},{1... | collective-permute-start | bytes 196616 | tf_op jit(solution)/shard_map/ppermute | solution.py:459
  67.9 5.8 %collective-permute-start.24 = (bf16[8,16,128]{2,1,0:T(8,128)(2,1)S(1)}, bf16[8,16,128]{2,1,0:T(8,128)(2,1)S(1)}, u32[]{:S(2)}, u32[]{:S(2)}) collective-permute-start(bf16[8,16,128]{2,1,0:T(8,128)(2,1)S(1)} %get-tuple-element.102), channel_id=1, source_target_pairs={{0,12},{4,8},{8,4},{12,0},{1,13},{5,9},{9,5},{13,1},{2,14},{6,10},... | collective-permute-start | bytes 98312 | tf_op jit(solution)/shard_map/ppermute | solution.py:459
  70.4 4.8 %collective-permute-start.23 = (bf16[8,16,128]{2,1,0:T(8,128)(2,1)S(1)}, bf16[8,16,128]{2,1,0:T(8,128)(2,1)S(1)}, u32[]{:S(2)}, u32[]{:S(2)}) collective-permute-start(bf16[8,16,128]{2,1,0:T(8,128)(2,1)S(1)} %get-tuple-element.102), channel_id=1, source_target_pairs={{0,8},{4,12},{8,0},{12,4},{1,9},{5,13},{9,1},{13,5},{2,10},{6,14},... | collective-permute-start | bytes 98312 | tf_op jit(solution)/shard_map/ppermute | solution.py:459
  70.4 4.8 %collective-permute-start.22 = (bf16[8,16,128]{2,1,0:T(8,128)(2,1)S(1)}, bf16[8,16,128]{2,1,0:T(8,128)(2,1)S(1)}, u32[]{:S(2)}, u32[]{:S(2)}) collective-permute-start(bf16[8,16,128]{2,1,0:T(8,128)(2,1)S(1)} %get-tuple-element.102), channel_id=1, source_target_pairs={{0,4},{4,0},{8,12},{12,8},{1,5},{5,1},{9,13},{13,9},{2,6},{6,2},{1... | collective-permute-start | bytes 98312 | tf_op jit(solution)/shard_map/ppermute | solution.py:459
  79.1 4.3 %collective-permute-start.27 = (f32[8,16,128]{2,1,0:T(8,128)S(1)}, f32[8,16,128]{2,1,0:T(8,128)S(1)}, u32[]{:S(2)}, u32[]{:S(2)}) collective-permute-start(f32[8,16,128]{2,1,0:T(8,128)S(1)} %add.118), channel_id=1, source_target_pairs={{0,2},{2,0},{1,3},{3,1},{4,6},{6,4},{5,7},{7,5},{8,10},{10,8},{9,1... | collective-permute-start | bytes 196616 | tf_op jit(solution)/shard_map/ppermute | solution.py:506
  85.7 1.6 %collective-permute-start.29 = (f32[32,16,128]{2,1,0:T(8,128)S(1)}, f32[32,16,128]{2,1,0:T(8,128)S(1)}, u32[]{:S(2)}, u32[]{:S(2)}) collective-permute-start(f32[32,16,128]{2,1,0:T(8,128)S(1)} %get-tuple-element.81), channel_id=1, source_target_pairs={{0,1},{1,0},{2,3},{3,2},{4,5},{5,4},{6,7},{7,6},{8,9},{9,8},{10,11... | collective-permute-start | bytes 786440 | tf_op jit(solution)/shard_map/ppermute | solution.py:464
  87.3 6.6 %collective-permute-start.32 = (f32[8,16,128]{2,1,0:T(8,128)S(1)}, f32[8,16,128]{2,1,0:T(8,128)S(1)}, u32[]{:S(2)}, u32[]{:S(2)}) collective-permute-start(f32[8,16,128]{2,1,0:T(8,128)S(1)} %get-tuple-element.113), channel_id=1, source_target_pairs={{0,12},{4,8},{8,4},{12,0},{1,13},{5,9},{9,5},{13,1},{2,14},{6,10},... | collective-permute-start | bytes 196616 | tf_op jit(solution)/shard_map/ppermute | solution.py:459
  89.0 7.7 %collective-permute-start.31 = (f32[8,16,128]{2,1,0:T(8,128)S(1)}, f32[8,16,128]{2,1,0:T(8,128)S(1)}, u32[]{:S(2)}, u32[]{:S(2)}) collective-permute-start(f32[8,16,128]{2,1,0:T(8,128)S(1)} %get-tuple-element.114), channel_id=1, source_target_pairs={{0,8},{4,12},{8,0},{12,4},{1,9},{5,13},{9,1},{13,5},{2,10},{6,14},... | collective-permute-start | bytes 196616 | tf_op jit(solution)/shard_map/ppermute | solution.py:459
  90.1 6.5 %collective-permute-start.30 = (f32[8,16,128]{2,1,0:T(8,128)S(1)}, f32[8,16,128]{2,1,0:T(8,128)S(1)}, u32[]{:S(2)}, u32[]{:S(2)}) collective-permute-start(f32[8,16,128]{2,1,0:T(8,128)S(1)} %get-tuple-element.115), channel_id=1, source_target_pairs={{0,4},{4,0},{8,12},{12,8},{1,5},{5,1},{9,13},{13,9},{2,6},{6,2},{1... | collective-permute-start | bytes 196616 | tf_op jit(solution)/shard_map/ppermute | solution.py:459
  96.7 5.8 %collective-permute-start.35 = (bf16[8,16,128]{2,1,0:T(8,128)(2,1)S(1)}, bf16[8,16,128]{2,1,0:T(8,128)(2,1)S(1)}, u32[]{:S(2)}, u32[]{:S(2)}) collective-permute-start(bf16[8,16,128]{2,1,0:T(8,128)(2,1)S(1)} %get-tuple-element.100), channel_id=1, source_target_pairs={{0,12},{4,8},{8,4},{12,0},{1,13},{5,9},{9,5},{13,1},{2,14},{6,10},... | collective-permute-start | bytes 98312 | tf_op jit(solution)/shard_map/ppermute | solution.py:459
  99.3 4.8 %collective-permute-start.34 = (bf16[8,16,128]{2,1,0:T(8,128)(2,1)S(1)}, bf16[8,16,128]{2,1,0:T(8,128)(2,1)S(1)}, u32[]{:S(2)}, u32[]{:S(2)}) collective-permute-start(bf16[8,16,128]{2,1,0:T(8,128)(2,1)S(1)} %get-tuple-element.100), channel_id=1, source_target_pairs={{0,8},{4,12},{8,0},{12,4},{1,9},{5,13},{9,1},{13,5},{2,10},{6,14},... | collective-permute-start | bytes 98312 | tf_op jit(solution)/shard_map/ppermute | solution.py:459
  99.3 4.8 %collective-permute-start.33 = (bf16[8,16,128]{2,1,0:T(8,128)(2,1)S(1)}, bf16[8,16,128]{2,1,0:T(8,128)(2,1)S(1)}, u32[]{:S(2)}, u32[]{:S(2)}) collective-permute-start(bf16[8,16,128]{2,1,0:T(8,128)(2,1)S(1)} %get-tuple-element.100), channel_id=1, source_target_pairs={{0,4},{4,0},{8,12},{12,8},{1,5},{5,1},{9,13},{13,9},{2,6},{6,2},{1... | collective-permute-start | bytes 98312 | tf_op jit(solution)/shard_map/ppermute | solution.py:459
  107.9 4.3 %collective-permute-start.38 = (f32[8,16,128]{2,1,0:T(8,128)S(1)}, f32[8,16,128]{2,1,0:T(8,128)S(1)}, u32[]{:S(2)}, u32[]{:S(2)}) collective-permute-start(f32[8,16,128]{2,1,0:T(8,128)S(1)} %add.126), channel_id=1, source_target_pairs={{0,2},{2,0},{1,3},{3,1},{4,6},{6,4},{5,7},{7,5},{8,10},{10,8},{9,1... | collective-permute-start | bytes 196616 | tf_op jit(solution)/shard_map/ppermute | solution.py:506
  116.1 6.5 %collective-permute-start.43 = (f32[8,16,128]{2,1,0:T(8,128)S(1)}, f32[8,16,128]{2,1,0:T(8,128)S(1)}, u32[]{:S(2)}, u32[]{:S(2)}) collective-permute-start(f32[8,16,128]{2,1,0:T(8,128)S(1)} %get-tuple-element.110), channel_id=1, source_target_pairs={{0,12},{4,8},{8,4},{12,0},{1,13},{5,9},{9,5},{13,1},{2,14},{6,10},... | collective-permute-start | bytes 196616 | tf_op jit(solution)/shard_map/ppermute | solution.py:459
  117.8 7.6 %collective-permute-start.42 = (f32[8,16,128]{2,1,0:T(8,128)S(1)}, f32[8,16,128]{2,1,0:T(8,128)S(1)}, u32[]{:S(2)}, u32[]{:S(2)}) collective-permute-start(f32[8,16,128]{2,1,0:T(8,128)S(1)} %get-tuple-element.111), channel_id=1, source_target_pairs={{0,8},{4,12},{8,0},{12,4},{1,9},{5,13},{9,1},{13,5},{2,10},{6,14},... | collective-permute-start | bytes 196616 | tf_op jit(solution)/shard_map/ppermute | solution.py:459
  119.0 6.5 %collective-permute-start.41 = (f32[8,16,128]{2,1,0:T(8,128)S(1)}, f32[8,16,128]{2,1,0:T(8,128)S(1)}, u32[]{:S(2)}, u32[]{:S(2)}) collective-permute-start(f32[8,16,128]{2,1,0:T(8,128)S(1)} %get-tuple-element.112), channel_id=1, source_target_pairs={{0,4},{4,0},{8,12},{12,8},{1,5},{5,1},{9,13},{13,9},{2,6},{6,2},{1... | collective-permute-start | bytes 196616 | tf_op jit(solution)/shard_map/ppermute | solution.py:459
  (20 other events, 46.2 us)

commit v8 on v7

--- a/solution.py
+++ b/solution.py
@@ -32,8 +32,16 @@
     return 2 * slots // 3
 
 
-def index_kernel(n_vox, columns, runs, steps, me, cols, exps, live, after, *refs):
-    outs, sides, packed, *tables, sems = refs[:5], *refs[5:]
+def prepare_kernel(n_vox, columns, runs, steps, me, cols, exps, live, stored, *refs):
+    outs, kept, me_out, sides, packed, *tables, sems, load_sems = refs[:5], *refs[5:]
+    loads = [
+        row_copy(False, runs, cols.shape[2], me, stored, kept, load_sems, jnp.int32(b))
+        for b in range(load_sems.shape[0])
+    ]
+    for load in loads:
+        load.start()
+    for i in range(me.shape[0]):
+        me_out[i] = me[i]
     z, core = me[0], me[1]
     rows, _, slots = cols.shape
     own = columns // (2 * n_vox)
@@ -87,27 +95,33 @@
     for e, (at, bit) in enumerate(steps):
         side = jnp.where((me[at] & bit) == 0, 1.0, 0.0).astype(F32)
         sides[e] = jnp.full(sides.shape[1:], side)
-    for copy in copies:
+    for copy in copies + loads:
         copy.wait()
 
 
-def indices(n_vox, columns, runs, steps, me, cols, exps, live, after):
+def prepare(n_vox, columns, runs, steps, me, cols, exps, live, tiles):
     rows, _, slots = cols.shape
     shapes = [((rows, slots), t) for t in (jnp.int32, jnp.int32, jnp.int32, F32)]
     shapes.append(((rows // RUN, 128), jnp.int32))
-    return pl.pallas_call(
-        functools.partial(index_kernel, n_vox, columns, runs, steps),
-        in_specs=[in_smem()] + [in_vmem()] * 2 + [in_smem(), pl.BlockSpec(memory_space=pl.ANY)],
-        out_specs=[in_smem()] * 5 + [in_vmem()],
+    half = (tiles.shape[0] // 2,) + tiles.shape[1:]
+    in_hbm = [pltpu.with_memory_space_constraint(a, pltpu.HBM) for a in (cols, exps, tiles)]
+    *tables, kept, me, sides = pl.pallas_call(
+        functools.partial(prepare_kernel, n_vox, columns, runs, steps),
+        in_specs=[in_smem()]
+        + [in_vmem()] * 2
+        + [in_smem(), pl.BlockSpec(memory_space=pltpu.HBM)],
+        out_specs=[in_smem()] * 5 + [in_vmem(), in_smem(), in_vmem()],
         out_shape=[pltpu.SMEM(*shape) for shape in shapes]
+        + [pltpu.VMEM(half, tiles.dtype), pltpu.SMEM(me.shape, me.dtype)]
         + [jax.ShapeDtypeStruct((len(steps), 8, 128), F32)],
         scratch_shapes=[pltpu.VMEM((rows, slots), jnp.int32)]
         + [pltpu.VMEM(*shape) for shape in shapes]
-        + [pltpu.SemaphoreType.DMA((len(shapes),))],
-        compiler_params=PARAMS,
-        cost_estimate=pl.CostEstimate(flops=0, bytes_accessed=2**21, transcendentals=0),
-        name="indices",
-    )(me, *(pltpu.with_memory_space_constraint(a, pltpu.HBM) for a in (cols, exps)), live, after)
+        + [pltpu.SemaphoreType.DMA((len(shapes),)), pltpu.SemaphoreType.DMA((rows // 2,))],
+        compiler_params=PARAMS,
+        cost_estimate=pl.CostEstimate(flops=0, bytes_accessed=2 * tiles.size, transcendentals=0),
+        name="prepare",
+    )(me, *in_hbm[:2], live, in_hbm[2])
+    return tables, kept, me, sides
 
 
 def turn_kernel(kept, after, turned):
@@ -152,63 +166,51 @@
     return left, [blocks[slot[b, k]] for k in chosen]
 
 
-def row_copies(mine, runs, slots, me, stored, kept, sems):
-    rows = sems.shape[0]
-    n = rows // runs
+def row_copy(mine, runs, slots, me, stored, kept, sems, b):
+    n = sems.shape[0] // runs
     half = me[1] if mine else 1 - me[1]
-    return [
-        pltpu.make_async_copy(
-            stored.at[pl.ds(((2 * (b // n) + half) * n + b % n) * slots, slots)],
-            kept.at[pl.ds(b * slots, slots)],
-            sems.at[b],
-        )
-        for b in range(rows)
-    ]
-
-
-def load_kernel(runs, slots, me, stored, kept, me_out, sems):
-    copies = row_copies(False, runs, slots, me, stored, kept, sems)
-    for copy in copies:
-        copy.start()
-    for i in range(me.shape[0]):
-        me_out[i] = me[i]
-    for copy in copies:
-        copy.wait()
-
-
-def load_others(runs, rows, me, tiles):
-    shape = (tiles.shape[0] // 2,) + tiles.shape[1:]
-    return pl.pallas_call(
-        functools.partial(load_kernel, runs, tiles.shape[0] // rows),
-        in_specs=[in_smem(), pl.BlockSpec(memory_space=pltpu.HBM)],
-        out_specs=[in_vmem(), in_smem()],
-        out_shape=[pltpu.VMEM(shape, tiles.dtype), pltpu.SMEM(me.shape, me.dtype)],
-        scratch_shapes=[pltpu.SemaphoreType.DMA((rows // 2,))],
-        compiler_params=PARAMS,
-        cost_estimate=pl.CostEstimate(flops=0, bytes_accessed=2 * tiles.size, transcendentals=0),
-        name="load_others",
-    )(me, pltpu.with_memory_space_constraint(tiles, pltpu.HBM))
+    return pltpu.make_async_copy(
+        stored.at[pl.ds(((2 * lax.div(b, n) + half) * n + lax.rem(b, n)) * slots, slots)],
+        kept.at[pl.ds(b * slots, slots)],
+        sems.at[b],
+    )
 
 
 def first_forward_kernel(runs, me, slot, index, *refs):
     pieces, (kept_others, stored, given, dose, kept_mine, scaled, sems) = refs[:-7], refs[-7:]
     slots = slot.shape[1]
-    copies = row_copies(True, runs, slots, me, stored, kept_mine, sems)
-    for copy in copies:
+    rows = dose.shape[0]
+
+    def copies(t):
+        rows_of_run = [t * RUN + u for u in range(RUN)]
+        return [row_copy(True, runs, slots, me, stored, kept_mine, sems, b) for b in rows_of_run]
+
+    for copy in copies(jnp.int32(0)):
         copy.start()
     scale_weights(pieces, scaled)
-    rows = dose.shape[0]
     for kept, out, row0 in ((kept_others, given, rows), (kept_mine, dose, 0)):
-        for t in range(0, rows, RUN):
+
+        def run(t, carry, kept=kept, out=out, row0=row0):
             if kept is kept_mine:
-                for b in range(t, t + RUN):
-                    copies[b].wait()
-            for b in range(t, t + RUN):
+                for copy in copies(t):
+                    copy.wait()
+            for u in range(RUN):
+                b = t * RUN + u
                 left, blocks = row_operands(range(slots), row0 + b, slot, index, scaled, kept)
                 right = jnp.concatenate(blocks, axis=1)
                 out[b] = lax.dot_general(
                     left, right, (((1,), (1,)), ((), ())), preferred_element_type=F32
                 )
+            if kept is kept_others:
+
+                @pl.when(t + 1 < rows // RUN)
+                def _():
+                    for copy in copies(t + 1):
+                        copy.start()
+
+            return carry
+
+        lax.fori_loop(0, rows // RUN, run, 0)
 
 
 def row_dose(chosen, b, slot, index, scaled, turned):
@@ -254,10 +256,13 @@
 
         @pl.when(over[b0 // RUN, 0] > 0)
         def _():
-            for u in range(RUN):
+            def rest(u, carry):
                 dose[t * RUN + u] += row_dose(
                     range(cut, slots), b0 + u, slot, index, scaled, turned
                 )
+                return carry
+
+            lax.fori_loop(0, RUN, rest, 0)
 
         return carry
 
@@ -361,8 +366,11 @@
 
         @pl.when(over[b0 // RUN, 0] > 0)
         def _():
-            for u in range(RUN):
+            def rest(u, carry):
                 add_row(range(cut, slots), b0 + u, tables, slope[t * RUN + u], kept, total)
+                return carry
+
+            lax.fori_loop(0, RUN, rest, 0)
 
         return carry
 
@@ -473,18 +481,15 @@
 
     bits = [1 << i for i in range(n_spot.bit_length() - 1)]
     pieces = gather_weights(weights)
-    kept_others, me = load_others(n_spot, rows, me, tiles)
+    steps = [(1, 1)] + [(2, bit) for bit in bits]
+    live = live_counts.reshape(rows)
+    tables, kept_others, me, sides = prepare(
+        n_vox, columns, n_spot, steps, me, block_cols, block_exps, live, tiles
+    )
     pieces, kept_others = lax.optimization_barrier((pieces, kept_others))
-    steps = [(1, 1)] + [(2, bit) for bit in bits]
-    near = jnp.concatenate(pieces, axis=0)
-    live = live_counts.reshape(rows)
-    *tables, sides = indices(
-        n_vox, columns, n_spot, steps, me, block_cols, block_exps, live, near
-    )
 
     for step in range(ITERS):
-        if step > 0:
-            near = jnp.concatenate(pieces, axis=0)
+        near = jnp.concatenate(pieces, axis=0)
         other_half = over_rep(near)
         if step == 0:
             given, dose, kept_mine = first_forward(

time: 128 us -> 126 us (0.984)
  Pallas kernels: 37.8 us -> 34.2 us
  starting transfers between devices: 44.7 us -> 47.8 us
  waiting for transfers between devices: 41 us -> 39.5 us
    ppermute x4, starting transfers between devices: 4.53 us -> 7.86 us  [per_device(): got = lax.ppermute(sent, 'spot', [(i, i ^ bit) for i in range(n_spot)])]
    ppermute x4, waiting for transfers between devices: 13 us -> 9.97 us  [per_device(): got = lax.ppermute(sent, 'spot', [(i, i ^ bit) for i in range(n_spot)])]
    pallas_call x2 -> x1, Pallas kernels: 5.71 us -> 3.84 us  [prepare(): pl.pallas_call(functools.partial(prepare_kernel, n_vox, columns, runs, st...]
    pallas_call x1, Pallas kernels: 5.39 us -> 4.01 us  [first_forward(): pl.pallas_call(functools.partial(first_forward_kernel, runs), in_specs=[i...]
  transfers between devices with their start and end apart: 45 -> 45, of which waited for: 25 -> 31; matrix products, arithmetic and copies ran while one was open for 0% -> 0% of each run, Pallas kernels for 20% -> 19%
where the time goes in v8:
time: 126 us; the launch traced here: 127 us
  starting transfers between devices  47.8 us (38%)
  waiting for transfers between devices  39.5 us (31%)
  Pallas kernels  34.2 us (27%)
  local copies, waits for them, and re-layouts  3.43 us (3%)
    ppermute x24, starting transfers between devices, over_vox(): lax.ppermute(a, 'vox', [(i, i ^ d) for i in range(n_vox)])  36.9 us
    ppermute x24, waiting for transfers between devices, over_vox(): lax.ppermute(a, 'vox', [(i, i ^ d) for i in range(n_vox)])  23.1 us
    ppermute x4, waiting for transfers between devices, per_device(): got = lax.ppermute(sent, 'spot', [(i, i ^ bit) for i in range(n_spot)])  9.97 us
    ppermute x4, starting transfers between devices, per_device(): got = lax.ppermute(sent, 'spot', [(i, i ^ bit) for i in range(n_spot)])  7.86 us
    pallas_call x8, Pallas kernels, backward(): pl.pallas_call(functools.partial(backward_kernel, mine, row0), in_specs=[...  7.18 us
    ppermute x17, waiting for transfers between devices, over_rep(): return lax.ppermute(array, 'rep', [(0, 1), (1, 0)])  6.45 us
    pallas_call x2, Pallas kernels, turn(): pl.pallas_call(turn_kernel, in_specs=[in_vmem(), pl.BlockSpec(memory_spac...  5.85 us
    pallas_call x6, Pallas kernels, forward(): pl.pallas_call(functools.partial(forward_kernel, row0), in_specs=[in_smem...  5.38 us
  transfers between devices with their start and end apart: 45, of which 31 were waited for; matrix products, arithmetic and copies ran while one was open for 0% of the time, Pallas kernels for 19%

profile of v8, /device:TPU:0, one launch (start us, length us, event | category | flops | bytes accessed | tf_op | source)
XLA Modules:
  0.0 126.9 jit_solution(9202380640700992073)
XLA Ops:
  1.6 5.1 %collective-permute-start.2 = (bf16[8,16,128]{2,1,0:T(8,128)(2,1)S(1)}, bf16[8,16,128]{2,1,0:T(8,128)(2,1)S(1)}, u32[]{:S(2)}, u32[]{:S(2)}) collective-permute-start(bf16[8,16,128]{2,1,0:T(8,128)(2,1)S(1)} %bitcast.57), channel_id=1, source_target_pairs={{0,12},{4,8},{8,4},{12,0},{1,13},{5,9},{9,5},{13,1},{2,14},{6,10},... | collective-permute-start | bytes 98312 | tf_op jit(solution)/shard_map/ppermute | solution.py:467
  8.1 3.8 %prepare.1 = (s32[16,24]{1,0:T(8,128)S(4)}, s32[16,24]{1,0:T(8,128)S(4)}, s32[16,24]{1,0:T(8,128)S(4)}, f32[16,24]{1,0:T(8,128)S(4)}, s32[4,128]{1,0:T(4,128)S(4...) custom-call(s32[3]{0:T(128)S(1)} %pad_add_fusion.me, s32[16,1,24]{2,1,0:T(1,128)} %cols.1, ...), custom_call_target="tpu_custom_call" | custom-call | bytes 12582912 | tf_op jit(solution)/shard_map/prepare/pallas_call | solution.py:108
  13.4 4.0 %first_forward.1 = (f32[8,16,128]{2,1,0:T(8,128)S(1)}, f32[8,16,128]{2,1,0:T(8,128)S(1)}, bf16[192,128,128]{2,1,0:T(8,128)(2,1)S(1)}) custom-call(s32[3]{0:T(128)S(4)} %get-tuple-element.51.me, s32[16,24]{1,0:T(8,128)S(4)} %get-tuple-element.47.slot, s32[16,24]{1,0:T(8,128)S(4)} %get-tuple-element.52.index, ...), custom_call_target="tpu_custom_call" | custom-call | flops 201326592 | bytes 12582912 | tf_op jit(solution)/shard_map/first_forward/pallas_call | solution.py:316
  18.8 1.7 %collective-permute-start.5 = (f32[9,16,128]{2,1,0:T(8,128)S(1)}, f32[9,16,128]{2,1,0:T(8,128)S(1)}, u32[]{:S(2)}, u32[]{:S(2)}) collective-permute-start(f32[9,16,128]{2,1,0:T(8,128)S(1)} %pad_maximum_fusion.3), channel_id=1, source_target_pairs={{0,2},{2,0},{1,3},{3,1},{4,6},{6,4},{5,7},{7,5},{8,10},{10,8},{9,1... | collective-permute-start | bytes 221192 | tf_op jit(solution)/shard_map/ppermute | solution.py:511
  20.8 2.4 %collective-permute-done.5 = f32[9,16,128]{2,1,0:T(8,128)S(1)} collective-permute-done((f32[9,16,128]{2,1,0:T(8,128)S(1)}, f32[9,16,128]{2,1,0:T(8,128)S(1)}, u32[]{:S(2)}, u32[]{:S(2)}) %collective-permute-start.5) | collective-permute-done | bytes 73760 | tf_op jit(solution)/shard_map/ppermute | solution.py:511
  27.3 3.8 %collective-permute-start.10 = (f32[8,16,128]{2,1,0:T(8,128)S(1)}, f32[8,16,128]{2,1,0:T(8,128)S(1)}, u32[]{:S(2)}, u32[]{:S(2)}) collective-permute-start(f32[8,16,128]{2,1,0:T(8,128)S(1)} %get-tuple-element.119), channel_id=1, source_target_pairs={{0,12},{4,8},{8,4},{12,0},{1,13},{5,9},{9,5},{13,1},{2,14},{6,10},... | collective-permute-start | bytes 196616 | tf_op jit(solution)/shard_map/ppermute | solution.py:467
  31.7 2.9 %turn.2.turned_mine.turned = bf16[192,128,128]{2,1,0:T(8,128)(2,1)S(1)} custom-call(bf16[192,128,128]{2,1,0:T(8,128)(2,1)S(1)} %get-tuple-element.63.kept.kept_mine, f32[32,16,128]{2,1,0:T(8,128)S(1)} %add.106.after), custom_call_target="tpu_custom_call" | custom-call | bytes 12582912 | tf_op jit(solution)/shard_map/turn/pallas_call | solution.py:140
  34.7 2.1 %collective-permute-done.9 = f32[8,16,128]{2,1,0:T(8,128)S(1)} collective-permute-done((f32[8,16,128]{2,1,0:T(8,128)S(1)}, f32[8,16,128]{2,1,0:T(8,128)S(1)}, u32[]{:S(2)}, u32[]{:S(2)}) %collective-permute-start.9) | collective-permute-done | bytes 65568 | tf_op jit(solution)/shard_map/ppermute | solution.py:467
  36.8 2.4 %collective-permute-start.13 = (bf16[8,16,128]{2,1,0:T(8,128)(2,1)S(1)}, bf16[8,16,128]{2,1,0:T(8,128)(2,1)S(1)}, u32[]{:S(2)}, u32[]{:S(2)}) collective-permute-start(bf16[8,16,128]{2,1,0:T(8,128)(2,1)S(1)} %get-tuple-element.69.after), channel_id=1, source_target_pairs={{0,12},{4,8},{8,4},{12,0},{1,13},{5,9},{9,5},{13,1},{2,14},{6,10},... | collective-permute-start | bytes 98312 | tf_op jit(solution)/shard_map/ppermute | solution.py:467
  41.2 2.9 %turn.3.turned_others.turned = bf16[192,128,128]{2,1,0:T(8,128)(2,1)S(1)} custom-call(bf16[192,128,128]{2,1,0:T(8,128)(2,1)S(1)} %get-tuple-element.58.refs_2_.kept.kept_others, bf16[8,16,128]{2,1,0:T(8,128)(2,1)S(1)} %get-tuple-element.69.after), custom_call_target="tpu_custom_call" | custom-call | bytes 12582912 | tf_op jit(solution)/shard_map/turn/pallas_call | solution.py:140
  47.9 1.9 %collective-permute-start.16 = (f32[8,16,128]{2,1,0:T(8,128)S(1)}, f32[8,16,128]{2,1,0:T(8,128)S(1)}, u32[]{:S(2)}, u32[]{:S(2)}) collective-permute-start(f32[8,16,128]{2,1,0:T(8,128)S(1)} %add.110), channel_id=1, source_target_pairs={{0,2},{2,0},{1,3},{3,1},{4,6},{6,4},{5,7},{7,5},{8,10},{10,8},{9,1... | collective-permute-start | bytes 196616 | tf_op jit(solution)/shard_map/ppermute | solution.py:511
  49.8 2.5 %collective-permute-done.16 = f32[8,16,128]{2,1,0:T(8,128)S(1)} collective-permute-done((f32[8,16,128]{2,1,0:T(8,128)S(1)}, f32[8,16,128]{2,1,0:T(8,128)S(1)}, u32[]{:S(2)}, u32[]{:S(2)}) %collective-permute-start.16) | collective-permute-done | bytes 65568 | tf_op jit(solution)/shard_map/ppermute | solution.py:511
  56.2 2.6 %collective-permute-start.21 = (f32[8,16,128]{2,1,0:T(8,128)S(1)}, f32[8,16,128]{2,1,0:T(8,128)S(1)}, u32[]{:S(2)}, u32[]{:S(2)}) collective-permute-start(f32[8,16,128]{2,1,0:T(8,128)S(1)} %get-tuple-element.116), channel_id=1, source_target_pairs={{0,12},{4,8},{8,4},{12,0},{1,13},{5,9},{9,5},{13,1},{2,14},{6,10},... | collective-permute-start | bytes 196616 | tf_op jit(solution)/shard_map/ppermute | solution.py:467
  58.9 1.7 %collective-permute-start.19 = (f32[8,16,128]{2,1,0:T(8,128)S(1)}, f32[8,16,128]{2,1,0:T(8,128)S(1)}, u32[]{:S(2)}, u32[]{:S(2)}) collective-permute-start(f32[8,16,128]{2,1,0:T(8,128)S(1)} %get-tuple-element.118), channel_id=1, source_target_pairs={{0,4},{4,0},{8,12},{12,8},{1,5},{5,1},{9,13},{13,9},{2,6},{6,2},{1... | collective-permute-start | bytes 196616 | tf_op jit(solution)/shard_map/ppermute | solution.py:467
  60.6 1.8 %collective-permute-done.21 = f32[8,16,128]{2,1,0:T(8,128)S(1)} collective-permute-done((f32[8,16,128]{2,1,0:T(8,128)S(1)}, f32[8,16,128]{2,1,0:T(8,128)S(1)}, u32[]{:S(2)}, u32[]{:S(2)}) %collective-permute-start.21) | collective-permute-done | bytes 65568 | tf_op jit(solution)/shard_map/ppermute | solution.py:467
  62.5 3.0 %collective-permute-done.20 = f32[8,16,128]{2,1,0:T(8,128)S(1)} collective-permute-done((f32[8,16,128]{2,1,0:T(8,128)S(1)}, f32[8,16,128]{2,1,0:T(8,128)S(1)}, u32[]{:S(2)}, u32[]{:S(2)}) %collective-permute-start.20) | collective-permute-done | bytes 65568 | tf_op jit(solution)/shard_map/ppermute | solution.py:467
  65.5 2.8 %collective-permute-start.24 = (bf16[8,16,128]{2,1,0:T(8,128)(2,1)S(1)}, bf16[8,16,128]{2,1,0:T(8,128)(2,1)S(1)}, u32[]{:S(2)}, u32[]{:S(2)}) collective-permute-start(bf16[8,16,128]{2,1,0:T(8,128)(2,1)S(1)} %get-tuple-element.102), channel_id=1, source_target_pairs={{0,12},{4,8},{8,4},{12,0},{1,13},{5,9},{9,5},{13,1},{2,14},{6,10},... | collective-permute-start | bytes 98312 | tf_op jit(solution)/shard_map/ppermute | solution.py:467
  71.3 1.8 %collective-permute-done.23 = bf16[8,16,128]{2,1,0:T(8,128)(2,1)S(1)} collective-permute-done((bf16[8,16,128]{2,1,0:T(8,128)(2,1)S(1)}, bf16[8,16,128]{2,1,0:T(8,128)(2,1)S(1)}, u32[]{:S(2)}, u32[]{:S(2)}) %collective-permute-start.23) | collective-permute-done | bytes 32800 | tf_op jit(solution)/shard_map/ppermute | solution.py:467
  76.8 2.4 %collective-permute-start.27 = (f32[8,16,128]{2,1,0:T(8,128)S(1)}, f32[8,16,128]{2,1,0:T(8,128)S(1)}, u32[]{:S(2)}, u32[]{:S(2)}) collective-permute-start(f32[8,16,128]{2,1,0:T(8,128)S(1)} %add.118), channel_id=1, source_target_pairs={{0,2},{2,0},{1,3},{3,1},{4,6},{6,4},{5,7},{7,5},{8,10},{10,8},{9,1... | collective-permute-start | bytes 196616 | tf_op jit(solution)/shard_map/ppermute | solution.py:511
  79.2 2.5 %collective-permute-done.27 = f32[8,16,128]{2,1,0:T(8,128)S(1)} collective-permute-done((f32[8,16,128]{2,1,0:T(8,128)S(1)}, f32[8,16,128]{2,1,0:T(8,128)S(1)}, u32[]{:S(2)}, u32[]{:S(2)}) %collective-permute-start.27) | collective-permute-done | bytes 65568 | tf_op jit(solution)/shard_map/ppermute | solution.py:511
  85.6 1.8 %collective-permute-start.32 = (f32[8,16,128]{2,1,0:T(8,128)S(1)}, f32[8,16,128]{2,1,0:T(8,128)S(1)}, u32[]{:S(2)}, u32[]{:S(2)}) collective-permute-start(f32[8,16,128]{2,1,0:T(8,128)S(1)} %get-tuple-element.113), channel_id=1, source_target_pairs={{0,12},{4,8},{8,4},{12,0},{1,13},{5,9},{9,5},{13,1},{2,14},{6,10},... | collective-permute-start | bytes 196616 | tf_op jit(solution)/shard_map/ppermute | solution.py:467
  88.3 1.7 %collective-permute-start.30 = (f32[8,16,128]{2,1,0:T(8,128)S(1)}, f32[8,16,128]{2,1,0:T(8,128)S(1)}, u32[]{:S(2)}, u32[]{:S(2)}) collective-permute-start(f32[8,16,128]{2,1,0:T(8,128)S(1)} %get-tuple-element.115), channel_id=1, source_target_pairs={{0,4},{4,0},{8,12},{12,8},{1,5},{5,1},{9,13},{13,9},{2,6},{6,2},{1... | collective-permute-start | bytes 196616 | tf_op jit(solution)/shard_map/ppermute | solution.py:467
  90.0 1.9 %collective-permute-done.32 = f32[8,16,128]{2,1,0:T(8,128)S(1)} collective-permute-done((f32[8,16,128]{2,1,0:T(8,128)S(1)}, f32[8,16,128]{2,1,0:T(8,128)S(1)}, u32[]{:S(2)}, u32[]{:S(2)}) %collective-permute-start.32) | collective-permute-done | bytes 65568 | tf_op jit(solution)/shard_map/ppermute | solution.py:467
  91.9 3.0 %collective-permute-done.31 = f32[8,16,128]{2,1,0:T(8,128)S(1)} collective-permute-done((f32[8,16,128]{2,1,0:T(8,128)S(1)}, f32[8,16,128]{2,1,0:T(8,128)S(1)}, u32[]{:S(2)}, u32[]{:S(2)}) %collective-permute-start.31) | collective-permute-done | bytes 65568 | tf_op jit(solution)/shard_map/ppermute | solution.py:467
  95.0 2.7 %collective-permute-start.35 = (bf16[8,16,128]{2,1,0:T(8,128)(2,1)S(1)}, bf16[8,16,128]{2,1,0:T(8,128)(2,1)S(1)}, u32[]{:S(2)}, u32[]{:S(2)}) collective-permute-start(bf16[8,16,128]{2,1,0:T(8,128)(2,1)S(1)} %get-tuple-element.100), channel_id=1, source_target_pairs={{0,12},{4,8},{8,4},{12,0},{1,13},{5,9},{9,5},{13,1},{2,14},{6,10},... | collective-permute-start | bytes 98312 | tf_op jit(solution)/shard_map/ppermute | solution.py:467
  97.7 1.7 %collective-permute-start.33 = (bf16[8,16,128]{2,1,0:T(8,128)(2,1)S(1)}, bf16[8,16,128]{2,1,0:T(8,128)(2,1)S(1)}, u32[]{:S(2)}, u32[]{:S(2)}) collective-permute-start(bf16[8,16,128]{2,1,0:T(8,128)(2,1)S(1)} %get-tuple-element.100), channel_id=1, source_target_pairs={{0,4},{4,0},{8,12},{12,8},{1,5},{5,1},{9,13},{13,9},{2,6},{6,2},{1... | collective-permute-start | bytes 98312 | tf_op jit(solution)/shard_map/ppermute | solution.py:467
  100.8 1.7 %collective-permute-done.34 = bf16[8,16,128]{2,1,0:T(8,128)(2,1)S(1)} collective-permute-done((bf16[8,16,128]{2,1,0:T(8,128)(2,1)S(1)}, bf16[8,16,128]{2,1,0:T(8,128)(2,1)S(1)}, u32[]{:S(2)}, u32[]{:S(2)}) %collective-permute-start.34) | collective-permute-done | bytes 32800 | tf_op jit(solution)/shard_map/ppermute | solution.py:467
  106.2 1.9 %collective-permute-start.38 = (f32[8,16,128]{2,1,0:T(8,128)S(1)}, f32[8,16,128]{2,1,0:T(8,128)S(1)}, u32[]{:S(2)}, u32[]{:S(2)}) collective-permute-start(f32[8,16,128]{2,1,0:T(8,128)S(1)} %add.126), channel_id=1, source_target_pairs={{0,2},{2,0},{1,3},{3,1},{4,6},{6,4},{5,7},{7,5},{8,10},{10,8},{9,1... | collective-permute-start | bytes 196616 | tf_op jit(solution)/shard_map/ppermute | solution.py:511
  108.1 2.5 %collective-permute-done.38 = f32[8,16,128]{2,1,0:T(8,128)S(1)} collective-permute-done((f32[8,16,128]{2,1,0:T(8,128)S(1)}, f32[8,16,128]{2,1,0:T(8,128)S(1)}, u32[]{:S(2)}, u32[]{:S(2)}) %collective-permute-start.38) | collective-permute-done | bytes 65568 | tf_op jit(solution)/shard_map/ppermute | solution.py:511
  114.5 2.0 %collective-permute-start.43 = (f32[8,16,128]{2,1,0:T(8,128)S(1)}, f32[8,16,128]{2,1,0:T(8,128)S(1)}, u32[]{:S(2)}, u32[]{:S(2)}) collective-permute-start(f32[8,16,128]{2,1,0:T(8,128)S(1)} %get-tuple-element.110), channel_id=1, source_target_pairs={{0,12},{4,8},{8,4},{12,0},{1,13},{5,9},{9,5},{13,1},{2,14},{6,10},... | collective-permute-start | bytes 196616 | tf_op jit(solution)/shard_map/ppermute | solution.py:467
  118.9 1.8 %collective-permute-done.43 = f32[8,16,128]{2,1,0:T(8,128)S(1)} collective-permute-done((f32[8,16,128]{2,1,0:T(8,128)S(1)}, f32[8,16,128]{2,1,0:T(8,128)S(1)}, u32[]{:S(2)}, u32[]{:S(2)}) %collective-permute-start.43) | collective-permute-done | bytes 65568 | tf_op jit(solution)/shard_map/ppermute | solution.py:467
  120.8 3.1 %collective-permute-done.42 = f32[8,16,128]{2,1,0:T(8,128)S(1)} collective-permute-done((f32[8,16,128]{2,1,0:T(8,128)S(1)}, f32[8,16,128]{2,1,0:T(8,128)S(1)}, u32[]{:S(2)}, u32[]{:S(2)}) %collective-permute-start.42) | collective-permute-done | bytes 65568 | tf_op jit(solution)/shard_map/ppermute | solution.py:467
  (146 shorter events, 45.3 us)
Async XLA Ops:
  1.6 10.3 %collective-permute-start.2 = (bf16[8,16,128]{2,1,0:T(8,128)(2,1)S(1)}, bf16[8,16,128]{2,1,0:T(8,128)(2,1)S(1)}, u32[]{:S(2)}, u32[]{:S(2)}) collective-permute-start(bf16[8,16,128]{2,1,0:T(8,128)(2,1)S(1)} %bitcast.57), channel_id=1, source_target_pairs={{0,12},{4,8},{8,4},{12,0},{1,13},{5,9},{9,5},{13,1},{2,14},{6,10},... | collective-permute-start | bytes 98312 | tf_op jit(solution)/shard_map/ppermute | solution.py:467
  6.7 5.2 %collective-permute-start.1 = (bf16[8,16,128]{2,1,0:T(8,128)(2,1)S(1)}, bf16[8,16,128]{2,1,0:T(8,128)(2,1)S(1)}, u32[]{:S(2)}, u32[]{:S(2)}) collective-permute-start(bf16[8,16,128]{2,1,0:T(8,128)(2,1)S(1)} %bitcast.58), channel_id=1, source_target_pairs={{0,8},{4,12},{8,0},{12,4},{1,9},{5,13},{9,1},{13,5},{2,10},{6,14},... | collective-permute-start | bytes 98312 | tf_op jit(solution)/shard_map/ppermute | solution.py:467
  6.7 5.3 %collective-permute-start = (bf16[8,16,128]{2,1,0:T(8,128)(2,1)S(1)}, bf16[8,16,128]{2,1,0:T(8,128)(2,1)S(1)}, u32[]{:S(2)}, u32[]{:S(2)}) collective-permute-start(bf16[8,16,128]{2,1,0:T(8,128)(2,1)S(1)} %bitcast.59), channel_id=1, source_target_pairs={{0,4},{4,0},{8,12},{12,8},{1,5},{5,1},{9,13},{13,9},{2,6},{6,2},{1... | collective-permute-start | bytes 98312 | tf_op jit(solution)/shard_map/ppermute | solution.py:467
  18.8 4.4 %collective-permute-start.5 = (f32[9,16,128]{2,1,0:T(8,128)S(1)}, f32[9,16,128]{2,1,0:T(8,128)S(1)}, u32[]{:S(2)}, u32[]{:S(2)}) collective-permute-start(f32[9,16,128]{2,1,0:T(8,128)S(1)} %pad_maximum_fusion.3), channel_id=1, source_target_pairs={{0,2},{2,0},{1,3},{3,1},{4,6},{6,4},{5,7},{7,5},{8,10},{10,8},{9,1... | collective-permute-start | bytes 221192 | tf_op jit(solution)/shard_map/ppermute | solution.py:511
  25.6 1.6 %collective-permute-start.7 = (f32[32,16,128]{2,1,0:T(8,128)S(1)}, f32[32,16,128]{2,1,0:T(8,128)S(1)}, u32[]{:S(2)}, u32[]{:S(2)}) collective-permute-start(f32[32,16,128]{2,1,0:T(8,128)S(1)} %get-tuple-element.65), channel_id=1, source_target_pairs={{0,1},{1,0},{2,3},{3,2},{4,5},{5,4},{6,7},{7,6},{8,9},{9,8},{10,11... | collective-permute-start | bytes 786440 | tf_op jit(solution)/shard_map/ppermute | solution.py:472
  27.3 7.4 %collective-permute-start.10 = (f32[8,16,128]{2,1,0:T(8,128)S(1)}, f32[8,16,128]{2,1,0:T(8,128)S(1)}, u32[]{:S(2)}, u32[]{:S(2)}) collective-permute-start(f32[8,16,128]{2,1,0:T(8,128)S(1)} %get-tuple-element.119), channel_id=1, source_target_pairs={{0,12},{4,8},{8,4},{12,0},{1,13},{5,9},{9,5},{13,1},{2,14},{6,10},... | collective-permute-start | bytes 196616 | tf_op jit(solution)/shard_map/ppermute | solution.py:467
  31.1 5.7 %collective-permute-start.9 = (f32[8,16,128]{2,1,0:T(8,128)S(1)}, f32[8,16,128]{2,1,0:T(8,128)S(1)}, u32[]{:S(2)}, u32[]{:S(2)}) collective-permute-start(f32[8,16,128]{2,1,0:T(8,128)S(1)} %get-tuple-element.120), channel_id=1, source_target_pairs={{0,8},{4,12},{8,0},{12,4},{1,9},{5,13},{9,1},{13,5},{2,10},{6,14},... | collective-permute-start | bytes 196616 | tf_op jit(solution)/shard_map/ppermute | solution.py:467
  31.1 5.7 %collective-permute-start.8 = (f32[8,16,128]{2,1,0:T(8,128)S(1)}, f32[8,16,128]{2,1,0:T(8,128)S(1)}, u32[]{:S(2)}, u32[]{:S(2)}) collective-permute-start(f32[8,16,128]{2,1,0:T(8,128)S(1)} %get-tuple-element.121), channel_id=1, source_target_pairs={{0,4},{4,0},{8,12},{12,8},{1,5},{5,1},{9,13},{13,9},{2,6},{6,2},{1... | collective-permute-start | bytes 196616 | tf_op jit(solution)/shard_map/ppermute | solution.py:467
  36.8 7.4 %collective-permute-start.13 = (bf16[8,16,128]{2,1,0:T(8,128)(2,1)S(1)}, bf16[8,16,128]{2,1,0:T(8,128)(2,1)S(1)}, u32[]{:S(2)}, u32[]{:S(2)}) collective-permute-start(bf16[8,16,128]{2,1,0:T(8,128)(2,1)S(1)} %get-tuple-element.69.after), channel_id=1, source_target_pairs={{0,12},{4,8},{8,4},{12,0},{1,13},{5,9},{9,5},{13,1},{2,14},{6,10},... | collective-permute-start | bytes 98312 | tf_op jit(solution)/shard_map/ppermute | solution.py:467
  39.2 5.0 %collective-permute-start.12 = (bf16[8,16,128]{2,1,0:T(8,128)(2,1)S(1)}, bf16[8,16,128]{2,1,0:T(8,128)(2,1)S(1)}, u32[]{:S(2)}, u32[]{:S(2)}) collective-permute-start(bf16[8,16,128]{2,1,0:T(8,128)(2,1)S(1)} %get-tuple-element.69.after), channel_id=1, source_target_pairs={{0,8},{4,12},{8,0},{12,4},{1,9},{5,13},{9,1},{13,5},{2,10},{6,14},... | collective-permute-start | bytes 98312 | tf_op jit(solution)/shard_map/ppermute | solution.py:467
  39.7 4.5 %collective-permute-start.11 = (bf16[8,16,128]{2,1,0:T(8,128)(2,1)S(1)}, bf16[8,16,128]{2,1,0:T(8,128)(2,1)S(1)}, u32[]{:S(2)}, u32[]{:S(2)}) collective-permute-start(bf16[8,16,128]{2,1,0:T(8,128)(2,1)S(1)} %get-tuple-element.69.after), channel_id=1, source_target_pairs={{0,4},{4,0},{8,12},{12,8},{1,5},{5,1},{9,13},{13,9},{2,6},{6,2},{1... | collective-permute-start | bytes 98312 | tf_op jit(solution)/shard_map/ppermute | solution.py:467
  47.9 4.4 %collective-permute-start.16 = (f32[8,16,128]{2,1,0:T(8,128)S(1)}, f32[8,16,128]{2,1,0:T(8,128)S(1)}, u32[]{:S(2)}, u32[]{:S(2)}) collective-permute-start(f32[8,16,128]{2,1,0:T(8,128)S(1)} %add.110), channel_id=1, source_target_pairs={{0,2},{2,0},{1,3},{3,1},{4,6},{6,4},{5,7},{7,5},{8,10},{10,8},{9,1... | collective-permute-start | bytes 196616 | tf_op jit(solution)/shard_map/ppermute | solution.py:511
  54.5 1.6 %collective-permute-start.18 = (f32[32,16,128]{2,1,0:T(8,128)S(1)}, f32[32,16,128]{2,1,0:T(8,128)S(1)}, u32[]{:S(2)}, u32[]{:S(2)}) collective-permute-start(f32[32,16,128]{2,1,0:T(8,128)S(1)} %get-tuple-element.76), channel_id=1, source_target_pairs={{0,1},{1,0},{2,3},{3,2},{4,5},{5,4},{6,7},{7,6},{8,9},{9,8},{10,11... | collective-permute-start | bytes 786440 | tf_op jit(solution)/shard_map/ppermute | solution.py:472
  56.2 6.3 %collective-permute-start.21 = (f32[8,16,128]{2,1,0:T(8,128)S(1)}, f32[8,16,128]{2,1,0:T(8,128)S(1)}, u32[]{:S(2)}, u32[]{:S(2)}) collective-permute-start(f32[8,16,128]{2,1,0:T(8,128)S(1)} %get-tuple-element.116), channel_id=1, source_target_pairs={{0,12},{4,8},{8,4},{12,0},{1,13},{5,9},{9,5},{13,1},{2,14},{6,10},... | collective-permute-start | bytes 196616 | tf_op jit(solution)/shard_map/ppermute | solution.py:467
  58.8 6.7 %collective-permute-start.20 = (f32[8,16,128]{2,1,0:T(8,128)S(1)}, f32[8,16,128]{2,1,0:T(8,128)S(1)}, u32[]{:S(2)}, u32[]{:S(2)}) collective-permute-start(f32[8,16,128]{2,1,0:T(8,128)S(1)} %get-tuple-element.117), channel_id=1, source_target_pairs={{0,8},{4,12},{8,0},{12,4},{1,9},{5,13},{9,1},{13,5},{2,10},{6,14},... | collective-permute-start | bytes 196616 | tf_op jit(solution)/shard_map/ppermute | solution.py:467
  58.9 6.6 %collective-permute-start.19 = (f32[8,16,128]{2,1,0:T(8,128)S(1)}, f32[8,16,128]{2,1,0:T(8,128)S(1)}, u32[]{:S(2)}, u32[]{:S(2)}) collective-permute-start(f32[8,16,128]{2,1,0:T(8,128)S(1)} %get-tuple-element.118), channel_id=1, source_target_pairs={{0,4},{4,0},{8,12},{12,8},{1,5},{5,1},{9,13},{13,9},{2,6},{6,2},{1... | collective-permute-start | bytes 196616 | tf_op jit(solution)/shard_map/ppermute | solution.py:467
  65.5 5.8 %collective-permute-start.24 = (bf16[8,16,128]{2,1,0:T(8,128)(2,1)S(1)}, bf16[8,16,128]{2,1,0:T(8,128)(2,1)S(1)}, u32[]{:S(2)}, u32[]{:S(2)}) collective-permute-start(bf16[8,16,128]{2,1,0:T(8,128)(2,1)S(1)} %get-tuple-element.102), channel_id=1, source_target_pairs={{0,12},{4,8},{8,4},{12,0},{1,13},{5,9},{9,5},{13,1},{2,14},{6,10},... | collective-permute-start | bytes 98312 | tf_op jit(solution)/shard_map/ppermute | solution.py:467
  68.3 4.8 %collective-permute-start.23 = (bf16[8,16,128]{2,1,0:T(8,128)(2,1)S(1)}, bf16[8,16,128]{2,1,0:T(8,128)(2,1)S(1)}, u32[]{:S(2)}, u32[]{:S(2)}) collective-permute-start(bf16[8,16,128]{2,1,0:T(8,128)(2,1)S(1)} %get-tuple-element.102), channel_id=1, source_target_pairs={{0,8},{4,12},{8,0},{12,4},{1,9},{5,13},{9,1},{13,5},{2,10},{6,14},... | collective-permute-start | bytes 98312 | tf_op jit(solution)/shard_map/ppermute | solution.py:467
  68.3 4.8 %collective-permute-start.22 = (bf16[8,16,128]{2,1,0:T(8,128)(2,1)S(1)}, bf16[8,16,128]{2,1,0:T(8,128)(2,1)S(1)}, u32[]{:S(2)}, u32[]{:S(2)}) collective-permute-start(bf16[8,16,128]{2,1,0:T(8,128)(2,1)S(1)} %get-tuple-element.102), channel_id=1, source_target_pairs={{0,4},{4,0},{8,12},{12,8},{1,5},{5,1},{9,13},{13,9},{2,6},{6,2},{1... | collective-permute-start | bytes 98312 | tf_op jit(solution)/shard_map/ppermute | solution.py:467
  76.8 4.9 %collective-permute-start.27 = (f32[8,16,128]{2,1,0:T(8,128)S(1)}, f32[8,16,128]{2,1,0:T(8,128)S(1)}, u32[]{:S(2)}, u32[]{:S(2)}) collective-permute-start(f32[8,16,128]{2,1,0:T(8,128)S(1)} %add.118), channel_id=1, source_target_pairs={{0,2},{2,0},{1,3},{3,1},{4,6},{6,4},{5,7},{7,5},{8,10},{10,8},{9,1... | collective-permute-start | bytes 196616 | tf_op jit(solution)/shard_map/ppermute | solution.py:511
  83.9 1.6 %collective-permute-start.29 = (f32[32,16,128]{2,1,0:T(8,128)S(1)}, f32[32,16,128]{2,1,0:T(8,128)S(1)}, u32[]{:S(2)}, u32[]{:S(2)}) collective-permute-start(f32[32,16,128]{2,1,0:T(8,128)S(1)} %get-tuple-element.81), channel_id=1, source_target_pairs={{0,1},{1,0},{2,3},{3,2},{4,5},{5,4},{6,7},{7,6},{8,9},{9,8},{10,11... | collective-permute-start | bytes 786440 | tf_op jit(solution)/shard_map/ppermute | solution.py:472
  85.6 6.4 %collective-permute-start.32 = (f32[8,16,128]{2,1,0:T(8,128)S(1)}, f32[8,16,128]{2,1,0:T(8,128)S(1)}, u32[]{:S(2)}, u32[]{:S(2)}) collective-permute-start(f32[8,16,128]{2,1,0:T(8,128)S(1)} %get-tuple-element.113), channel_id=1, source_target_pairs={{0,12},{4,8},{8,4},{12,0},{1,13},{5,9},{9,5},{13,1},{2,14},{6,10},... | collective-permute-start | bytes 196616 | tf_op jit(solution)/shard_map/ppermute | solution.py:467
  87.4 7.6 %collective-permute-start.31 = (f32[8,16,128]{2,1,0:T(8,128)S(1)}, f32[8,16,128]{2,1,0:T(8,128)S(1)}, u32[]{:S(2)}, u32[]{:S(2)}) collective-permute-start(f32[8,16,128]{2,1,0:T(8,128)S(1)} %get-tuple-element.114), channel_id=1, source_target_pairs={{0,8},{4,12},{8,0},{12,4},{1,9},{5,13},{9,1},{13,5},{2,10},{6,14},... | collective-permute-start | bytes 196616 | tf_op jit(solution)/shard_map/ppermute | solution.py:467
  88.3 6.7 %collective-permute-start.30 = (f32[8,16,128]{2,1,0:T(8,128)S(1)}, f32[8,16,128]{2,1,0:T(8,128)S(1)}, u32[]{:S(2)}, u32[]{:S(2)}) collective-permute-start(f32[8,16,128]{2,1,0:T(8,128)S(1)} %get-tuple-element.115), channel_id=1, source_target_pairs={{0,4},{4,0},{8,12},{12,8},{1,5},{5,1},{9,13},{13,9},{2,6},{6,2},{1... | collective-permute-start | bytes 196616 | tf_op jit(solution)/shard_map/ppermute | solution.py:467
  95.0 5.8 %collective-permute-start.35 = (bf16[8,16,128]{2,1,0:T(8,128)(2,1)S(1)}, bf16[8,16,128]{2,1,0:T(8,128)(2,1)S(1)}, u32[]{:S(2)}, u32[]{:S(2)}) collective-permute-start(bf16[8,16,128]{2,1,0:T(8,128)(2,1)S(1)} %get-tuple-element.100), channel_id=1, source_target_pairs={{0,12},{4,8},{8,4},{12,0},{1,13},{5,9},{9,5},{13,1},{2,14},{6,10},... | collective-permute-start | bytes 98312 | tf_op jit(solution)/shard_map/ppermute | solution.py:467
  97.7 4.8 %collective-permute-start.34 = (bf16[8,16,128]{2,1,0:T(8,128)(2,1)S(1)}, bf16[8,16,128]{2,1,0:T(8,128)(2,1)S(1)}, u32[]{:S(2)}, u32[]{:S(2)}) collective-permute-start(bf16[8,16,128]{2,1,0:T(8,128)(2,1)S(1)} %get-tuple-element.100), channel_id=1, source_target_pairs={{0,8},{4,12},{8,0},{12,4},{1,9},{5,13},{9,1},{13,5},{2,10},{6,14},... | collective-permute-start | bytes 98312 | tf_op jit(solution)/shard_map/ppermute | solution.py:467
  97.7 4.8 %collective-permute-start.33 = (bf16[8,16,128]{2,1,0:T(8,128)(2,1)S(1)}, bf16[8,16,128]{2,1,0:T(8,128)(2,1)S(1)}, u32[]{:S(2)}, u32[]{:S(2)}) collective-permute-start(bf16[8,16,128]{2,1,0:T(8,128)(2,1)S(1)} %get-tuple-element.100), channel_id=1, source_target_pairs={{0,4},{4,0},{8,12},{12,8},{1,5},{5,1},{9,13},{13,9},{2,6},{6,2},{1... | collective-permute-start | bytes 98312 | tf_op jit(solution)/shard_map/ppermute | solution.py:467
  106.2 4.4 %collective-permute-start.38 = (f32[8,16,128]{2,1,0:T(8,128)S(1)}, f32[8,16,128]{2,1,0:T(8,128)S(1)}, u32[]{:S(2)}, u32[]{:S(2)}) collective-permute-start(f32[8,16,128]{2,1,0:T(8,128)S(1)} %add.126), channel_id=1, source_target_pairs={{0,2},{2,0},{1,3},{3,1},{4,6},{6,4},{5,7},{7,5},{8,10},{10,8},{9,1... | collective-permute-start | bytes 196616 | tf_op jit(solution)/shard_map/ppermute | solution.py:511
  112.8 1.6 %collective-permute-start.40 = (f32[32,16,128]{2,1,0:T(8,128)S(1)}, f32[32,16,128]{2,1,0:T(8,128)S(1)}, u32[]{:S(2)}, u32[]{:S(2)}) collective-permute-start(f32[32,16,128]{2,1,0:T(8,128)S(1)} %get-tuple-element.86), channel_id=1, source_target_pairs={{0,1},{1,0},{2,3},{3,2},{4,5},{5,4},{6,7},{7,6},{8,9},{9,8},{10,11... | collective-permute-start | bytes 786440 | tf_op jit(solution)/shard_map/ppermute | solution.py:472
  114.5 6.3 %collective-permute-start.43 = (f32[8,16,128]{2,1,0:T(8,128)S(1)}, f32[8,16,128]{2,1,0:T(8,128)S(1)}, u32[]{:S(2)}, u32[]{:S(2)}) collective-permute-start(f32[8,16,128]{2,1,0:T(8,128)S(1)} %get-tuple-element.110), channel_id=1, source_target_pairs={{0,12},{4,8},{8,4},{12,0},{1,13},{5,9},{9,5},{13,1},{2,14},{6,10},... | collective-permute-start | bytes 196616 | tf_op jit(solution)/shard_map/ppermute | solution.py:467
  116.5 7.4 %collective-permute-start.42 = (f32[8,16,128]{2,1,0:T(8,128)S(1)}, f32[8,16,128]{2,1,0:T(8,128)S(1)}, u32[]{:S(2)}, u32[]{:S(2)}) collective-permute-start(f32[8,16,128]{2,1,0:T(8,128)S(1)} %get-tuple-element.111), channel_id=1, source_target_pairs={{0,8},{4,12},{8,0},{12,4},{1,9},{5,13},{9,1},{13,5},{2,10},{6,14},... | collective-permute-start | bytes 196616 | tf_op jit(solution)/shard_map/ppermute | solution.py:467
  117.5 6.5 %collective-permute-start.41 = (f32[8,16,128]{2,1,0:T(8,128)S(1)}, f32[8,16,128]{2,1,0:T(8,128)S(1)}, u32[]{:S(2)}, u32[]{:S(2)}) collective-permute-start(f32[8,16,128]{2,1,0:T(8,128)S(1)} %get-tuple-element.112), channel_id=1, source_target_pairs={{0,4},{4,0},{8,12},{12,8},{1,5},{5,1},{9,13},{13,9},{2,6},{6,2},{1... | collective-permute-start | bytes 196616 | tf_op jit(solution)/shard_map/ppermute | solution.py:467
  (20 other events, 39.2 us)

commit v9 on v8

--- a/solution.py
+++ b/solution.py
@@ -104,7 +104,7 @@
     shapes = [((rows, slots), t) for t in (jnp.int32, jnp.int32, jnp.int32, F32)]
     shapes.append(((rows // RUN, 128), jnp.int32))
     half = (tiles.shape[0] // 2,) + tiles.shape[1:]
-    in_hbm = [pltpu.with_memory_space_constraint(a, pltpu.HBM) for a in (cols, exps, tiles)]
+    in_hbm = [pltpu.with_memory_space_constraint(a, pltpu.HBM) for a in (cols, exps, live, tiles)]
     *tables, kept, me, sides = pl.pallas_call(
         functools.partial(prepare_kernel, n_vox, columns, runs, steps),
         in_specs=[in_smem()]
@@ -120,7 +120,7 @@
         compiler_params=PARAMS,
         cost_estimate=pl.CostEstimate(flops=0, bytes_accessed=2 * tiles.size, transcendentals=0),
         name="prepare",
-    )(me, *in_hbm[:2], live, in_hbm[2])
+    )(me, *in_hbm)
     return tables, kept, me, sides
 
 
@@ -256,13 +256,10 @@
 
         @pl.when(over[b0 // RUN, 0] > 0)
         def _():
-            def rest(u, carry):
+            for u in range(RUN):
                 dose[t * RUN + u] += row_dose(
                     range(cut, slots), b0 + u, slot, index, scaled, turned
                 )
-                return carry
-
-            lax.fori_loop(0, RUN, rest, 0)
 
         return carry
 
@@ -366,11 +363,8 @@
 
         @pl.when(over[b0 // RUN, 0] > 0)
         def _():
-            def rest(u, carry):
+            for u in range(RUN):
                 add_row(range(cut, slots), b0 + u, tables, slope[t * RUN + u], kept, total)
-                return carry
-
-            lax.fori_loop(0, RUN, rest, 0)
 
         return carry
 
@@ -437,6 +431,28 @@
         cost_estimate=work_of(rows, slots - cut_of(slots), weightings, width),
         name="near_backward",
     )(tables[0], *tables[2:], slope_mine, slope_others, held(kept_mine), held(kept_others), near)
+
+
+def finish_kernel(me, mine, other, weights, gradient):
+    own, _, width = mine.shape[1:]
+    for out, i in ((weights, 0), (gradient, 1)):
+        for c in range(2 * own):
+            held_here = me[1] == c // own
+            tile = jnp.where(held_here, mine[i, c % own], other[i, c % own])
+            out[:, 0, c * width : (c + 1) * width] = tile
+
+
+def finish(me, mine, other):
+    _, own, weightings, width = mine.shape
+    out = jax.ShapeDtypeStruct((weightings, 1, 2 * own * width), F32)
+    return pl.pallas_call(
+        finish_kernel,
+        in_specs=[in_smem(), in_vmem(), in_vmem()],
+        out_specs=[in_vmem()] * 2,
+        out_shape=[out] * 2,
+        compiler_params=PARAMS,
+        name="finish",
+    )(me, mine, other)
 
 
 def per_device(
@@ -548,13 +564,7 @@
                 pieces, turned_others = lax.optimization_barrier((pieces, turned_others))
 
     mine = jnp.stack([weights, gradient])
-    other = over_rep(mine)
-    first = sides[0, :1] > 0
-    both = jnp.concatenate(
-        [jnp.where(first, mine, other), jnp.where(first, other, mine)], axis=1
-    )
-    both = both.transpose(0, 2, 1, 3).reshape(2, weightings, 1, chunk_spots)
-    return both[0], both[1]
+    return tuple(finish(me, mine, over_rep(mine)))
 
 
 def solution(mesh):

time: 126 us -> 124 us (0.984)
  starting transfers between devices: 47.8 us -> 43.3 us
  waiting for transfers between devices: 39.5 us -> 42.9 us
  local copies, waits for them, and re-layouts: 3.43 us -> 1.36 us
    ppermute x17, waiting for transfers between devices: 6.45 us -> 9.85 us  [over_rep(): return lax.ppermute(array, 'rep', [(0, 1), (1, 0)])]
    ppermute x4, starting transfers between devices: 7.86 us -> 5.02 us  [per_device(): got = lax.ppermute(sent, 'spot', [(i, i ^ bit) for i in range(n_spot)])]
    ppermute x24, waiting for transfers between devices: 23.1 us -> 20.9 us  [over_vox(): lax.ppermute(a, 'vox', [(i, i ^ d) for i in range(n_vox)])]
    ppermute x4, waiting for transfers between devices: 9.97 us -> 12.1 us  [per_device(): got = lax.ppermute(sent, 'spot', [(i, i ^ bit) for i in range(n_spot)])]
    ppermute x17, starting transfers between devices: 2.96 us -> 1.36 us  [over_rep(): return lax.ppermute(array, 'rep', [(0, 1), (1, 0)])]
    slice x3 -> x0, local copies, waits for them, and re-layouts: 1.41 us -> none  [per_device(): return (both[0], both[1])]
  transfers between devices with their start and end apart: 45 -> 45, of which waited for: 31 -> 33; matrix products, arithmetic and copies ran while one was open for 0% -> 0% of each run, Pallas kernels for 19% -> 18%
where the time goes in v9:
time: 124 us; the launch traced here: 125 us
  starting transfers between devices  43.3 us (35%)
  waiting for transfers between devices  42.9 us (35%)
  Pallas kernels  35.1 us (28%)
  local copies, waits for them, and re-layouts  1.36 us (1%)
    ppermute x24, starting transfers between devices, over_vox(): lax.ppermute(a, 'vox', [(i, i ^ d) for i in range(n_vox)])  36.9 us
    ppermute x24, waiting for transfers between devices, over_vox(): lax.ppermute(a, 'vox', [(i, i ^ d) for i in range(n_vox)])  20.9 us
    ppermute x4, waiting for transfers between devices, per_device(): got = lax.ppermute(sent, 'spot', [(i, i ^ bit) for i in range(n_spot)])  12.1 us
    ppermute x17, waiting for transfers between devices, over_rep(): return lax.ppermute(array, 'rep', [(0, 1), (1, 0)])  9.85 us
    pallas_call x8, Pallas kernels, backward(): pl.pallas_call(functools.partial(backward_kernel, mine, row0), in_specs=[...  8.41 us
    pallas_call x6, Pallas kernels, forward(): pl.pallas_call(functools.partial(forward_kernel, row0), in_specs=[in_smem...  6.13 us
    pallas_call x2, Pallas kernels, turn(): pl.pallas_call(turn_kernel, in_specs=[in_vmem(), pl.BlockSpec(memory_spac...  5.85 us
    ppermute x4, starting transfers between devices, per_device(): got = lax.ppermute(sent, 'spot', [(i, i ^ bit) for i in range(n_spot)])  5.02 us
  transfers between devices with their start and end apart: 45, of which 33 were waited for; matrix products, arithmetic and copies ran while one was open for 0% of the time, Pallas kernels for 18%

profile of v9, /device:TPU:0, one launch (start us, length us, event | category | flops | bytes accessed | tf_op | source)
XLA Modules:
  0.0 124.6 jit_solution(13051295917859684189)
XLA Ops:
  1.6 5.1 %collective-permute-start.2 = (bf16[8,16,128]{2,1,0:T(8,128)(2,1)S(1)}, bf16[8,16,128]{2,1,0:T(8,128)(2,1)S(1)}, u32[]{:S(2)}, u32[]{:S(2)}) collective-permute-start(bf16[8,16,128]{2,1,0:T(8,128)(2,1)S(1)} %bitcast.49), channel_id=1, source_target_pairs={{0,12},{4,8},{8,4},{12,0},{1,13},{5,9},{9,5},{13,1},{2,14},{6,10},... | collective-permute-start | bytes 98312 | tf_op jit(solution)/shard_map/ppermute | solution.py:483
  7.4 3.9 %prepare.1 = (s32[16,24]{1,0:T(8,128)S(4)}, s32[16,24]{1,0:T(8,128)S(4)}, s32[16,24]{1,0:T(8,128)S(4)}, f32[16,24]{1,0:T(8,128)S(4)}, s32[4,128]{1,0:T(4,128)S(4...) custom-call(s32[3]{0:T(128)S(1)} %pad_add_fusion.me, s32[16,1,24]{2,1,0:T(1,128)} %cols.1, ...), custom_call_target="tpu_custom_call" | custom-call | bytes 12582912 | tf_op jit(solution)/shard_map/prepare/pallas_call | solution.py:108
  13.0 4.0 %first_forward.1 = (f32[8,16,128]{2,1,0:T(8,128)S(1)}, f32[8,16,128]{2,1,0:T(8,128)S(1)}, bf16[192,128,128]{2,1,0:T(8,128)(2,1)S(1)}) custom-call(s32[3]{0:T(128)S(4)} %get-tuple-element.46.me, s32[16,24]{1,0:T(8,128)S(4)} %get-tuple-element.47.slot, s32[16,24]{1,0:T(8,128)S(4)} %get-tuple-element.52.index, ...), custom_call_target="tpu_custom_call" | custom-call | flops 201326592 | bytes 12582912 | tf_op jit(solution)/shard_map/first_forward/pallas_call | solution.py:313
  18.3 1.6 %collective-permute-start.5 = (f32[9,16,128]{2,1,0:T(8,128)S(1)}, f32[9,16,128]{2,1,0:T(8,128)S(1)}, u32[]{:S(2)}, u32[]{:S(2)}) collective-permute-start(f32[9,16,128]{2,1,0:T(8,128)S(1)} %pad_maximum_fusion.3), channel_id=1, source_target_pairs={{0,2},{2,0},{1,3},{3,1},{4,6},{6,4},{5,7},{7,5},{8,10},{10,8},{9,1... | collective-permute-start | bytes 221192 | tf_op jit(solution)/shard_map/ppermute | solution.py:527
  20.2 2.6 %collective-permute-done.5 = f32[9,16,128]{2,1,0:T(8,128)S(1)} collective-permute-done((f32[9,16,128]{2,1,0:T(8,128)S(1)}, f32[9,16,128]{2,1,0:T(8,128)S(1)}, u32[]{:S(2)}, u32[]{:S(2)}) %collective-permute-start.5) | collective-permute-done | bytes 73760 | tf_op jit(solution)/shard_map/ppermute | solution.py:527
  27.1 3.4 %collective-permute-start.10 = (f32[8,16,128]{2,1,0:T(8,128)S(1)}, f32[8,16,128]{2,1,0:T(8,128)S(1)}, u32[]{:S(2)}, u32[]{:S(2)}) collective-permute-start(f32[8,16,128]{2,1,0:T(8,128)S(1)} %get-tuple-element.115), channel_id=1, source_target_pairs={{0,12},{4,8},{8,4},{12,0},{1,13},{5,9},{9,5},{13,1},{2,14},{6,10},... | collective-permute-start | bytes 196616 | tf_op jit(solution)/shard_map/ppermute | solution.py:483
  31.5 2.9 %turn.2.turned_mine.turned = bf16[192,128,128]{2,1,0:T(8,128)(2,1)S(1)} custom-call(bf16[192,128,128]{2,1,0:T(8,128)(2,1)S(1)} %get-tuple-element.63.kept.kept_mine, f32[32,16,128]{2,1,0:T(8,128)S(1)} %add.106.after), custom_call_target="tpu_custom_call" | custom-call | bytes 12582912 | tf_op jit(solution)/shard_map/turn/pallas_call | solution.py:140
  34.5 1.8 %collective-permute-done.9 = f32[8,16,128]{2,1,0:T(8,128)S(1)} collective-permute-done((f32[8,16,128]{2,1,0:T(8,128)S(1)}, f32[8,16,128]{2,1,0:T(8,128)S(1)}, u32[]{:S(2)}, u32[]{:S(2)}) %collective-permute-start.9) | collective-permute-done | bytes 65568 | tf_op jit(solution)/shard_map/ppermute | solution.py:483
  36.3 2.4 %collective-permute-start.13 = (bf16[8,16,128]{2,1,0:T(8,128)(2,1)S(1)}, bf16[8,16,128]{2,1,0:T(8,128)(2,1)S(1)}, u32[]{:S(2)}, u32[]{:S(2)}) collective-permute-start(bf16[8,16,128]{2,1,0:T(8,128)(2,1)S(1)} %get-tuple-element.69.after), channel_id=1, source_target_pairs={{0,12},{4,8},{8,4},{12,0},{1,13},{5,9},{9,5},{13,1},{2,14},{6,10},... | collective-permute-start | bytes 98312 | tf_op jit(solution)/shard_map/ppermute | solution.py:483
  39.1 1.7 %collective-permute-start.11 = (bf16[8,16,128]{2,1,0:T(8,128)(2,1)S(1)}, bf16[8,16,128]{2,1,0:T(8,128)(2,1)S(1)}, u32[]{:S(2)}, u32[]{:S(2)}) collective-permute-start(bf16[8,16,128]{2,1,0:T(8,128)(2,1)S(1)} %get-tuple-element.69.after), channel_id=1, source_target_pairs={{0,4},{4,0},{8,12},{12,8},{1,5},{5,1},{9,13},{13,9},{2,6},{6,2},{1... | collective-permute-start | bytes 98312 | tf_op jit(solution)/shard_map/ppermute | solution.py:483
  40.8 2.9 %turn.3.turned_others.turned = bf16[192,128,128]{2,1,0:T(8,128)(2,1)S(1)} custom-call(bf16[192,128,128]{2,1,0:T(8,128)(2,1)S(1)} %get-tuple-element.58.refs_2_.kept.kept_others, bf16[8,16,128]{2,1,0:T(8,128)(2,1)S(1)} %get-tuple-element.69.after), custom_call_target="tpu_custom_call" | custom-call | bytes 12582912 | tf_op jit(solution)/shard_map/turn/pallas_call | solution.py:140
  48.8 3.2 %collective-permute-done.16 = f32[8,16,128]{2,1,0:T(8,128)S(1)} collective-permute-done((f32[8,16,128]{2,1,0:T(8,128)S(1)}, f32[8,16,128]{2,1,0:T(8,128)S(1)}, u32[]{:S(2)}, u32[]{:S(2)}) %collective-permute-start.16) | collective-permute-done | bytes 65568 | tf_op jit(solution)/shard_map/ppermute | solution.py:527
  56.2 1.9 %collective-permute-start.21 = (f32[8,16,128]{2,1,0:T(8,128)S(1)}, f32[8,16,128]{2,1,0:T(8,128)S(1)}, u32[]{:S(2)}, u32[]{:S(2)}) collective-permute-start(f32[8,16,128]{2,1,0:T(8,128)S(1)} %get-tuple-element.112), channel_id=1, source_target_pairs={{0,12},{4,8},{8,4},{12,0},{1,13},{5,9},{9,5},{13,1},{2,14},{6,10},... | collective-permute-start | bytes 196616 | tf_op jit(solution)/shard_map/ppermute | solution.py:483
  58.4 2.3 %collective-permute-start.19 = (f32[8,16,128]{2,1,0:T(8,128)S(1)}, f32[8,16,128]{2,1,0:T(8,128)S(1)}, u32[]{:S(2)}, u32[]{:S(2)}) collective-permute-start(f32[8,16,128]{2,1,0:T(8,128)S(1)} %get-tuple-element.114), channel_id=1, source_target_pairs={{0,4},{4,0},{8,12},{12,8},{1,5},{5,1},{9,13},{13,9},{2,6},{6,2},{1... | collective-permute-start | bytes 196616 | tf_op jit(solution)/shard_map/ppermute | solution.py:483
  60.6 2.4 %collective-permute-done.21 = f32[8,16,128]{2,1,0:T(8,128)S(1)} collective-permute-done((f32[8,16,128]{2,1,0:T(8,128)S(1)}, f32[8,16,128]{2,1,0:T(8,128)S(1)}, u32[]{:S(2)}, u32[]{:S(2)}) %collective-permute-start.21) | collective-permute-done | bytes 65568 | tf_op jit(solution)/shard_map/ppermute | solution.py:483
  63.0 2.0 %collective-permute-done.20 = f32[8,16,128]{2,1,0:T(8,128)S(1)} collective-permute-done((f32[8,16,128]{2,1,0:T(8,128)S(1)}, f32[8,16,128]{2,1,0:T(8,128)S(1)}, u32[]{:S(2)}, u32[]{:S(2)}) %collective-permute-start.20) | collective-permute-done | bytes 65568 | tf_op jit(solution)/shard_map/ppermute | solution.py:483
  65.0 2.0 %collective-permute-start.24 = (bf16[8,16,128]{2,1,0:T(8,128)(2,1)S(1)}, bf16[8,16,128]{2,1,0:T(8,128)(2,1)S(1)}, u32[]{:S(2)}, u32[]{:S(2)}) collective-permute-start(bf16[8,16,128]{2,1,0:T(8,128)(2,1)S(1)} %get-tuple-element.102), channel_id=1, source_target_pairs={{0,12},{4,8},{8,4},{12,0},{1,13},{5,9},{9,5},{13,1},{2,14},{6,10},... | collective-permute-start | bytes 98312 | tf_op jit(solution)/shard_map/ppermute | solution.py:483
  67.0 2.5 %collective-permute-start.22 = (bf16[8,16,128]{2,1,0:T(8,128)(2,1)S(1)}, bf16[8,16,128]{2,1,0:T(8,128)(2,1)S(1)}, u32[]{:S(2)}, u32[]{:S(2)}) collective-permute-start(bf16[8,16,128]{2,1,0:T(8,128)(2,1)S(1)} %get-tuple-element.102), channel_id=1, source_target_pairs={{0,4},{4,0},{8,12},{12,8},{1,5},{5,1},{9,13},{13,9},{2,6},{6,2},{1... | collective-permute-start | bytes 98312 | tf_op jit(solution)/shard_map/ppermute | solution.py:483
  69.5 1.4 %collective-permute-done.24 = bf16[8,16,128]{2,1,0:T(8,128)(2,1)S(1)} collective-permute-done((bf16[8,16,128]{2,1,0:T(8,128)(2,1)S(1)}, bf16[8,16,128]{2,1,0:T(8,128)(2,1)S(1)}, u32[]{:S(2)}, u32[]{:S(2)}) %collective-permute-start.24) | collective-permute-done | bytes 32800 | tf_op jit(solution)/shard_map/ppermute | solution.py:483
  77.0 3.0 %collective-permute-done.27 = f32[8,16,128]{2,1,0:T(8,128)S(1)} collective-permute-done((f32[8,16,128]{2,1,0:T(8,128)S(1)}, f32[8,16,128]{2,1,0:T(8,128)S(1)}, u32[]{:S(2)}, u32[]{:S(2)}) %collective-permute-start.27) | collective-permute-done | bytes 65568 | tf_op jit(solution)/shard_map/ppermute | solution.py:527
  84.4 1.5 %collective-permute-start.32 = (f32[8,16,128]{2,1,0:T(8,128)S(1)}, f32[8,16,128]{2,1,0:T(8,128)S(1)}, u32[]{:S(2)}, u32[]{:S(2)}) collective-permute-start(f32[8,16,128]{2,1,0:T(8,128)S(1)} %get-tuple-element.109), channel_id=1, source_target_pairs={{0,12},{4,8},{8,4},{12,0},{1,13},{5,9},{9,5},{13,1},{2,14},{6,10},... | collective-permute-start | bytes 196616 | tf_op jit(solution)/shard_map/ppermute | solution.py:483
  87.2 1.6 %collective-permute-start.30 = (f32[8,16,128]{2,1,0:T(8,128)S(1)}, f32[8,16,128]{2,1,0:T(8,128)S(1)}, u32[]{:S(2)}, u32[]{:S(2)}) collective-permute-start(f32[8,16,128]{2,1,0:T(8,128)S(1)} %get-tuple-element.111), channel_id=1, source_target_pairs={{0,4},{4,0},{8,12},{12,8},{1,5},{5,1},{9,13},{13,9},{2,6},{6,2},{1... | collective-permute-start | bytes 196616 | tf_op jit(solution)/shard_map/ppermute | solution.py:483
  88.8 2.4 %collective-permute-done.32 = f32[8,16,128]{2,1,0:T(8,128)S(1)} collective-permute-done((f32[8,16,128]{2,1,0:T(8,128)S(1)}, f32[8,16,128]{2,1,0:T(8,128)S(1)}, u32[]{:S(2)}, u32[]{:S(2)}) %collective-permute-start.32) | collective-permute-done | bytes 65568 | tf_op jit(solution)/shard_map/ppermute | solution.py:483
  91.2 2.5 %collective-permute-done.31 = f32[8,16,128]{2,1,0:T(8,128)S(1)} collective-permute-done((f32[8,16,128]{2,1,0:T(8,128)S(1)}, f32[8,16,128]{2,1,0:T(8,128)S(1)}, u32[]{:S(2)}, u32[]{:S(2)}) %collective-permute-start.31) | collective-permute-done | bytes 65568 | tf_op jit(solution)/shard_map/ppermute | solution.py:483
  93.8 1.6 %collective-permute-start.35 = (bf16[8,16,128]{2,1,0:T(8,128)(2,1)S(1)}, bf16[8,16,128]{2,1,0:T(8,128)(2,1)S(1)}, u32[]{:S(2)}, u32[]{:S(2)}) collective-permute-start(bf16[8,16,128]{2,1,0:T(8,128)(2,1)S(1)} %get-tuple-element.100), channel_id=1, source_target_pairs={{0,12},{4,8},{8,4},{12,0},{1,13},{5,9},{9,5},{13,1},{2,14},{6,10},... | collective-permute-start | bytes 98312 | tf_op jit(solution)/shard_map/ppermute | solution.py:483
  95.4 2.8 %collective-permute-start.33 = (bf16[8,16,128]{2,1,0:T(8,128)(2,1)S(1)}, bf16[8,16,128]{2,1,0:T(8,128)(2,1)S(1)}, u32[]{:S(2)}, u32[]{:S(2)}) collective-permute-start(bf16[8,16,128]{2,1,0:T(8,128)(2,1)S(1)} %get-tuple-element.100), channel_id=1, source_target_pairs={{0,4},{4,0},{8,12},{12,8},{1,5},{5,1},{9,13},{13,9},{2,6},{6,2},{1... | collective-permute-start | bytes 98312 | tf_op jit(solution)/shard_map/ppermute | solution.py:483
  98.2 1.5 %collective-permute-done.35 = bf16[8,16,128]{2,1,0:T(8,128)(2,1)S(1)} collective-permute-done((bf16[8,16,128]{2,1,0:T(8,128)(2,1)S(1)}, bf16[8,16,128]{2,1,0:T(8,128)(2,1)S(1)}, u32[]{:S(2)}, u32[]{:S(2)}) %collective-permute-start.35) | collective-permute-done | bytes 32800 | tf_op jit(solution)/shard_map/ppermute | solution.py:483
  105.4 3.3 %collective-permute-done.38 = f32[8,16,128]{2,1,0:T(8,128)S(1)} collective-permute-done((f32[8,16,128]{2,1,0:T(8,128)S(1)}, f32[8,16,128]{2,1,0:T(8,128)S(1)}, u32[]{:S(2)}, u32[]{:S(2)}) %collective-permute-start.38) | collective-permute-done | bytes 65568 | tf_op jit(solution)/shard_map/ppermute | solution.py:527
  112.9 1.5 %collective-permute-start.43 = (f32[8,16,128]{2,1,0:T(8,128)S(1)}, f32[8,16,128]{2,1,0:T(8,128)S(1)}, u32[]{:S(2)}, u32[]{:S(2)}) collective-permute-start(f32[8,16,128]{2,1,0:T(8,128)S(1)} %get-tuple-element.106), channel_id=1, source_target_pairs={{0,12},{4,8},{8,4},{12,0},{1,13},{5,9},{9,5},{13,1},{2,14},{6,10},... | collective-permute-start | bytes 196616 | tf_op jit(solution)/shard_map/ppermute | solution.py:483
  115.8 1.6 %collective-permute-start.41 = (f32[8,16,128]{2,1,0:T(8,128)S(1)}, f32[8,16,128]{2,1,0:T(8,128)S(1)}, u32[]{:S(2)}, u32[]{:S(2)}) collective-permute-start(f32[8,16,128]{2,1,0:T(8,128)S(1)} %get-tuple-element.108), channel_id=1, source_target_pairs={{0,4},{4,0},{8,12},{12,8},{1,5},{5,1},{9,13},{13,9},{2,6},{6,2},{1... | collective-permute-start | bytes 196616 | tf_op jit(solution)/shard_map/ppermute | solution.py:483
  117.4 2.4 %collective-permute-done.43 = f32[8,16,128]{2,1,0:T(8,128)S(1)} collective-permute-done((f32[8,16,128]{2,1,0:T(8,128)S(1)}, f32[8,16,128]{2,1,0:T(8,128)S(1)}, u32[]{:S(2)}, u32[]{:S(2)}) %collective-permute-start.43) | collective-permute-done | bytes 65568 | tf_op jit(solution)/shard_map/ppermute | solution.py:483
  119.8 2.6 %collective-permute-done.42 = f32[8,16,128]{2,1,0:T(8,128)S(1)} collective-permute-done((f32[8,16,128]{2,1,0:T(8,128)S(1)}, f32[8,16,128]{2,1,0:T(8,128)S(1)}, u32[]{:S(2)}, u32[]{:S(2)}) %collective-permute-start.42) | collective-permute-done | bytes 65568 | tf_op jit(solution)/shard_map/ppermute | solution.py:483
  (140 shorter events, 45.2 us)
Async XLA Ops:
  1.6 9.7 %collective-permute-start.2 = (bf16[8,16,128]{2,1,0:T(8,128)(2,1)S(1)}, bf16[8,16,128]{2,1,0:T(8,128)(2,1)S(1)}, u32[]{:S(2)}, u32[]{:S(2)}) collective-permute-start(bf16[8,16,128]{2,1,0:T(8,128)(2,1)S(1)} %bitcast.49), channel_id=1, source_target_pairs={{0,12},{4,8},{8,4},{12,0},{1,13},{5,9},{9,5},{13,1},{2,14},{6,10},... | collective-permute-start | bytes 98312 | tf_op jit(solution)/shard_map/ppermute | solution.py:483
  6.7 4.8 %collective-permute-start.1 = (bf16[8,16,128]{2,1,0:T(8,128)(2,1)S(1)}, bf16[8,16,128]{2,1,0:T(8,128)(2,1)S(1)}, u32[]{:S(2)}, u32[]{:S(2)}) collective-permute-start(bf16[8,16,128]{2,1,0:T(8,128)(2,1)S(1)} %bitcast.50), channel_id=1, source_target_pairs={{0,8},{4,12},{8,0},{12,4},{1,9},{5,13},{9,1},{13,5},{2,10},{6,14},... | collective-permute-start | bytes 98312 | tf_op jit(solution)/shard_map/ppermute | solution.py:483
  6.7 4.8 %collective-permute-start = (bf16[8,16,128]{2,1,0:T(8,128)(2,1)S(1)}, bf16[8,16,128]{2,1,0:T(8,128)(2,1)S(1)}, u32[]{:S(2)}, u32[]{:S(2)}) collective-permute-start(bf16[8,16,128]{2,1,0:T(8,128)(2,1)S(1)} %bitcast.51), channel_id=1, source_target_pairs={{0,4},{4,0},{8,12},{12,8},{1,5},{5,1},{9,13},{13,9},{2,6},{6,2},{1... | collective-permute-start | bytes 98312 | tf_op jit(solution)/shard_map/ppermute | solution.py:483
  18.3 4.4 %collective-permute-start.5 = (f32[9,16,128]{2,1,0:T(8,128)S(1)}, f32[9,16,128]{2,1,0:T(8,128)S(1)}, u32[]{:S(2)}, u32[]{:S(2)}) collective-permute-start(f32[9,16,128]{2,1,0:T(8,128)S(1)} %pad_maximum_fusion.3), channel_id=1, source_target_pairs={{0,2},{2,0},{1,3},{3,1},{4,6},{6,4},{5,7},{7,5},{8,10},{10,8},{9,1... | collective-permute-start | bytes 221192 | tf_op jit(solution)/shard_map/ppermute | solution.py:527
  25.4 1.6 %collective-permute-start.7 = (f32[32,16,128]{2,1,0:T(8,128)S(1)}, f32[32,16,128]{2,1,0:T(8,128)S(1)}, u32[]{:S(2)}, u32[]{:S(2)}) collective-permute-start(f32[32,16,128]{2,1,0:T(8,128)S(1)} %get-tuple-element.65), channel_id=1, source_target_pairs={{0,1},{1,0},{2,3},{3,2},{4,5},{5,4},{6,7},{7,6},{8,9},{9,8},{10,11... | collective-permute-start | bytes 786440 | tf_op jit(solution)/shard_map/ppermute | solution.py:488
  27.1 7.4 %collective-permute-start.10 = (f32[8,16,128]{2,1,0:T(8,128)S(1)}, f32[8,16,128]{2,1,0:T(8,128)S(1)}, u32[]{:S(2)}, u32[]{:S(2)}) collective-permute-start(f32[8,16,128]{2,1,0:T(8,128)S(1)} %get-tuple-element.115), channel_id=1, source_target_pairs={{0,12},{4,8},{8,4},{12,0},{1,13},{5,9},{9,5},{13,1},{2,14},{6,10},... | collective-permute-start | bytes 196616 | tf_op jit(solution)/shard_map/ppermute | solution.py:483
  30.5 5.8 %collective-permute-start.9 = (f32[8,16,128]{2,1,0:T(8,128)S(1)}, f32[8,16,128]{2,1,0:T(8,128)S(1)}, u32[]{:S(2)}, u32[]{:S(2)}) collective-permute-start(f32[8,16,128]{2,1,0:T(8,128)S(1)} %get-tuple-element.116), channel_id=1, source_target_pairs={{0,8},{4,12},{8,0},{12,4},{1,9},{5,13},{9,1},{13,5},{2,10},{6,14},... | collective-permute-start | bytes 196616 | tf_op jit(solution)/shard_map/ppermute | solution.py:483
  30.5 5.8 %collective-permute-start.8 = (f32[8,16,128]{2,1,0:T(8,128)S(1)}, f32[8,16,128]{2,1,0:T(8,128)S(1)}, u32[]{:S(2)}, u32[]{:S(2)}) collective-permute-start(f32[8,16,128]{2,1,0:T(8,128)S(1)} %get-tuple-element.117), channel_id=1, source_target_pairs={{0,4},{4,0},{8,12},{12,8},{1,5},{5,1},{9,13},{13,9},{2,6},{6,2},{1... | collective-permute-start | bytes 196616 | tf_op jit(solution)/shard_map/ppermute | solution.py:483
  36.3 7.4 %collective-permute-start.13 = (bf16[8,16,128]{2,1,0:T(8,128)(2,1)S(1)}, bf16[8,16,128]{2,1,0:T(8,128)(2,1)S(1)}, u32[]{:S(2)}, u32[]{:S(2)}) collective-permute-start(bf16[8,16,128]{2,1,0:T(8,128)(2,1)S(1)} %get-tuple-element.69.after), channel_id=1, source_target_pairs={{0,12},{4,8},{8,4},{12,0},{1,13},{5,9},{9,5},{13,1},{2,14},{6,10},... | collective-permute-start | bytes 98312 | tf_op jit(solution)/shard_map/ppermute | solution.py:483
  38.7 5.0 %collective-permute-start.12 = (bf16[8,16,128]{2,1,0:T(8,128)(2,1)S(1)}, bf16[8,16,128]{2,1,0:T(8,128)(2,1)S(1)}, u32[]{:S(2)}, u32[]{:S(2)}) collective-permute-start(bf16[8,16,128]{2,1,0:T(8,128)(2,1)S(1)} %get-tuple-element.69.after), channel_id=1, source_target_pairs={{0,8},{4,12},{8,0},{12,4},{1,9},{5,13},{9,1},{13,5},{2,10},{6,14},... | collective-permute-start | bytes 98312 | tf_op jit(solution)/shard_map/ppermute | solution.py:483
  39.1 4.7 %collective-permute-start.11 = (bf16[8,16,128]{2,1,0:T(8,128)(2,1)S(1)}, bf16[8,16,128]{2,1,0:T(8,128)(2,1)S(1)}, u32[]{:S(2)}, u32[]{:S(2)}) collective-permute-start(bf16[8,16,128]{2,1,0:T(8,128)(2,1)S(1)} %get-tuple-element.69.after), channel_id=1, source_target_pairs={{0,4},{4,0},{8,12},{12,8},{1,5},{5,1},{9,13},{13,9},{2,6},{6,2},{1... | collective-permute-start | bytes 98312 | tf_op jit(solution)/shard_map/ppermute | solution.py:483
  47.7 4.3 %collective-permute-start.16 = (f32[8,16,128]{2,1,0:T(8,128)S(1)}, f32[8,16,128]{2,1,0:T(8,128)S(1)}, u32[]{:S(2)}, u32[]{:S(2)}) collective-permute-start(f32[8,16,128]{2,1,0:T(8,128)S(1)} %add.110), channel_id=1, source_target_pairs={{0,2},{2,0},{1,3},{3,1},{4,6},{6,4},{5,7},{7,5},{8,10},{10,8},{9,1... | collective-permute-start | bytes 196616 | tf_op jit(solution)/shard_map/ppermute | solution.py:527
  54.5 1.6 %collective-permute-start.18 = (f32[32,16,128]{2,1,0:T(8,128)S(1)}, f32[32,16,128]{2,1,0:T(8,128)S(1)}, u32[]{:S(2)}, u32[]{:S(2)}) collective-permute-start(f32[32,16,128]{2,1,0:T(8,128)S(1)} %get-tuple-element.76), channel_id=1, source_target_pairs={{0,1},{1,0},{2,3},{3,2},{4,5},{5,4},{6,7},{7,6},{8,9},{9,8},{10,11... | collective-permute-start | bytes 786440 | tf_op jit(solution)/shard_map/ppermute | solution.py:488
  56.2 6.8 %collective-permute-start.21 = (f32[8,16,128]{2,1,0:T(8,128)S(1)}, f32[8,16,128]{2,1,0:T(8,128)S(1)}, u32[]{:S(2)}, u32[]{:S(2)}) collective-permute-start(f32[8,16,128]{2,1,0:T(8,128)S(1)} %get-tuple-element.112), channel_id=1, source_target_pairs={{0,12},{4,8},{8,4},{12,0},{1,13},{5,9},{9,5},{13,1},{2,14},{6,10},... | collective-permute-start | bytes 196616 | tf_op jit(solution)/shard_map/ppermute | solution.py:483
  58.0 7.0 %collective-permute-start.20 = (f32[8,16,128]{2,1,0:T(8,128)S(1)}, f32[8,16,128]{2,1,0:T(8,128)S(1)}, u32[]{:S(2)}, u32[]{:S(2)}) collective-permute-start(f32[8,16,128]{2,1,0:T(8,128)S(1)} %get-tuple-element.113), channel_id=1, source_target_pairs={{0,8},{4,12},{8,0},{12,4},{1,9},{5,13},{9,1},{13,5},{2,10},{6,14},... | collective-permute-start | bytes 196616 | tf_op jit(solution)/shard_map/ppermute | solution.py:483
  58.4 6.6 %collective-permute-start.19 = (f32[8,16,128]{2,1,0:T(8,128)S(1)}, f32[8,16,128]{2,1,0:T(8,128)S(1)}, u32[]{:S(2)}, u32[]{:S(2)}) collective-permute-start(f32[8,16,128]{2,1,0:T(8,128)S(1)} %get-tuple-element.114), channel_id=1, source_target_pairs={{0,4},{4,0},{8,12},{12,8},{1,5},{5,1},{9,13},{13,9},{2,6},{6,2},{1... | collective-permute-start | bytes 196616 | tf_op jit(solution)/shard_map/ppermute | solution.py:483
  65.0 5.9 %collective-permute-start.24 = (bf16[8,16,128]{2,1,0:T(8,128)(2,1)S(1)}, bf16[8,16,128]{2,1,0:T(8,128)(2,1)S(1)}, u32[]{:S(2)}, u32[]{:S(2)}) collective-permute-start(bf16[8,16,128]{2,1,0:T(8,128)(2,1)S(1)} %get-tuple-element.102), channel_id=1, source_target_pairs={{0,12},{4,8},{8,4},{12,0},{1,13},{5,9},{9,5},{13,1},{2,14},{6,10},... | collective-permute-start | bytes 98312 | tf_op jit(solution)/shard_map/ppermute | solution.py:483
  67.0 4.8 %collective-permute-start.23 = (bf16[8,16,128]{2,1,0:T(8,128)(2,1)S(1)}, bf16[8,16,128]{2,1,0:T(8,128)(2,1)S(1)}, u32[]{:S(2)}, u32[]{:S(2)}) collective-permute-start(bf16[8,16,128]{2,1,0:T(8,128)(2,1)S(1)} %get-tuple-element.102), channel_id=1, source_target_pairs={{0,8},{4,12},{8,0},{12,4},{1,9},{5,13},{9,1},{13,5},{2,10},{6,14},... | collective-permute-start | bytes 98312 | tf_op jit(solution)/shard_map/ppermute | solution.py:483
  67.0 4.8 %collective-permute-start.22 = (bf16[8,16,128]{2,1,0:T(8,128)(2,1)S(1)}, bf16[8,16,128]{2,1,0:T(8,128)(2,1)S(1)}, u32[]{:S(2)}, u32[]{:S(2)}) collective-permute-start(bf16[8,16,128]{2,1,0:T(8,128)(2,1)S(1)} %get-tuple-element.102), channel_id=1, source_target_pairs={{0,4},{4,0},{8,12},{12,8},{1,5},{5,1},{9,13},{13,9},{2,6},{6,2},{1... | collective-permute-start | bytes 98312 | tf_op jit(solution)/shard_map/ppermute | solution.py:483
  75.7 4.3 %collective-permute-start.27 = (f32[8,16,128]{2,1,0:T(8,128)S(1)}, f32[8,16,128]{2,1,0:T(8,128)S(1)}, u32[]{:S(2)}, u32[]{:S(2)}) collective-permute-start(f32[8,16,128]{2,1,0:T(8,128)S(1)} %add.118), channel_id=1, source_target_pairs={{0,2},{2,0},{1,3},{3,1},{4,6},{6,4},{5,7},{7,5},{8,10},{10,8},{9,1... | collective-permute-start | bytes 196616 | tf_op jit(solution)/shard_map/ppermute | solution.py:527
  82.7 1.6 %collective-permute-start.29 = (f32[32,16,128]{2,1,0:T(8,128)S(1)}, f32[32,16,128]{2,1,0:T(8,128)S(1)}, u32[]{:S(2)}, u32[]{:S(2)}) collective-permute-start(f32[32,16,128]{2,1,0:T(8,128)S(1)} %get-tuple-element.81), channel_id=1, source_target_pairs={{0,1},{1,0},{2,3},{3,2},{4,5},{5,4},{6,7},{7,6},{8,9},{9,8},{10,11... | collective-permute-start | bytes 786440 | tf_op jit(solution)/shard_map/ppermute | solution.py:488
  84.4 6.8 %collective-permute-start.32 = (f32[8,16,128]{2,1,0:T(8,128)S(1)}, f32[8,16,128]{2,1,0:T(8,128)S(1)}, u32[]{:S(2)}, u32[]{:S(2)}) collective-permute-start(f32[8,16,128]{2,1,0:T(8,128)S(1)} %get-tuple-element.109), channel_id=1, source_target_pairs={{0,12},{4,8},{8,4},{12,0},{1,13},{5,9},{9,5},{13,1},{2,14},{6,10},... | collective-permute-start | bytes 196616 | tf_op jit(solution)/shard_map/ppermute | solution.py:483
  85.9 7.9 %collective-permute-start.31 = (f32[8,16,128]{2,1,0:T(8,128)S(1)}, f32[8,16,128]{2,1,0:T(8,128)S(1)}, u32[]{:S(2)}, u32[]{:S(2)}) collective-permute-start(f32[8,16,128]{2,1,0:T(8,128)S(1)} %get-tuple-element.110), channel_id=1, source_target_pairs={{0,8},{4,12},{8,0},{12,4},{1,9},{5,13},{9,1},{13,5},{2,10},{6,14},... | collective-permute-start | bytes 196616 | tf_op jit(solution)/shard_map/ppermute | solution.py:483
  87.2 6.5 %collective-permute-start.30 = (f32[8,16,128]{2,1,0:T(8,128)S(1)}, f32[8,16,128]{2,1,0:T(8,128)S(1)}, u32[]{:S(2)}, u32[]{:S(2)}) collective-permute-start(f32[8,16,128]{2,1,0:T(8,128)S(1)} %get-tuple-element.111), channel_id=1, source_target_pairs={{0,4},{4,0},{8,12},{12,8},{1,5},{5,1},{9,13},{13,9},{2,6},{6,2},{1... | collective-permute-start | bytes 196616 | tf_op jit(solution)/shard_map/ppermute | solution.py:483
  93.8 6.0 %collective-permute-start.35 = (bf16[8,16,128]{2,1,0:T(8,128)(2,1)S(1)}, bf16[8,16,128]{2,1,0:T(8,128)(2,1)S(1)}, u32[]{:S(2)}, u32[]{:S(2)}) collective-permute-start(bf16[8,16,128]{2,1,0:T(8,128)(2,1)S(1)} %get-tuple-element.100), channel_id=1, source_target_pairs={{0,12},{4,8},{8,4},{12,0},{1,13},{5,9},{9,5},{13,1},{2,14},{6,10},... | collective-permute-start | bytes 98312 | tf_op jit(solution)/shard_map/ppermute | solution.py:483
  95.4 5.1 %collective-permute-start.34 = (bf16[8,16,128]{2,1,0:T(8,128)(2,1)S(1)}, bf16[8,16,128]{2,1,0:T(8,128)(2,1)S(1)}, u32[]{:S(2)}, u32[]{:S(2)}) collective-permute-start(bf16[8,16,128]{2,1,0:T(8,128)(2,1)S(1)} %get-tuple-element.100), channel_id=1, source_target_pairs={{0,8},{4,12},{8,0},{12,4},{1,9},{5,13},{9,1},{13,5},{2,10},{6,14},... | collective-permute-start | bytes 98312 | tf_op jit(solution)/shard_map/ppermute | solution.py:483
  95.4 5.1 %collective-permute-start.33 = (bf16[8,16,128]{2,1,0:T(8,128)(2,1)S(1)}, bf16[8,16,128]{2,1,0:T(8,128)(2,1)S(1)}, u32[]{:S(2)}, u32[]{:S(2)}) collective-permute-start(bf16[8,16,128]{2,1,0:T(8,128)(2,1)S(1)} %get-tuple-element.100), channel_id=1, source_target_pairs={{0,4},{4,0},{8,12},{12,8},{1,5},{5,1},{9,13},{13,9},{2,6},{6,2},{1... | collective-permute-start | bytes 98312 | tf_op jit(solution)/shard_map/ppermute | solution.py:483
  104.4 4.3 %collective-permute-start.38 = (f32[8,16,128]{2,1,0:T(8,128)S(1)}, f32[8,16,128]{2,1,0:T(8,128)S(1)}, u32[]{:S(2)}, u32[]{:S(2)}) collective-permute-start(f32[8,16,128]{2,1,0:T(8,128)S(1)} %add.126), channel_id=1, source_target_pairs={{0,2},{2,0},{1,3},{3,1},{4,6},{6,4},{5,7},{7,5},{8,10},{10,8},{9,1... | collective-permute-start | bytes 196616 | tf_op jit(solution)/shard_map/ppermute | solution.py:527
  111.3 1.6 %collective-permute-start.40 = (f32[32,16,128]{2,1,0:T(8,128)S(1)}, f32[32,16,128]{2,1,0:T(8,128)S(1)}, u32[]{:S(2)}, u32[]{:S(2)}) collective-permute-start(f32[32,16,128]{2,1,0:T(8,128)S(1)} %get-tuple-element.86), channel_id=1, source_target_pairs={{0,1},{1,0},{2,3},{3,2},{4,5},{5,4},{6,7},{7,6},{8,9},{9,8},{10,11... | collective-permute-start | bytes 786440 | tf_op jit(solution)/shard_map/ppermute | solution.py:488
  112.9 6.8 %collective-permute-start.43 = (f32[8,16,128]{2,1,0:T(8,128)S(1)}, f32[8,16,128]{2,1,0:T(8,128)S(1)}, u32[]{:S(2)}, u32[]{:S(2)}) collective-permute-start(f32[8,16,128]{2,1,0:T(8,128)S(1)} %get-tuple-element.106), channel_id=1, source_target_pairs={{0,12},{4,8},{8,4},{12,0},{1,13},{5,9},{9,5},{13,1},{2,14},{6,10},... | collective-permute-start | bytes 196616 | tf_op jit(solution)/shard_map/ppermute | solution.py:483
  114.5 7.9 %collective-permute-start.42 = (f32[8,16,128]{2,1,0:T(8,128)S(1)}, f32[8,16,128]{2,1,0:T(8,128)S(1)}, u32[]{:S(2)}, u32[]{:S(2)}) collective-permute-start(f32[8,16,128]{2,1,0:T(8,128)S(1)} %get-tuple-element.107), channel_id=1, source_target_pairs={{0,8},{4,12},{8,0},{12,4},{1,9},{5,13},{9,1},{13,5},{2,10},{6,14},... | collective-permute-start | bytes 196616 | tf_op jit(solution)/shard_map/ppermute | solution.py:483
  115.8 6.5 %collective-permute-start.41 = (f32[8,16,128]{2,1,0:T(8,128)S(1)}, f32[8,16,128]{2,1,0:T(8,128)S(1)}, u32[]{:S(2)}, u32[]{:S(2)}) collective-permute-start(f32[8,16,128]{2,1,0:T(8,128)S(1)} %get-tuple-element.108), channel_id=1, source_target_pairs={{0,4},{4,0},{8,12},{12,8},{1,5},{5,1},{9,13},{13,9},{2,6},{6,2},{1... | collective-permute-start | bytes 196616 | tf_op jit(solution)/shard_map/ppermute | solution.py:483
  (19 other events, 39.4 us)

commit v10 on v9

--- a/solution.py
+++ b/solution.py
@@ -26,6 +26,7 @@
 
 
 RUN = 4
+LONG_RUN = 8
 
 
 def cut_of(slots):
@@ -247,23 +248,28 @@
     scale_weights([near, far], scaled)
     slots = slot.shape[1]
     cut = cut_of(slots)
-
-    def run(t, carry):
-        b0 = row0 + t * RUN
-        for u in range(RUN):
-            value = row_dose(range(cut), b0 + u, slot, index, scaled, turned)
-            dose[t * RUN + u] = part[b0 + u] + value
-
-        @pl.when(over[b0 // RUN, 0] > 0)
+    rows = dose.shape[0]
+    step = LONG_RUN if rows % LONG_RUN == 0 else RUN
+
+    def some_rows(t, carry):
+        for u in range(step):
+            b = t * step + u
+            value = row_dose(range(cut), row0 + b, slot, index, scaled, turned)
+            dose[b] = part[row0 + b] + value
+        return carry
+
+    lax.fori_loop(0, rows // step, some_rows, 0)
+
+    def rest(t, carry):
+        @pl.when(over[row0 // RUN + t, 0] > 0)
         def _():
             for u in range(RUN):
-                dose[t * RUN + u] += row_dose(
-                    range(cut, slots), b0 + u, slot, index, scaled, turned
-                )
+                b = t * RUN + u
+                dose[b] += row_dose(range(cut, slots), row0 + b, slot, index, scaled, turned)
 
         return carry
 
-    lax.fori_loop(0, dose.shape[0] // RUN, run, 0)
+    lax.fori_loop(0, rows // RUN, rest, 0)
 
 
 def work_of(rows, slots, weightings, width):
@@ -356,19 +362,27 @@
     slots = slot.shape[1]
     cut = cut_of(slots)
 
-    def run(t, carry):
-        b0 = row0 + t * RUN
-        for u in range(RUN):
-            add_row(range(cut), b0 + u, tables, slope[t * RUN + u], kept, total)
-
-        @pl.when(over[b0 // RUN, 0] > 0)
+    rows = slope.shape[0]
+    step = LONG_RUN if rows % LONG_RUN == 0 else RUN
+
+    def some_rows(t, carry):
+        for u in range(step):
+            b = t * step + u
+            add_row(range(cut), row0 + b, tables, slope[b], kept, total)
+        return carry
+
+    lax.fori_loop(0, rows // step, some_rows, 0)
+
+    def rest(t, carry):
+        @pl.when(over[row0 // RUN + t, 0] > 0)
         def _():
             for u in range(RUN):
-                add_row(range(cut, slots), b0 + u, tables, slope[t * RUN + u], kept, total)
+                b = t * RUN + u
+                add_row(range(cut, slots), row0 + b, tables, slope[b], kept, total)
 
         return carry
 
-    lax.fori_loop(0, slope.shape[0] // RUN, run, 0)
+    lax.fori_loop(0, rows // RUN, rest, 0)
     if mine:
         before[0][...] = total[:columns]
     else:

time: 124 us -> 123 us (level)
  waiting for transfers between devices: 42.9 us -> 39.9 us
  starting transfers between devices: 43.3 us -> 46 us
  Pallas kernels: 35.1 us -> 33.4 us
    pallas_call x8, Pallas kernels: 8.41 us -> 6.09 us  [backward(): pl.pallas_call(functools.partial(backward_kernel, mine, row0), in_specs=[...]
    ppermute x17, waiting for transfers between devices: 9.85 us -> 7.64 us  [over_rep(): return lax.ppermute(array, 'rep', [(0, 1), (1, 0)])]
    ppermute x17, starting transfers between devices: 1.36 us -> 2.73 us  [over_rep(): return lax.ppermute(array, 'rep', [(0, 1), (1, 0)])]
    ppermute x4, starting transfers between devices: 5.02 us -> 6.31 us  [per_device(): got = lax.ppermute(sent, 'spot', [(i, i ^ bit) for i in range(n_spot)])]
    ppermute x4, waiting for transfers between devices: 12.1 us -> 10.8 us  [per_device(): got = lax.ppermute(sent, 'spot', [(i, i ^ bit) for i in range(n_spot)])]
  transfers between devices with their start and end apart: 45 -> 45, of which waited for: 33 -> 33; matrix products, arithmetic and copies ran while one was open for 0% -> 0% of each run, Pallas kernels for 18% -> 19%
where the time goes in v10:
time: 123 us
  starting transfers between devices  46 us (37%)
  waiting for transfers between devices  39.9 us (32%)
  Pallas kernels  33.4 us (27%)
  local copies, waits for them, and re-layouts  1.36 us (1%)
    ppermute x24, starting transfers between devices, over_vox(): lax.ppermute(a, 'vox', [(i, i ^ d) for i in range(n_vox)])  36.9 us
    ppermute x24, waiting for transfers between devices, over_vox(): lax.ppermute(a, 'vox', [(i, i ^ d) for i in range(n_vox)])  21.5 us
    ppermute x4, waiting for transfers between devices, per_device(): got = lax.ppermute(sent, 'spot', [(i, i ^ bit) for i in range(n_spot)])  10.8 us
    ppermute x17, waiting for transfers between devices, over_rep(): return lax.ppermute(array, 'rep', [(0, 1), (1, 0)])  7.64 us
    ppermute x4, starting transfers between devices, per_device(): got = lax.ppermute(sent, 'spot', [(i, i ^ bit) for i in range(n_spot)])  6.31 us
    pallas_call x8, Pallas kernels, backward(): pl.pallas_call(functools.partial(backward_kernel, mine, row0), in_specs=[...  6.09 us
    pallas_call x2, Pallas kernels, turn(): pl.pallas_call(turn_kernel, in_specs=[in_vmem(), pl.BlockSpec(memory_spac...  5.85 us
    pallas_call x6, Pallas kernels, forward(): pl.pallas_call(functools.partial(forward_kernel, row0), in_specs=[in_smem...  4.98 us
  transfers between devices with their start and end apart: 45, of which 33 were waited for; matrix products, arithmetic and copies ran while one was open for 0% of the time, Pallas kernels for 19%

profile of v10, /device:TPU:0, one launch (start us, length us, event | category | flops | bytes accessed | tf_op | source)
XLA Modules:
  0.0 122.6 jit_solution(17403961446942992806)
XLA Ops:
  1.6 5.1 %collective-permute-start.2 = (bf16[8,16,128]{2,1,0:T(8,128)(2,1)S(1)}, bf16[8,16,128]{2,1,0:T(8,128)(2,1)S(1)}, u32[]{:S(2)}, u32[]{:S(2)}) collective-permute-start(bf16[8,16,128]{2,1,0:T(8,128)(2,1)S(1)} %bitcast.49), channel_id=1, source_target_pairs={{0,12},{4,8},{8,4},{12,0},{1,13},{5,9},{9,5},{13,1},{2,14},{6,10},... | collective-permute-start | bytes 98312 | tf_op jit(solution)/shard_map/ppermute | solution.py:497
  7.4 3.9 %prepare.1 = (s32[16,24]{1,0:T(8,128)S(4)}, s32[16,24]{1,0:T(8,128)S(4)}, s32[16,24]{1,0:T(8,128)S(4)}, f32[16,24]{1,0:T(8,128)S(4)}, s32[4,128]{1,0:T(4,128)S(4...) custom-call(s32[3]{0:T(128)S(1)} %pad_add_fusion.me, s32[16,1,24]{2,1,0:T(1,128)} %cols.1, ...), custom_call_target="tpu_custom_call" | custom-call | bytes 12582912 | tf_op jit(solution)/shard_map/prepare/pallas_call | solution.py:109
  13.0 4.0 %first_forward.1 = (f32[8,16,128]{2,1,0:T(8,128)S(1)}, f32[8,16,128]{2,1,0:T(8,128)S(1)}, bf16[192,128,128]{2,1,0:T(8,128)(2,1)S(1)}) custom-call(s32[3]{0:T(128)S(4)} %get-tuple-element.46.me, s32[16,24]{1,0:T(8,128)S(4)} %get-tuple-element.47.slot, s32[16,24]{1,0:T(8,128)S(4)} %get-tuple-element.52.index, ...), custom_call_target="tpu_custom_call" | custom-call | flops 201326592 | bytes 12582912 | tf_op jit(solution)/shard_map/first_forward/pallas_call | solution.py:319
  18.3 1.6 %collective-permute-start.5 = (f32[9,16,128]{2,1,0:T(8,128)S(1)}, f32[9,16,128]{2,1,0:T(8,128)S(1)}, u32[]{:S(2)}, u32[]{:S(2)}) collective-permute-start(f32[9,16,128]{2,1,0:T(8,128)S(1)} %pad_maximum_fusion.3), channel_id=1, source_target_pairs={{0,2},{2,0},{1,3},{3,1},{4,6},{6,4},{5,7},{7,5},{8,10},{10,8},{9,1... | collective-permute-start | bytes 221192 | tf_op jit(solution)/shard_map/ppermute | solution.py:541
  20.2 2.6 %collective-permute-done.5 = f32[9,16,128]{2,1,0:T(8,128)S(1)} collective-permute-done((f32[9,16,128]{2,1,0:T(8,128)S(1)}, f32[9,16,128]{2,1,0:T(8,128)S(1)}, u32[]{:S(2)}, u32[]{:S(2)}) %collective-permute-start.5) | collective-permute-done | bytes 73760 | tf_op jit(solution)/shard_map/ppermute | solution.py:541
  26.7 3.7 %collective-permute-start.10 = (f32[8,16,128]{2,1,0:T(8,128)S(1)}, f32[8,16,128]{2,1,0:T(8,128)S(1)}, u32[]{:S(2)}, u32[]{:S(2)}) collective-permute-start(f32[8,16,128]{2,1,0:T(8,128)S(1)} %get-tuple-element.115), channel_id=1, source_target_pairs={{0,12},{4,8},{8,4},{12,0},{1,13},{5,9},{9,5},{13,1},{2,14},{6,10},... | collective-permute-start | bytes 196616 | tf_op jit(solution)/shard_map/ppermute | solution.py:497
  31.1 2.9 %turn.2.turned_mine.turned = bf16[192,128,128]{2,1,0:T(8,128)(2,1)S(1)} custom-call(bf16[192,128,128]{2,1,0:T(8,128)(2,1)S(1)} %get-tuple-element.63.kept.kept_mine, f32[32,16,128]{2,1,0:T(8,128)S(1)} %add.106.after), custom_call_target="tpu_custom_call" | custom-call | bytes 12582912 | tf_op jit(solution)/shard_map/turn/pallas_call | solution.py:141
  34.1 1.9 %collective-permute-done.9 = f32[8,16,128]{2,1,0:T(8,128)S(1)} collective-permute-done((f32[8,16,128]{2,1,0:T(8,128)S(1)}, f32[8,16,128]{2,1,0:T(8,128)S(1)}, u32[]{:S(2)}, u32[]{:S(2)}) %collective-permute-start.9) | collective-permute-done | bytes 65568 | tf_op jit(solution)/shard_map/ppermute | solution.py:497
  36.0 2.5 %collective-permute-start.13 = (bf16[8,16,128]{2,1,0:T(8,128)(2,1)S(1)}, bf16[8,16,128]{2,1,0:T(8,128)(2,1)S(1)}, u32[]{:S(2)}, u32[]{:S(2)}) collective-permute-start(bf16[8,16,128]{2,1,0:T(8,128)(2,1)S(1)} %get-tuple-element.69.after), channel_id=1, source_target_pairs={{0,12},{4,8},{8,4},{12,0},{1,13},{5,9},{9,5},{13,1},{2,14},{6,10},... | collective-permute-start | bytes 98312 | tf_op jit(solution)/shard_map/ppermute | solution.py:497
  38.9 1.6 %collective-permute-start.11 = (bf16[8,16,128]{2,1,0:T(8,128)(2,1)S(1)}, bf16[8,16,128]{2,1,0:T(8,128)(2,1)S(1)}, u32[]{:S(2)}, u32[]{:S(2)}) collective-permute-start(bf16[8,16,128]{2,1,0:T(8,128)(2,1)S(1)} %get-tuple-element.69.after), channel_id=1, source_target_pairs={{0,4},{4,0},{8,12},{12,8},{1,5},{5,1},{9,13},{13,9},{2,6},{6,2},{1... | collective-permute-start | bytes 98312 | tf_op jit(solution)/shard_map/ppermute | solution.py:497
  40.5 2.9 %turn.3.turned_others.turned = bf16[192,128,128]{2,1,0:T(8,128)(2,1)S(1)} custom-call(bf16[192,128,128]{2,1,0:T(8,128)(2,1)S(1)} %get-tuple-element.58.refs_2_.kept.kept_others, bf16[8,16,128]{2,1,0:T(8,128)(2,1)S(1)} %get-tuple-element.69.after), custom_call_target="tpu_custom_call" | custom-call | bytes 12582912 | tf_op jit(solution)/shard_map/turn/pallas_call | solution.py:141
  48.6 2.8 %collective-permute-done.16 = f32[8,16,128]{2,1,0:T(8,128)S(1)} collective-permute-done((f32[8,16,128]{2,1,0:T(8,128)S(1)}, f32[8,16,128]{2,1,0:T(8,128)S(1)}, u32[]{:S(2)}, u32[]{:S(2)}) %collective-permute-start.16) | collective-permute-done | bytes 65568 | tf_op jit(solution)/shard_map/ppermute | solution.py:541
  55.1 2.5 %collective-permute-start.21 = (f32[8,16,128]{2,1,0:T(8,128)S(1)}, f32[8,16,128]{2,1,0:T(8,128)S(1)}, u32[]{:S(2)}, u32[]{:S(2)}) collective-permute-start(f32[8,16,128]{2,1,0:T(8,128)S(1)} %get-tuple-element.112), channel_id=1, source_target_pairs={{0,12},{4,8},{8,4},{12,0},{1,13},{5,9},{9,5},{13,1},{2,14},{6,10},... | collective-permute-start | bytes 196616 | tf_op jit(solution)/shard_map/ppermute | solution.py:497
  57.6 2.0 %collective-permute-start.19 = (f32[8,16,128]{2,1,0:T(8,128)S(1)}, f32[8,16,128]{2,1,0:T(8,128)S(1)}, u32[]{:S(2)}, u32[]{:S(2)}) collective-permute-start(f32[8,16,128]{2,1,0:T(8,128)S(1)} %get-tuple-element.114), channel_id=1, source_target_pairs={{0,4},{4,0},{8,12},{12,8},{1,5},{5,1},{9,13},{13,9},{2,6},{6,2},{1... | collective-permute-start | bytes 196616 | tf_op jit(solution)/shard_map/ppermute | solution.py:497
  59.6 2.4 %collective-permute-done.21 = f32[8,16,128]{2,1,0:T(8,128)S(1)} collective-permute-done((f32[8,16,128]{2,1,0:T(8,128)S(1)}, f32[8,16,128]{2,1,0:T(8,128)S(1)}, u32[]{:S(2)}, u32[]{:S(2)}) %collective-permute-start.21) | collective-permute-done | bytes 65568 | tf_op jit(solution)/shard_map/ppermute | solution.py:497
  62.0 2.1 %collective-permute-done.20 = f32[8,16,128]{2,1,0:T(8,128)S(1)} collective-permute-done((f32[8,16,128]{2,1,0:T(8,128)S(1)}, f32[8,16,128]{2,1,0:T(8,128)S(1)}, u32[]{:S(2)}, u32[]{:S(2)}) %collective-permute-start.20) | collective-permute-done | bytes 65568 | tf_op jit(solution)/shard_map/ppermute | solution.py:497
  64.1 2.5 %collective-permute-start.24 = (bf16[8,16,128]{2,1,0:T(8,128)(2,1)S(1)}, bf16[8,16,128]{2,1,0:T(8,128)(2,1)S(1)}, u32[]{:S(2)}, u32[]{:S(2)}) collective-permute-start(bf16[8,16,128]{2,1,0:T(8,128)(2,1)S(1)} %get-tuple-element.102), channel_id=1, source_target_pairs={{0,12},{4,8},{8,4},{12,0},{1,13},{5,9},{9,5},{13,1},{2,14},{6,10},... | collective-permute-start | bytes 98312 | tf_op jit(solution)/shard_map/ppermute | solution.py:497
  66.6 2.0 %collective-permute-start.22 = (bf16[8,16,128]{2,1,0:T(8,128)(2,1)S(1)}, bf16[8,16,128]{2,1,0:T(8,128)(2,1)S(1)}, u32[]{:S(2)}, u32[]{:S(2)}) collective-permute-start(bf16[8,16,128]{2,1,0:T(8,128)(2,1)S(1)} %get-tuple-element.102), channel_id=1, source_target_pairs={{0,4},{4,0},{8,12},{12,8},{1,5},{5,1},{9,13},{13,9},{2,6},{6,2},{1... | collective-permute-start | bytes 98312 | tf_op jit(solution)/shard_map/ppermute | solution.py:497
  75.1 1.6 %collective-permute-start.27 = (f32[8,16,128]{2,1,0:T(8,128)S(1)}, f32[8,16,128]{2,1,0:T(8,128)S(1)}, u32[]{:S(2)}, u32[]{:S(2)}) collective-permute-start(f32[8,16,128]{2,1,0:T(8,128)S(1)} %add.118), channel_id=1, source_target_pairs={{0,2},{2,0},{1,3},{3,1},{4,6},{6,4},{5,7},{7,5},{8,10},{10,8},{9,1... | collective-permute-start | bytes 196616 | tf_op jit(solution)/shard_map/ppermute | solution.py:541
  76.7 2.7 %collective-permute-done.27 = f32[8,16,128]{2,1,0:T(8,128)S(1)} collective-permute-done((f32[8,16,128]{2,1,0:T(8,128)S(1)}, f32[8,16,128]{2,1,0:T(8,128)S(1)}, u32[]{:S(2)}, u32[]{:S(2)}) %collective-permute-start.27) | collective-permute-done | bytes 65568 | tf_op jit(solution)/shard_map/ppermute | solution.py:541
  83.2 2.1 %collective-permute-start.32 = (f32[8,16,128]{2,1,0:T(8,128)S(1)}, f32[8,16,128]{2,1,0:T(8,128)S(1)}, u32[]{:S(2)}, u32[]{:S(2)}) collective-permute-start(f32[8,16,128]{2,1,0:T(8,128)S(1)} %get-tuple-element.109), channel_id=1, source_target_pairs={{0,12},{4,8},{8,4},{12,0},{1,13},{5,9},{9,5},{13,1},{2,14},{6,10},... | collective-permute-start | bytes 196616 | tf_op jit(solution)/shard_map/ppermute | solution.py:497
  85.8 1.8 %collective-permute-start.30 = (f32[8,16,128]{2,1,0:T(8,128)S(1)}, f32[8,16,128]{2,1,0:T(8,128)S(1)}, u32[]{:S(2)}, u32[]{:S(2)}) collective-permute-start(f32[8,16,128]{2,1,0:T(8,128)S(1)} %get-tuple-element.111), channel_id=1, source_target_pairs={{0,4},{4,0},{8,12},{12,8},{1,5},{5,1},{9,13},{13,9},{2,6},{6,2},{1... | collective-permute-start | bytes 196616 | tf_op jit(solution)/shard_map/ppermute | solution.py:497
  87.7 2.3 %collective-permute-done.32 = f32[8,16,128]{2,1,0:T(8,128)S(1)} collective-permute-done((f32[8,16,128]{2,1,0:T(8,128)S(1)}, f32[8,16,128]{2,1,0:T(8,128)S(1)}, u32[]{:S(2)}, u32[]{:S(2)}) %collective-permute-start.32) | collective-permute-done | bytes 65568 | tf_op jit(solution)/shard_map/ppermute | solution.py:497
  90.0 2.3 %collective-permute-done.31 = f32[8,16,128]{2,1,0:T(8,128)S(1)} collective-permute-done((f32[8,16,128]{2,1,0:T(8,128)S(1)}, f32[8,16,128]{2,1,0:T(8,128)S(1)}, u32[]{:S(2)}, u32[]{:S(2)}) %collective-permute-start.31) | collective-permute-done | bytes 65568 | tf_op jit(solution)/shard_map/ppermute | solution.py:497
  92.3 2.5 %collective-permute-start.35 = (bf16[8,16,128]{2,1,0:T(8,128)(2,1)S(1)}, bf16[8,16,128]{2,1,0:T(8,128)(2,1)S(1)}, u32[]{:S(2)}, u32[]{:S(2)}) collective-permute-start(bf16[8,16,128]{2,1,0:T(8,128)(2,1)S(1)} %get-tuple-element.100), channel_id=1, source_target_pairs={{0,12},{4,8},{8,4},{12,0},{1,13},{5,9},{9,5},{13,1},{2,14},{6,10},... | collective-permute-start | bytes 98312 | tf_op jit(solution)/shard_map/ppermute | solution.py:497
  94.8 2.0 %collective-permute-start.33 = (bf16[8,16,128]{2,1,0:T(8,128)(2,1)S(1)}, bf16[8,16,128]{2,1,0:T(8,128)(2,1)S(1)}, u32[]{:S(2)}, u32[]{:S(2)}) collective-permute-start(bf16[8,16,128]{2,1,0:T(8,128)(2,1)S(1)} %get-tuple-element.100), channel_id=1, source_target_pairs={{0,4},{4,0},{8,12},{12,8},{1,5},{5,1},{9,13},{13,9},{2,6},{6,2},{1... | collective-permute-start | bytes 98312 | tf_op jit(solution)/shard_map/ppermute | solution.py:497
  103.2 1.6 %collective-permute-start.38 = (f32[8,16,128]{2,1,0:T(8,128)S(1)}, f32[8,16,128]{2,1,0:T(8,128)S(1)}, u32[]{:S(2)}, u32[]{:S(2)}) collective-permute-start(f32[8,16,128]{2,1,0:T(8,128)S(1)} %add.126), channel_id=1, source_target_pairs={{0,2},{2,0},{1,3},{3,1},{4,6},{6,4},{5,7},{7,5},{8,10},{10,8},{9,1... | collective-permute-start | bytes 196616 | tf_op jit(solution)/shard_map/ppermute | solution.py:541
  104.7 2.8 %collective-permute-done.38 = f32[8,16,128]{2,1,0:T(8,128)S(1)} collective-permute-done((f32[8,16,128]{2,1,0:T(8,128)S(1)}, f32[8,16,128]{2,1,0:T(8,128)S(1)}, u32[]{:S(2)}, u32[]{:S(2)}) %collective-permute-start.38) | collective-permute-done | bytes 65568 | tf_op jit(solution)/shard_map/ppermute | solution.py:541
  111.3 1.9 %collective-permute-start.43 = (f32[8,16,128]{2,1,0:T(8,128)S(1)}, f32[8,16,128]{2,1,0:T(8,128)S(1)}, u32[]{:S(2)}, u32[]{:S(2)}) collective-permute-start(f32[8,16,128]{2,1,0:T(8,128)S(1)} %get-tuple-element.106), channel_id=1, source_target_pairs={{0,12},{4,8},{8,4},{12,0},{1,13},{5,9},{9,5},{13,1},{2,14},{6,10},... | collective-permute-start | bytes 196616 | tf_op jit(solution)/shard_map/ppermute | solution.py:497
  113.9 1.8 %collective-permute-start.41 = (f32[8,16,128]{2,1,0:T(8,128)S(1)}, f32[8,16,128]{2,1,0:T(8,128)S(1)}, u32[]{:S(2)}, u32[]{:S(2)}) collective-permute-start(f32[8,16,128]{2,1,0:T(8,128)S(1)} %get-tuple-element.108), channel_id=1, source_target_pairs={{0,4},{4,0},{8,12},{12,8},{1,5},{5,1},{9,13},{13,9},{2,6},{6,2},{1... | collective-permute-start | bytes 196616 | tf_op jit(solution)/shard_map/ppermute | solution.py:497
  115.7 2.3 %collective-permute-done.43 = f32[8,16,128]{2,1,0:T(8,128)S(1)} collective-permute-done((f32[8,16,128]{2,1,0:T(8,128)S(1)}, f32[8,16,128]{2,1,0:T(8,128)S(1)}, u32[]{:S(2)}, u32[]{:S(2)}) %collective-permute-start.43) | collective-permute-done | bytes 65568 | tf_op jit(solution)/shard_map/ppermute | solution.py:497
  118.1 2.3 %collective-permute-done.42 = f32[8,16,128]{2,1,0:T(8,128)S(1)} collective-permute-done((f32[8,16,128]{2,1,0:T(8,128)S(1)}, f32[8,16,128]{2,1,0:T(8,128)S(1)}, u32[]{:S(2)}, u32[]{:S(2)}) %collective-permute-start.42) | collective-permute-done | bytes 65568 | tf_op jit(solution)/shard_map/ppermute | solution.py:497
  (140 shorter events, 42.8 us)
Async XLA Ops:
  1.6 9.7 %collective-permute-start.2 = (bf16[8,16,128]{2,1,0:T(8,128)(2,1)S(1)}, bf16[8,16,128]{2,1,0:T(8,128)(2,1)S(1)}, u32[]{:S(2)}, u32[]{:S(2)}) collective-permute-start(bf16[8,16,128]{2,1,0:T(8,128)(2,1)S(1)} %bitcast.49), channel_id=1, source_target_pairs={{0,12},{4,8},{8,4},{12,0},{1,13},{5,9},{9,5},{13,1},{2,14},{6,10},... | collective-permute-start | bytes 98312 | tf_op jit(solution)/shard_map/ppermute | solution.py:497
  6.7 4.8 %collective-permute-start.1 = (bf16[8,16,128]{2,1,0:T(8,128)(2,1)S(1)}, bf16[8,16,128]{2,1,0:T(8,128)(2,1)S(1)}, u32[]{:S(2)}, u32[]{:S(2)}) collective-permute-start(bf16[8,16,128]{2,1,0:T(8,128)(2,1)S(1)} %bitcast.50), channel_id=1, source_target_pairs={{0,8},{4,12},{8,0},{12,4},{1,9},{5,13},{9,1},{13,5},{2,10},{6,14},... | collective-permute-start | bytes 98312 | tf_op jit(solution)/shard_map/ppermute | solution.py:497
  6.7 4.8 %collective-permute-start = (bf16[8,16,128]{2,1,0:T(8,128)(2,1)S(1)}, bf16[8,16,128]{2,1,0:T(8,128)(2,1)S(1)}, u32[]{:S(2)}, u32[]{:S(2)}) collective-permute-start(bf16[8,16,128]{2,1,0:T(8,128)(2,1)S(1)} %bitcast.51), channel_id=1, source_target_pairs={{0,4},{4,0},{8,12},{12,8},{1,5},{5,1},{9,13},{13,9},{2,6},{6,2},{1... | collective-permute-start | bytes 98312 | tf_op jit(solution)/shard_map/ppermute | solution.py:497
  18.3 4.4 %collective-permute-start.5 = (f32[9,16,128]{2,1,0:T(8,128)S(1)}, f32[9,16,128]{2,1,0:T(8,128)S(1)}, u32[]{:S(2)}, u32[]{:S(2)}) collective-permute-start(f32[9,16,128]{2,1,0:T(8,128)S(1)} %pad_maximum_fusion.3), channel_id=1, source_target_pairs={{0,2},{2,0},{1,3},{3,1},{4,6},{6,4},{5,7},{7,5},{8,10},{10,8},{9,1... | collective-permute-start | bytes 221192 | tf_op jit(solution)/shard_map/ppermute | solution.py:541
  25.0 1.6 %collective-permute-start.7 = (f32[32,16,128]{2,1,0:T(8,128)S(1)}, f32[32,16,128]{2,1,0:T(8,128)S(1)}, u32[]{:S(2)}, u32[]{:S(2)}) collective-permute-start(f32[32,16,128]{2,1,0:T(8,128)S(1)} %get-tuple-element.65), channel_id=1, source_target_pairs={{0,1},{1,0},{2,3},{3,2},{4,5},{5,4},{6,7},{7,6},{8,9},{9,8},{10,11... | collective-permute-start | bytes 786440 | tf_op jit(solution)/shard_map/ppermute | solution.py:502
  26.7 7.4 %collective-permute-start.10 = (f32[8,16,128]{2,1,0:T(8,128)S(1)}, f32[8,16,128]{2,1,0:T(8,128)S(1)}, u32[]{:S(2)}, u32[]{:S(2)}) collective-permute-start(f32[8,16,128]{2,1,0:T(8,128)S(1)} %get-tuple-element.115), channel_id=1, source_target_pairs={{0,12},{4,8},{8,4},{12,0},{1,13},{5,9},{9,5},{13,1},{2,14},{6,10},... | collective-permute-start | bytes 196616 | tf_op jit(solution)/shard_map/ppermute | solution.py:497
  30.3 5.7 %collective-permute-start.9 = (f32[8,16,128]{2,1,0:T(8,128)S(1)}, f32[8,16,128]{2,1,0:T(8,128)S(1)}, u32[]{:S(2)}, u32[]{:S(2)}) collective-permute-start(f32[8,16,128]{2,1,0:T(8,128)S(1)} %get-tuple-element.116), channel_id=1, source_target_pairs={{0,8},{4,12},{8,0},{12,4},{1,9},{5,13},{9,1},{13,5},{2,10},{6,14},... | collective-permute-start | bytes 196616 | tf_op jit(solution)/shard_map/ppermute | solution.py:497
  30.3 5.7 %collective-permute-start.8 = (f32[8,16,128]{2,1,0:T(8,128)S(1)}, f32[8,16,128]{2,1,0:T(8,128)S(1)}, u32[]{:S(2)}, u32[]{:S(2)}) collective-permute-start(f32[8,16,128]{2,1,0:T(8,128)S(1)} %get-tuple-element.117), channel_id=1, source_target_pairs={{0,4},{4,0},{8,12},{12,8},{1,5},{5,1},{9,13},{13,9},{2,6},{6,2},{1... | collective-permute-start | bytes 196616 | tf_op jit(solution)/shard_map/ppermute | solution.py:497
  36.0 7.4 %collective-permute-start.13 = (bf16[8,16,128]{2,1,0:T(8,128)(2,1)S(1)}, bf16[8,16,128]{2,1,0:T(8,128)(2,1)S(1)}, u32[]{:S(2)}, u32[]{:S(2)}) collective-permute-start(bf16[8,16,128]{2,1,0:T(8,128)(2,1)S(1)} %get-tuple-element.69.after), channel_id=1, source_target_pairs={{0,12},{4,8},{8,4},{12,0},{1,13},{5,9},{9,5},{13,1},{2,14},{6,10},... | collective-permute-start | bytes 98312 | tf_op jit(solution)/shard_map/ppermute | solution.py:497
  38.5 4.9 %collective-permute-start.12 = (bf16[8,16,128]{2,1,0:T(8,128)(2,1)S(1)}, bf16[8,16,128]{2,1,0:T(8,128)(2,1)S(1)}, u32[]{:S(2)}, u32[]{:S(2)}) collective-permute-start(bf16[8,16,128]{2,1,0:T(8,128)(2,1)S(1)} %get-tuple-element.69.after), channel_id=1, source_target_pairs={{0,8},{4,12},{8,0},{12,4},{1,9},{5,13},{9,1},{13,5},{2,10},{6,14},... | collective-permute-start | bytes 98312 | tf_op jit(solution)/shard_map/ppermute | solution.py:497
  38.9 4.5 %collective-permute-start.11 = (bf16[8,16,128]{2,1,0:T(8,128)(2,1)S(1)}, bf16[8,16,128]{2,1,0:T(8,128)(2,1)S(1)}, u32[]{:S(2)}, u32[]{:S(2)}) collective-permute-start(bf16[8,16,128]{2,1,0:T(8,128)(2,1)S(1)} %get-tuple-element.69.after), channel_id=1, source_target_pairs={{0,4},{4,0},{8,12},{12,8},{1,5},{5,1},{9,13},{13,9},{2,6},{6,2},{1... | collective-permute-start | bytes 98312 | tf_op jit(solution)/shard_map/ppermute | solution.py:497
  47.1 4.3 %collective-permute-start.16 = (f32[8,16,128]{2,1,0:T(8,128)S(1)}, f32[8,16,128]{2,1,0:T(8,128)S(1)}, u32[]{:S(2)}, u32[]{:S(2)}) collective-permute-start(f32[8,16,128]{2,1,0:T(8,128)S(1)} %add.110), channel_id=1, source_target_pairs={{0,2},{2,0},{1,3},{3,1},{4,6},{6,4},{5,7},{7,5},{8,10},{10,8},{9,1... | collective-permute-start | bytes 196616 | tf_op jit(solution)/shard_map/ppermute | solution.py:541
  53.5 1.6 %collective-permute-start.18 = (f32[32,16,128]{2,1,0:T(8,128)S(1)}, f32[32,16,128]{2,1,0:T(8,128)S(1)}, u32[]{:S(2)}, u32[]{:S(2)}) collective-permute-start(f32[32,16,128]{2,1,0:T(8,128)S(1)} %get-tuple-element.76), channel_id=1, source_target_pairs={{0,1},{1,0},{2,3},{3,2},{4,5},{5,4},{6,7},{7,6},{8,9},{9,8},{10,11... | collective-permute-start | bytes 786440 | tf_op jit(solution)/shard_map/ppermute | solution.py:502
  55.1 6.8 %collective-permute-start.21 = (f32[8,16,128]{2,1,0:T(8,128)S(1)}, f32[8,16,128]{2,1,0:T(8,128)S(1)}, u32[]{:S(2)}, u32[]{:S(2)}) collective-permute-start(f32[8,16,128]{2,1,0:T(8,128)S(1)} %get-tuple-element.112), channel_id=1, source_target_pairs={{0,12},{4,8},{8,4},{12,0},{1,13},{5,9},{9,5},{13,1},{2,14},{6,10},... | collective-permute-start | bytes 196616 | tf_op jit(solution)/shard_map/ppermute | solution.py:497
  57.6 6.5 %collective-permute-start.20 = (f32[8,16,128]{2,1,0:T(8,128)S(1)}, f32[8,16,128]{2,1,0:T(8,128)S(1)}, u32[]{:S(2)}, u32[]{:S(2)}) collective-permute-start(f32[8,16,128]{2,1,0:T(8,128)S(1)} %get-tuple-element.113), channel_id=1, source_target_pairs={{0,8},{4,12},{8,0},{12,4},{1,9},{5,13},{9,1},{13,5},{2,10},{6,14},... | collective-permute-start | bytes 196616 | tf_op jit(solution)/shard_map/ppermute | solution.py:497
  57.6 6.5 %collective-permute-start.19 = (f32[8,16,128]{2,1,0:T(8,128)S(1)}, f32[8,16,128]{2,1,0:T(8,128)S(1)}, u32[]{:S(2)}, u32[]{:S(2)}) collective-permute-start(f32[8,16,128]{2,1,0:T(8,128)S(1)} %get-tuple-element.114), channel_id=1, source_target_pairs={{0,4},{4,0},{8,12},{12,8},{1,5},{5,1},{9,13},{13,9},{2,6},{6,2},{1... | collective-permute-start | bytes 196616 | tf_op jit(solution)/shard_map/ppermute | solution.py:497
  64.1 5.8 %collective-permute-start.24 = (bf16[8,16,128]{2,1,0:T(8,128)(2,1)S(1)}, bf16[8,16,128]{2,1,0:T(8,128)(2,1)S(1)}, u32[]{:S(2)}, u32[]{:S(2)}) collective-permute-start(bf16[8,16,128]{2,1,0:T(8,128)(2,1)S(1)} %get-tuple-element.102), channel_id=1, source_target_pairs={{0,12},{4,8},{8,4},{12,0},{1,13},{5,9},{9,5},{13,1},{2,14},{6,10},... | collective-permute-start | bytes 98312 | tf_op jit(solution)/shard_map/ppermute | solution.py:497
  66.6 4.8 %collective-permute-start.23 = (bf16[8,16,128]{2,1,0:T(8,128)(2,1)S(1)}, bf16[8,16,128]{2,1,0:T(8,128)(2,1)S(1)}, u32[]{:S(2)}, u32[]{:S(2)}) collective-permute-start(bf16[8,16,128]{2,1,0:T(8,128)(2,1)S(1)} %get-tuple-element.102), channel_id=1, source_target_pairs={{0,8},{4,12},{8,0},{12,4},{1,9},{5,13},{9,1},{13,5},{2,10},{6,14},... | collective-permute-start | bytes 98312 | tf_op jit(solution)/shard_map/ppermute | solution.py:497
  66.6 4.8 %collective-permute-start.22 = (bf16[8,16,128]{2,1,0:T(8,128)(2,1)S(1)}, bf16[8,16,128]{2,1,0:T(8,128)(2,1)S(1)}, u32[]{:S(2)}, u32[]{:S(2)}) collective-permute-start(bf16[8,16,128]{2,1,0:T(8,128)(2,1)S(1)} %get-tuple-element.102), channel_id=1, source_target_pairs={{0,4},{4,0},{8,12},{12,8},{1,5},{5,1},{9,13},{13,9},{2,6},{6,2},{1... | collective-permute-start | bytes 98312 | tf_op jit(solution)/shard_map/ppermute | solution.py:497
  75.1 4.3 %collective-permute-start.27 = (f32[8,16,128]{2,1,0:T(8,128)S(1)}, f32[8,16,128]{2,1,0:T(8,128)S(1)}, u32[]{:S(2)}, u32[]{:S(2)}) collective-permute-start(f32[8,16,128]{2,1,0:T(8,128)S(1)} %add.118), channel_id=1, source_target_pairs={{0,2},{2,0},{1,3},{3,1},{4,6},{6,4},{5,7},{7,5},{8,10},{10,8},{9,1... | collective-permute-start | bytes 196616 | tf_op jit(solution)/shard_map/ppermute | solution.py:541
  81.6 1.6 %collective-permute-start.29 = (f32[32,16,128]{2,1,0:T(8,128)S(1)}, f32[32,16,128]{2,1,0:T(8,128)S(1)}, u32[]{:S(2)}, u32[]{:S(2)}) collective-permute-start(f32[32,16,128]{2,1,0:T(8,128)S(1)} %get-tuple-element.81), channel_id=1, source_target_pairs={{0,1},{1,0},{2,3},{3,2},{4,5},{5,4},{6,7},{7,6},{8,9},{9,8},{10,11... | collective-permute-start | bytes 786440 | tf_op jit(solution)/shard_map/ppermute | solution.py:502
  83.2 6.8 %collective-permute-start.32 = (f32[8,16,128]{2,1,0:T(8,128)S(1)}, f32[8,16,128]{2,1,0:T(8,128)S(1)}, u32[]{:S(2)}, u32[]{:S(2)}) collective-permute-start(f32[8,16,128]{2,1,0:T(8,128)S(1)} %get-tuple-element.109), channel_id=1, source_target_pairs={{0,12},{4,8},{8,4},{12,0},{1,13},{5,9},{9,5},{13,1},{2,14},{6,10},... | collective-permute-start | bytes 196616 | tf_op jit(solution)/shard_map/ppermute | solution.py:497
  85.3 7.0 %collective-permute-start.31 = (f32[8,16,128]{2,1,0:T(8,128)S(1)}, f32[8,16,128]{2,1,0:T(8,128)S(1)}, u32[]{:S(2)}, u32[]{:S(2)}) collective-permute-start(f32[8,16,128]{2,1,0:T(8,128)S(1)} %get-tuple-element.110), channel_id=1, source_target_pairs={{0,8},{4,12},{8,0},{12,4},{1,9},{5,13},{9,1},{13,5},{2,10},{6,14},... | collective-permute-start | bytes 196616 | tf_op jit(solution)/shard_map/ppermute | solution.py:497
  85.8 6.5 %collective-permute-start.30 = (f32[8,16,128]{2,1,0:T(8,128)S(1)}, f32[8,16,128]{2,1,0:T(8,128)S(1)}, u32[]{:S(2)}, u32[]{:S(2)}) collective-permute-start(f32[8,16,128]{2,1,0:T(8,128)S(1)} %get-tuple-element.111), channel_id=1, source_target_pairs={{0,4},{4,0},{8,12},{12,8},{1,5},{5,1},{9,13},{13,9},{2,6},{6,2},{1... | collective-permute-start | bytes 196616 | tf_op jit(solution)/shard_map/ppermute | solution.py:497
  92.3 5.9 %collective-permute-start.35 = (bf16[8,16,128]{2,1,0:T(8,128)(2,1)S(1)}, bf16[8,16,128]{2,1,0:T(8,128)(2,1)S(1)}, u32[]{:S(2)}, u32[]{:S(2)}) collective-permute-start(bf16[8,16,128]{2,1,0:T(8,128)(2,1)S(1)} %get-tuple-element.100), channel_id=1, source_target_pairs={{0,12},{4,8},{8,4},{12,0},{1,13},{5,9},{9,5},{13,1},{2,14},{6,10},... | collective-permute-start | bytes 98312 | tf_op jit(solution)/shard_map/ppermute | solution.py:497
  94.8 4.8 %collective-permute-start.34 = (bf16[8,16,128]{2,1,0:T(8,128)(2,1)S(1)}, bf16[8,16,128]{2,1,0:T(8,128)(2,1)S(1)}, u32[]{:S(2)}, u32[]{:S(2)}) collective-permute-start(bf16[8,16,128]{2,1,0:T(8,128)(2,1)S(1)} %get-tuple-element.100), channel_id=1, source_target_pairs={{0,8},{4,12},{8,0},{12,4},{1,9},{5,13},{9,1},{13,5},{2,10},{6,14},... | collective-permute-start | bytes 98312 | tf_op jit(solution)/shard_map/ppermute | solution.py:497
  94.8 4.8 %collective-permute-start.33 = (bf16[8,16,128]{2,1,0:T(8,128)(2,1)S(1)}, bf16[8,16,128]{2,1,0:T(8,128)(2,1)S(1)}, u32[]{:S(2)}, u32[]{:S(2)}) collective-permute-start(bf16[8,16,128]{2,1,0:T(8,128)(2,1)S(1)} %get-tuple-element.100), channel_id=1, source_target_pairs={{0,4},{4,0},{8,12},{12,8},{1,5},{5,1},{9,13},{13,9},{2,6},{6,2},{1... | collective-permute-start | bytes 98312 | tf_op jit(solution)/shard_map/ppermute | solution.py:497
  103.2 4.3 %collective-permute-start.38 = (f32[8,16,128]{2,1,0:T(8,128)S(1)}, f32[8,16,128]{2,1,0:T(8,128)S(1)}, u32[]{:S(2)}, u32[]{:S(2)}) collective-permute-start(f32[8,16,128]{2,1,0:T(8,128)S(1)} %add.126), channel_id=1, source_target_pairs={{0,2},{2,0},{1,3},{3,1},{4,6},{6,4},{5,7},{7,5},{8,10},{10,8},{9,1... | collective-permute-start | bytes 196616 | tf_op jit(solution)/shard_map/ppermute | solution.py:541
  109.6 1.6 %collective-permute-start.40 = (f32[32,16,128]{2,1,0:T(8,128)S(1)}, f32[32,16,128]{2,1,0:T(8,128)S(1)}, u32[]{:S(2)}, u32[]{:S(2)}) collective-permute-start(f32[32,16,128]{2,1,0:T(8,128)S(1)} %get-tuple-element.86), channel_id=1, source_target_pairs={{0,1},{1,0},{2,3},{3,2},{4,5},{5,4},{6,7},{7,6},{8,9},{9,8},{10,11... | collective-permute-start | bytes 786440 | tf_op jit(solution)/shard_map/ppermute | solution.py:502
  111.3 6.8 %collective-permute-start.43 = (f32[8,16,128]{2,1,0:T(8,128)S(1)}, f32[8,16,128]{2,1,0:T(8,128)S(1)}, u32[]{:S(2)}, u32[]{:S(2)}) collective-permute-start(f32[8,16,128]{2,1,0:T(8,128)S(1)} %get-tuple-element.106), channel_id=1, source_target_pairs={{0,12},{4,8},{8,4},{12,0},{1,13},{5,9},{9,5},{13,1},{2,14},{6,10},... | collective-permute-start | bytes 196616 | tf_op jit(solution)/shard_map/ppermute | solution.py:497
  113.1 7.2 %collective-permute-start.42 = (f32[8,16,128]{2,1,0:T(8,128)S(1)}, f32[8,16,128]{2,1,0:T(8,128)S(1)}, u32[]{:S(2)}, u32[]{:S(2)}) collective-permute-start(f32[8,16,128]{2,1,0:T(8,128)S(1)} %get-tuple-element.107), channel_id=1, source_target_pairs={{0,8},{4,12},{8,0},{12,4},{1,9},{5,13},{9,1},{13,5},{2,10},{6,14},... | collective-permute-start | bytes 196616 | tf_op jit(solution)/shard_map/ppermute | solution.py:497
  113.9 6.5 %collective-permute-start.41 = (f32[8,16,128]{2,1,0:T(8,128)S(1)}, f32[8,16,128]{2,1,0:T(8,128)S(1)}, u32[]{:S(2)}, u32[]{:S(2)}) collective-permute-start(f32[8,16,128]{2,1,0:T(8,128)S(1)} %get-tuple-element.108), channel_id=1, source_target_pairs={{0,4},{4,0},{8,12},{12,8},{1,5},{5,1},{9,13},{13,9},{2,6},{6,2},{1... | collective-permute-start | bytes 196616 | tf_op jit(solution)/shard_map/ppermute | solution.py:497
  (19 other events, 39.4 us)

commit v11 on v10

--- a/solution.py
+++ b/solution.py
@@ -30,7 +30,7 @@
 
 
 def cut_of(slots):
-    return 2 * slots // 3
+    return 17 * slots // 24
 
 
 def prepare_kernel(n_vox, columns, runs, steps, me, cols, exps, live, stored, *refs):
@@ -342,9 +342,9 @@
 def add_row(chosen, b, tables, left, kept, total):
     slot, places, factor = tables
     width = kept.shape[-1]
-    group = 8 if len(chosen) % 8 == 0 else 1
-    for k0 in range(0, len(chosen), group):
-        some = chosen[k0 : k0 + group]
+    size = -(-len(chosen) // max(1, len(chosen) // 8))
+    for k0 in range(0, len(chosen), size):
+        some = chosen[k0 : k0 + size]
         right = jnp.concatenate([kept[slot[b, k]] for k in some], axis=1)
         product = jnp.dot(left, right, preferred_element_type=F32)
         at = [places[b, k] for k in some]

time: 123 us -> 123 us (level)
  transfers between devices with their start and end apart: 45 -> 45, of which waited for: 33 -> 32; matrix products, arithmetic and copies ran while one was open for 0% -> 0% of each run, Pallas kernels for 19% -> 19%
where the time goes in v11:
time: 123 us
  starting transfers between devices  46 us (37%)
  waiting for transfers between devices  39.5 us (32%)
  Pallas kernels  34.2 us (28%)
  local copies, waits for them, and re-layouts  1.36 us (1%)
    ppermute x24, starting transfers between devices, over_vox(): lax.ppermute(a, 'vox', [(i, i ^ d) for i in range(n_vox)])  36.9 us
    ppermute x24, waiting for transfers between devices, over_vox(): lax.ppermute(a, 'vox', [(i, i ^ d) for i in range(n_vox)])  21.5 us
    ppermute x4, waiting for transfers between devices, per_device(): got = lax.ppermute(sent, 'spot', [(i, i ^ bit) for i in range(n_spot)])  11 us
    ppermute x17, waiting for transfers between devices, over_rep(): return lax.ppermute(array, 'rep', [(0, 1), (1, 0)])  7.04 us
    pallas_call x8, Pallas kernels, backward(): pl.pallas_call(functools.partial(backward_kernel, mine, row0), in_specs=[...  6.54 us
    ppermute x4, starting transfers between devices, per_device(): got = lax.ppermute(sent, 'spot', [(i, i ^ bit) for i in range(n_spot)])  6.19 us
    pallas_call x2, Pallas kernels, turn(): pl.pallas_call(turn_kernel, in_specs=[in_vmem(), pl.BlockSpec(memory_spac...  5.85 us
    pallas_call x6, Pallas kernels, forward(): pl.pallas_call(functools.partial(forward_kernel, row0), in_specs=[in_smem...  5.19 us
  transfers between devices with their start and end apart: 45, of which 32 were waited for; matrix products, arithmetic and copies ran while one was open for 0% of the time, Pallas kernels for 19%

profile of v11, /device:TPU:0, one launch (start us, length us, event | category | flops | bytes accessed | tf_op | source)
XLA Modules:
  0.0 123.1 jit_solution(16460039041803283500)
XLA Ops:
  1.6 5.1 %collective-permute-start.2 = (bf16[8,16,128]{2,1,0:T(8,128)(2,1)S(1)}, bf16[8,16,128]{2,1,0:T(8,128)(2,1)S(1)}, u32[]{:S(2)}, u32[]{:S(2)}) collective-permute-start(bf16[8,16,128]{2,1,0:T(8,128)(2,1)S(1)} %bitcast.49), channel_id=1, source_target_pairs={{0,12},{4,8},{8,4},{12,0},{1,13},{5,9},{9,5},{13,1},{2,14},{6,10},... | collective-permute-start | bytes 98312 | tf_op jit(solution)/shard_map/ppermute | solution.py:497
  7.4 3.9 %prepare.1 = (s32[16,24]{1,0:T(8,128)S(4)}, s32[16,24]{1,0:T(8,128)S(4)}, s32[16,24]{1,0:T(8,128)S(4)}, f32[16,24]{1,0:T(8,128)S(4)}, s32[4,128]{1,0:T(4,128)S(4...) custom-call(s32[3]{0:T(128)S(1)} %pad_add_fusion.me, s32[16,1,24]{2,1,0:T(1,128)} %cols.1, ...), custom_call_target="tpu_custom_call" | custom-call | bytes 12582912 | tf_op jit(solution)/shard_map/prepare/pallas_call | solution.py:109
  13.0 4.0 %first_forward.1 = (f32[8,16,128]{2,1,0:T(8,128)S(1)}, f32[8,16,128]{2,1,0:T(8,128)S(1)}, bf16[192,128,128]{2,1,0:T(8,128)(2,1)S(1)}) custom-call(s32[3]{0:T(128)S(4)} %get-tuple-element.46.me, s32[16,24]{1,0:T(8,128)S(4)} %get-tuple-element.47.slot, s32[16,24]{1,0:T(8,128)S(4)} %get-tuple-element.52.index, ...), custom_call_target="tpu_custom_call" | custom-call | flops 201326592 | bytes 12582912 | tf_op jit(solution)/shard_map/first_forward/pallas_call | solution.py:319
  18.3 1.6 %collective-permute-start.5 = (f32[9,16,128]{2,1,0:T(8,128)S(1)}, f32[9,16,128]{2,1,0:T(8,128)S(1)}, u32[]{:S(2)}, u32[]{:S(2)}) collective-permute-start(f32[9,16,128]{2,1,0:T(8,128)S(1)} %pad_maximum_fusion.3), channel_id=1, source_target_pairs={{0,2},{2,0},{1,3},{3,1},{4,6},{6,4},{5,7},{7,5},{8,10},{10,8},{9,1... | collective-permute-start | bytes 221192 | tf_op jit(solution)/shard_map/ppermute | solution.py:541
  20.2 2.6 %collective-permute-done.5 = f32[9,16,128]{2,1,0:T(8,128)S(1)} collective-permute-done((f32[9,16,128]{2,1,0:T(8,128)S(1)}, f32[9,16,128]{2,1,0:T(8,128)S(1)}, u32[]{:S(2)}, u32[]{:S(2)}) %collective-permute-start.5) | collective-permute-done | bytes 73760 | tf_op jit(solution)/shard_map/ppermute | solution.py:541
  26.7 3.7 %collective-permute-start.10 = (f32[8,16,128]{2,1,0:T(8,128)S(1)}, f32[8,16,128]{2,1,0:T(8,128)S(1)}, u32[]{:S(2)}, u32[]{:S(2)}) collective-permute-start(f32[8,16,128]{2,1,0:T(8,128)S(1)} %get-tuple-element.115), channel_id=1, source_target_pairs={{0,12},{4,8},{8,4},{12,0},{1,13},{5,9},{9,5},{13,1},{2,14},{6,10},... | collective-permute-start | bytes 196616 | tf_op jit(solution)/shard_map/ppermute | solution.py:497
  31.2 2.9 %turn.2.turned_mine.turned = bf16[192,128,128]{2,1,0:T(8,128)(2,1)S(1)} custom-call(bf16[192,128,128]{2,1,0:T(8,128)(2,1)S(1)} %get-tuple-element.63.kept.kept_mine, f32[32,16,128]{2,1,0:T(8,128)S(1)} %add.106.after), custom_call_target="tpu_custom_call" | custom-call | bytes 12582912 | tf_op jit(solution)/shard_map/turn/pallas_call | solution.py:141
  34.1 1.9 %collective-permute-done.9 = f32[8,16,128]{2,1,0:T(8,128)S(1)} collective-permute-done((f32[8,16,128]{2,1,0:T(8,128)S(1)}, f32[8,16,128]{2,1,0:T(8,128)S(1)}, u32[]{:S(2)}, u32[]{:S(2)}) %collective-permute-start.9) | collective-permute-done | bytes 65568 | tf_op jit(solution)/shard_map/ppermute | solution.py:497
  36.1 2.5 %collective-permute-start.13 = (bf16[8,16,128]{2,1,0:T(8,128)(2,1)S(1)}, bf16[8,16,128]{2,1,0:T(8,128)(2,1)S(1)}, u32[]{:S(2)}, u32[]{:S(2)}) collective-permute-start(bf16[8,16,128]{2,1,0:T(8,128)(2,1)S(1)} %get-tuple-element.69.after), channel_id=1, source_target_pairs={{0,12},{4,8},{8,4},{12,0},{1,13},{5,9},{9,5},{13,1},{2,14},{6,10},... | collective-permute-start | bytes 98312 | tf_op jit(solution)/shard_map/ppermute | solution.py:497
  39.0 1.6 %collective-permute-start.11 = (bf16[8,16,128]{2,1,0:T(8,128)(2,1)S(1)}, bf16[8,16,128]{2,1,0:T(8,128)(2,1)S(1)}, u32[]{:S(2)}, u32[]{:S(2)}) collective-permute-start(bf16[8,16,128]{2,1,0:T(8,128)(2,1)S(1)} %get-tuple-element.69.after), channel_id=1, source_target_pairs={{0,4},{4,0},{8,12},{12,8},{1,5},{5,1},{9,13},{13,9},{2,6},{6,2},{1... | collective-permute-start | bytes 98312 | tf_op jit(solution)/shard_map/ppermute | solution.py:497
  40.5 2.9 %turn.3.turned_others.turned = bf16[192,128,128]{2,1,0:T(8,128)(2,1)S(1)} custom-call(bf16[192,128,128]{2,1,0:T(8,128)(2,1)S(1)} %get-tuple-element.58.refs_2_.kept.kept_others, bf16[8,16,128]{2,1,0:T(8,128)(2,1)S(1)} %get-tuple-element.69.after), custom_call_target="tpu_custom_call" | custom-call | bytes 12582912 | tf_op jit(solution)/shard_map/turn/pallas_call | solution.py:141
  47.2 1.6 %collective-permute-start.16 = (f32[8,16,128]{2,1,0:T(8,128)S(1)}, f32[8,16,128]{2,1,0:T(8,128)S(1)}, u32[]{:S(2)}, u32[]{:S(2)}) collective-permute-start(f32[8,16,128]{2,1,0:T(8,128)S(1)} %add.110), channel_id=1, source_target_pairs={{0,2},{2,0},{1,3},{3,1},{4,6},{6,4},{5,7},{7,5},{8,10},{10,8},{9,1... | collective-permute-start | bytes 196616 | tf_op jit(solution)/shard_map/ppermute | solution.py:541
  48.7 2.8 %collective-permute-done.16 = f32[8,16,128]{2,1,0:T(8,128)S(1)} collective-permute-done((f32[8,16,128]{2,1,0:T(8,128)S(1)}, f32[8,16,128]{2,1,0:T(8,128)S(1)}, u32[]{:S(2)}, u32[]{:S(2)}) %collective-permute-start.16) | collective-permute-done | bytes 65568 | tf_op jit(solution)/shard_map/ppermute | solution.py:541
  55.4 2.5 %collective-permute-start.21 = (f32[8,16,128]{2,1,0:T(8,128)S(1)}, f32[8,16,128]{2,1,0:T(8,128)S(1)}, u32[]{:S(2)}, u32[]{:S(2)}) collective-permute-start(f32[8,16,128]{2,1,0:T(8,128)S(1)} %get-tuple-element.112), channel_id=1, source_target_pairs={{0,12},{4,8},{8,4},{12,0},{1,13},{5,9},{9,5},{13,1},{2,14},{6,10},... | collective-permute-start | bytes 196616 | tf_op jit(solution)/shard_map/ppermute | solution.py:497
  57.8 2.0 %collective-permute-start.19 = (f32[8,16,128]{2,1,0:T(8,128)S(1)}, f32[8,16,128]{2,1,0:T(8,128)S(1)}, u32[]{:S(2)}, u32[]{:S(2)}) collective-permute-start(f32[8,16,128]{2,1,0:T(8,128)S(1)} %get-tuple-element.114), channel_id=1, source_target_pairs={{0,4},{4,0},{8,12},{12,8},{1,5},{5,1},{9,13},{13,9},{2,6},{6,2},{1... | collective-permute-start | bytes 196616 | tf_op jit(solution)/shard_map/ppermute | solution.py:497
  59.8 2.4 %collective-permute-done.21 = f32[8,16,128]{2,1,0:T(8,128)S(1)} collective-permute-done((f32[8,16,128]{2,1,0:T(8,128)S(1)}, f32[8,16,128]{2,1,0:T(8,128)S(1)}, u32[]{:S(2)}, u32[]{:S(2)}) %collective-permute-start.21) | collective-permute-done | bytes 65568 | tf_op jit(solution)/shard_map/ppermute | solution.py:497
  62.2 2.1 %collective-permute-done.20 = f32[8,16,128]{2,1,0:T(8,128)S(1)} collective-permute-done((f32[8,16,128]{2,1,0:T(8,128)S(1)}, f32[8,16,128]{2,1,0:T(8,128)S(1)}, u32[]{:S(2)}, u32[]{:S(2)}) %collective-permute-start.20) | collective-permute-done | bytes 65568 | tf_op jit(solution)/shard_map/ppermute | solution.py:497
  64.3 2.5 %collective-permute-start.24 = (bf16[8,16,128]{2,1,0:T(8,128)(2,1)S(1)}, bf16[8,16,128]{2,1,0:T(8,128)(2,1)S(1)}, u32[]{:S(2)}, u32[]{:S(2)}) collective-permute-start(bf16[8,16,128]{2,1,0:T(8,128)(2,1)S(1)} %get-tuple-element.102), channel_id=1, source_target_pairs={{0,12},{4,8},{8,4},{12,0},{1,13},{5,9},{9,5},{13,1},{2,14},{6,10},... | collective-permute-start | bytes 98312 | tf_op jit(solution)/shard_map/ppermute | solution.py:497
  66.8 2.0 %collective-permute-start.22 = (bf16[8,16,128]{2,1,0:T(8,128)(2,1)S(1)}, bf16[8,16,128]{2,1,0:T(8,128)(2,1)S(1)}, u32[]{:S(2)}, u32[]{:S(2)}) collective-permute-start(bf16[8,16,128]{2,1,0:T(8,128)(2,1)S(1)} %get-tuple-element.102), channel_id=1, source_target_pairs={{0,4},{4,0},{8,12},{12,8},{1,5},{5,1},{9,13},{13,9},{2,6},{6,2},{1... | collective-permute-start | bytes 98312 | tf_op jit(solution)/shard_map/ppermute | solution.py:497
  75.3 1.5 %collective-permute-start.27 = (f32[8,16,128]{2,1,0:T(8,128)S(1)}, f32[8,16,128]{2,1,0:T(8,128)S(1)}, u32[]{:S(2)}, u32[]{:S(2)}) collective-permute-start(f32[8,16,128]{2,1,0:T(8,128)S(1)} %add.118), channel_id=1, source_target_pairs={{0,2},{2,0},{1,3},{3,1},{4,6},{6,4},{5,7},{7,5},{8,10},{10,8},{9,1... | collective-permute-start | bytes 196616 | tf_op jit(solution)/shard_map/ppermute | solution.py:541
  76.8 2.9 %collective-permute-done.27 = f32[8,16,128]{2,1,0:T(8,128)S(1)} collective-permute-done((f32[8,16,128]{2,1,0:T(8,128)S(1)}, f32[8,16,128]{2,1,0:T(8,128)S(1)}, u32[]{:S(2)}, u32[]{:S(2)}) %collective-permute-start.27) | collective-permute-done | bytes 65568 | tf_op jit(solution)/shard_map/ppermute | solution.py:541
  83.5 2.1 %collective-permute-start.32 = (f32[8,16,128]{2,1,0:T(8,128)S(1)}, f32[8,16,128]{2,1,0:T(8,128)S(1)}, u32[]{:S(2)}, u32[]{:S(2)}) collective-permute-start(f32[8,16,128]{2,1,0:T(8,128)S(1)} %get-tuple-element.109), channel_id=1, source_target_pairs={{0,12},{4,8},{8,4},{12,0},{1,13},{5,9},{9,5},{13,1},{2,14},{6,10},... | collective-permute-start | bytes 196616 | tf_op jit(solution)/shard_map/ppermute | solution.py:497
  86.2 1.8 %collective-permute-start.30 = (f32[8,16,128]{2,1,0:T(8,128)S(1)}, f32[8,16,128]{2,1,0:T(8,128)S(1)}, u32[]{:S(2)}, u32[]{:S(2)}) collective-permute-start(f32[8,16,128]{2,1,0:T(8,128)S(1)} %get-tuple-element.111), channel_id=1, source_target_pairs={{0,4},{4,0},{8,12},{12,8},{1,5},{5,1},{9,13},{13,9},{2,6},{6,2},{1... | collective-permute-start | bytes 196616 | tf_op jit(solution)/shard_map/ppermute | solution.py:497
  88.0 2.3 %collective-permute-done.32 = f32[8,16,128]{2,1,0:T(8,128)S(1)} collective-permute-done((f32[8,16,128]{2,1,0:T(8,128)S(1)}, f32[8,16,128]{2,1,0:T(8,128)S(1)}, u32[]{:S(2)}, u32[]{:S(2)}) %collective-permute-start.32) | collective-permute-done | bytes 65568 | tf_op jit(solution)/shard_map/ppermute | solution.py:497
  90.3 2.3 %collective-permute-done.31 = f32[8,16,128]{2,1,0:T(8,128)S(1)} collective-permute-done((f32[8,16,128]{2,1,0:T(8,128)S(1)}, f32[8,16,128]{2,1,0:T(8,128)S(1)}, u32[]{:S(2)}, u32[]{:S(2)}) %collective-permute-start.31) | collective-permute-done | bytes 65568 | tf_op jit(solution)/shard_map/ppermute | solution.py:497
  92.6 2.5 %collective-permute-start.35 = (bf16[8,16,128]{2,1,0:T(8,128)(2,1)S(1)}, bf16[8,16,128]{2,1,0:T(8,128)(2,1)S(1)}, u32[]{:S(2)}, u32[]{:S(2)}) collective-permute-start(bf16[8,16,128]{2,1,0:T(8,128)(2,1)S(1)} %get-tuple-element.100), channel_id=1, source_target_pairs={{0,12},{4,8},{8,4},{12,0},{1,13},{5,9},{9,5},{13,1},{2,14},{6,10},... | collective-permute-start | bytes 98312 | tf_op jit(solution)/shard_map/ppermute | solution.py:497
  95.1 2.0 %collective-permute-start.33 = (bf16[8,16,128]{2,1,0:T(8,128)(2,1)S(1)}, bf16[8,16,128]{2,1,0:T(8,128)(2,1)S(1)}, u32[]{:S(2)}, u32[]{:S(2)}) collective-permute-start(bf16[8,16,128]{2,1,0:T(8,128)(2,1)S(1)} %get-tuple-element.100), channel_id=1, source_target_pairs={{0,4},{4,0},{8,12},{12,8},{1,5},{5,1},{9,13},{13,9},{2,6},{6,2},{1... | collective-permute-start | bytes 98312 | tf_op jit(solution)/shard_map/ppermute | solution.py:497
  105.1 2.8 %collective-permute-done.38 = f32[8,16,128]{2,1,0:T(8,128)S(1)} collective-permute-done((f32[8,16,128]{2,1,0:T(8,128)S(1)}, f32[8,16,128]{2,1,0:T(8,128)S(1)}, u32[]{:S(2)}, u32[]{:S(2)}) %collective-permute-start.38) | collective-permute-done | bytes 65568 | tf_op jit(solution)/shard_map/ppermute | solution.py:541
  111.7 1.8 %collective-permute-start.43 = (f32[8,16,128]{2,1,0:T(8,128)S(1)}, f32[8,16,128]{2,1,0:T(8,128)S(1)}, u32[]{:S(2)}, u32[]{:S(2)}) collective-permute-start(f32[8,16,128]{2,1,0:T(8,128)S(1)} %get-tuple-element.106), channel_id=1, source_target_pairs={{0,12},{4,8},{8,4},{12,0},{1,13},{5,9},{9,5},{13,1},{2,14},{6,10},... | collective-permute-start | bytes 196616 | tf_op jit(solution)/shard_map/ppermute | solution.py:497
  114.3 1.8 %collective-permute-start.41 = (f32[8,16,128]{2,1,0:T(8,128)S(1)}, f32[8,16,128]{2,1,0:T(8,128)S(1)}, u32[]{:S(2)}, u32[]{:S(2)}) collective-permute-start(f32[8,16,128]{2,1,0:T(8,128)S(1)} %get-tuple-element.108), channel_id=1, source_target_pairs={{0,4},{4,0},{8,12},{12,8},{1,5},{5,1},{9,13},{13,9},{2,6},{6,2},{1... | collective-permute-start | bytes 196616 | tf_op jit(solution)/shard_map/ppermute | solution.py:497
  116.2 2.3 %collective-permute-done.43 = f32[8,16,128]{2,1,0:T(8,128)S(1)} collective-permute-done((f32[8,16,128]{2,1,0:T(8,128)S(1)}, f32[8,16,128]{2,1,0:T(8,128)S(1)}, u32[]{:S(2)}, u32[]{:S(2)}) %collective-permute-start.43) | collective-permute-done | bytes 65568 | tf_op jit(solution)/shard_map/ppermute | solution.py:497
  118.5 2.3 %collective-permute-done.42 = f32[8,16,128]{2,1,0:T(8,128)S(1)} collective-permute-done((f32[8,16,128]{2,1,0:T(8,128)S(1)}, f32[8,16,128]{2,1,0:T(8,128)S(1)}, u32[]{:S(2)}, u32[]{:S(2)}) %collective-permute-start.42) | collective-permute-done | bytes 65568 | tf_op jit(solution)/shard_map/ppermute | solution.py:497
  (140 shorter events, 43.1 us)
Async XLA Ops:
  1.6 9.7 %collective-permute-start.2 = (bf16[8,16,128]{2,1,0:T(8,128)(2,1)S(1)}, bf16[8,16,128]{2,1,0:T(8,128)(2,1)S(1)}, u32[]{:S(2)}, u32[]{:S(2)}) collective-permute-start(bf16[8,16,128]{2,1,0:T(8,128)(2,1)S(1)} %bitcast.49), channel_id=1, source_target_pairs={{0,12},{4,8},{8,4},{12,0},{1,13},{5,9},{9,5},{13,1},{2,14},{6,10},... | collective-permute-start | bytes 98312 | tf_op jit(solution)/shard_map/ppermute | solution.py:497
  6.7 4.8 %collective-permute-start.1 = (bf16[8,16,128]{2,1,0:T(8,128)(2,1)S(1)}, bf16[8,16,128]{2,1,0:T(8,128)(2,1)S(1)}, u32[]{:S(2)}, u32[]{:S(2)}) collective-permute-start(bf16[8,16,128]{2,1,0:T(8,128)(2,1)S(1)} %bitcast.50), channel_id=1, source_target_pairs={{0,8},{4,12},{8,0},{12,4},{1,9},{5,13},{9,1},{13,5},{2,10},{6,14},... | collective-permute-start | bytes 98312 | tf_op jit(solution)/shard_map/ppermute | solution.py:497
  6.7 4.8 %collective-permute-start = (bf16[8,16,128]{2,1,0:T(8,128)(2,1)S(1)}, bf16[8,16,128]{2,1,0:T(8,128)(2,1)S(1)}, u32[]{:S(2)}, u32[]{:S(2)}) collective-permute-start(bf16[8,16,128]{2,1,0:T(8,128)(2,1)S(1)} %bitcast.51), channel_id=1, source_target_pairs={{0,4},{4,0},{8,12},{12,8},{1,5},{5,1},{9,13},{13,9},{2,6},{6,2},{1... | collective-permute-start | bytes 98312 | tf_op jit(solution)/shard_map/ppermute | solution.py:497
  18.3 4.4 %collective-permute-start.5 = (f32[9,16,128]{2,1,0:T(8,128)S(1)}, f32[9,16,128]{2,1,0:T(8,128)S(1)}, u32[]{:S(2)}, u32[]{:S(2)}) collective-permute-start(f32[9,16,128]{2,1,0:T(8,128)S(1)} %pad_maximum_fusion.3), channel_id=1, source_target_pairs={{0,2},{2,0},{1,3},{3,1},{4,6},{6,4},{5,7},{7,5},{8,10},{10,8},{9,1... | collective-permute-start | bytes 221192 | tf_op jit(solution)/shard_map/ppermute | solution.py:541
  25.1 1.6 %collective-permute-start.7 = (f32[32,16,128]{2,1,0:T(8,128)S(1)}, f32[32,16,128]{2,1,0:T(8,128)S(1)}, u32[]{:S(2)}, u32[]{:S(2)}) collective-permute-start(f32[32,16,128]{2,1,0:T(8,128)S(1)} %get-tuple-element.65), channel_id=1, source_target_pairs={{0,1},{1,0},{2,3},{3,2},{4,5},{5,4},{6,7},{7,6},{8,9},{9,8},{10,11... | collective-permute-start | bytes 786440 | tf_op jit(solution)/shard_map/ppermute | solution.py:502
  26.7 7.4 %collective-permute-start.10 = (f32[8,16,128]{2,1,0:T(8,128)S(1)}, f32[8,16,128]{2,1,0:T(8,128)S(1)}, u32[]{:S(2)}, u32[]{:S(2)}) collective-permute-start(f32[8,16,128]{2,1,0:T(8,128)S(1)} %get-tuple-element.115), channel_id=1, source_target_pairs={{0,12},{4,8},{8,4},{12,0},{1,13},{5,9},{9,5},{13,1},{2,14},{6,10},... | collective-permute-start | bytes 196616 | tf_op jit(solution)/shard_map/ppermute | solution.py:497
  30.4 5.7 %collective-permute-start.9 = (f32[8,16,128]{2,1,0:T(8,128)S(1)}, f32[8,16,128]{2,1,0:T(8,128)S(1)}, u32[]{:S(2)}, u32[]{:S(2)}) collective-permute-start(f32[8,16,128]{2,1,0:T(8,128)S(1)} %get-tuple-element.116), channel_id=1, source_target_pairs={{0,8},{4,12},{8,0},{12,4},{1,9},{5,13},{9,1},{13,5},{2,10},{6,14},... | collective-permute-start | bytes 196616 | tf_op jit(solution)/shard_map/ppermute | solution.py:497
  30.4 5.7 %collective-permute-start.8 = (f32[8,16,128]{2,1,0:T(8,128)S(1)}, f32[8,16,128]{2,1,0:T(8,128)S(1)}, u32[]{:S(2)}, u32[]{:S(2)}) collective-permute-start(f32[8,16,128]{2,1,0:T(8,128)S(1)} %get-tuple-element.117), channel_id=1, source_target_pairs={{0,4},{4,0},{8,12},{12,8},{1,5},{5,1},{9,13},{13,9},{2,6},{6,2},{1... | collective-permute-start | bytes 196616 | tf_op jit(solution)/shard_map/ppermute | solution.py:497
  36.1 7.4 %collective-permute-start.13 = (bf16[8,16,128]{2,1,0:T(8,128)(2,1)S(1)}, bf16[8,16,128]{2,1,0:T(8,128)(2,1)S(1)}, u32[]{:S(2)}, u32[]{:S(2)}) collective-permute-start(bf16[8,16,128]{2,1,0:T(8,128)(2,1)S(1)} %get-tuple-element.69.after), channel_id=1, source_target_pairs={{0,12},{4,8},{8,4},{12,0},{1,13},{5,9},{9,5},{13,1},{2,14},{6,10},... | collective-permute-start | bytes 98312 | tf_op jit(solution)/shard_map/ppermute | solution.py:497
  38.6 4.9 %collective-permute-start.12 = (bf16[8,16,128]{2,1,0:T(8,128)(2,1)S(1)}, bf16[8,16,128]{2,1,0:T(8,128)(2,1)S(1)}, u32[]{:S(2)}, u32[]{:S(2)}) collective-permute-start(bf16[8,16,128]{2,1,0:T(8,128)(2,1)S(1)} %get-tuple-element.69.after), channel_id=1, source_target_pairs={{0,8},{4,12},{8,0},{12,4},{1,9},{5,13},{9,1},{13,5},{2,10},{6,14},... | collective-permute-start | bytes 98312 | tf_op jit(solution)/shard_map/ppermute | solution.py:497
  39.0 4.5 %collective-permute-start.11 = (bf16[8,16,128]{2,1,0:T(8,128)(2,1)S(1)}, bf16[8,16,128]{2,1,0:T(8,128)(2,1)S(1)}, u32[]{:S(2)}, u32[]{:S(2)}) collective-permute-start(bf16[8,16,128]{2,1,0:T(8,128)(2,1)S(1)} %get-tuple-element.69.after), channel_id=1, source_target_pairs={{0,4},{4,0},{8,12},{12,8},{1,5},{5,1},{9,13},{13,9},{2,6},{6,2},{1... | collective-permute-start | bytes 98312 | tf_op jit(solution)/shard_map/ppermute | solution.py:497
  47.2 4.3 %collective-permute-start.16 = (f32[8,16,128]{2,1,0:T(8,128)S(1)}, f32[8,16,128]{2,1,0:T(8,128)S(1)}, u32[]{:S(2)}, u32[]{:S(2)}) collective-permute-start(f32[8,16,128]{2,1,0:T(8,128)S(1)} %add.110), channel_id=1, source_target_pairs={{0,2},{2,0},{1,3},{3,1},{4,6},{6,4},{5,7},{7,5},{8,10},{10,8},{9,1... | collective-permute-start | bytes 196616 | tf_op jit(solution)/shard_map/ppermute | solution.py:541
  53.7 1.6 %collective-permute-start.18 = (f32[32,16,128]{2,1,0:T(8,128)S(1)}, f32[32,16,128]{2,1,0:T(8,128)S(1)}, u32[]{:S(2)}, u32[]{:S(2)}) collective-permute-start(f32[32,16,128]{2,1,0:T(8,128)S(1)} %get-tuple-element.76), channel_id=1, source_target_pairs={{0,1},{1,0},{2,3},{3,2},{4,5},{5,4},{6,7},{7,6},{8,9},{9,8},{10,11... | collective-permute-start | bytes 786440 | tf_op jit(solution)/shard_map/ppermute | solution.py:502
  55.4 6.8 %collective-permute-start.21 = (f32[8,16,128]{2,1,0:T(8,128)S(1)}, f32[8,16,128]{2,1,0:T(8,128)S(1)}, u32[]{:S(2)}, u32[]{:S(2)}) collective-permute-start(f32[8,16,128]{2,1,0:T(8,128)S(1)} %get-tuple-element.112), channel_id=1, source_target_pairs={{0,12},{4,8},{8,4},{12,0},{1,13},{5,9},{9,5},{13,1},{2,14},{6,10},... | collective-permute-start | bytes 196616 | tf_op jit(solution)/shard_map/ppermute | solution.py:497
  57.8 6.5 %collective-permute-start.20 = (f32[8,16,128]{2,1,0:T(8,128)S(1)}, f32[8,16,128]{2,1,0:T(8,128)S(1)}, u32[]{:S(2)}, u32[]{:S(2)}) collective-permute-start(f32[8,16,128]{2,1,0:T(8,128)S(1)} %get-tuple-element.113), channel_id=1, source_target_pairs={{0,8},{4,12},{8,0},{12,4},{1,9},{5,13},{9,1},{13,5},{2,10},{6,14},... | collective-permute-start | bytes 196616 | tf_op jit(solution)/shard_map/ppermute | solution.py:497
  57.8 6.5 %collective-permute-start.19 = (f32[8,16,128]{2,1,0:T(8,128)S(1)}, f32[8,16,128]{2,1,0:T(8,128)S(1)}, u32[]{:S(2)}, u32[]{:S(2)}) collective-permute-start(f32[8,16,128]{2,1,0:T(8,128)S(1)} %get-tuple-element.114), channel_id=1, source_target_pairs={{0,4},{4,0},{8,12},{12,8},{1,5},{5,1},{9,13},{13,9},{2,6},{6,2},{1... | collective-permute-start | bytes 196616 | tf_op jit(solution)/shard_map/ppermute | solution.py:497
  64.3 5.8 %collective-permute-start.24 = (bf16[8,16,128]{2,1,0:T(8,128)(2,1)S(1)}, bf16[8,16,128]{2,1,0:T(8,128)(2,1)S(1)}, u32[]{:S(2)}, u32[]{:S(2)}) collective-permute-start(bf16[8,16,128]{2,1,0:T(8,128)(2,1)S(1)} %get-tuple-element.102), channel_id=1, source_target_pairs={{0,12},{4,8},{8,4},{12,0},{1,13},{5,9},{9,5},{13,1},{2,14},{6,10},... | collective-permute-start | bytes 98312 | tf_op jit(solution)/shard_map/ppermute | solution.py:497
  66.8 4.8 %collective-permute-start.23 = (bf16[8,16,128]{2,1,0:T(8,128)(2,1)S(1)}, bf16[8,16,128]{2,1,0:T(8,128)(2,1)S(1)}, u32[]{:S(2)}, u32[]{:S(2)}) collective-permute-start(bf16[8,16,128]{2,1,0:T(8,128)(2,1)S(1)} %get-tuple-element.102), channel_id=1, source_target_pairs={{0,8},{4,12},{8,0},{12,4},{1,9},{5,13},{9,1},{13,5},{2,10},{6,14},... | collective-permute-start | bytes 98312 | tf_op jit(solution)/shard_map/ppermute | solution.py:497
  66.8 4.8 %collective-permute-start.22 = (bf16[8,16,128]{2,1,0:T(8,128)(2,1)S(1)}, bf16[8,16,128]{2,1,0:T(8,128)(2,1)S(1)}, u32[]{:S(2)}, u32[]{:S(2)}) collective-permute-start(bf16[8,16,128]{2,1,0:T(8,128)(2,1)S(1)} %get-tuple-element.102), channel_id=1, source_target_pairs={{0,4},{4,0},{8,12},{12,8},{1,5},{5,1},{9,13},{13,9},{2,6},{6,2},{1... | collective-permute-start | bytes 98312 | tf_op jit(solution)/shard_map/ppermute | solution.py:497
  75.3 4.4 %collective-permute-start.27 = (f32[8,16,128]{2,1,0:T(8,128)S(1)}, f32[8,16,128]{2,1,0:T(8,128)S(1)}, u32[]{:S(2)}, u32[]{:S(2)}) collective-permute-start(f32[8,16,128]{2,1,0:T(8,128)S(1)} %add.118), channel_id=1, source_target_pairs={{0,2},{2,0},{1,3},{3,1},{4,6},{6,4},{5,7},{7,5},{8,10},{10,8},{9,1... | collective-permute-start | bytes 196616 | tf_op jit(solution)/shard_map/ppermute | solution.py:541
  81.9 1.6 %collective-permute-start.29 = (f32[32,16,128]{2,1,0:T(8,128)S(1)}, f32[32,16,128]{2,1,0:T(8,128)S(1)}, u32[]{:S(2)}, u32[]{:S(2)}) collective-permute-start(f32[32,16,128]{2,1,0:T(8,128)S(1)} %get-tuple-element.81), channel_id=1, source_target_pairs={{0,1},{1,0},{2,3},{3,2},{4,5},{5,4},{6,7},{7,6},{8,9},{9,8},{10,11... | collective-permute-start | bytes 786440 | tf_op jit(solution)/shard_map/ppermute | solution.py:502
  83.5 6.8 %collective-permute-start.32 = (f32[8,16,128]{2,1,0:T(8,128)S(1)}, f32[8,16,128]{2,1,0:T(8,128)S(1)}, u32[]{:S(2)}, u32[]{:S(2)}) collective-permute-start(f32[8,16,128]{2,1,0:T(8,128)S(1)} %get-tuple-element.109), channel_id=1, source_target_pairs={{0,12},{4,8},{8,4},{12,0},{1,13},{5,9},{9,5},{13,1},{2,14},{6,10},... | collective-permute-start | bytes 196616 | tf_op jit(solution)/shard_map/ppermute | solution.py:497
  85.6 7.0 %collective-permute-start.31 = (f32[8,16,128]{2,1,0:T(8,128)S(1)}, f32[8,16,128]{2,1,0:T(8,128)S(1)}, u32[]{:S(2)}, u32[]{:S(2)}) collective-permute-start(f32[8,16,128]{2,1,0:T(8,128)S(1)} %get-tuple-element.110), channel_id=1, source_target_pairs={{0,8},{4,12},{8,0},{12,4},{1,9},{5,13},{9,1},{13,5},{2,10},{6,14},... | collective-permute-start | bytes 196616 | tf_op jit(solution)/shard_map/ppermute | solution.py:497
  86.2 6.5 %collective-permute-start.30 = (f32[8,16,128]{2,1,0:T(8,128)S(1)}, f32[8,16,128]{2,1,0:T(8,128)S(1)}, u32[]{:S(2)}, u32[]{:S(2)}) collective-permute-start(f32[8,16,128]{2,1,0:T(8,128)S(1)} %get-tuple-element.111), channel_id=1, source_target_pairs={{0,4},{4,0},{8,12},{12,8},{1,5},{5,1},{9,13},{13,9},{2,6},{6,2},{1... | collective-permute-start | bytes 196616 | tf_op jit(solution)/shard_map/ppermute | solution.py:497
  92.6 5.9 %collective-permute-start.35 = (bf16[8,16,128]{2,1,0:T(8,128)(2,1)S(1)}, bf16[8,16,128]{2,1,0:T(8,128)(2,1)S(1)}, u32[]{:S(2)}, u32[]{:S(2)}) collective-permute-start(bf16[8,16,128]{2,1,0:T(8,128)(2,1)S(1)} %get-tuple-element.100), channel_id=1, source_target_pairs={{0,12},{4,8},{8,4},{12,0},{1,13},{5,9},{9,5},{13,1},{2,14},{6,10},... | collective-permute-start | bytes 98312 | tf_op jit(solution)/shard_map/ppermute | solution.py:497
  95.1 4.8 %collective-permute-start.34 = (bf16[8,16,128]{2,1,0:T(8,128)(2,1)S(1)}, bf16[8,16,128]{2,1,0:T(8,128)(2,1)S(1)}, u32[]{:S(2)}, u32[]{:S(2)}) collective-permute-start(bf16[8,16,128]{2,1,0:T(8,128)(2,1)S(1)} %get-tuple-element.100), channel_id=1, source_target_pairs={{0,8},{4,12},{8,0},{12,4},{1,9},{5,13},{9,1},{13,5},{2,10},{6,14},... | collective-permute-start | bytes 98312 | tf_op jit(solution)/shard_map/ppermute | solution.py:497
  95.1 4.8 %collective-permute-start.33 = (bf16[8,16,128]{2,1,0:T(8,128)(2,1)S(1)}, bf16[8,16,128]{2,1,0:T(8,128)(2,1)S(1)}, u32[]{:S(2)}, u32[]{:S(2)}) collective-permute-start(bf16[8,16,128]{2,1,0:T(8,128)(2,1)S(1)} %get-tuple-element.100), channel_id=1, source_target_pairs={{0,4},{4,0},{8,12},{12,8},{1,5},{5,1},{9,13},{13,9},{2,6},{6,2},{1... | collective-permute-start | bytes 98312 | tf_op jit(solution)/shard_map/ppermute | solution.py:497
  103.6 4.3 %collective-permute-start.38 = (f32[8,16,128]{2,1,0:T(8,128)S(1)}, f32[8,16,128]{2,1,0:T(8,128)S(1)}, u32[]{:S(2)}, u32[]{:S(2)}) collective-permute-start(f32[8,16,128]{2,1,0:T(8,128)S(1)} %add.126), channel_id=1, source_target_pairs={{0,2},{2,0},{1,3},{3,1},{4,6},{6,4},{5,7},{7,5},{8,10},{10,8},{9,1... | collective-permute-start | bytes 196616 | tf_op jit(solution)/shard_map/ppermute | solution.py:541
  110.1 1.6 %collective-permute-start.40 = (f32[32,16,128]{2,1,0:T(8,128)S(1)}, f32[32,16,128]{2,1,0:T(8,128)S(1)}, u32[]{:S(2)}, u32[]{:S(2)}) collective-permute-start(f32[32,16,128]{2,1,0:T(8,128)S(1)} %get-tuple-element.86), channel_id=1, source_target_pairs={{0,1},{1,0},{2,3},{3,2},{4,5},{5,4},{6,7},{7,6},{8,9},{9,8},{10,11... | collective-permute-start | bytes 786440 | tf_op jit(solution)/shard_map/ppermute | solution.py:502
  111.7 6.8 %collective-permute-start.43 = (f32[8,16,128]{2,1,0:T(8,128)S(1)}, f32[8,16,128]{2,1,0:T(8,128)S(1)}, u32[]{:S(2)}, u32[]{:S(2)}) collective-permute-start(f32[8,16,128]{2,1,0:T(8,128)S(1)} %get-tuple-element.106), channel_id=1, source_target_pairs={{0,12},{4,8},{8,4},{12,0},{1,13},{5,9},{9,5},{13,1},{2,14},{6,10},... | collective-permute-start | bytes 196616 | tf_op jit(solution)/shard_map/ppermute | solution.py:497
  113.6 7.2 %collective-permute-start.42 = (f32[8,16,128]{2,1,0:T(8,128)S(1)}, f32[8,16,128]{2,1,0:T(8,128)S(1)}, u32[]{:S(2)}, u32[]{:S(2)}) collective-permute-start(f32[8,16,128]{2,1,0:T(8,128)S(1)} %get-tuple-element.107), channel_id=1, source_target_pairs={{0,8},{4,12},{8,0},{12,4},{1,9},{5,13},{9,1},{13,5},{2,10},{6,14},... | collective-permute-start | bytes 196616 | tf_op jit(solution)/shard_map/ppermute | solution.py:497
  114.3 6.5 %collective-permute-start.41 = (f32[8,16,128]{2,1,0:T(8,128)S(1)}, f32[8,16,128]{2,1,0:T(8,128)S(1)}, u32[]{:S(2)}, u32[]{:S(2)}) collective-permute-start(f32[8,16,128]{2,1,0:T(8,128)S(1)} %get-tuple-element.108), channel_id=1, source_target_pairs={{0,4},{4,0},{8,12},{12,8},{1,5},{5,1},{9,13},{13,9},{2,6},{6,2},{1... | collective-permute-start | bytes 196616 | tf_op jit(solution)/shard_map/ppermute | solution.py:497
  (19 other events, 39.4 us)

commit v12 on v11

--- a/solution.py
+++ b/solution.py
@@ -29,8 +29,8 @@
 LONG_RUN = 8
 
 
-def cut_of(slots):
-    return 17 * slots // 24
+def cut_of(slots, mine):
+    return (18 if mine else 17) * slots // 24
 
 
 def prepare_kernel(n_vox, columns, runs, steps, me, cols, exps, live, stored, *refs):
@@ -86,7 +86,7 @@
     for r in range(rows // RUN):
         most = jnp.max(others[r * RUN : (r + 1) * RUN], axis=0, keepdims=True)
         most = jnp.broadcast_to(most, (1, over.shape[1]))
-        over[r : r + 1] = jnp.where(most > cut_of(slots), 1, 0)
+        over[r : r + 1] = jnp.where(most > cut_of(slots, 2 * r * RUN < rows), 1, 0)
     copies = [
         pltpu.make_async_copy(table, out, sems.at[i])
         for i, (table, out) in enumerate(zip(tables, outs, strict=True))
@@ -222,10 +222,11 @@
 def near_forward_kernel(slot, index, over, near, turned_mine, turned_others, dose, scaled):
     scale_weights([near], scaled)
     rows, slots = slot.shape
-    last = range(cut_of(slots), slots)
     for turned, row0 in ((turned_mine, 0), (turned_others, rows // 2)):
 
-        def run(t, carry, turned=turned, row0=row0):
+        last = range(cut_of(slots, row0 == 0), slots)
+
+        def run(t, carry, turned=turned, row0=row0, last=last):
             b0 = row0 + t * RUN
             skip = over[b0 // RUN, 0] > 0
 
@@ -247,7 +248,7 @@
 def forward_kernel(row0, slot, index, over, near, far, turned, part, dose, scaled):
     scale_weights([near, far], scaled)
     slots = slot.shape[1]
-    cut = cut_of(slots)
+    cut = cut_of(slots, row0 == 0)
     rows = dose.shape[0]
     step = LONG_RUN if rows % LONG_RUN == 0 else RUN
 
@@ -290,7 +291,7 @@
         out_shape=jax.ShapeDtypeStruct((rows, weightings, width), F32),
         scratch_shapes=[pltpu.VMEM((6 * half + 1, weightings, width), BF16)],
         compiler_params=PARAMS,
-        cost_estimate=work_of(rows, slots - cut_of(slots), weightings, width),
+        cost_estimate=work_of(rows, slots - cut_of(slots, True), weightings, width),
         name="near_forward",
     )(*tables[:2], tables[4], near, held(turned_mine), held(turned_others))
 
@@ -305,7 +306,7 @@
         out_shape=jax.ShapeDtypeStruct((rows // 2, weightings, width), F32),
         scratch_shapes=[pltpu.VMEM((6 * half + 1, weightings, width), BF16)],
         compiler_params=PARAMS,
-        cost_estimate=work_of(rows // 2, cut_of(slots), weightings, width),
+        cost_estimate=work_of(rows // 2, cut_of(slots, True), weightings, width),
         name="forward",
     )(*tables[:2], tables[4], near, far, held(turned), part)
 
@@ -360,7 +361,7 @@
     total[:columns] = jnp.zeros_like(total[:columns]) if mine else before.pop(0)[...]
     tables = (slot, places, factor)
     slots = slot.shape[1]
-    cut = cut_of(slots)
+    cut = cut_of(slots, mine)
 
     rows = slope.shape[0]
     step = LONG_RUN if rows % LONG_RUN == 0 else RUN
@@ -399,10 +400,11 @@
     total[2 * half :] = jnp.zeros_like(total[2 * half :])
     tables = (slot, places, factor)
     rows, slots = slot.shape
-    last = range(cut_of(slots), slots)
     for slope, kept, row0 in ((slope_mine, kept_mine, 0), (slope_others, kept_others, rows // 2)):
 
-        def run(t, carry, slope=slope, kept=kept, row0=row0):
+        last = range(cut_of(slots, row0 == 0), slots)
+
+        def run(t, carry, slope=slope, kept=kept, row0=row0, last=last):
             b0 = row0 + t * RUN
 
             @pl.when(over[b0 // RUN, 0] == 0)
@@ -427,7 +429,7 @@
         out_shape=[jax.ShapeDtypeStruct(shape, F32) for shape in out],
         scratch_shapes=[pltpu.VMEM((columns + slots, weightings, width), F32)],
         compiler_params=PARAMS,
-        cost_estimate=work_of(half_rows, cut_of(slots), weightings, width),
+        cost_estimate=work_of(half_rows, cut_of(slots, True), weightings, width),
         name="backward",
     )(tables[0], *tables[2:], slope, held(kept), *total)
 
@@ -442,7 +444,7 @@
         out_shape=jax.ShapeDtypeStruct(near.shape, F32),
         scratch_shapes=[pltpu.VMEM((2 * half + slots, weightings, width), F32)],
         compiler_params=PARAMS,
-        cost_estimate=work_of(rows, slots - cut_of(slots), weightings, width),
+        cost_estimate=work_of(rows, slots - cut_of(slots, True), weightings, width),
         name="near_backward",
     )(tables[0], *tables[2:], slope_mine, slope_others, held(kept_mine), held(kept_others), near)
 

time: 123 us -> 123 us (level)
  no operation moved by 1% of the time
where the time goes in v12:
time: 123 us
  starting transfers between devices  46 us (37%)
  waiting for transfers between devices  39.6 us (32%)
  Pallas kernels  34.1 us (28%)
  local copies, waits for them, and re-layouts  1.36 us (1%)
    ppermute x24, starting transfers between devices, over_vox(): lax.ppermute(a, 'vox', [(i, i ^ d) for i in range(n_vox)])  36.9 us
    ppermute x24, waiting for transfers between devices, over_vox(): lax.ppermute(a, 'vox', [(i, i ^ d) for i in range(n_vox)])  21.5 us
    ppermute x4, waiting for transfers between devices, per_device(): got = lax.ppermute(sent, 'spot', [(i, i ^ bit) for i in range(n_spot)])  11 us
    ppermute x17, waiting for transfers between devices, over_rep(): return lax.ppermute(array, 'rep', [(0, 1), (1, 0)])  7.13 us
    pallas_call x8, Pallas kernels, backward(): pl.pallas_call(functools.partial(backward_kernel, mine, row0), in_specs=[...  6.81 us
    ppermute x4, starting transfers between devices, per_device(): got = lax.ppermute(sent, 'spot', [(i, i ^ bit) for i in range(n_spot)])  6.23 us
    pallas_call x2, Pallas kernels, turn(): pl.pallas_call(turn_kernel, in_specs=[in_vmem(), pl.BlockSpec(memory_spac...  5.85 us
    pallas_call x6, Pallas kernels, forward(): pl.pallas_call(functools.partial(forward_kernel, row0), in_specs=[in_smem...  5.23 us
  transfers between devices with their start and end apart: 45, of which 32 were waited for; matrix products, arithmetic and copies ran while one was open for 0% of the time, Pallas kernels for 19%

profile of v12, /device:TPU:0, one launch (start us, length us, event | category | flops | bytes accessed | tf_op | source)
XLA Modules:
  0.0 123.0 jit_solution(1381137628815300106)
XLA Ops:
  1.6 5.1 %collective-permute-start.2 = (bf16[8,16,128]{2,1,0:T(8,128)(2,1)S(1)}, bf16[8,16,128]{2,1,0:T(8,128)(2,1)S(1)}, u32[]{:S(2)}, u32[]{:S(2)}) collective-permute-start(bf16[8,16,128]{2,1,0:T(8,128)(2,1)S(1)} %bitcast.49), channel_id=1, source_target_pairs={{0,12},{4,8},{8,4},{12,0},{1,13},{5,9},{9,5},{13,1},{2,14},{6,10},... | collective-permute-start | bytes 98312 | tf_op jit(solution)/shard_map/ppermute | solution.py:499
  7.4 3.9 %prepare.1 = (s32[16,24]{1,0:T(8,128)S(4)}, s32[16,24]{1,0:T(8,128)S(4)}, s32[16,24]{1,0:T(8,128)S(4)}, f32[16,24]{1,0:T(8,128)S(4)}, s32[4,128]{1,0:T(4,128)S(4...) custom-call(s32[3]{0:T(128)S(1)} %pad_add_fusion.me, s32[16,1,24]{2,1,0:T(1,128)} %cols.1, ...), custom_call_target="tpu_custom_call" | custom-call | bytes 12582912 | tf_op jit(solution)/shard_map/prepare/pallas_call | solution.py:109
  13.0 4.0 %first_forward.1 = (f32[8,16,128]{2,1,0:T(8,128)S(1)}, f32[8,16,128]{2,1,0:T(8,128)S(1)}, bf16[192,128,128]{2,1,0:T(8,128)(2,1)S(1)}) custom-call(s32[3]{0:T(128)S(4)} %get-tuple-element.46.me, s32[16,24]{1,0:T(8,128)S(4)} %get-tuple-element.47.slot, s32[16,24]{1,0:T(8,128)S(4)} %get-tuple-element.52.index, ...), custom_call_target="tpu_custom_call" | custom-call | flops 201326592 | bytes 12582912 | tf_op jit(solution)/shard_map/first_forward/pallas_call | solution.py:320
  18.3 1.6 %collective-permute-start.5 = (f32[9,16,128]{2,1,0:T(8,128)S(1)}, f32[9,16,128]{2,1,0:T(8,128)S(1)}, u32[]{:S(2)}, u32[]{:S(2)}) collective-permute-start(f32[9,16,128]{2,1,0:T(8,128)S(1)} %pad_maximum_fusion.3), channel_id=1, source_target_pairs={{0,2},{2,0},{1,3},{3,1},{4,6},{6,4},{5,7},{7,5},{8,10},{10,8},{9,1... | collective-permute-start | bytes 221192 | tf_op jit(solution)/shard_map/ppermute | solution.py:543
  20.2 2.6 %collective-permute-done.5 = f32[9,16,128]{2,1,0:T(8,128)S(1)} collective-permute-done((f32[9,16,128]{2,1,0:T(8,128)S(1)}, f32[9,16,128]{2,1,0:T(8,128)S(1)}, u32[]{:S(2)}, u32[]{:S(2)}) %collective-permute-start.5) | collective-permute-done | bytes 73760 | tf_op jit(solution)/shard_map/ppermute | solution.py:543
  26.7 3.7 %collective-permute-start.10 = (f32[8,16,128]{2,1,0:T(8,128)S(1)}, f32[8,16,128]{2,1,0:T(8,128)S(1)}, u32[]{:S(2)}, u32[]{:S(2)}) collective-permute-start(f32[8,16,128]{2,1,0:T(8,128)S(1)} %get-tuple-element.115), channel_id=1, source_target_pairs={{0,12},{4,8},{8,4},{12,0},{1,13},{5,9},{9,5},{13,1},{2,14},{6,10},... | collective-permute-start | bytes 196616 | tf_op jit(solution)/shard_map/ppermute | solution.py:499
  31.2 2.9 %turn.2.turned_mine.turned = bf16[192,128,128]{2,1,0:T(8,128)(2,1)S(1)} custom-call(bf16[192,128,128]{2,1,0:T(8,128)(2,1)S(1)} %get-tuple-element.63.kept.kept_mine, f32[32,16,128]{2,1,0:T(8,128)S(1)} %add.106.after), custom_call_target="tpu_custom_call" | custom-call | bytes 12582912 | tf_op jit(solution)/shard_map/turn/pallas_call | solution.py:141
  34.1 1.9 %collective-permute-done.9 = f32[8,16,128]{2,1,0:T(8,128)S(1)} collective-permute-done((f32[8,16,128]{2,1,0:T(8,128)S(1)}, f32[8,16,128]{2,1,0:T(8,128)S(1)}, u32[]{:S(2)}, u32[]{:S(2)}) %collective-permute-start.9) | collective-permute-done | bytes 65568 | tf_op jit(solution)/shard_map/ppermute | solution.py:499
  36.1 2.5 %collective-permute-start.13 = (bf16[8,16,128]{2,1,0:T(8,128)(2,1)S(1)}, bf16[8,16,128]{2,1,0:T(8,128)(2,1)S(1)}, u32[]{:S(2)}, u32[]{:S(2)}) collective-permute-start(bf16[8,16,128]{2,1,0:T(8,128)(2,1)S(1)} %get-tuple-element.69.after), channel_id=1, source_target_pairs={{0,12},{4,8},{8,4},{12,0},{1,13},{5,9},{9,5},{13,1},{2,14},{6,10},... | collective-permute-start | bytes 98312 | tf_op jit(solution)/shard_map/ppermute | solution.py:499
  40.5 2.9 %turn.3.turned_others.turned = bf16[192,128,128]{2,1,0:T(8,128)(2,1)S(1)} custom-call(bf16[192,128,128]{2,1,0:T(8,128)(2,1)S(1)} %get-tuple-element.58.refs_2_.kept.kept_others, bf16[8,16,128]{2,1,0:T(8,128)(2,1)S(1)} %get-tuple-element.69.after), custom_call_target="tpu_custom_call" | custom-call | bytes 12582912 | tf_op jit(solution)/shard_map/turn/pallas_call | solution.py:141
  47.2 1.6 %collective-permute-start.16 = (f32[8,16,128]{2,1,0:T(8,128)S(1)}, f32[8,16,128]{2,1,0:T(8,128)S(1)}, u32[]{:S(2)}, u32[]{:S(2)}) collective-permute-start(f32[8,16,128]{2,1,0:T(8,128)S(1)} %add.110), channel_id=1, source_target_pairs={{0,2},{2,0},{1,3},{3,1},{4,6},{6,4},{5,7},{7,5},{8,10},{10,8},{9,1... | collective-permute-start | bytes 196616 | tf_op jit(solution)/shard_map/ppermute | solution.py:543
  48.8 2.8 %collective-permute-done.16 = f32[8,16,128]{2,1,0:T(8,128)S(1)} collective-permute-done((f32[8,16,128]{2,1,0:T(8,128)S(1)}, f32[8,16,128]{2,1,0:T(8,128)S(1)}, u32[]{:S(2)}, u32[]{:S(2)}) %collective-permute-start.16) | collective-permute-done | bytes 65568 | tf_op jit(solution)/shard_map/ppermute | solution.py:543
  55.3 2.5 %collective-permute-start.21 = (f32[8,16,128]{2,1,0:T(8,128)S(1)}, f32[8,16,128]{2,1,0:T(8,128)S(1)}, u32[]{:S(2)}, u32[]{:S(2)}) collective-permute-start(f32[8,16,128]{2,1,0:T(8,128)S(1)} %get-tuple-element.112), channel_id=1, source_target_pairs={{0,12},{4,8},{8,4},{12,0},{1,13},{5,9},{9,5},{13,1},{2,14},{6,10},... | collective-permute-start | bytes 196616 | tf_op jit(solution)/shard_map/ppermute | solution.py:499
  57.8 2.0 %collective-permute-start.19 = (f32[8,16,128]{2,1,0:T(8,128)S(1)}, f32[8,16,128]{2,1,0:T(8,128)S(1)}, u32[]{:S(2)}, u32[]{:S(2)}) collective-permute-start(f32[8,16,128]{2,1,0:T(8,128)S(1)} %get-tuple-element.114), channel_id=1, source_target_pairs={{0,4},{4,0},{8,12},{12,8},{1,5},{5,1},{9,13},{13,9},{2,6},{6,2},{1... | collective-permute-start | bytes 196616 | tf_op jit(solution)/shard_map/ppermute | solution.py:499
  59.8 2.4 %collective-permute-done.21 = f32[8,16,128]{2,1,0:T(8,128)S(1)} collective-permute-done((f32[8,16,128]{2,1,0:T(8,128)S(1)}, f32[8,16,128]{2,1,0:T(8,128)S(1)}, u32[]{:S(2)}, u32[]{:S(2)}) %collective-permute-start.21) | collective-permute-done | bytes 65568 | tf_op jit(solution)/shard_map/ppermute | solution.py:499
  62.2 2.0 %collective-permute-done.20 = f32[8,16,128]{2,1,0:T(8,128)S(1)} collective-permute-done((f32[8,16,128]{2,1,0:T(8,128)S(1)}, f32[8,16,128]{2,1,0:T(8,128)S(1)}, u32[]{:S(2)}, u32[]{:S(2)}) %collective-permute-start.20) | collective-permute-done | bytes 65568 | tf_op jit(solution)/shard_map/ppermute | solution.py:499
  64.3 2.5 %collective-permute-start.24 = (bf16[8,16,128]{2,1,0:T(8,128)(2,1)S(1)}, bf16[8,16,128]{2,1,0:T(8,128)(2,1)S(1)}, u32[]{:S(2)}, u32[]{:S(2)}) collective-permute-start(bf16[8,16,128]{2,1,0:T(8,128)(2,1)S(1)} %get-tuple-element.102), channel_id=1, source_target_pairs={{0,12},{4,8},{8,4},{12,0},{1,13},{5,9},{9,5},{13,1},{2,14},{6,10},... | collective-permute-start | bytes 98312 | tf_op jit(solution)/shard_map/ppermute | solution.py:499
  66.8 2.0 %collective-permute-start.22 = (bf16[8,16,128]{2,1,0:T(8,128)(2,1)S(1)}, bf16[8,16,128]{2,1,0:T(8,128)(2,1)S(1)}, u32[]{:S(2)}, u32[]{:S(2)}) collective-permute-start(bf16[8,16,128]{2,1,0:T(8,128)(2,1)S(1)} %get-tuple-element.102), channel_id=1, source_target_pairs={{0,4},{4,0},{8,12},{12,8},{1,5},{5,1},{9,13},{13,9},{2,6},{6,2},{1... | collective-permute-start | bytes 98312 | tf_op jit(solution)/shard_map/ppermute | solution.py:499
  75.3 1.6 %collective-permute-start.27 = (f32[8,16,128]{2,1,0:T(8,128)S(1)}, f32[8,16,128]{2,1,0:T(8,128)S(1)}, u32[]{:S(2)}, u32[]{:S(2)}) collective-permute-start(f32[8,16,128]{2,1,0:T(8,128)S(1)} %add.118), channel_id=1, source_target_pairs={{0,2},{2,0},{1,3},{3,1},{4,6},{6,4},{5,7},{7,5},{8,10},{10,8},{9,1... | collective-permute-start | bytes 196616 | tf_op jit(solution)/shard_map/ppermute | solution.py:543
  76.8 2.9 %collective-permute-done.27 = f32[8,16,128]{2,1,0:T(8,128)S(1)} collective-permute-done((f32[8,16,128]{2,1,0:T(8,128)S(1)}, f32[8,16,128]{2,1,0:T(8,128)S(1)}, u32[]{:S(2)}, u32[]{:S(2)}) %collective-permute-start.27) | collective-permute-done | bytes 65568 | tf_op jit(solution)/shard_map/ppermute | solution.py:543
  83.5 2.0 %collective-permute-start.32 = (f32[8,16,128]{2,1,0:T(8,128)S(1)}, f32[8,16,128]{2,1,0:T(8,128)S(1)}, u32[]{:S(2)}, u32[]{:S(2)}) collective-permute-start(f32[8,16,128]{2,1,0:T(8,128)S(1)} %get-tuple-element.109), channel_id=1, source_target_pairs={{0,12},{4,8},{8,4},{12,0},{1,13},{5,9},{9,5},{13,1},{2,14},{6,10},... | collective-permute-start | bytes 196616 | tf_op jit(solution)/shard_map/ppermute | solution.py:499
  86.1 1.9 %collective-permute-start.30 = (f32[8,16,128]{2,1,0:T(8,128)S(1)}, f32[8,16,128]{2,1,0:T(8,128)S(1)}, u32[]{:S(2)}, u32[]{:S(2)}) collective-permute-start(f32[8,16,128]{2,1,0:T(8,128)S(1)} %get-tuple-element.111), channel_id=1, source_target_pairs={{0,4},{4,0},{8,12},{12,8},{1,5},{5,1},{9,13},{13,9},{2,6},{6,2},{1... | collective-permute-start | bytes 196616 | tf_op jit(solution)/shard_map/ppermute | solution.py:499
  87.9 2.3 %collective-permute-done.32 = f32[8,16,128]{2,1,0:T(8,128)S(1)} collective-permute-done((f32[8,16,128]{2,1,0:T(8,128)S(1)}, f32[8,16,128]{2,1,0:T(8,128)S(1)}, u32[]{:S(2)}, u32[]{:S(2)}) %collective-permute-start.32) | collective-permute-done | bytes 65568 | tf_op jit(solution)/shard_map/ppermute | solution.py:499
  90.3 2.2 %collective-permute-done.31 = f32[8,16,128]{2,1,0:T(8,128)S(1)} collective-permute-done((f32[8,16,128]{2,1,0:T(8,128)S(1)}, f32[8,16,128]{2,1,0:T(8,128)S(1)}, u32[]{:S(2)}, u32[]{:S(2)}) %collective-permute-start.31) | collective-permute-done | bytes 65568 | tf_op jit(solution)/shard_map/ppermute | solution.py:499
  92.6 2.5 %collective-permute-start.35 = (bf16[8,16,128]{2,1,0:T(8,128)(2,1)S(1)}, bf16[8,16,128]{2,1,0:T(8,128)(2,1)S(1)}, u32[]{:S(2)}, u32[]{:S(2)}) collective-permute-start(bf16[8,16,128]{2,1,0:T(8,128)(2,1)S(1)} %get-tuple-element.100), channel_id=1, source_target_pairs={{0,12},{4,8},{8,4},{12,0},{1,13},{5,9},{9,5},{13,1},{2,14},{6,10},... | collective-permute-start | bytes 98312 | tf_op jit(solution)/shard_map/ppermute | solution.py:499
  95.1 2.0 %collective-permute-start.33 = (bf16[8,16,128]{2,1,0:T(8,128)(2,1)S(1)}, bf16[8,16,128]{2,1,0:T(8,128)(2,1)S(1)}, u32[]{:S(2)}, u32[]{:S(2)}) collective-permute-start(bf16[8,16,128]{2,1,0:T(8,128)(2,1)S(1)} %get-tuple-element.100), channel_id=1, source_target_pairs={{0,4},{4,0},{8,12},{12,8},{1,5},{5,1},{9,13},{13,9},{2,6},{6,2},{1... | collective-permute-start | bytes 98312 | tf_op jit(solution)/shard_map/ppermute | solution.py:499
  103.5 1.6 %collective-permute-start.38 = (f32[8,16,128]{2,1,0:T(8,128)S(1)}, f32[8,16,128]{2,1,0:T(8,128)S(1)}, u32[]{:S(2)}, u32[]{:S(2)}) collective-permute-start(f32[8,16,128]{2,1,0:T(8,128)S(1)} %add.126), channel_id=1, source_target_pairs={{0,2},{2,0},{1,3},{3,1},{4,6},{6,4},{5,7},{7,5},{8,10},{10,8},{9,1... | collective-permute-start | bytes 196616 | tf_op jit(solution)/shard_map/ppermute | solution.py:543
  105.1 2.8 %collective-permute-done.38 = f32[8,16,128]{2,1,0:T(8,128)S(1)} collective-permute-done((f32[8,16,128]{2,1,0:T(8,128)S(1)}, f32[8,16,128]{2,1,0:T(8,128)S(1)}, u32[]{:S(2)}, u32[]{:S(2)}) %collective-permute-start.38) | collective-permute-done | bytes 65568 | tf_op jit(solution)/shard_map/ppermute | solution.py:543
  111.7 1.8 %collective-permute-start.43 = (f32[8,16,128]{2,1,0:T(8,128)S(1)}, f32[8,16,128]{2,1,0:T(8,128)S(1)}, u32[]{:S(2)}, u32[]{:S(2)}) collective-permute-start(f32[8,16,128]{2,1,0:T(8,128)S(1)} %get-tuple-element.106), channel_id=1, source_target_pairs={{0,12},{4,8},{8,4},{12,0},{1,13},{5,9},{9,5},{13,1},{2,14},{6,10},... | collective-permute-start | bytes 196616 | tf_op jit(solution)/shard_map/ppermute | solution.py:499
  114.3 1.9 %collective-permute-start.41 = (f32[8,16,128]{2,1,0:T(8,128)S(1)}, f32[8,16,128]{2,1,0:T(8,128)S(1)}, u32[]{:S(2)}, u32[]{:S(2)}) collective-permute-start(f32[8,16,128]{2,1,0:T(8,128)S(1)} %get-tuple-element.108), channel_id=1, source_target_pairs={{0,4},{4,0},{8,12},{12,8},{1,5},{5,1},{9,13},{13,9},{2,6},{6,2},{1... | collective-permute-start | bytes 196616 | tf_op jit(solution)/shard_map/ppermute | solution.py:499
  116.1 2.3 %collective-permute-done.43 = f32[8,16,128]{2,1,0:T(8,128)S(1)} collective-permute-done((f32[8,16,128]{2,1,0:T(8,128)S(1)}, f32[8,16,128]{2,1,0:T(8,128)S(1)}, u32[]{:S(2)}, u32[]{:S(2)}) %collective-permute-start.43) | collective-permute-done | bytes 65568 | tf_op jit(solution)/shard_map/ppermute | solution.py:499
  118.5 2.3 %collective-permute-done.42 = f32[8,16,128]{2,1,0:T(8,128)S(1)} collective-permute-done((f32[8,16,128]{2,1,0:T(8,128)S(1)}, f32[8,16,128]{2,1,0:T(8,128)S(1)}, u32[]{:S(2)}, u32[]{:S(2)}) %collective-permute-start.42) | collective-permute-done | bytes 65568 | tf_op jit(solution)/shard_map/ppermute | solution.py:499
  (140 shorter events, 43.2 us)
Async XLA Ops:
  1.6 9.7 %collective-permute-start.2 = (bf16[8,16,128]{2,1,0:T(8,128)(2,1)S(1)}, bf16[8,16,128]{2,1,0:T(8,128)(2,1)S(1)}, u32[]{:S(2)}, u32[]{:S(2)}) collective-permute-start(bf16[8,16,128]{2,1,0:T(8,128)(2,1)S(1)} %bitcast.49), channel_id=1, source_target_pairs={{0,12},{4,8},{8,4},{12,0},{1,13},{5,9},{9,5},{13,1},{2,14},{6,10},... | collective-permute-start | bytes 98312 | tf_op jit(solution)/shard_map/ppermute | solution.py:499
  6.7 4.8 %collective-permute-start.1 = (bf16[8,16,128]{2,1,0:T(8,128)(2,1)S(1)}, bf16[8,16,128]{2,1,0:T(8,128)(2,1)S(1)}, u32[]{:S(2)}, u32[]{:S(2)}) collective-permute-start(bf16[8,16,128]{2,1,0:T(8,128)(2,1)S(1)} %bitcast.50), channel_id=1, source_target_pairs={{0,8},{4,12},{8,0},{12,4},{1,9},{5,13},{9,1},{13,5},{2,10},{6,14},... | collective-permute-start | bytes 98312 | tf_op jit(solution)/shard_map/ppermute | solution.py:499
  6.7 4.8 %collective-permute-start = (bf16[8,16,128]{2,1,0:T(8,128)(2,1)S(1)}, bf16[8,16,128]{2,1,0:T(8,128)(2,1)S(1)}, u32[]{:S(2)}, u32[]{:S(2)}) collective-permute-start(bf16[8,16,128]{2,1,0:T(8,128)(2,1)S(1)} %bitcast.51), channel_id=1, source_target_pairs={{0,4},{4,0},{8,12},{12,8},{1,5},{5,1},{9,13},{13,9},{2,6},{6,2},{1... | collective-permute-start | bytes 98312 | tf_op jit(solution)/shard_map/ppermute | solution.py:499
  18.3 4.4 %collective-permute-start.5 = (f32[9,16,128]{2,1,0:T(8,128)S(1)}, f32[9,16,128]{2,1,0:T(8,128)S(1)}, u32[]{:S(2)}, u32[]{:S(2)}) collective-permute-start(f32[9,16,128]{2,1,0:T(8,128)S(1)} %pad_maximum_fusion.3), channel_id=1, source_target_pairs={{0,2},{2,0},{1,3},{3,1},{4,6},{6,4},{5,7},{7,5},{8,10},{10,8},{9,1... | collective-permute-start | bytes 221192 | tf_op jit(solution)/shard_map/ppermute | solution.py:543
  25.1 1.6 %collective-permute-start.7 = (f32[32,16,128]{2,1,0:T(8,128)S(1)}, f32[32,16,128]{2,1,0:T(8,128)S(1)}, u32[]{:S(2)}, u32[]{:S(2)}) collective-permute-start(f32[32,16,128]{2,1,0:T(8,128)S(1)} %get-tuple-element.65), channel_id=1, source_target_pairs={{0,1},{1,0},{2,3},{3,2},{4,5},{5,4},{6,7},{7,6},{8,9},{9,8},{10,11... | collective-permute-start | bytes 786440 | tf_op jit(solution)/shard_map/ppermute | solution.py:504
  26.7 7.4 %collective-permute-start.10 = (f32[8,16,128]{2,1,0:T(8,128)S(1)}, f32[8,16,128]{2,1,0:T(8,128)S(1)}, u32[]{:S(2)}, u32[]{:S(2)}) collective-permute-start(f32[8,16,128]{2,1,0:T(8,128)S(1)} %get-tuple-element.115), channel_id=1, source_target_pairs={{0,12},{4,8},{8,4},{12,0},{1,13},{5,9},{9,5},{13,1},{2,14},{6,10},... | collective-permute-start | bytes 196616 | tf_op jit(solution)/shard_map/ppermute | solution.py:499
  30.4 5.7 %collective-permute-start.9 = (f32[8,16,128]{2,1,0:T(8,128)S(1)}, f32[8,16,128]{2,1,0:T(8,128)S(1)}, u32[]{:S(2)}, u32[]{:S(2)}) collective-permute-start(f32[8,16,128]{2,1,0:T(8,128)S(1)} %get-tuple-element.116), channel_id=1, source_target_pairs={{0,8},{4,12},{8,0},{12,4},{1,9},{5,13},{9,1},{13,5},{2,10},{6,14},... | collective-permute-start | bytes 196616 | tf_op jit(solution)/shard_map/ppermute | solution.py:499
  30.4 5.7 %collective-permute-start.8 = (f32[8,16,128]{2,1,0:T(8,128)S(1)}, f32[8,16,128]{2,1,0:T(8,128)S(1)}, u32[]{:S(2)}, u32[]{:S(2)}) collective-permute-start(f32[8,16,128]{2,1,0:T(8,128)S(1)} %get-tuple-element.117), channel_id=1, source_target_pairs={{0,4},{4,0},{8,12},{12,8},{1,5},{5,1},{9,13},{13,9},{2,6},{6,2},{1... | collective-permute-start | bytes 196616 | tf_op jit(solution)/shard_map/ppermute | solution.py:499
  36.1 7.4 %collective-permute-start.13 = (bf16[8,16,128]{2,1,0:T(8,128)(2,1)S(1)}, bf16[8,16,128]{2,1,0:T(8,128)(2,1)S(1)}, u32[]{:S(2)}, u32[]{:S(2)}) collective-permute-start(bf16[8,16,128]{2,1,0:T(8,128)(2,1)S(1)} %get-tuple-element.69.after), channel_id=1, source_target_pairs={{0,12},{4,8},{8,4},{12,0},{1,13},{5,9},{9,5},{13,1},{2,14},{6,10},... | collective-permute-start | bytes 98312 | tf_op jit(solution)/shard_map/ppermute | solution.py:499
  38.6 4.9 %collective-permute-start.12 = (bf16[8,16,128]{2,1,0:T(8,128)(2,1)S(1)}, bf16[8,16,128]{2,1,0:T(8,128)(2,1)S(1)}, u32[]{:S(2)}, u32[]{:S(2)}) collective-permute-start(bf16[8,16,128]{2,1,0:T(8,128)(2,1)S(1)} %get-tuple-element.69.after), channel_id=1, source_target_pairs={{0,8},{4,12},{8,0},{12,4},{1,9},{5,13},{9,1},{13,5},{2,10},{6,14},... | collective-permute-start | bytes 98312 | tf_op jit(solution)/shard_map/ppermute | solution.py:499
  39.0 4.5 %collective-permute-start.11 = (bf16[8,16,128]{2,1,0:T(8,128)(2,1)S(1)}, bf16[8,16,128]{2,1,0:T(8,128)(2,1)S(1)}, u32[]{:S(2)}, u32[]{:S(2)}) collective-permute-start(bf16[8,16,128]{2,1,0:T(8,128)(2,1)S(1)} %get-tuple-element.69.after), channel_id=1, source_target_pairs={{0,4},{4,0},{8,12},{12,8},{1,5},{5,1},{9,13},{13,9},{2,6},{6,2},{1... | collective-permute-start | bytes 98312 | tf_op jit(solution)/shard_map/ppermute | solution.py:499
  47.2 4.3 %collective-permute-start.16 = (f32[8,16,128]{2,1,0:T(8,128)S(1)}, f32[8,16,128]{2,1,0:T(8,128)S(1)}, u32[]{:S(2)}, u32[]{:S(2)}) collective-permute-start(f32[8,16,128]{2,1,0:T(8,128)S(1)} %add.110), channel_id=1, source_target_pairs={{0,2},{2,0},{1,3},{3,1},{4,6},{6,4},{5,7},{7,5},{8,10},{10,8},{9,1... | collective-permute-start | bytes 196616 | tf_op jit(solution)/shard_map/ppermute | solution.py:543
  53.7 1.6 %collective-permute-start.18 = (f32[32,16,128]{2,1,0:T(8,128)S(1)}, f32[32,16,128]{2,1,0:T(8,128)S(1)}, u32[]{:S(2)}, u32[]{:S(2)}) collective-permute-start(f32[32,16,128]{2,1,0:T(8,128)S(1)} %get-tuple-element.76), channel_id=1, source_target_pairs={{0,1},{1,0},{2,3},{3,2},{4,5},{5,4},{6,7},{7,6},{8,9},{9,8},{10,11... | collective-permute-start | bytes 786440 | tf_op jit(solution)/shard_map/ppermute | solution.py:504
  55.3 6.9 %collective-permute-start.21 = (f32[8,16,128]{2,1,0:T(8,128)S(1)}, f32[8,16,128]{2,1,0:T(8,128)S(1)}, u32[]{:S(2)}, u32[]{:S(2)}) collective-permute-start(f32[8,16,128]{2,1,0:T(8,128)S(1)} %get-tuple-element.112), channel_id=1, source_target_pairs={{0,12},{4,8},{8,4},{12,0},{1,13},{5,9},{9,5},{13,1},{2,14},{6,10},... | collective-permute-start | bytes 196616 | tf_op jit(solution)/shard_map/ppermute | solution.py:499
  57.8 6.4 %collective-permute-start.20 = (f32[8,16,128]{2,1,0:T(8,128)S(1)}, f32[8,16,128]{2,1,0:T(8,128)S(1)}, u32[]{:S(2)}, u32[]{:S(2)}) collective-permute-start(f32[8,16,128]{2,1,0:T(8,128)S(1)} %get-tuple-element.113), channel_id=1, source_target_pairs={{0,8},{4,12},{8,0},{12,4},{1,9},{5,13},{9,1},{13,5},{2,10},{6,14},... | collective-permute-start | bytes 196616 | tf_op jit(solution)/shard_map/ppermute | solution.py:499
  57.8 6.4 %collective-permute-start.19 = (f32[8,16,128]{2,1,0:T(8,128)S(1)}, f32[8,16,128]{2,1,0:T(8,128)S(1)}, u32[]{:S(2)}, u32[]{:S(2)}) collective-permute-start(f32[8,16,128]{2,1,0:T(8,128)S(1)} %get-tuple-element.114), channel_id=1, source_target_pairs={{0,4},{4,0},{8,12},{12,8},{1,5},{5,1},{9,13},{13,9},{2,6},{6,2},{1... | collective-permute-start | bytes 196616 | tf_op jit(solution)/shard_map/ppermute | solution.py:499
  64.3 5.8 %collective-permute-start.24 = (bf16[8,16,128]{2,1,0:T(8,128)(2,1)S(1)}, bf16[8,16,128]{2,1,0:T(8,128)(2,1)S(1)}, u32[]{:S(2)}, u32[]{:S(2)}) collective-permute-start(bf16[8,16,128]{2,1,0:T(8,128)(2,1)S(1)} %get-tuple-element.102), channel_id=1, source_target_pairs={{0,12},{4,8},{8,4},{12,0},{1,13},{5,9},{9,5},{13,1},{2,14},{6,10},... | collective-permute-start | bytes 98312 | tf_op jit(solution)/shard_map/ppermute | solution.py:499
  66.8 4.8 %collective-permute-start.23 = (bf16[8,16,128]{2,1,0:T(8,128)(2,1)S(1)}, bf16[8,16,128]{2,1,0:T(8,128)(2,1)S(1)}, u32[]{:S(2)}, u32[]{:S(2)}) collective-permute-start(bf16[8,16,128]{2,1,0:T(8,128)(2,1)S(1)} %get-tuple-element.102), channel_id=1, source_target_pairs={{0,8},{4,12},{8,0},{12,4},{1,9},{5,13},{9,1},{13,5},{2,10},{6,14},... | collective-permute-start | bytes 98312 | tf_op jit(solution)/shard_map/ppermute | solution.py:499
  66.8 4.8 %collective-permute-start.22 = (bf16[8,16,128]{2,1,0:T(8,128)(2,1)S(1)}, bf16[8,16,128]{2,1,0:T(8,128)(2,1)S(1)}, u32[]{:S(2)}, u32[]{:S(2)}) collective-permute-start(bf16[8,16,128]{2,1,0:T(8,128)(2,1)S(1)} %get-tuple-element.102), channel_id=1, source_target_pairs={{0,4},{4,0},{8,12},{12,8},{1,5},{5,1},{9,13},{13,9},{2,6},{6,2},{1... | collective-permute-start | bytes 98312 | tf_op jit(solution)/shard_map/ppermute | solution.py:499
  75.3 4.4 %collective-permute-start.27 = (f32[8,16,128]{2,1,0:T(8,128)S(1)}, f32[8,16,128]{2,1,0:T(8,128)S(1)}, u32[]{:S(2)}, u32[]{:S(2)}) collective-permute-start(f32[8,16,128]{2,1,0:T(8,128)S(1)} %add.118), channel_id=1, source_target_pairs={{0,2},{2,0},{1,3},{3,1},{4,6},{6,4},{5,7},{7,5},{8,10},{10,8},{9,1... | collective-permute-start | bytes 196616 | tf_op jit(solution)/shard_map/ppermute | solution.py:543
  81.8 1.6 %collective-permute-start.29 = (f32[32,16,128]{2,1,0:T(8,128)S(1)}, f32[32,16,128]{2,1,0:T(8,128)S(1)}, u32[]{:S(2)}, u32[]{:S(2)}) collective-permute-start(f32[32,16,128]{2,1,0:T(8,128)S(1)} %get-tuple-element.81), channel_id=1, source_target_pairs={{0,1},{1,0},{2,3},{3,2},{4,5},{5,4},{6,7},{7,6},{8,9},{9,8},{10,11... | collective-permute-start | bytes 786440 | tf_op jit(solution)/shard_map/ppermute | solution.py:504
  83.5 6.8 %collective-permute-start.32 = (f32[8,16,128]{2,1,0:T(8,128)S(1)}, f32[8,16,128]{2,1,0:T(8,128)S(1)}, u32[]{:S(2)}, u32[]{:S(2)}) collective-permute-start(f32[8,16,128]{2,1,0:T(8,128)S(1)} %get-tuple-element.109), channel_id=1, source_target_pairs={{0,12},{4,8},{8,4},{12,0},{1,13},{5,9},{9,5},{13,1},{2,14},{6,10},... | collective-permute-start | bytes 196616 | tf_op jit(solution)/shard_map/ppermute | solution.py:499
  85.4 7.1 %collective-permute-start.31 = (f32[8,16,128]{2,1,0:T(8,128)S(1)}, f32[8,16,128]{2,1,0:T(8,128)S(1)}, u32[]{:S(2)}, u32[]{:S(2)}) collective-permute-start(f32[8,16,128]{2,1,0:T(8,128)S(1)} %get-tuple-element.110), channel_id=1, source_target_pairs={{0,8},{4,12},{8,0},{12,4},{1,9},{5,13},{9,1},{13,5},{2,10},{6,14},... | collective-permute-start | bytes 196616 | tf_op jit(solution)/shard_map/ppermute | solution.py:499
  86.1 6.5 %collective-permute-start.30 = (f32[8,16,128]{2,1,0:T(8,128)S(1)}, f32[8,16,128]{2,1,0:T(8,128)S(1)}, u32[]{:S(2)}, u32[]{:S(2)}) collective-permute-start(f32[8,16,128]{2,1,0:T(8,128)S(1)} %get-tuple-element.111), channel_id=1, source_target_pairs={{0,4},{4,0},{8,12},{12,8},{1,5},{5,1},{9,13},{13,9},{2,6},{6,2},{1... | collective-permute-start | bytes 196616 | tf_op jit(solution)/shard_map/ppermute | solution.py:499
  92.6 5.8 %collective-permute-start.35 = (bf16[8,16,128]{2,1,0:T(8,128)(2,1)S(1)}, bf16[8,16,128]{2,1,0:T(8,128)(2,1)S(1)}, u32[]{:S(2)}, u32[]{:S(2)}) collective-permute-start(bf16[8,16,128]{2,1,0:T(8,128)(2,1)S(1)} %get-tuple-element.100), channel_id=1, source_target_pairs={{0,12},{4,8},{8,4},{12,0},{1,13},{5,9},{9,5},{13,1},{2,14},{6,10},... | collective-permute-start | bytes 98312 | tf_op jit(solution)/shard_map/ppermute | solution.py:499
  95.0 4.8 %collective-permute-start.34 = (bf16[8,16,128]{2,1,0:T(8,128)(2,1)S(1)}, bf16[8,16,128]{2,1,0:T(8,128)(2,1)S(1)}, u32[]{:S(2)}, u32[]{:S(2)}) collective-permute-start(bf16[8,16,128]{2,1,0:T(8,128)(2,1)S(1)} %get-tuple-element.100), channel_id=1, source_target_pairs={{0,8},{4,12},{8,0},{12,4},{1,9},{5,13},{9,1},{13,5},{2,10},{6,14},... | collective-permute-start | bytes 98312 | tf_op jit(solution)/shard_map/ppermute | solution.py:499
  95.1 4.8 %collective-permute-start.33 = (bf16[8,16,128]{2,1,0:T(8,128)(2,1)S(1)}, bf16[8,16,128]{2,1,0:T(8,128)(2,1)S(1)}, u32[]{:S(2)}, u32[]{:S(2)}) collective-permute-start(bf16[8,16,128]{2,1,0:T(8,128)(2,1)S(1)} %get-tuple-element.100), channel_id=1, source_target_pairs={{0,4},{4,0},{8,12},{12,8},{1,5},{5,1},{9,13},{13,9},{2,6},{6,2},{1... | collective-permute-start | bytes 98312 | tf_op jit(solution)/shard_map/ppermute | solution.py:499
  103.5 4.3 %collective-permute-start.38 = (f32[8,16,128]{2,1,0:T(8,128)S(1)}, f32[8,16,128]{2,1,0:T(8,128)S(1)}, u32[]{:S(2)}, u32[]{:S(2)}) collective-permute-start(f32[8,16,128]{2,1,0:T(8,128)S(1)} %add.126), channel_id=1, source_target_pairs={{0,2},{2,0},{1,3},{3,1},{4,6},{6,4},{5,7},{7,5},{8,10},{10,8},{9,1... | collective-permute-start | bytes 196616 | tf_op jit(solution)/shard_map/ppermute | solution.py:543
  110.0 1.6 %collective-permute-start.40 = (f32[32,16,128]{2,1,0:T(8,128)S(1)}, f32[32,16,128]{2,1,0:T(8,128)S(1)}, u32[]{:S(2)}, u32[]{:S(2)}) collective-permute-start(f32[32,16,128]{2,1,0:T(8,128)S(1)} %get-tuple-element.86), channel_id=1, source_target_pairs={{0,1},{1,0},{2,3},{3,2},{4,5},{5,4},{6,7},{7,6},{8,9},{9,8},{10,11... | collective-permute-start | bytes 786440 | tf_op jit(solution)/shard_map/ppermute | solution.py:504
  111.7 6.8 %collective-permute-start.43 = (f32[8,16,128]{2,1,0:T(8,128)S(1)}, f32[8,16,128]{2,1,0:T(8,128)S(1)}, u32[]{:S(2)}, u32[]{:S(2)}) collective-permute-start(f32[8,16,128]{2,1,0:T(8,128)S(1)} %get-tuple-element.106), channel_id=1, source_target_pairs={{0,12},{4,8},{8,4},{12,0},{1,13},{5,9},{9,5},{13,1},{2,14},{6,10},... | collective-permute-start | bytes 196616 | tf_op jit(solution)/shard_map/ppermute | solution.py:499
  113.5 7.2 %collective-permute-start.42 = (f32[8,16,128]{2,1,0:T(8,128)S(1)}, f32[8,16,128]{2,1,0:T(8,128)S(1)}, u32[]{:S(2)}, u32[]{:S(2)}) collective-permute-start(f32[8,16,128]{2,1,0:T(8,128)S(1)} %get-tuple-element.107), channel_id=1, source_target_pairs={{0,8},{4,12},{8,0},{12,4},{1,9},{5,13},{9,1},{13,5},{2,10},{6,14},... | collective-permute-start | bytes 196616 | tf_op jit(solution)/shard_map/ppermute | solution.py:499
  114.3 6.5 %collective-permute-start.41 = (f32[8,16,128]{2,1,0:T(8,128)S(1)}, f32[8,16,128]{2,1,0:T(8,128)S(1)}, u32[]{:S(2)}, u32[]{:S(2)}) collective-permute-start(f32[8,16,128]{2,1,0:T(8,128)S(1)} %get-tuple-element.108), channel_id=1, source_target_pairs={{0,4},{4,0},{8,12},{12,8},{1,5},{5,1},{9,13},{13,9},{2,6},{6,2},{1... | collective-permute-start | bytes 196616 | tf_op jit(solution)/shard_map/ppermute | solution.py:499
  (19 other events, 39.4 us)
